TPU v7x, 128 devices: a whole 4x4x4 slice. The times are simulated.
128 devices in a mesh: expert: 4 (over x), zero: 32 (over z, y, core).
Axes of the slice: x: 4, y: 4, z: 4, core: 2. Of those that a mesh axis runs over, the one named last changes fastest.
Arguments:
- tokens: bfloat16 [16384, 1024], P(('expert', 'zero')), may hold values from -6 to 6
- grads_out: bfloat16 [16384, 1024], P(('expert', 'zero')), may hold values from -1.1953125 to 1.1953125
- routes: int32 [16384, 2], P(('expert', 'zero')), may hold values from 0 to 3, as said below
- slots: int32 [16384, 2], P(('expert', 'zero')), may hold values from 0 to 64, as said below
- combine: bfloat16 [16384, 2], P(('expert', 'zero')), may hold values from 0.049804688 to 1
- w_in: bfloat16 [4, 1024, 4096], P('expert', None, 'zero'), may hold values from -0.1875 to 0.1875
- b_in: bfloat16 [4, 4096], P('expert', 'zero'), may hold values from -3 to 3
- w_out: bfloat16 [4, 4096, 1024], P('expert', 'zero'), may hold values from -0.09375 to 0.09375
- b_out: bfloat16 [4, 1024], P('expert'), may hold values from -0.59765625 to 0.59765625
Outputs:
- grad_tokens: bfloat16 [16384, 1024], P(('expert', 'zero'))
- grad_combine: float32 [16384, 2], P(('expert', 'zero'))
- grad_w_in: bfloat16 [4, 1024, 4096], P('expert', None, 'zero')
- grad_b_in: float32 [4, 4096], P('expert', 'zero')
- grad_w_out: bfloat16 [4, 4096, 1024], P('expert', 'zero')
- grad_b_out: float32 [4, 1024], P('expert')
Inputs may be any that keep to these rules, and one draw needn't show every extreme that they name: `routes`: each row names 2 different experts. Within the rows of one device (aligned blocks of 128 rows), the choices that name one expert, taken in order of row and then of column, hold the slots 0, 1, 2 and so on; once 64 of them are taken, every further such choice holds 64 and is dropped.
All inputs are finite; a program needn't handle non-finite values.
Results may differ from a plain program's by a relative error of at most 0.0065.
Values may be sent and summed in bfloat16 or wider, within the bound.
No kernel may reach another device: no remote copies, remote signals or barrier semaphores. Data moves between devices by JAX's collectives and lax.ppermute only.
A program may use at most 128 MiB of HBM per device.

v0:
```python
import jax
import jax.numpy as jnp
from jax import lax
from jax.sharding import PartitionSpec as P

TOP = 2


def gelu_parts(pre):
    cdf = 0.5 * (1.0 + lax.erf(pre * 0.7071067811865476))
    dens = jnp.exp(-0.5 * pre * pre) * 0.3989422804014327
    return (pre * cdf, cdf + pre * dens)


def forward_back(rows_x, rows_g, rows_c, weight_in, bias_in, weight_out):
    pre = (
        jnp.dot(rows_x, weight_in, preferred_element_type=jnp.float32)
        + bias_in.astype(jnp.float32)[None, :]
    )
    hidden32, slope = gelu_parts(pre)
    back = jnp.einsum("rd,fd->rf", rows_g, weight_out, preferred_element_type=jnp.float32)
    weight = rows_c.astype(jnp.float32)[:, None]
    inner = jnp.sum(hidden32 * back, axis=1)
    dout = (weight * rows_g.astype(jnp.float32)).astype(jnp.bfloat16)
    dpre = (weight * back * slope).astype(jnp.bfloat16)
    return (hidden32.astype(jnp.bfloat16), inner, dout, dpre)


def group_partials(left, right, groups):
    left_g = left.reshape(groups, -1, left.shape[1])
    right_g = right.reshape(groups, -1, right.shape[1])
    parts = jnp.einsum("nra,nrb->nab", left_g, right_g, preferred_element_type=jnp.float32).astype(
        jnp.bfloat16
    )
    parts = lax.optimization_barrier(parts)
    return jnp.sum(parts.astype(jnp.float32), axis=0).astype(jnp.bfloat16)


def on_device(tokens, grads_out, routes, slots, combine, w_in, b_in, w_out, b_out):
    n_expert = lax.axis_size("expert")
    n_zero = lax.axis_size("zero")
    tok_rows = tokens.shape[0]
    cap_rows = TOP * tok_rows // n_expert
    width = n_expert * cap_rows
    spots = jnp.arange(width, dtype=jnp.int32)
    places = jnp.where(slots < cap_rows, routes * cap_rows + slots, -1)
    picks = (places[:, :, None] == spots[None, None, :]).astype(jnp.bfloat16)
    both = picks[:, 0] + picks[:, 1]
    send_x = jnp.einsum("tp,td->pd", both, tokens, preferred_element_type=jnp.float32).astype(
        jnp.bfloat16
    )
    send_g = jnp.einsum("tp,td->pd", both, grads_out, preferred_element_type=jnp.float32).astype(
        jnp.bfloat16
    )
    send_c = jnp.einsum("tkp,tk->p", picks, combine, preferred_element_type=jnp.float32).astype(
        jnp.bfloat16
    )
    got_x, got_g, got_c = (
        lax.all_to_all(
            send_x.reshape(n_expert, cap_rows, -1),
            "expert",
            split_axis=0,
            concat_axis=0,
            tiled=True,
        ),
        lax.all_to_all(
            send_g.reshape(n_expert, cap_rows, -1),
            "expert",
            split_axis=0,
            concat_axis=0,
            tiled=True,
        ),
        lax.all_to_all(
            send_c.reshape(n_expert, cap_rows), "expert", split_axis=0, concat_axis=0, tiled=True
        ),
    )
    rows_x = got_x.reshape(width, -1)
    rows_g = got_g.reshape(width, -1)
    rows_c = got_c.reshape(width)
    bias_out = b_out[0].astype(jnp.float32)
    full_in, full_out, full_bias = (
        lax.all_gather(w_in, "zero", axis=2, tiled=True),
        lax.all_gather(w_out, "zero", axis=1, tiled=True),
        lax.all_gather(b_in, "zero", axis=1, tiled=True),
    )
    hidden, inner, dout, dpre = forward_back(
        rows_x, rows_g, rows_c, full_in[0], full_bias[0], full_out[0]
    )
    slot_dx = jnp.einsum("rf,df->rd", dpre, full_in[0], preferred_element_type=jnp.float32)
    slot_dc = inner + jnp.sum(rows_g.astype(jnp.float32) * bias_out[None, :], axis=1)
    all_hidden, all_dpre = (
        lax.all_to_all(hidden, "zero", split_axis=1, concat_axis=0, tiled=True),
        lax.all_to_all(dpre, "zero", split_axis=1, concat_axis=0, tiled=True),
    )
    all_x, all_dout = (
        lax.all_gather(rows_x, "zero", axis=0, tiled=True),
        lax.all_gather(dout, "zero", axis=0, tiled=True),
    )
    grad_w_in = group_partials(all_x, all_dpre, n_zero)[None]
    grad_w_out = group_partials(all_hidden, all_dout, n_zero)[None]
    grad_b_in = jnp.sum(all_dpre.astype(jnp.float32), axis=0)[None]
    grad_b_out = jnp.sum(all_dout.astype(jnp.float32), axis=0)[None]
    back_dx, back_dc = (
        lax.all_to_all(
            slot_dx.reshape(n_expert, cap_rows, -1),
            "expert",
            split_axis=0,
            concat_axis=0,
            tiled=True,
        ),
        lax.all_to_all(
            slot_dc.reshape(n_expert, cap_rows), "expert", split_axis=0, concat_axis=0, tiled=True
        ),
    )
    picks_wide = picks.astype(jnp.float32)
    grad_tokens = jnp.dot(
        picks_wide[:, 0] + picks_wide[:, 1],
        back_dx.reshape(width, -1),
        precision=lax.Precision.HIGHEST,
    ).astype(jnp.bfloat16)
    grad_combine = jnp.einsum(
        "tkp,p->tk", picks_wide, back_dc.reshape(width), precision=lax.Precision.HIGHEST
    )
    return (grad_tokens, grad_combine, grad_w_in, grad_b_in, grad_w_out, grad_b_out)


def solution(mesh):
    in_specs = (
        P(("expert", "zero"), None),
        P(("expert", "zero"), None),
        P(("expert", "zero"), None),
        P(("expert", "zero"), None),
        P(("expert", "zero"), None),
        P("expert", None, "zero"),
        P("expert", "zero"),
        P("expert", "zero", None),
        P("expert", None),
    )
    out_specs = (
        P(("expert", "zero"), None),
        P(("expert", "zero"), None),
        P("expert", None, "zero"),
        P("expert", "zero"),
        P("expert", "zero", None),
        P("expert", None),
    )
    return jax.shard_map(
        on_device, mesh=mesh, in_specs=in_specs, out_specs=out_specs, check_vma=False
    )
```

profile of v0, /device:TPU:0, one launch (start us, length us, event | category | flops | bytes accessed | tf_op | source)
XLA Modules:
  0.0 350.7 jit_solution(14206522954558377646)
XLA Ops:
  7.2 0.0 copy-start
  7.2 0.0 copy-start.6
  7.2 0.0 copy-start.5
  7.2 0.0 all-gather.7.cloned.1.call-start
  7.3 0.7 all-gather.7.cloned.1.call-update
  7.9 0.0 all-gather.5.cloned.1.call-start
  8.0 0.7 all-gather.5.cloned.1.call-update
  8.7 0.0 all-gather.9.cloned.1.call-start
  8.7 0.7 compare_select_fusion
  9.4 0.8 fusion.26
  10.2 0.0 copy-done
  10.2 0.3 convolution_convert_fusion.2
  10.6 13.8 %all_to_all.63 = bf16[4,64,1024]{2,1,0:T(8,128)(2,1)} all-to-all(bf16[4,64,1024]{2,1,0:T(8,128)(2,1)S(1)} %bitcast.71), channel_id=1, replica_groups=mesh['expert'=4,'zero'=32] {'expert'}, dimensions={0} | all-to-all | bytes 1048576 | tf_op jit(solution)/shard_map/all_to_all | solution.py:59
  24.3 0.0 copy-start.3
  24.3 0.0 all-gather.9.cloned.1.call-update
  24.4 0.9 fusion.18
  25.3 0.7 all_to_all.55
  26.0 3.2 all-to-all-start
  29.2 2.1 convolution_convert_fusion.3
  31.3 3.1 all-to-all-done
  34.3 3.5 all-to-all-start.1
  37.8 0.0 all-gather.11.cloned.1.call-start
  37.9 0.1 reshape.100
  38.0 7.9 %all-to-all-done.1 = bf16[4,64,1024]{2,1,0:T(8,128)(2,1)S(1)} async-done(((bf16[4,64,1024]{2,1,0:T(8,128)(2,1)}), bf16[4,64,1024]{2,1,0:T(8,128)(2,1)S(1)}, u32[]{:S(2)}, u32[]{:S(2)}) %all-to-all-start.1) | async-done | bytes 524320 | tf_op jit(solution)/shard_map/all_to_all | solution.py:66
  45.9 0.9 multiply_convert_fusion.1
  46.8 0.0 all-gather.11.cloned.1.call-update
  46.8 0.0 copy-done.6
  46.8 22.9 %all_gather.17 = bf16[1,4096]{1,0:T(2,128)(2,1)S(1)} all-gather(bf16[1,128]{1,0:T(2,128)(2,1)S(1)} %copy-done.6), channel_id=1, replica_groups=mesh['expert'=4,'zero'=32] {'zero'}, dimensions={1}, use_global_device_ids=true | all-gather | bytes 8448 | tf_op jit(solution)/shard_map/all_gather | solution.py:84
  69.8 0.0 copy-done.5
  69.8 0.2 multiply_reduce_fusion.1
  70.0 2.5 all-gather.7.cloned.1.call-done
  72.4 0.0 copy-done.3
  72.4 7.8 %fusion.6 = f32[256,4096]{1,0:T(8,128)} fusion(bf16[256,1024]{1,0:T(8,128)(2,1)S(1)} %bitcast.70, bf16[1,1024,4096]{2,1,0:T(8,128)(2,1)} %all-gather.7.cloned.1.call-done, f32[4096]{0:T(1024)S(1)} %bitcast.75), kind=kOutput, calls=%fused_computation.10 | convolution fusion | flops 2148532224 | bytes 13123584 | tf_op jit(solution)/shard_map/dot_general | solution.py:17
  80.2 47.1 %all-gather.5.cloned.1.call-done = bf16[1,4096,1024]{2,1,0:T(8,128)(2,1)} async-done(((bf16[1,128,1024]{2,1,0:T(8,128)(2,1)}), bf16[1,4096,1024]{2,1,0:T(8,128)(2,1)}) %all-gather.5.cloned.1.call-update) | async-done | bytes 8388624 | tf_op jit(solution)/shard_map/all_gather | solution.py:83
  127.3 8.0 %multiply_reduce_fusion = (f32[256]{0:T(256)S(1)}, bf16[256,4096]{1,0:T(8,128)(2,1)S(1)}, bf16[256,4096]{1,0:T(8,128)(2,1)}) fusion(f32[256,4096]{1,0:T(8,128)} %fusion.6, f32[256]{0:T(256)S(1)} %reshape.100, bf16[256,1024]{1,0:T(8,128)(2,1)S(1)} %bitcast.66, bf16[1,4096,1024]{2,1,0:T(8,128)(2,1)} %all-gather.5.cloned.1.call-done), kind=kOutput, calls=%fused_computation.18 | convolution fusion | flops 2163212032 | bytes 17303552 | tf_op jit(solution)/shard_map/rd,fd->rf/dot_general | solution.py:21
  135.3 0.1 reduce_sum.65
  135.4 0.7 add.60
  136.1 4.2 %all-to-all-start.4 = ((f32[4,1,64]{2,1,0:T(1,128)}), f32[4,1,64]{2,1,0:T(1,128)S(1)}, u32[]{:S(2)}, u32[]{:S(2)}) async-start(f32[4,1,64]{2,1,0:T(1,128)} %add.60), calls=%async_computation.4 | async-start | bytes 4096 | tf_op jit(solution)/shard_map/all_to_all | solution.py:111
  140.3 6.7 %fusion = f32[4,64,1024]{2,1,0:T(8,128)} fusion(bf16[4,64,4096]{2,1,0:T(8,128)(2,1)S(1)} %bitcast.68, bf16[1,1024,4096]{2,1,0:T(8,128)(2,1)} %all-gather.7.cloned.1.call-done), kind=kOutput, calls=%fused_computation.1 | convolution fusion | flops 2147483648 | bytes 11534336 | tf_op jit(solution)/shard_map/rf,df->rd/dot_general | solution.py:89
  147.0 0.0 copy-done.2
  147.0 0.0 all-to-all-done.4
  147.0 4.8 %all-to-all-start.3 = ((f32[4,64,1024]{2,1,0:T(8,128)}), f32[4,64,1024]{2,1,0:T(8,128)S(1)}, u32[]{:S(2)}, u32[]{:S(2)}) async-start(f32[4,64,1024]{2,1,0:T(8,128)} %fusion), calls=%async_computation.3 | async-start | bytes 2097152 | tf_op jit(solution)/shard_map/all_to_all | solution.py:104
  151.8 3.6 %copy_bitcast_fusion = bf16[256,32,128]{2,0,1:T(8,128)(2,1)} fusion(bf16[256,4096]{1,0:T(8,128)(2,1)} %copy-done.2), kind=kLoop, calls=%fused_computation.20 | loop fusion | bytes 4194304 | tf_op jit(solution)/shard_map/all_to_all | solution.py:93
  155.4 11.4 %all-to-all-done.3 = f32[4,64,1024]{2,1,0:T(8,128)S(1)} async-done(((f32[4,64,1024]{2,1,0:T(8,128)}), f32[4,64,1024]{2,1,0:T(8,128)S(1)}, u32[]{:S(2)}, u32[]{:S(2)}) %all-to-all-start.3) | async-done | bytes 1048608 | tf_op jit(solution)/shard_map/all_to_all | solution.py:104
  166.8 5.8 %all-to-all-start.5 = ((bf16[256,32,128]{2,0,1:T(8,128)(2,1)}), bf16[256,32,128]{2,0,1:T(8,128)(2,1)S(1)}, u32[]{:S(2)}, u32[]{:S(2)}) async-start(bf16[256,32,128]{2,0,1:T(8,128)(2,1)} %copy_bitcast_fusion), calls=%async_computation.5 | async-start | bytes 4194304 | tf_op jit(solution)/shard_map/all_to_all | solution.py:93
  172.6 0.0 copy-start.4
  172.7 4.1 %copy.28 = bf16[256,4096]{0,1:T(8,128)(2,1)} copy(bf16[256,4096]{1,0:T(8,128)(2,1)} %get-tuple-element.8) | data formatting | bytes 4194304 | tf_op jit(solution)/shard_map/all_to_all | solution.py:92
  176.8 0.5 broadcast.16
  177.3 0.7 reduce.11
  178.0 0.1 reshape.106
  178.0 0.9 fusion.17
  178.9 45.0 %all-to-all-done.5 = bf16[256,32,128]{2,0,1:T(8,128)(2,1)S(1)} async-done(((bf16[256,32,128]{2,0,1:T(8,128)(2,1)}), bf16[256,32,128]{2,0,1:T(8,128)(2,1)S(1)}, u32[]{:S(2)}, u32[]{:S(2)}) %all-to-all-start.5) | async-done | bytes 2097184 | tf_op jit(solution)/shard_map/all_to_all | solution.py:93
  223.9 4.9 %all-to-all-start.6 = ((bf16[256,32,128]{0,2,1:T(8,128)(2,1)}), bf16[256,32,128]{0,2,1:T(8,128)(2,1)}, u32[]{:S(2)}, u32[]{:S(2)}) async-start(bf16[256,32,128]{0,2,1:T(8,128)(2,1)} %bitcast.65), calls=%async_computation.6 | async-start | bytes 4194304 | tf_op jit(solution)/shard_map/all_to_all | solution.py:92
  228.9 0.0 copy-done.4
  228.9 1.4 convolution_convert_fusion.4
  230.3 1.6 convert_reduce_fusion.1
  231.9 10.8 %convolution_convert_fusion.1 = bf16[32,1024,128]{2,1,0:T(8,128)(2,1)} fusion(bf16[32,256,1024]{2,1,0:T(8,128)(2,1)} %bitcast.64, bf16[256,32,128]{2,0,1:T(8,128)(2,1)S(1)} %all-to-all-done.5), kind=kOutput, calls=%fused_computation.8 | convolution fusion | flops 2151677952 | bytes 27262976 | tf_op jit(solution)/shard_map/nra,nrb->nab/dot_general | solution.py:32
  242.8 23.0 %all-to-all-done.6 = bf16[256,32,128]{0,2,1:T(8,128)(2,1)} async-done(((bf16[256,32,128]{0,2,1:T(8,128)(2,1)}), bf16[256,32,128]{0,2,1:T(8,128)(2,1)}, u32[]{:S(2)}, u32[]{:S(2)}) %all-to-all-start.6) | async-done | bytes 2097184 | tf_op jit(solution)/shard_map/all_to_all | solution.py:92
  265.7 43.7 %all-gather.11.cloned.1.call-done = bf16[8192,1024]{1,0:T(8,128)(2,1)} async-done(((bf16[256,1024]{1,0:T(8,128)(2,1)}), bf16[8192,1024]{1,0:T(8,128)(2,1)}) %all-gather.11.cloned.1.call-update) | async-done | bytes 16777232 | tf_op jit(solution)/shard_map/all_gather | solution.py:97
  309.4 12.0 %convolution_convert_fusion = bf16[32,128,1024]{2,1,0:T(8,128)(2,1)} fusion(bf16[32,256,1024]{2,1,0:T(8,128)(2,1)} %bitcast.63, bf16[256,32,128]{0,2,1:T(8,128)(2,1)} %all-to-all-done.6), kind=kOutput, calls=%fused_computation.7 | convolution fusion | flops 2151677952 | bytes 27262976 | tf_op jit(solution)/shard_map/nra,nrb->nab/dot_general | solution.py:32
  321.4 5.5 %reduce_sum.68 = bf16[1024,128]{1,0:T(8,128)(2,1)} reduce(bf16[32,1024,128]{2,1,0:T(8,128)(2,1)} %convolution_convert_fusion.1, bf16[]{:T(256)} %constant.18.clone.1), dimensions={0}, to_apply=%region_2.3 | reduce | flops 4063232 | bytes 8650754 | tf_op jit(solution)/shard_map/reduce_sum | solution.py:36
  326.9 6.3 %reduce_sum.70 = bf16[128,1024]{1,0:T(8,128)(2,1)} reduce(bf16[32,128,1024]{2,1,0:T(8,128)(2,1)} %convolution_convert_fusion, bf16[]{:T(256)} %constant.18.clone.1), dimensions={0}, to_apply=%region_4.5 | reduce | flops 4063232 | bytes 8650754 | tf_op jit(solution)/shard_map/reduce_sum | solution.py:36
  333.2 10.9 %convert_reduce_fusion = f32[1024]{0:T(1024)} fusion(bf16[8192,1024]{1,0:T(8,128)(2,1)} %all-gather.11.cloned.1.call-done), kind=kLoop, calls=%fused_computation | loop fusion | flops 16776192 | bytes 16781312 | tf_op jit(solution)/shard_map/reduce_sum | solution.py:102
  344.1 0.0 copy-done.1
  (7 shorter events, 0.1 us)
Async XLA Ops:
  7.2 3.1 copy-start
  7.2 39.6 %copy-start.6 = (bf16[1,128]{1,0:T(2,128)(2,1)S(1)}, bf16[1,128]{1,0:T(2,128)(2,1)}, u32[]{:S(2)}) copy-start(bf16[1,128]{1,0:T(2,128)(2,1)} %param.15) | copy-start | bytes 772
  7.2 62.6 %copy-start.5 = (bf16[1,1024]{1,0:T(2,128)(2,1)S(1)}, bf16[1,1024]{1,0:T(2,128)(2,1)}, u32[]{:S(2)}) copy-start(bf16[1,1024]{1,0:T(2,128)(2,1)} %param.17) | copy-start | bytes 6148
  7.2 65.2 %all-gather.7.cloned.1.call-start = ((), (), s32[]{:S(2)}) async-start(), calls=%async_computation.8 | async-start | bytes 8650752 | tf_op jit(solution)/shard_map/all_gather | solution.py:82
  7.9 119.4 %all-gather.5.cloned.1.call-start = ((), (), s32[]{:S(2)}) async-start(), calls=%async_computation.7 | async-start | bytes 8650752 | tf_op jit(solution)/shard_map/all_gather | solution.py:83
  8.7 223.3 %all-gather.9.cloned.1.call-start = ((), (), s32[]{:S(2)}) async-start(), calls=%async_computation.9 | async-start | bytes 17301504 | tf_op jit(solution)/shard_map/all_gather | solution.py:96
  24.3 48.1 %copy-start.3 = (bf16[4,64,1024]{2,1,0:T(8,128)(2,1)S(1)}, bf16[4,64,1024]{2,1,0:T(8,128)(2,1)}, u32[]{:S(2)}) copy-start(bf16[4,64,1024]{2,1,0:T(8,128)(2,1)} %all_to_all.63) | copy-start | bytes 1572868
  26.0 8.4 %all-to-all-start = ((bf16[4,1,64]{2,1,0:T(2,128)(2,1)}), bf16[4,1,64]{2,1,0:T(2,128)(2,1)S(1)}, u32[]{:S(2)}, u32[]{:S(2)}) async-start(bf16[4,1,64]{2,1,0:T(2,128)(2,1)} %all_to_all.55), calls=%async_computation | async-start | bytes 4096 | tf_op jit(solution)/shard_map/all_to_all | solution.py:73
  34.3 11.5 %all-to-all-start.1 = ((bf16[4,64,1024]{2,1,0:T(8,128)(2,1)}), bf16[4,64,1024]{2,1,0:T(8,128)(2,1)S(1)}, u32[]{:S(2)}, u32[]{:S(2)}) async-start(bf16[4,64,1024]{2,1,0:T(8,128)(2,1)} %bitcast.4), calls=%async_computation.1 | async-start | bytes 1048576 | tf_op jit(solution)/shard_map/all_to_all | solution.py:66
  37.8 271.6 %all-gather.11.cloned.1.call-start = ((), (), s32[]{:S(2)}) async-start(), calls=%async_computation.10 | async-start | bytes 17301504 | tf_op jit(solution)/shard_map/all_gather | solution.py:97
  135.3 11.7 %copy-start.2 = (bf16[256,4096]{1,0:T(8,128)(2,1)}, bf16[256,4096]{1,0:T(8,128)(2,1)S(1)}, u32[]{:S(2)}) copy-start(bf16[256,4096]{1,0:T(8,128)(2,1)S(1)} %get-tuple-element.7) | copy-start | bytes 6291460
  136.1 11.0 %all-to-all-start.4 = ((f32[4,1,64]{2,1,0:T(1,128)}), f32[4,1,64]{2,1,0:T(1,128)S(1)}, u32[]{:S(2)}, u32[]{:S(2)}) async-start(f32[4,1,64]{2,1,0:T(1,128)} %add.60), calls=%async_computation.4 | async-start | bytes 4096 | tf_op jit(solution)/shard_map/all_to_all | solution.py:111
  147.0 19.8 %all-to-all-start.3 = ((f32[4,64,1024]{2,1,0:T(8,128)}), f32[4,64,1024]{2,1,0:T(8,128)S(1)}, u32[]{:S(2)}, u32[]{:S(2)}) async-start(f32[4,64,1024]{2,1,0:T(8,128)} %fusion), calls=%async_computation.3 | async-start | bytes 2097152 | tf_op jit(solution)/shard_map/all_to_all | solution.py:104
  166.8 57.1 %all-to-all-start.5 = ((bf16[256,32,128]{2,0,1:T(8,128)(2,1)}), bf16[256,32,128]{2,0,1:T(8,128)(2,1)S(1)}, u32[]{:S(2)}, u32[]{:S(2)}) async-start(bf16[256,32,128]{2,0,1:T(8,128)(2,1)} %copy_bitcast_fusion), calls=%async_computation.5 | async-start | bytes 4194304 | tf_op jit(solution)/shard_map/all_to_all | solution.py:93
  172.6 56.3 %copy-start.4 = (f32[128,2,256]{2,0,1:T(8,128)S(1)}, f32[128,2,256]{2,0,1:T(8,128)}, u32[]{:S(2)}) copy-start(f32[128,2,256]{2,0,1:T(8,128)} %get-tuple-element.9) | copy-start | bytes 786436
  223.9 41.8 %all-to-all-start.6 = ((bf16[256,32,128]{0,2,1:T(8,128)(2,1)}), bf16[256,32,128]{0,2,1:T(8,128)(2,1)}, u32[]{:S(2)}, u32[]{:S(2)}) async-start(bf16[256,32,128]{0,2,1:T(8,128)(2,1)} %bitcast.65), calls=%async_computation.6 | async-start | bytes 4194304 | tf_op jit(solution)/shard_map/all_to_all | solution.py:92
  333.2 10.9 %copy-start.1 = (bf16[128,1024]{1,0:T(8,128)(2,1)S(1)}, bf16[128,1024]{1,0:T(8,128)(2,1)}, u32[]{:S(2)}) copy-start(bf16[128,1024]{1,0:T(8,128)(2,1)} %param.9) | copy-start | bytes 786436
Sparse Core Ops, SparseCore 0:
  10.2 62.1 all-gather.6
  74.7 52.5 all-gather.4
  129.6 94.0 all-gather.8
  225.8 83.6 all-gather.10
where the time goes:
time: 353 us; the launch traced here: 351 us
  waiting for transfers between devices  185 us (52%)
  matrix products  50.9 us (14%)
  blocking collectives  36.7 us (10%)
  other arithmetic  28.3 us (8%)
  starting transfers between devices  26.7 us (8%)
  between operations  13.9 us (4%)
  local copies, waits for them, and re-layouts  9.16 us (3%)
    all_gather x1, waiting for transfers between devices, on_device(): lax.all_gather(w_out, 'zero', axis=1, tiled=True)  47.1 us
    all_to_all x1, waiting for transfers between devices, on_device(): lax.all_to_all(dpre, 'zero', split_axis=1, concat_axis=0, tiled=True)  45 us
    all_gather x1, waiting for transfers between devices, on_device(): lax.all_gather(dout, 'zero', axis=0, tiled=True)  43.7 us
    all_to_all x1, waiting for transfers between devices, on_device(): lax.all_to_all(hidden, 'zero', split_axis=1, concat_axis=0, tiled=True)  23 us
    all_gather x1, blocking collectives, on_device(): lax.all_gather(b_in, 'zero', axis=1, tiled=True)  22.9 us
    dot_general x2, matrix products, group_partials(): jnp.einsum('nra,nrb->nab', left_g, right_g, preferred_element_type=jnp.fl...  22.8 us
    all_to_all x1, blocking collectives, on_device(): lax.all_to_all(send_x.reshape(n_expert, cap_rows, -1), 'expert', split_ax...  13.8 us
    reduce_sum x2, other arithmetic, group_partials(): return jnp.sum(parts.astype(jnp.float32), axis=0).astype(jnp.bfloat16)  11.8 us
  transfers between devices with their start and end apart: 10, of which 8 were waited for; matrix products, arithmetic and copies ran while one was open for 15% of the time, Pallas kernels for 0%

commit v1 on v0

v1 whole, which is shorter than its diff:
```python
import functools

import jax
import jax.numpy as jnp
from jax import lax
from jax.experimental import pallas as pl
from jax.experimental.pallas import tpu as pltpu
from jax.sharding import Mesh, PartitionSpec as P

BF = jnp.bfloat16
F32 = jnp.float32
EXTRA = 16
NT = (((1,), (1,)), ((), ()))
NN = (((1,), (0,)), ((), ()))
TN = (((0,), (0,)), ((), ()))


def dot(a, b, dims):
    return lax.dot_general(a, b, dims, preferred_element_type=F32)


def shift(value, axis, step):
    n = lax.axis_size(axis)
    return lax.ppermute(value, axis, [(i, (i + step) % n) for i in range(n)])


def call(kernel, name, out_shape, flops=0, bytes_accessed=0, **options):
    return pl.pallas_call(
        kernel,
        out_shape=out_shape,
        compiler_params=pltpu.CompilerParams(vmem_limit_bytes=48 * 1024 * 1024),
        cost_estimate=pl.CostEstimate(
            flops=flops, bytes_accessed=bytes_accessed, transcendentals=0
        ),
        name=name,
        **options,
    )


def shape(rows, columns, dtype=BF):
    return jax.ShapeDtypeStruct((rows, columns), dtype)


def high_low(value):
    high = value.astype(BF).astype(F32)
    return high, value - high


def pack_kernel(places, weights, tokens, grads, *outs):
    slots = outs[0].shape[1]
    spots = lax.broadcasted_iota(jnp.int32, (len(outs) * slots, tokens.shape[0]), 0)
    first = places[0:1, :] == spots
    second = places[1:2, :] == spots
    picks = jnp.where(first | second, 1.0, 0.0).astype(BF)
    scaled = (
        jnp.where(first, weights[0:1, :], 0.0) + jnp.where(second, weights[1:2, :], 0.0)
    ).astype(BF)
    rows_x = dot(picks, tokens[...], NN).astype(BF)
    rows_d = dot(scaled, grads[...], NN).astype(BF)
    for s, out in enumerate(outs):
        out[0] = rows_x[s * slots : (s + 1) * slots]
        out[1] = rows_d[s * slots : (s + 1) * slots]


def rows_kernel(counts, lead, n_w, block, *refs):
    n_parts = len(counts)
    n_z = 4
    refs = list(refs)
    parts_x = [[refs.pop(0) for _ in range(n_parts)] for _ in range(n_z)]
    parts_d = [[refs.pop(0) for _ in range(n_parts)] for _ in range(n_z)]
    w = [refs.pop(0) for _ in range(n_w)]
    b_out = refs.pop(0)
    x, d, dpre, hidden, *dxs = refs[: 4 + n_z]
    acc, prod = refs[4 + n_z :]
    m = sum(counts)
    width = x.shape[1]
    for z in range(n_z):
        at = z * m
        for p, count in enumerate(counts):
            x[at : at + count] = parts_x[z][p][...].reshape(count, width)
            d[at : at + count] = parts_d[z][p][...].reshape(count, width)
            at += count
    unit = 128
    tiles = []
    for k in range(4):
        if k < 3:
            ours, other = w[2 * k], w[2 * k + 1]
            halves = [(r[0:unit], r[unit : unit + 1], r[unit + EXTRA :]) for r in (ours, other)]
        else:
            halves = [
                (r[0:unit], r[unit : unit + 1], s[...]) for r, s in ((w[6], w[7]), (w[8], w[9]))
            ]
        tiles.append(halves)

    def body(i, _):
        rows = pl.ds(pl.multiple_of(i * block, block), block)
        xb = x[rows]
        db = d[rows]
        total = None
        term = None
        for k, halves in enumerate(tiles):
            w_in = jnp.concatenate([h[0] for h in halves], axis=0)
            bias = jnp.concatenate([h[1][:, 0:unit] for h in halves], axis=1).astype(F32)
            w_out = jnp.concatenate([h[2] for h in halves], axis=0)
            pre = dot(xb, w_in, NT) + bias
            back = dot(db, w_out, NT)
            cdf = 0.5 * (1.0 + lax.erf(pre * 0.7071067811865476))
            dens = jnp.exp(-0.5 * pre * pre) * 0.3989422804014327
            hidden32 = pre * cdf
            grad = (back * (cdf + pre * dens)).astype(BF)
            hid = hidden32.astype(BF)
            for c in range(2):
                columns = slice((4 * c + k) * unit, (4 * c + k + 1) * unit)
                dpre[rows, columns] = grad[:, c * unit : (c + 1) * unit]
                hidden[rows, columns] = hid[:, c * unit : (c + 1) * unit]
            new = hidden32 * back
            part = dot(grad, w_in, NN)
            total = part if k == 0 else total + part
            term = new if k == 0 else term + new
        acc[rows] = total
        prod[i] = jnp.broadcast_to(jnp.sum(term.T, axis=0, keepdims=True), prod.shape[1:])
        return 0

    n_blocks = n_z * m // block
    lax.fori_loop(0, n_blocks, body, 0)
    by_bias = jnp.sum((d[0:m].astype(F32) * b_out[...].astype(F32)).T, axis=0, keepdims=True)
    for z in range(n_z):
        out = dxs[z]
        out[0:m] = acc[z * m : (z + 1) * m].astype(out.dtype)
        if block == m:
            line = prod[z][0:1, 0:m]
        else:
            line = prod[0][0:1, z * m : (z + 1) * m]
        if z == 0:
            line = line + by_bias
        if out.dtype == F32:
            lines = [line, jnp.zeros_like(line)]
        else:
            lines = list(high_low(line))
        sums = jnp.concatenate(lines + [jnp.zeros((EXTRA - 2, m), F32)], axis=0)
        out[m:] = jnp.zeros((EXTRA, width), out.dtype)
        out[m:, 0:m] = sums.astype(out.dtype)


def rows_set(parts_x, parts_d, w, b_out, block):
    counts = [a.shape[1] for a, _ in parts_x[0]]
    m = sum(counts)
    width = b_out.shape[1]
    units = 1024

    def piece(pair):
        array, index = pair
        return pl.BlockSpec((1, *array.shape[1:]), lambda i, index=index: (index, 0, 0))

    def full(a):
        return pl.BlockSpec(a.shape, lambda i: (0,) * len(a.shape))

    pieces = [pair for z in parts_x for pair in z] + [pair for z in parts_d for pair in z]
    out_shape = [shape(4 * m, width), shape(4 * m, width), shape(4 * m, units), shape(4 * m, units)]
    out_shape += [shape(m + EXTRA, width, F32 if z == 0 else BF) for z in range(4)]
    return call(
        functools.partial(rows_kernel, counts, None, len(w), block),
        "rows",
        out_shape,
        flops=24 * m * units * width,
        bytes_accessed=4 * units * width + 32 * m * width,
        grid=(1,),
        in_specs=[piece(p) for p in pieces] + [full(a) for a in w] + [full(b_out)],
        out_specs=[full(s) for s in out_shape],
        scratch_shapes=[
            pltpu.VMEM((4 * m, width), F32),
            pltpu.VMEM((4 * m // block, 8, block), F32),
        ],
    )(*[a for a, _ in pieces], *w, b_out)


def weights_kernel(n_sets, with_add, *refs):
    xs, ds, dpres, hiddens = (refs[k * n_sets : (k + 1) * n_sets] for k in range(4))
    rest = refs[4 * n_sets :]
    adds, outs = (rest[:4], rest[4:]) if with_add else ((), rest)
    unit = dpres[0].shape[1] // 4
    total_in = sum(dot(p[...], x[...], TN) for p, x in zip(dpres, xs))
    total_out = sum(dot(h[...], d[...], TN) for h, d in zip(hiddens, ds))
    sum_in = sum(jnp.sum(p[...].astype(F32), axis=0, keepdims=True) for p in dpres)
    sum_out = sum(jnp.sum(d[...].astype(F32), axis=0, keepdims=True) for d in ds)
    width = total_in.shape[1]
    for k, out in enumerate(outs):
        grad_in = total_in[k * unit : (k + 1) * unit]
        grad_out = total_out[k * unit : (k + 1) * unit]
        line_in = sum_in[:, k * unit : (k + 1) * unit]
        line_out = sum_out
        if with_add:
            a = adds[k]
            grad_in = grad_in + a[0:unit].astype(F32)
            grad_out = grad_out + a[unit : 2 * unit].astype(F32)
            tail = a[2 * unit :].astype(F32)
            line_in = line_in + tail[0:1, 0:unit] + tail[1:2, 0:unit]
            line_out = line_out + tail[2:3] + tail[3:4]
        line_in = jnp.concatenate([line_in, jnp.zeros((1, width - unit), F32)], axis=1)
        lines = [line_in, line_out]
        if out.dtype == F32:
            lines = [line_in, jnp.zeros_like(line_in), line_out, jnp.zeros_like(line_out)]
        else:
            lines = [*high_low(line_in), *high_low(line_out)]
        out[0:unit] = grad_in.astype(out.dtype)
        out[unit : 2 * unit] = grad_out.astype(out.dtype)
        lines.append(jnp.zeros((EXTRA - 4, width), F32))
        out[2 * unit :] = jnp.concatenate(lines, axis=0).astype(out.dtype)


def weights_part(sets, other_core, adds):
    (x, d, dpre, hidden) = zip(*sets)
    units = dpre[0].shape[1] // 2
    width = x[0].shape[1]
    rows = sum(a.shape[0] for a in x)

    def full(a):
        return pl.BlockSpec(a.shape, lambda i: (0,) * len(a.shape))

    def cut(a):
        return pl.BlockSpec((a.shape[0], units), lambda i: (0, int(other_core)))

    height = 2 * units // 4 + EXTRA
    out_shape = [shape(height, width, F32 if adds and k == 0 else BF) for k in range(4)]
    return call(
        functools.partial(weights_kernel, len(sets), bool(adds)),
        "weights",
        out_shape,
        flops=4 * rows * units * width,
        bytes_accessed=4 * rows * width + 4 * rows * units + 4 * units * width,
        grid=(1,),
        in_specs=[full(a) for a in x + d]
        + [cut(a) for a in dpre + hidden]
        + [full(a) for a in adds],
        out_specs=[full(s) for s in out_shape],
    )(*x, *d, *dpre, *hidden, *adds)


def sum_kernel(n_out, own, *refs):
    parts, outs = refs[:-n_out], refs[-n_out:]
    m = own.shape[0] - EXTRA
    total = own[...]
    for p in parts:
        total = total + p[...].astype(F32)
    line = total[m : m + 1] + total[m + 1 : m + 2]
    lines = jnp.concatenate(
        [*high_low(line), jnp.zeros((EXTRA - 2, own.shape[1]), F32)], axis=0
    ).astype(BF)
    slots = m // n_out
    for s, out in enumerate(outs):
        out[0:slots] = total[s * slots : (s + 1) * slots].astype(BF)
        out[slots:] = lines


def sum_z(own, parts, n_out):
    slots = (own.shape[0] - EXTRA) // n_out
    return call(
        functools.partial(sum_kernel, n_out),
        "sum_z",
        [shape(slots + EXTRA, own.shape[1])] * n_out,
        bytes_accessed=12 * own.size,
    )(own, *parts)


def finish_kernel(offsets, places, weights, *refs):
    pieces, (out, by_weight) = refs[:-2], refs[-2:]
    slots = pieces[0].shape[0] - EXTRA
    n_tok = places.shape[1]
    total = None
    sums = [None, None]
    for s, piece in enumerate(pieces):
        spots = lax.broadcasted_iota(jnp.int32, (slots, n_tok), 0) + s * slots
        picks = jnp.where((places[0:1, :] == spots) | (places[1:2, :] == spots), 1.0, 0.0)
        part = dot(picks.astype(BF), piece[0:slots], TN)
        total = part if total is None else total + part
        span = lax.broadcasted_iota(jnp.int32, (256, n_tok), 0) - offsets[s]
        inside = (span >= 0) & (span < slots)
        for k in range(2):
            pick = jnp.where(inside & (places[k : k + 1, :] == span + s * slots), 1.0, 0.0)
            found = dot(piece[slots:, 0:256], pick.astype(BF), NN)
            line = found[0:1] + found[1:2]
            sums[k] = line if sums[k] is None else sums[k] + line
    out[...] = total.astype(BF)
    by_weight[...] = jnp.concatenate(sums, axis=0) / weights[...]


def on_device(tokens, grads_out, routes, slots, combine, w_in, b_in, w_out, b_out):
    n_expert = lax.axis_size("x")
    tok_rows, width = tokens.shape
    cap = 2 * tok_rows // n_expert
    me = lax.axis_index("x")

    turned = lax.rem(routes - me + n_expert, n_expert)
    places = jnp.where(slots < cap, turned * cap + slots, -1).T
    scales = combine.T.astype(F32)
    sent = call(pack_kernel, "pack", [jax.ShapeDtypeStruct((2, cap, width), BF)] * n_expert)(
        places, scales, tokens, grads_out
    )
    got_left = shift(sent[1], "x", 1)
    got_right = shift(sent[3], "x", -1)
    got_far = shift(sent[2], "x", 2)

    def along_z(part):
        below = shift(part, "z", 1)
        above = shift(part, "z", -1)
        far_x = shift(below[0:1], "z", 1)
        far_d = shift(above[1:2], "z", -1)
        x = [(part, 0), (below, 0), (above, 0), (far_x, 0)]
        d = [(part, 1), (below, 1), (above, 1), (far_d, 0)]
        return x, d

    x_a, d_a = along_z(sent[0])
    x_b, d_b = along_z(jnp.concatenate([got_left, got_right], axis=1))
    x_c, d_c = along_z(got_far)

    units = w_in.shape[2]
    bias_rows = jnp.pad(b_in, ((0, EXTRA - 1), (0, width - units)))
    mine = jnp.concatenate([w_in[0].T, bias_rows, w_out[0]], axis=0)
    below = shift(mine, "y", 1)
    above = shift(mine, "y", -1)
    cut = units + EXTRA
    far_in = shift(below[:cut], "y", 1)
    far_out = shift(above[cut:], "y", -1)
    w = []
    for a in (mine, below, above):
        w += [a, shift(a, "c", 1)]
    w += [far_in, far_out, shift(far_in, "c", 1), shift(far_out, "c", 1)]

    ab = rows_set(
        [[p, q] for p, q in zip(x_a, x_b)], [[p, q] for p, q in zip(d_a, d_b)], w, b_out, 3 * cap
    )
    c = rows_set([[p] for p in x_c], [[p] for p in d_c], w, b_out, 4 * cap)
    ways = [0, -1, 1, 2]
    pieces = {}
    for key, res, names in (("ab", ab, (0, 1, 3)), ("c", c, (2,))):
        dx = res[4:]
        moved = [shift(dx[k], "z", ways[k]) for k in (3, 1, 2)]
        for s, piece in zip(names, sum_z(dx[0], moved, len(names))):
            pieces[s] = piece

    sets = [ab[:4], c[:4]]
    away = weights_part(sets, True, ())
    home = weights_part(sets, False, [shift(a, "c", 1) for a in away])
    moved = [shift(home[k], "y", ways[k]) for k in (3, 1, 2)]
    total = home[0] + sum(a.astype(F32) for a in moved)
    grad_w_in = total[:units].T.astype(BF)[None]
    grad_w_out = total[units : 2 * units].astype(BF)[None]
    tail = total[2 * units :]
    grad_b_in = (tail[0] + tail[1])[:units][None]
    grad_b_out = (tail[2] + tail[3])[None]

    back = {0: 0, 1: -1, 2: 2, 3: 1}
    final = [shift(pieces[s], "x", back[s]) if s else pieces[s] for s in range(n_expert)]
    grad_tokens, by_weight = call(
        functools.partial(finish_kernel, (0, cap, 0, 2 * cap)),
        "finish",
        [shape(tok_rows, width), shape(2, tok_rows, F32)],
    )(places, scales, *final)
    return (grad_tokens, by_weight.T, grad_w_in, grad_b_in, grad_w_out, grad_b_out)


def solution(mesh):
    fine = Mesh(mesh.devices.reshape(4, 4, 4, 2), ("x", "z", "y", "c"))
    zero = ("z", "y", "c")
    every = ("x", "z", "y", "c")
    rows = P(every, None)
    in_specs = (rows,) * 5 + (
        P("x", None, zero),
        P("x", zero),
        P("x", zero, None),
        P("x", None),
    )
    out_specs = (
        rows,
        rows,
        P("x", None, zero),
        P("x", zero),
        P("x", zero, None),
        P("x", None),
    )
    return jax.shard_map(
        on_device, mesh=fine, in_specs=in_specs, out_specs=out_specs, check_vma=False
    )
```

time: 353 us -> 157 us (0.44)
  waiting for transfers between devices: 185 us -> 63.4 us
  matrix products: 50.9 us -> 0 us
  blocking collectives: 36.7 us -> 0 us
  Pallas kernels: 0 us -> 29.7 us
  starting transfers between devices: 26.7 us -> 53 us
  other arithmetic: 28.3 us -> 3.56 us
  between operations: 13.9 us -> 1.01 us
    all_gather x4 -> x0, waiting for transfers between devices: 93.3 us -> none  [the longest x1 47.1 us: on_device(): lax.all_gather(w_out, 'zero', axis=1, tiled=True)]
    all_to_all x6 -> x0, waiting for transfers between devices: 90.3 us -> none  [the longest x1 45 us: on_device(): lax.all_to_all(dpre, 'zero', split_axis=1, concat_axis=0, tiled=True)]
    ppermute x0 -> x40, waiting for transfers between devices: none -> 63.4 us  [shift(): return lax.ppermute(value, axis, [(i, (i + step) % n) for i in range(n)])]
    ppermute x0 -> x40, starting transfers between devices: none -> 53 us  [shift(): return lax.ppermute(value, axis, [(i, (i + step) % n) for i in range(n)])]
    dot_general x10 -> x0, matrix products: 50.9 us -> none  [the longest x2 22.8 us: group_partials(): jnp.einsum('nra,nrb->nab', left_g, right_g, preferred_element_type=jnp.fl...]
    pallas_call x0 -> x8, Pallas kernels: none -> 29.7 us  [the longest x2 17.9 us: rows_set(): call(functools.partial(rows_kernel, counts, None, len(w), block), 'rows',...]
    all_to_all x6 -> x0, starting transfers between devices: 26.5 us -> none  [the longest x1 5.82 us: on_device(): lax.all_to_all(dpre, 'zero', split_axis=1, concat_axis=0, tiled=True)]
    reduce_sum x5 -> x0, other arithmetic: 24.5 us -> none  [the longest x2 11.8 us: group_partials(): return jnp.sum(parts.astype(jnp.float32), axis=0).astype(jnp.bfloat16)]
  transfers between devices with their start and end apart: 10 -> 40, of which waited for: 8 -> 13; matrix products, arithmetic and copies ran while one was open for 15% -> 1% of each run, Pallas kernels for 0% -> 7%
where the time goes in v1:
time: 157 us
  waiting for transfers between devices  63.4 us (40%)
  starting transfers between devices  53 us (34%)
  Pallas kernels  29.7 us (19%)
  local copies, waits for them, and re-layouts  6.16 us (4%)
  other arithmetic  3.56 us (2%)
    ppermute x40, waiting for transfers between devices, shift(): return lax.ppermute(value, axis, [(i, (i + step) % n) for i in range(n)])  63.4 us
    ppermute x40, starting transfers between devices, shift(): return lax.ppermute(value, axis, [(i, (i + step) % n) for i in range(n)])  53 us
    pallas_call x2, Pallas kernels, rows_set(): call(functools.partial(rows_kernel, counts, None, len(w), block), 'rows',...  17.9 us
    pallas_call x2, Pallas kernels, weights_part(): call(functools.partial(weights_kernel, len(sets), bool(adds)), 'weights',...  9.83 us
    unnamed x27, local copies, waits for them, and re-layouts  5.29 us
  transfers between devices with their start and end apart: 40, of which 13 were waited for; matrix products, arithmetic and copies ran while one was open for 1% of the time, Pallas kernels for 7%

profile of v1, /device:TPU:0, one launch (start us, length us, event | category | flops | bytes accessed | tf_op | source)
XLA Modules:
  0.0 156.8 jit_solution(7508025478096216693)
XLA Ops:
  0.6 0.7 convert_bitcast_fusion.weights
  1.3 0.7 fusion.4.places
  2.0 0.9 copy-done.3
  3.0 0.9 copy-done.4
  3.9 0.4 pack.1
  4.3 1.6 %collective-permute-start = (bf16[2,64,1024]{2,1,0:T(8,128)(2,1)S(1)}, bf16[2,64,1024]{2,1,0:T(8,128)(2,1)S(1)}, u32[]{:S(2)}, u32[]{:S(2)}) collective-permute-start(bf16[2,64,1024]{2,1,0:T(8,128)(2,1)S(1)} %get-tuple-element.40), channel_id=1, source_target_pairs={{0,32},{32,64},{64,96},{96,0},{1,33},{33,65},{65,97},{97,1},{2,34}... | collective-permute-start | bytes 786440 | tf_op jit(solution)/shard_map/ppermute | solution.py:24
  6.0 2.7 %collective-permute-start.23 = (bf16[2,64,1024]{2,1,0:T(8,128)(2,1)S(1)}, bf16[2,64,1024]{2,1,0:T(8,128)(2,1)S(1)}, u32[]{:S(2)}, u32[]{:S(2)}) collective-permute-start(bf16[2,64,1024]{2,1,0:T(8,128)(2,1)S(1)} %get-tuple-element.48), channel_id=1, source_target_pairs={{0,64},{32,96},{64,0},{96,32},{1,65},{33,97},{65,1},{97,33},{2,66}... | collective-permute-start | bytes 786440 | tf_op jit(solution)/shard_map/ppermute | solution.py:24
  8.7 1.4 collective-permute-start.1
  10.1 1.9 %collective-permute-start.2 = (bf16[2,64,1024]{2,1,0:T(8,128)(2,1)S(1)}, bf16[2,64,1024]{2,1,0:T(8,128)(2,1)S(1)}, u32[]{:S(2)}, u32[]{:S(2)}) collective-permute-start(bf16[2,64,1024]{2,1,0:T(8,128)(2,1)S(1)} %get-tuple-element.39.refs_0_.refs_8_), channel_id=1, source_target_pairs={{0,8},{8,16},{16,24},{24,0},{1,9},{9,17},{17,25},{25,1},{2,10},{10... | collective-permute-start | bytes 786440 | tf_op jit(solution)/shard_map/ppermute | solution.py:24
  12.1 2.1 %collective-permute-start.4 = (bf16[2,64,1024]{2,1,0:T(8,128)(2,1)S(1)}, bf16[2,64,1024]{2,1,0:T(8,128)(2,1)S(1)}, u32[]{:S(2)}, u32[]{:S(2)}) collective-permute-start(bf16[2,64,1024]{2,1,0:T(8,128)(2,1)S(1)} %get-tuple-element.39.refs_0_.refs_8_), channel_id=1, source_target_pairs={{0,24},{8,0},{16,8},{24,16},{1,25},{9,1},{17,9},{25,17},{2,26},{10... | collective-permute-start | bytes 786440 | tf_op jit(solution)/shard_map/ppermute | solution.py:24
  14.2 1.1 copy.15
  15.3 0.7 fusion.3.refs_16_.refs_8_
  16.0 3.1 %collective-permute-start.13 = (bf16[272,1024]{1,0:T(8,128)(2,1)S(1)}, bf16[272,1024]{1,0:T(8,128)(2,1)S(1)}, u32[]{:S(2)}, u32[]{:S(2)}) collective-permute-start(bf16[272,1024]{1,0:T(8,128)(2,1)S(1)} %fusion.3.refs_16_.refs_8_), channel_id=1, source_target_pairs={{0,6},{2,0},{4,2},{6,4},{1,7},{3,1},{5,3},{7,5},{8,14},{10,8},{12,... | collective-permute-start | bytes 1671176 | tf_op jit(solution)/shard_map/ppermute | solution.py:24
  19.1 1.3 collective-permute-done.23.refs_0_.refs_4_
  20.3 1.9 %collective-permute-start.24 = (bf16[2,64,1024]{2,1,0:T(8,128)(2,1)S(1)}, bf16[2,64,1024]{2,1,0:T(8,128)(2,1)S(1)}, u32[]{:S(2)}, u32[]{:S(2)}) collective-permute-start(bf16[2,64,1024]{2,1,0:T(8,128)(2,1)S(1)} %collective-permute-done.23.refs_0_.refs_4_), channel_id=1, source_target_pairs={{0,8},{8,16},{16,24},{24,0},{1,9},{9,17},{17,25},{25,1},{2,10},{10... | collective-permute-start | bytes 786440 | tf_op jit(solution)/shard_map/ppermute | solution.py:24
  22.3 0.1 collective-permute-start.10
  22.4 1.6 %collective-permute-start.11 = (bf16[272,1024]{1,0:T(8,128)(2,1)S(1)}, bf16[272,1024]{1,0:T(8,128)(2,1)S(1)}, u32[]{:S(2)}, u32[]{:S(2)}) collective-permute-start(bf16[272,1024]{1,0:T(8,128)(2,1)S(1)} %fusion.3.refs_16_.refs_8_), channel_id=1, source_target_pairs={{0,2},{2,4},{4,6},{6,0},{1,3},{3,5},{5,7},{7,1},{8,10},{10,12},{12... | collective-permute-start | bytes 1671176 | tf_op jit(solution)/shard_map/ppermute | solution.py:24
  24.1 2.0 %collective-permute-start.3 = (bf16[2,128,1024]{2,1,0:T(8,128)(2,1)S(1)}, bf16[2,128,1024]{2,1,0:T(8,128)(2,1)S(1)}, u32[]{:S(2)}, u32[]{:S(2)}) collective-permute-start(bf16[2,128,1024]{2,1,0:T(8,128)(2,1)S(1)} %constant_dynamic-update-slice_fusion.refs_1_.refs_9_), channel_id=1, source_target_pairs={{0,8},{8,16},{16,24},{24,0},{1,9},{9,17},{17,25},{25,1},{2,10},{10... | collective-permute-start | bytes 1572872 | tf_op jit(solution)/shard_map/ppermute | solution.py:24
  26.1 5.4 %collective-permute-done.24.refs_1_.refs_5_ = bf16[2,64,1024]{2,1,0:T(8,128)(2,1)S(1)} collective-permute-done((bf16[2,64,1024]{2,1,0:T(8,128)(2,1)S(1)}, bf16[2,64,1024]{2,1,0:T(8,128)(2,1)S(1)}, u32[]{:S(2)}, u32[]{:S(2)}) %collective-permute-start.24) | collective-permute-done | bytes 262176 | tf_op jit(solution)/shard_map/ppermute | solution.py:24
  31.5 2.2 %collective-permute-start.25 = (bf16[2,64,1024]{2,1,0:T(8,128)(2,1)S(1)}, bf16[2,64,1024]{2,1,0:T(8,128)(2,1)S(1)}, u32[]{:S(2)}, u32[]{:S(2)}) collective-permute-start(bf16[2,64,1024]{2,1,0:T(8,128)(2,1)S(1)} %collective-permute-done.23.refs_0_.refs_4_), channel_id=1, source_target_pairs={{0,24},{8,0},{16,8},{24,16},{1,25},{9,1},{17,9},{25,17},{2,26},{10... | collective-permute-start | bytes 786440 | tf_op jit(solution)/shard_map/ppermute | solution.py:24
  33.6 5.7 %collective-permute-done.25.refs_2_.refs_6_ = bf16[2,64,1024]{2,1,0:T(8,128)(2,1)S(1)} collective-permute-done((bf16[2,64,1024]{2,1,0:T(8,128)(2,1)S(1)}, bf16[2,64,1024]{2,1,0:T(8,128)(2,1)S(1)}, u32[]{:S(2)}, u32[]{:S(2)}) %collective-permute-start.25) | collective-permute-done | bytes 262176 | tf_op jit(solution)/shard_map/ppermute | solution.py:24
  39.4 2.8 %collective-permute-start.5 = (bf16[2,128,1024]{2,1,0:T(8,128)(2,1)S(1)}, bf16[2,128,1024]{2,1,0:T(8,128)(2,1)S(1)}, u32[]{:S(2)}, u32[]{:S(2)}) collective-permute-start(bf16[2,128,1024]{2,1,0:T(8,128)(2,1)S(1)} %constant_dynamic-update-slice_fusion.refs_1_.refs_9_), channel_id=1, source_target_pairs={{0,24},{8,0},{16,8},{24,16},{1,25},{9,1},{17,9},{25,17},{2,26},{10... | collective-permute-start | bytes 1572872 | tf_op jit(solution)/shard_map/ppermute | solution.py:24
  42.3 0.1 collective-permute-start.26
  42.4 3.4 %collective-permute-start.16 = (bf16[128,1024]{1,0:T(8,128)(2,1)S(1)}, bf16[128,1024]{1,0:T(8,128)(2,1)S(1)}, u32[]{:S(2)}, u32[]{:S(2)}) collective-permute-start(bf16[128,1024]{1,0:T(8,128)(2,1)S(1)} %slice.73), channel_id=1, source_target_pairs={{0,6},{2,0},{4,2},{6,4},{1,7},{3,1},{5,3},{7,5},{8,14},{10,8},{12,... | collective-permute-start | bytes 786440 | tf_op jit(solution)/shard_map/ppermute | solution.py:24
  45.8 0.1 collective-permute-start.15
  45.9 2.6 %collective-permute-done.26.refs_3_ = bf16[1,64,1024]{2,1,0:T(8,128)(2,1)S(1)} collective-permute-done((bf16[1,64,1024]{2,1,0:T(8,128)(2,1)S(1)}, bf16[1,64,1024]{2,1,0:T(8,128)(2,1)S(1)}, u32[]{:S(2)}, u32[]{:S(2)}) %collective-permute-start.26) | collective-permute-done | bytes 131104 | tf_op jit(solution)/shard_map/ppermute | solution.py:24
  48.5 0.5 collective-permute-start.14
  49.0 0.7 collective-permute-done.16.refs_23_.refs_15_
  49.7 4.2 %collective-permute-done.15.refs_22_.refs_14_ = bf16[144,1024]{1,0:T(8,128)(2,1)S(1)} collective-permute-done((bf16[144,1024]{1,0:T(8,128)(2,1)S(1)}, bf16[144,1024]{1,0:T(8,128)(2,1)S(1)}, u32[]{:S(2)}, u32[]{:S(2)}) %collective-permute-start.15) | collective-permute-done | bytes 294944 | tf_op jit(solution)/shard_map/ppermute | solution.py:24
  53.9 3.3 %collective-permute-start.27 = (bf16[1,64,1024]{2,1,0:T(8,128)(2,1)S(1)}, bf16[1,64,1024]{2,1,0:T(8,128)(2,1)S(1)}, u32[]{:S(2)}, u32[]{:S(2)}) collective-permute-start(bf16[1,64,1024]{2,1,0:T(8,128)(2,1)S(1)} %slice.75), channel_id=1, source_target_pairs={{0,24},{8,0},{16,8},{24,16},{1,25},{9,1},{17,9},{25,17},{2,26},{10... | collective-permute-start | bytes 393224 | tf_op jit(solution)/shard_map/ppermute | solution.py:24
  57.2 3.4 %collective-permute-done.27.refs_7_ = bf16[1,64,1024]{2,1,0:T(8,128)(2,1)S(1)} collective-permute-done((bf16[1,64,1024]{2,1,0:T(8,128)(2,1)S(1)}, bf16[1,64,1024]{2,1,0:T(8,128)(2,1)S(1)}, u32[]{:S(2)}, u32[]{:S(2)}) %collective-permute-start.27) | collective-permute-done | bytes 131104 | tf_op jit(solution)/shard_map/ppermute | solution.py:24
  60.6 3.7 %collective-permute-start.9 = (bf16[1,128,1024]{2,1,0:T(8,128)(2,1)S(1)}, bf16[1,128,1024]{2,1,0:T(8,128)(2,1)S(1)}, u32[]{:S(2)}, u32[]{:S(2)}) collective-permute-start(bf16[1,128,1024]{2,1,0:T(8,128)(2,1)S(1)} %slice.71), channel_id=1, source_target_pairs={{0,24},{8,0},{16,8},{24,16},{1,25},{9,1},{17,9},{25,17},{2,26},{10... | collective-permute-start | bytes 786440 | tf_op jit(solution)/shard_map/ppermute | solution.py:24
  64.3 0.1 collective-permute-start.6
  64.4 3.2 %collective-permute-start.8 = (bf16[1,64,1024]{2,1,0:T(8,128)(2,1)S(1)}, bf16[1,64,1024]{2,1,0:T(8,128)(2,1)S(1)}, u32[]{:S(2)}, u32[]{:S(2)}) collective-permute-start(bf16[1,64,1024]{2,1,0:T(8,128)(2,1)S(1)} %slice.70), channel_id=1, source_target_pairs={{0,24},{8,0},{16,8},{24,16},{1,25},{9,1},{17,9},{25,17},{2,26},{10... | collective-permute-start | bytes 393224 | tf_op jit(solution)/shard_map/ppermute | solution.py:24
  67.7 4.0 %rows.3 = (bf16[256,1024]{1,0:T(8,128)(2,1)S(1)}, bf16[256,1024]{1,0:T(8,128)(2,1)S(1)}, bf16[256,1024]{1,0:T(8,128)(2,1)S(1)}, bf16[256,1024]{1,0:T(8,128)(2,1)...) custom-call(bf16[2,64,1024]{2,1,0:T(8,128)(2,1)S(1)} %collective-per, ...), custom_call_target="tpu_custom_call" | custom-call | flops 1610612736 | bytes 6291456 | tf_op jit(solution)/shard_map/rows/pallas_call | solution.py:161
  71.7 1.6 %collective-permute-done.6.refs_6_ = bf16[1,64,1024]{2,1,0:T(8,128)(2,1)S(1)} collective-permute-done((bf16[1,64,1024]{2,1,0:T(8,128)(2,1)S(1)}, bf16[1,64,1024]{2,1,0:T(8,128)(2,1)S(1)}, u32[]{:S(2)}, u32[]{:S(2)}) %collective-permute-start.6) | collective-permute-done | bytes 131104 | tf_op jit(solution)/shard_map/ppermute | solution.py:24
  73.3 13.9 %rows.2 = (bf16[768,1024]{1,0:T(8,128)(2,1)}, bf16[768,1024]{1,0:T(8,128)(2,1)}, bf16[768,1024]{1,0:T(8,128)(2,1)}, bf16[768,1024]{1,0:T(8,128)(2,1)}, f32[208,1...) custom-call(bf16[2,64,1024]{2,1,0:T(8,128)(2,1)S(1)} %get-tuple-eleme, ...), custom_call_target="tpu_custom_call" | custom-call | flops 4831838208 | bytes 10485760 | tf_op jit(solution)/shard_map/rows/pallas_call | solution.py:161
  87.2 1.4 copy-done
  88.6 4.2 %weights.2 = (bf16[272,1024]{1,0:T(8,128)(2,1)S(1)}, bf16[272,1024]{1,0:T(8,128)(2,1)S(1)}, bf16[272,1024]{1,0:T(8,128)(2,1)S(1)}, bf16[272,1024]{1,0:T(8,128)(2,1)S(1)}) custom-call(bf16[768,1024]{1,0:T(8,128)(2,1)S(1)} %copy-done, bf16[256,1024]{1,0:T(8,128)(2,1)S(1)} %get-tuple-element.57.refs_1_, bf16[768,1024]{1,0:T(8,128)(2,1)} %get-tuple-element.58.refs_2_, ...), custom_call_target="tpu_custom_call" | custom-call | flops 2147483648 | bytes 8388608 | tf_op jit(solution)/shard_map/weights/pallas_call | solution.py:225
  92.8 0.1 collective-permute-start.33
  92.9 0.5 collective-permute-start.34
  93.4 0.1 collective-permute-start.35
  93.5 0.4 collective-permute-start.36
  93.9 2.9 %collective-permute-start.28 = (bf16[80,1024]{1,0:T(8,128)(2,1)S(1)}, bf16[80,1024]{1,0:T(8,128)(2,1)S(1)}, u32[]{:S(2)}, u32[]{:S(2)}) collective-permute-start(bf16[80,1024]{1,0:T(8,128)(2,1)S(1)} %get-tuple-element.50), channel_id=1, source_target_pairs={{0,16},{8,24},{16,0},{24,8},{1,17},{9,25},{17,1},{25,9},{2,18},{10... | collective-permute-start | bytes 491528 | tf_op jit(solution)/shard_map/ppermute | solution.py:24
  96.8 4.8 %collective-permute-done.28.refs_0_ = bf16[80,1024]{1,0:T(8,128)(2,1)S(1)} collective-permute-done((bf16[80,1024]{1,0:T(8,128)(2,1)S(1)}, bf16[80,1024]{1,0:T(8,128)(2,1)S(1)}, u32[]{:S(2)}, u32[]{:S(2)}) %collective-permute-start.28) | collective-permute-done | bytes 163872 | tf_op jit(solution)/shard_map/ppermute | solution.py:24
  101.6 2.9 %collective-permute-start.19 = (bf16[208,1024]{1,0:T(8,128)(2,1)S(1)}, bf16[208,1024]{1,0:T(8,128)(2,1)S(1)}, u32[]{:S(2)}, u32[]{:S(2)}) collective-permute-start(bf16[208,1024]{1,0:T(8,128)(2,1)S(1)} %get-tuple-element.43), channel_id=1, source_target_pairs={{0,16},{8,24},{16,0},{24,8},{1,17},{9,25},{17,1},{25,9},{2,18},{10... | collective-permute-start | bytes 1277960 | tf_op jit(solution)/shard_map/ppermute | solution.py:24
  104.5 0.9 collective-permute-start.20
  105.4 1.1 collective-permute-start.21
  106.5 2.1 %collective-permute-start.29 = (bf16[80,1024]{1,0:T(8,128)(2,1)S(1)}, bf16[80,1024]{1,0:T(8,128)(2,1)S(1)}, u32[]{:S(2)}, u32[]{:S(2)}) collective-permute-start(bf16[80,1024]{1,0:T(8,128)(2,1)S(1)} %get-tuple-element.51), channel_id=1, source_target_pairs={{0,24},{8,0},{16,8},{24,16},{1,25},{9,1},{17,9},{25,17},{2,26},{10... | collective-permute-start | bytes 491528 | tf_op jit(solution)/shard_map/ppermute | solution.py:24
  108.6 5.6 %weights.3 = (f32[272,1024]{1,0:T(8,128)}, bf16[272,1024]{1,0:T(8,128)(2,1)S(1)}, bf16[272,1024]{1,0:T(8,128)(2,1)S(1)}, bf16[272,1024]{1,0:T(8,128)(2,1)S(1)}) custom-call(bf16[768,1024]{1,0:T(8,128)(2,1)} %get-tuple-element.56.refs_0_, bf16[256,1024]{1,0:T(8,128)(2,1)S(1)} %get-tuple-element.57.refs_1_, bf16[768,1024]{1,0:T(8,128)(2,1)} %get-tuple-element.58.refs_2_, ...), custom_call_target="tpu_custom_call" | custom-call | flops 2147483648 | bytes 8388608 | tf_op jit(solution)/shard_map/weights/pallas_call | solution.py:225
  114.3 12.8 %collective-permute-done.29.refs_1_ = bf16[80,1024]{1,0:T(8,128)(2,1)S(1)} collective-permute-done((bf16[80,1024]{1,0:T(8,128)(2,1)S(1)}, bf16[80,1024]{1,0:T(8,128)(2,1)S(1)}, u32[]{:S(2)}, u32[]{:S(2)}) %collective-permute-start.29) | collective-permute-done | bytes 163872 | tf_op jit(solution)/shard_map/ppermute | solution.py:24
  127.0 3.2 %collective-permute-start.38 = (bf16[272,1024]{1,0:T(8,128)(2,1)S(1)}, bf16[272,1024]{1,0:T(8,128)(2,1)S(1)}, u32[]{:S(2)}, u32[]{:S(2)}) collective-permute-start(bf16[272,1024]{1,0:T(8,128)(2,1)S(1)} %get-tuple-element.70), channel_id=1, source_target_pairs={{0,6},{2,0},{4,2},{6,4},{1,7},{3,1},{5,3},{7,5},{8,14},{10,8},{12,... | collective-permute-start | bytes 1671176 | tf_op jit(solution)/shard_map/ppermute | solution.py:24
  130.3 0.1 sum_z.3
  130.4 0.8 collective-permute-start.31
  131.2 0.2 sum_z.2
  131.5 6.6 %collective-permute-done.31.refs_2_ = bf16[80,1024]{1,0:T(8,128)(2,1)S(1)} collective-permute-done((bf16[80,1024]{1,0:T(8,128)(2,1)S(1)}, bf16[80,1024]{1,0:T(8,128)(2,1)S(1)}, u32[]{:S(2)}, u32[]{:S(2)}) %collective-permute-start.31) | collective-permute-done | bytes 163872 | tf_op jit(solution)/shard_map/ppermute | solution.py:24
  138.2 6.5 %collective-permute-done.32.refs_3_ = bf16[80,1024]{1,0:T(8,128)(2,1)S(1)} collective-permute-done((bf16[80,1024]{1,0:T(8,128)(2,1)S(1)}, bf16[80,1024]{1,0:T(8,128)(2,1)S(1)}, u32[]{:S(2)}, u32[]{:S(2)}) %collective-permute-start.32) | collective-permute-done | bytes 163872 | tf_op jit(solution)/shard_map/ppermute | solution.py:24
  144.7 1.2 finish.1
  145.9 7.8 %collective-permute-done.39 = bf16[272,1024]{1,0:T(8,128)(2,1)S(1)} collective-permute-done((bf16[272,1024]{1,0:T(8,128)(2,1)S(1)}, bf16[272,1024]{1,0:T(8,128)(2,1)S(1)}, u32[]{:S(2)}, u32[]{:S(2)}) %collective-permute-start.39) | collective-permute-done | bytes 557088 | tf_op jit(solution)/shard_map/ppermute | solution.py:24
  153.7 0.4 fusion.8
  154.1 0.7 slice_bitcast_fusion
  154.8 0.8 copy.16
  155.6 0.6 slice_add_fusion
  156.3 0.5 slice_add_fusion.1
  (67 shorter events, 0.4 us)
Async XLA Ops:
  2.0 0.9 copy-start.3
  3.0 0.9 copy-start.4
  3.9 11.4 %copy-start.11 = (bf16[1,128,1024]{2,1,0:T(8,128)(2,1)S(1)}, bf16[1,128,1024]{2,1,0:T(8,128)(2,1)}, u32[]{:S(2)}) copy-start(bf16[1,128,1024]{2,1,0:T(8,128)(2,1)} %param.16) | copy-start | bytes 786436
  4.3 11.7 %collective-permute-start = (bf16[2,64,1024]{2,1,0:T(8,128)(2,1)S(1)}, bf16[2,64,1024]{2,1,0:T(8,128)(2,1)S(1)}, u32[]{:S(2)}, u32[]{:S(2)}) collective-permute-start(bf16[2,64,1024]{2,1,0:T(8,128)(2,1)S(1)} %get-tuple-element.40), channel_id=1, source_target_pairs={{0,32},{32,64},{64,96},{96,0},{1,33},{33,65},{65,97},{97,1},{2,34}... | collective-permute-start | bytes 786440 | tf_op jit(solution)/shard_map/ppermute | solution.py:24
  6.0 14.4 %collective-permute-start.23 = (bf16[2,64,1024]{2,1,0:T(8,128)(2,1)S(1)}, bf16[2,64,1024]{2,1,0:T(8,128)(2,1)S(1)}, u32[]{:S(2)}, u32[]{:S(2)}) collective-permute-start(bf16[2,64,1024]{2,1,0:T(8,128)(2,1)S(1)} %get-tuple-element.48), channel_id=1, source_target_pairs={{0,64},{32,96},{64,0},{96,32},{1,65},{33,97},{65,1},{97,33},{2,66}... | collective-permute-start | bytes 786440 | tf_op jit(solution)/shard_map/ppermute | solution.py:24
  8.7 13.6 %collective-permute-start.1 = (bf16[2,64,1024]{2,1,0:T(8,128)(2,1)S(1)}, bf16[2,64,1024]{2,1,0:T(8,128)(2,1)S(1)}, u32[]{:S(2)}, u32[]{:S(2)}) collective-permute-start(bf16[2,64,1024]{2,1,0:T(8,128)(2,1)S(1)} %get-tuple-element.41), channel_id=1, source_target_pairs={{0,96},{32,0},{64,32},{96,64},{1,97},{33,1},{65,33},{97,65},{2,98}... | collective-permute-start | bytes 786440 | tf_op jit(solution)/shard_map/ppermute | solution.py:24
  10.1 12.2 %collective-permute-start.2 = (bf16[2,64,1024]{2,1,0:T(8,128)(2,1)S(1)}, bf16[2,64,1024]{2,1,0:T(8,128)(2,1)S(1)}, u32[]{:S(2)}, u32[]{:S(2)}) collective-permute-start(bf16[2,64,1024]{2,1,0:T(8,128)(2,1)S(1)} %get-tuple-element.39.refs_0_.refs_8_), channel_id=1, source_target_pairs={{0,8},{8,16},{16,24},{24,0},{1,9},{9,17},{17,25},{25,1},{2,10},{10... | collective-permute-start | bytes 786440 | tf_op jit(solution)/shard_map/ppermute | solution.py:24
  12.1 12.0 %collective-permute-start.4 = (bf16[2,64,1024]{2,1,0:T(8,128)(2,1)S(1)}, bf16[2,64,1024]{2,1,0:T(8,128)(2,1)S(1)}, u32[]{:S(2)}, u32[]{:S(2)}) collective-permute-start(bf16[2,64,1024]{2,1,0:T(8,128)(2,1)S(1)} %get-tuple-element.39.refs_0_.refs_8_), channel_id=1, source_target_pairs={{0,24},{8,0},{16,8},{24,16},{1,25},{9,1},{17,9},{25,17},{2,26},{10... | collective-permute-start | bytes 786440 | tf_op jit(solution)/shard_map/ppermute | solution.py:24
  16.0 26.2 %collective-permute-start.13 = (bf16[272,1024]{1,0:T(8,128)(2,1)S(1)}, bf16[272,1024]{1,0:T(8,128)(2,1)S(1)}, u32[]{:S(2)}, u32[]{:S(2)}) collective-permute-start(bf16[272,1024]{1,0:T(8,128)(2,1)S(1)} %fusion.3.refs_16_.refs_8_), channel_id=1, source_target_pairs={{0,6},{2,0},{4,2},{6,4},{1,7},{3,1},{5,3},{7,5},{8,14},{10,8},{12,... | collective-permute-start | bytes 1671176 | tf_op jit(solution)/shard_map/ppermute | solution.py:24
  20.3 11.1 %collective-permute-start.24 = (bf16[2,64,1024]{2,1,0:T(8,128)(2,1)S(1)}, bf16[2,64,1024]{2,1,0:T(8,128)(2,1)S(1)}, u32[]{:S(2)}, u32[]{:S(2)}) collective-permute-start(bf16[2,64,1024]{2,1,0:T(8,128)(2,1)S(1)} %collective-permute-done.23.refs_0_.refs_4_), channel_id=1, source_target_pairs={{0,8},{8,16},{16,24},{24,0},{1,9},{9,17},{17,25},{25,1},{2,10},{10... | collective-permute-start | bytes 786440 | tf_op jit(solution)/shard_map/ppermute | solution.py:24
  22.3 23.5 %collective-permute-start.10 = (bf16[272,1024]{1,0:T(8,128)(2,1)S(1)}, bf16[272,1024]{1,0:T(8,128)(2,1)S(1)}, u32[]{:S(2)}, u32[]{:S(2)}) collective-permute-start(bf16[272,1024]{1,0:T(8,128)(2,1)S(1)} %fusion.3.refs_16_.refs_8_), channel_id=1, source_target_pairs={{0,1},{1,0},{2,3},{3,2},{4,5},{5,4},{6,7},{7,6},{8,9},{9,8},{10,11... | collective-permute-start | bytes 1671176 | tf_op jit(solution)/shard_map/ppermute | solution.py:24
  22.4 20.0 %collective-permute-start.11 = (bf16[272,1024]{1,0:T(8,128)(2,1)S(1)}, bf16[272,1024]{1,0:T(8,128)(2,1)S(1)}, u32[]{:S(2)}, u32[]{:S(2)}) collective-permute-start(bf16[272,1024]{1,0:T(8,128)(2,1)S(1)} %fusion.3.refs_16_.refs_8_), channel_id=1, source_target_pairs={{0,2},{2,4},{4,6},{6,0},{1,3},{3,5},{5,7},{7,1},{8,10},{10,12},{12... | collective-permute-start | bytes 1671176 | tf_op jit(solution)/shard_map/ppermute | solution.py:24
  24.1 24.4 %collective-permute-start.3 = (bf16[2,128,1024]{2,1,0:T(8,128)(2,1)S(1)}, bf16[2,128,1024]{2,1,0:T(8,128)(2,1)S(1)}, u32[]{:S(2)}, u32[]{:S(2)}) collective-permute-start(bf16[2,128,1024]{2,1,0:T(8,128)(2,1)S(1)} %constant_dynamic-update-slice_fusion.refs_1_.refs_9_), channel_id=1, source_target_pairs={{0,8},{8,16},{16,24},{24,0},{1,9},{9,17},{17,25},{25,1},{2,10},{10... | collective-permute-start | bytes 1572872 | tf_op jit(solution)/shard_map/ppermute | solution.py:24
  31.5 7.9 %collective-permute-start.25 = (bf16[2,64,1024]{2,1,0:T(8,128)(2,1)S(1)}, bf16[2,64,1024]{2,1,0:T(8,128)(2,1)S(1)}, u32[]{:S(2)}, u32[]{:S(2)}) collective-permute-start(bf16[2,64,1024]{2,1,0:T(8,128)(2,1)S(1)} %collective-permute-done.23.refs_0_.refs_4_), channel_id=1, source_target_pairs={{0,24},{8,0},{16,8},{24,16},{1,25},{9,1},{17,9},{25,17},{2,26},{10... | collective-permute-start | bytes 786440 | tf_op jit(solution)/shard_map/ppermute | solution.py:24
  39.4 14.5 %collective-permute-start.5 = (bf16[2,128,1024]{2,1,0:T(8,128)(2,1)S(1)}, bf16[2,128,1024]{2,1,0:T(8,128)(2,1)S(1)}, u32[]{:S(2)}, u32[]{:S(2)}) collective-permute-start(bf16[2,128,1024]{2,1,0:T(8,128)(2,1)S(1)} %constant_dynamic-update-slice_fusion.refs_1_.refs_9_), channel_id=1, source_target_pairs={{0,24},{8,0},{16,8},{24,16},{1,25},{9,1},{17,9},{25,17},{2,26},{10... | collective-permute-start | bytes 1572872 | tf_op jit(solution)/shard_map/ppermute | solution.py:24
  42.2 14.9 %copy-start.7 = (bf16[272,1024]{1,0:T(8,128)(2,1)}, bf16[272,1024]{1,0:T(8,128)(2,1)S(1)}, u32[]{:S(2)}) copy-start(bf16[272,1024]{1,0:T(8,128)(2,1)S(1)} %collective-permute-done.13.refs_20_.refs_12_) | copy-start | bytes 1671172
  42.3 6.2 %collective-permute-start.26 = (bf16[1,64,1024]{2,1,0:T(8,128)(2,1)S(1)}, bf16[1,64,1024]{2,1,0:T(8,128)(2,1)S(1)}, u32[]{:S(2)}, u32[]{:S(2)}) collective-permute-start(bf16[1,64,1024]{2,1,0:T(8,128)(2,1)S(1)} %slice.74), channel_id=1, source_target_pairs={{0,8},{8,16},{16,24},{24,0},{1,9},{9,17},{17,25},{25,1},{2,10},{10... | collective-permute-start | bytes 393224 | tf_op jit(solution)/shard_map/ppermute | solution.py:24
  42.4 25.3 %copy-start.5 = (bf16[1,1024]{1,0:T(2,128)(2,1)S(1)}, bf16[1,1024]{1,0:T(2,128)(2,1)}, u32[]{:S(2)}) copy-start(bf16[1,1024]{1,0:T(2,128)(2,1)} %refs_18_.1) | copy-start | bytes 6148
  42.4 21.9 %copy-start.6 = (bf16[272,1024]{1,0:T(8,128)(2,1)}, bf16[272,1024]{1,0:T(8,128)(2,1)S(1)}, u32[]{:S(2)}) copy-start(bf16[272,1024]{1,0:T(8,128)(2,1)S(1)} %collective-permute-done.11.refs_18_.refs_10_) | copy-start | bytes 1671172
  42.4 7.3 %collective-permute-start.16 = (bf16[128,1024]{1,0:T(8,128)(2,1)S(1)}, bf16[128,1024]{1,0:T(8,128)(2,1)S(1)}, u32[]{:S(2)}, u32[]{:S(2)}) collective-permute-start(bf16[128,1024]{1,0:T(8,128)(2,1)S(1)} %slice.73), channel_id=1, source_target_pairs={{0,6},{2,0},{4,2},{6,4},{1,7},{3,1},{5,3},{7,5},{8,14},{10,8},{12,... | collective-permute-start | bytes 786440 | tf_op jit(solution)/shard_map/ppermute | solution.py:24
  45.8 25.9 %copy-start.2 = (bf16[272,1024]{1,0:T(8,128)(2,1)}, bf16[272,1024]{1,0:T(8,128)(2,1)S(1)}, u32[]{:S(2)}) copy-start(bf16[272,1024]{1,0:T(8,128)(2,1)S(1)} %collective-permute-done.10.refs_17_.refs_9_) | copy-start | bytes 1671172
  45.8 8.0 %collective-permute-start.15 = (bf16[144,1024]{1,0:T(8,128)(2,1)S(1)}, bf16[144,1024]{1,0:T(8,128)(2,1)S(1)}, u32[]{:S(2)}, u32[]{:S(2)}) collective-permute-start(bf16[144,1024]{1,0:T(8,128)(2,1)S(1)} %slice.72), channel_id=1, source_target_pairs={{0,2},{2,4},{4,6},{6,0},{1,3},{3,5},{5,7},{7,1},{8,10},{10,12},{12... | collective-permute-start | bytes 884744 | tf_op jit(solution)/shard_map/ppermute | solution.py:24
  48.5 15.8 %collective-permute-start.12 = (bf16[272,1024]{1,0:T(8,128)(2,1)S(1)}, bf16[272,1024]{1,0:T(8,128)(2,1)S(1)}, u32[]{:S(2)}, u32[]{:S(2)}) collective-permute-start(bf16[272,1024]{1,0:T(8,128)(2,1)S(1)} %collective-permute-done.11.refs_18_.refs_10_), channel_id=1, source_target_pairs={{0,1},{1,0},{2,3},{3,2},{4,5},{5,4},{6,7},{7,6},{8,9},{9,8},{10,11... | collective-permute-start | bytes 1671176 | tf_op jit(solution)/shard_map/ppermute | solution.py:24
  48.5 15.9 %collective-permute-start.14 = (bf16[272,1024]{1,0:T(8,128)(2,1)S(1)}, bf16[272,1024]{1,0:T(8,128)(2,1)S(1)}, u32[]{:S(2)}, u32[]{:S(2)}) collective-permute-start(bf16[272,1024]{1,0:T(8,128)(2,1)S(1)} %collective-permute-done.13.refs_20_.refs_12_), channel_id=1, source_target_pairs={{0,1},{1,0},{2,3},{3,2},{4,5},{5,4},{6,7},{7,6},{8,9},{9,8},{10,11... | collective-permute-start | bytes 1671176 | tf_op jit(solution)/shard_map/ppermute | solution.py:24
  49.7 10.9 %collective-permute-start.18 = (bf16[128,1024]{1,0:T(8,128)(2,1)S(1)}, bf16[128,1024]{1,0:T(8,128)(2,1)S(1)}, u32[]{:S(2)}, u32[]{:S(2)}) collective-permute-start(bf16[128,1024]{1,0:T(8,128)(2,1)S(1)} %collective-permute-done.16.refs_23_.refs_15_), channel_id=1, source_target_pairs={{0,1},{1,0},{2,3},{3,2},{4,5},{5,4},{6,7},{7,6},{8,9},{9,8},{10,11... | collective-permute-start | bytes 786440 | tf_op jit(solution)/shard_map/ppermute | solution.py:24
  53.8 13.8 %collective-permute-start.17 = (bf16[144,1024]{1,0:T(8,128)(2,1)S(1)}, bf16[144,1024]{1,0:T(8,128)(2,1)S(1)}, u32[]{:S(2)}, u32[]{:S(2)}) collective-permute-start(bf16[144,1024]{1,0:T(8,128)(2,1)S(1)} %collective-permute-done.15.refs_22_.refs_14_), channel_id=1, source_target_pairs={{0,1},{1,0},{2,3},{3,2},{4,5},{5,4},{6,7},{7,6},{8,9},{9,8},{10,11... | collective-permute-start | bytes 884744 | tf_op jit(solution)/shard_map/ppermute | solution.py:24
  53.9 6.7 %collective-permute-start.27 = (bf16[1,64,1024]{2,1,0:T(8,128)(2,1)S(1)}, bf16[1,64,1024]{2,1,0:T(8,128)(2,1)S(1)}, u32[]{:S(2)}, u32[]{:S(2)}) collective-permute-start(bf16[1,64,1024]{2,1,0:T(8,128)(2,1)S(1)} %slice.75), channel_id=1, source_target_pairs={{0,24},{8,0},{16,8},{24,16},{1,25},{9,1},{17,9},{25,17},{2,26},{10... | collective-permute-start | bytes 393224 | tf_op jit(solution)/shard_map/ppermute | solution.py:24
  60.6 12.7 %collective-permute-start.7 = (bf16[1,128,1024]{2,1,0:T(8,128)(2,1)S(1)}, bf16[1,128,1024]{2,1,0:T(8,128)(2,1)S(1)}, u32[]{:S(2)}, u32[]{:S(2)}) collective-permute-start(bf16[1,128,1024]{2,1,0:T(8,128)(2,1)S(1)} %slice.69), channel_id=1, source_target_pairs={{0,8},{8,16},{16,24},{24,0},{1,9},{9,17},{17,25},{25,1},{2,10},{10... | collective-permute-start | bytes 786440 | tf_op jit(solution)/shard_map/ppermute | solution.py:24
  60.6 12.7 %collective-permute-start.9 = (bf16[1,128,1024]{2,1,0:T(8,128)(2,1)S(1)}, bf16[1,128,1024]{2,1,0:T(8,128)(2,1)S(1)}, u32[]{:S(2)}, u32[]{:S(2)}) collective-permute-start(bf16[1,128,1024]{2,1,0:T(8,128)(2,1)S(1)} %slice.71), channel_id=1, source_target_pairs={{0,24},{8,0},{16,8},{24,16},{1,25},{9,1},{17,9},{25,17},{2,26},{10... | collective-permute-start | bytes 786440 | tf_op jit(solution)/shard_map/ppermute | solution.py:24
  64.3 3.3 %copy-start.9 = (bf16[272,1024]{1,0:T(8,128)(2,1)}, bf16[272,1024]{1,0:T(8,128)(2,1)S(1)}, u32[]{:S(2)}) copy-start(bf16[272,1024]{1,0:T(8,128)(2,1)S(1)} %collective-permute-done.12.refs_19_.refs_11_) | copy-start | bytes 1671172
  64.3 8.9 %collective-permute-start.6 = (bf16[1,64,1024]{2,1,0:T(8,128)(2,1)S(1)}, bf16[1,64,1024]{2,1,0:T(8,128)(2,1)S(1)}, u32[]{:S(2)}, u32[]{:S(2)}) collective-permute-start(bf16[1,64,1024]{2,1,0:T(8,128)(2,1)S(1)} %slice.68), channel_id=1, source_target_pairs={{0,8},{8,16},{16,24},{24,0},{1,9},{9,17},{17,25},{25,1},{2,10},{10... | collective-permute-start | bytes 393224 | tf_op jit(solution)/shard_map/ppermute | solution.py:24
  64.4 3.2 %copy-start.10 = (bf16[272,1024]{1,0:T(8,128)(2,1)}, bf16[272,1024]{1,0:T(8,128)(2,1)S(1)}, u32[]{:S(2)}) copy-start(bf16[272,1024]{1,0:T(8,128)(2,1)S(1)} %collective-permute-done.14.refs_21_.refs_13_) | copy-start | bytes 1671172
  64.4 8.8 %collective-permute-start.8 = (bf16[1,64,1024]{2,1,0:T(8,128)(2,1)S(1)}, bf16[1,64,1024]{2,1,0:T(8,128)(2,1)S(1)}, u32[]{:S(2)}, u32[]{:S(2)}) collective-permute-start(bf16[1,64,1024]{2,1,0:T(8,128)(2,1)S(1)} %slice.70), channel_id=1, source_target_pairs={{0,24},{8,0},{16,8},{24,16},{1,25},{9,1},{17,9},{25,17},{2,26},{10... | collective-permute-start | bytes 393224 | tf_op jit(solution)/shard_map/ppermute | solution.py:24
  87.2 1.4 copy-start
  92.8 11.7 %collective-permute-start.33 = (bf16[272,1024]{1,0:T(8,128)(2,1)S(1)}, bf16[272,1024]{1,0:T(8,128)(2,1)S(1)}, u32[]{:S(2)}, u32[]{:S(2)}) collective-permute-start(bf16[272,1024]{1,0:T(8,128)(2,1)S(1)} %get-tuple-element.64), channel_id=1, source_target_pairs={{0,1},{1,0},{2,3},{3,2},{4,5},{5,4},{6,7},{7,6},{8,9},{9,8},{10,11... | collective-permute-start | bytes 1671176 | tf_op jit(solution)/shard_map/ppermute | solution.py:24
  92.9 12.5 %collective-permute-start.34 = (bf16[272,1024]{1,0:T(8,128)(2,1)S(1)}, bf16[272,1024]{1,0:T(8,128)(2,1)S(1)}, u32[]{:S(2)}, u32[]{:S(2)}) collective-permute-start(bf16[272,1024]{1,0:T(8,128)(2,1)S(1)} %get-tuple-element.65), channel_id=1, source_target_pairs={{0,1},{1,0},{2,3},{3,2},{4,5},{5,4},{6,7},{7,6},{8,9},{9,8},{10,11... | collective-permute-start | bytes 1671176 | tf_op jit(solution)/shard_map/ppermute | solution.py:24
  93.4 13.1 %collective-permute-start.35 = (bf16[272,1024]{1,0:T(8,128)(2,1)S(1)}, bf16[272,1024]{1,0:T(8,128)(2,1)S(1)}, u32[]{:S(2)}, u32[]{:S(2)}) collective-permute-start(bf16[272,1024]{1,0:T(8,128)(2,1)S(1)} %get-tuple-element.66), channel_id=1, source_target_pairs={{0,1},{1,0},{2,3},{3,2},{4,5},{5,4},{6,7},{7,6},{8,9},{9,8},{10,11... | collective-permute-start | bytes 1671176 | tf_op jit(solution)/shard_map/ppermute | solution.py:24
  93.5 15.1 %collective-permute-start.36 = (bf16[272,1024]{1,0:T(8,128)(2,1)S(1)}, bf16[272,1024]{1,0:T(8,128)(2,1)S(1)}, u32[]{:S(2)}, u32[]{:S(2)}) collective-permute-start(bf16[272,1024]{1,0:T(8,128)(2,1)S(1)} %get-tuple-element.67), channel_id=1, source_target_pairs={{0,1},{1,0},{2,3},{3,2},{4,5},{5,4},{6,7},{7,6},{8,9},{9,8},{10,11... | collective-permute-start | bytes 1671176 | tf_op jit(solution)/shard_map/ppermute | solution.py:24
  93.9 7.7 %collective-permute-start.28 = (bf16[80,1024]{1,0:T(8,128)(2,1)S(1)}, bf16[80,1024]{1,0:T(8,128)(2,1)S(1)}, u32[]{:S(2)}, u32[]{:S(2)}) collective-permute-start(bf16[80,1024]{1,0:T(8,128)(2,1)S(1)} %get-tuple-element.50), channel_id=1, source_target_pairs={{0,16},{8,24},{16,0},{24,8},{1,17},{9,25},{17,1},{25,9},{2,18},{10... | collective-permute-start | bytes 491528 | tf_op jit(solution)/shard_map/ppermute | solution.py:24
  101.6 28.6 %collective-permute-start.19 = (bf16[208,1024]{1,0:T(8,128)(2,1)S(1)}, bf16[208,1024]{1,0:T(8,128)(2,1)S(1)}, u32[]{:S(2)}, u32[]{:S(2)}) collective-permute-start(bf16[208,1024]{1,0:T(8,128)(2,1)S(1)} %get-tuple-element.43), channel_id=1, source_target_pairs={{0,16},{8,24},{16,0},{24,8},{1,17},{9,25},{17,1},{25,9},{2,18},{10... | collective-permute-start | bytes 1277960 | tf_op jit(solution)/shard_map/ppermute | solution.py:24
  104.5 25.9 %collective-permute-start.20 = (bf16[208,1024]{1,0:T(8,128)(2,1)S(1)}, bf16[208,1024]{1,0:T(8,128)(2,1)S(1)}, u32[]{:S(2)}, u32[]{:S(2)}) collective-permute-start(bf16[208,1024]{1,0:T(8,128)(2,1)S(1)} %get-tuple-element.44), channel_id=1, source_target_pairs={{0,24},{8,0},{16,8},{24,16},{1,25},{9,1},{17,9},{25,17},{2,26},{10... | collective-permute-start | bytes 1277960 | tf_op jit(solution)/shard_map/ppermute | solution.py:24
  105.4 25.8 %collective-permute-start.21 = (bf16[208,1024]{1,0:T(8,128)(2,1)S(1)}, bf16[208,1024]{1,0:T(8,128)(2,1)S(1)}, u32[]{:S(2)}, u32[]{:S(2)}) collective-permute-start(bf16[208,1024]{1,0:T(8,128)(2,1)S(1)} %get-tuple-element.45), channel_id=1, source_target_pairs={{0,8},{8,16},{16,24},{24,0},{1,9},{9,17},{17,25},{25,1},{2,10},{10... | collective-permute-start | bytes 1277960 | tf_op jit(solution)/shard_map/ppermute | solution.py:24
  106.5 20.5 %collective-permute-start.29 = (bf16[80,1024]{1,0:T(8,128)(2,1)S(1)}, bf16[80,1024]{1,0:T(8,128)(2,1)S(1)}, u32[]{:S(2)}, u32[]{:S(2)}) collective-permute-start(bf16[80,1024]{1,0:T(8,128)(2,1)S(1)} %get-tuple-element.51), channel_id=1, source_target_pairs={{0,24},{8,0},{16,8},{24,16},{1,25},{9,1},{17,9},{25,17},{2,26},{10... | collective-permute-start | bytes 491528 | tf_op jit(solution)/shard_map/ppermute | solution.py:24
  108.6 18.4 %collective-permute-start.30 = (bf16[80,1024]{1,0:T(8,128)(2,1)S(1)}, bf16[80,1024]{1,0:T(8,128)(2,1)S(1)}, u32[]{:S(2)}, u32[]{:S(2)}) collective-permute-start(bf16[80,1024]{1,0:T(8,128)(2,1)S(1)} %get-tuple-element.52), channel_id=1, source_target_pairs={{0,8},{8,16},{16,24},{24,0},{1,9},{9,17},{17,25},{25,1},{2,10},{10... | collective-permute-start | bytes 491528 | tf_op jit(solution)/shard_map/ppermute | solution.py:24
  114.3 17.0 %copy-start.1 = (f32[208,1024]{1,0:T(8,128)S(1)}, f32[208,1024]{1,0:T(8,128)}, u32[]{:S(2)}) copy-start(f32[208,1024]{1,0:T(8,128)} %get-tuple-element.42.own) | copy-start | bytes 2555908
  127.0 26.6 %collective-permute-start.39 = (bf16[272,1024]{1,0:T(8,128)(2,1)S(1)}, bf16[272,1024]{1,0:T(8,128)(2,1)S(1)}, u32[]{:S(2)}, u32[]{:S(2)}) collective-permute-start(bf16[272,1024]{1,0:T(8,128)(2,1)S(1)} %get-tuple-element.71), channel_id=1, source_target_pairs={{0,2},{2,4},{4,6},{6,0},{1,3},{3,5},{5,7},{7,1},{8,10},{10,12},{12... | collective-permute-start | bytes 1671176 | tf_op jit(solution)/shard_map/ppermute | solution.py:24
  127.0 26.6 %collective-permute-start.38 = (bf16[272,1024]{1,0:T(8,128)(2,1)S(1)}, bf16[272,1024]{1,0:T(8,128)(2,1)S(1)}, u32[]{:S(2)}, u32[]{:S(2)}) collective-permute-start(bf16[272,1024]{1,0:T(8,128)(2,1)S(1)} %get-tuple-element.70), channel_id=1, source_target_pairs={{0,6},{2,0},{4,2},{6,4},{1,7},{3,1},{5,3},{7,5},{8,14},{10,8},{12,... | collective-permute-start | bytes 1671176 | tf_op jit(solution)/shard_map/ppermute | solution.py:24
  130.3 23.4 %collective-permute-start.37 = (bf16[272,1024]{1,0:T(8,128)(2,1)S(1)}, bf16[272,1024]{1,0:T(8,128)(2,1)S(1)}, u32[]{:S(2)}, u32[]{:S(2)}) collective-permute-start(bf16[272,1024]{1,0:T(8,128)(2,1)S(1)} %get-tuple-element.69), channel_id=1, source_target_pairs={{0,4},{2,6},{4,0},{6,2},{1,5},{3,7},{5,1},{7,3},{8,12},{10,14},{12... | collective-permute-start | bytes 1671176 | tf_op jit(solution)/shard_map/ppermute | solution.py:24
  130.4 7.8 %collective-permute-start.31 = (bf16[80,1024]{1,0:T(8,128)(2,1)S(1)}, bf16[80,1024]{1,0:T(8,128)(2,1)S(1)}, u32[]{:S(2)}, u32[]{:S(2)}) collective-permute-start(bf16[80,1024]{1,0:T(8,128)(2,1)S(1)} %sum_z.3), channel_id=1, source_target_pairs={{0,64},{32,96},{64,0},{96,32},{1,65},{33,97},{65,1},{97,33},{2,66}... | collective-permute-start | bytes 491528 | tf_op jit(solution)/shard_map/ppermute | solution.py:24
  131.2 22.4 %copy-start.8 = (f32[272,1024]{1,0:T(8,128)S(1)}, f32[272,1024]{1,0:T(8,128)}, u32[]{:S(2)}) copy-start(f32[272,1024]{1,0:T(8,128)} %get-tuple-element.68) | copy-start | bytes 3342340
  131.4 6.7 %collective-permute-start.22 = (bf16[80,1024]{1,0:T(8,128)(2,1)S(1)}, bf16[80,1024]{1,0:T(8,128)(2,1)S(1)}, u32[]{:S(2)}, u32[]{:S(2)}) collective-permute-start(bf16[80,1024]{1,0:T(8,128)(2,1)S(1)} %get-tuple-element.47), channel_id=1, source_target_pairs={{0,96},{32,0},{64,32},{96,64},{1,97},{33,1},{65,33},{97,65},{2,98}... | collective-permute-start | bytes 491528 | tf_op jit(solution)/shard_map/ppermute | solution.py:24
  138.1 6.5 %collective-permute-start.32 = (bf16[80,1024]{1,0:T(8,128)(2,1)S(1)}, bf16[80,1024]{1,0:T(8,128)(2,1)S(1)}, u32[]{:S(2)}, u32[]{:S(2)}) collective-permute-start(bf16[80,1024]{1,0:T(8,128)(2,1)S(1)} %get-tuple-element.53), channel_id=1, source_target_pairs={{0,32},{32,64},{64,96},{96,0},{1,33},{33,65},{65,97},{97,1},{2,34}... | collective-permute-start | bytes 491528 | tf_op jit(solution)/shard_map/ppermute | solution.py:24

commit v2 on v0

v2 whole, which is shorter than its diff:
```python
import functools

import jax
import jax.numpy as jnp
from jax import lax
from jax.experimental import pallas as pl
from jax.experimental.pallas import tpu as pltpu
from jax.sharding import Mesh, PartitionSpec as P

BF = jnp.bfloat16
F32 = jnp.float32
EXTRA = 16
NT = (((1,), (1,)), ((), ()))
NN = (((1,), (0,)), ((), ()))
TN = (((0,), (0,)), ((), ()))


def dot(a, b, dims):
    return lax.dot_general(a, b, dims, preferred_element_type=F32)


def shift(value, axis, step):
    n = lax.axis_size(axis)
    return lax.ppermute(value, axis, [(i, (i + step) % n) for i in range(n)])


def shift_y(value, step, mirrored):
    n = lax.axis_size("y")
    moves = []
    for y in range(n):
        for c in range(2):
            to = (y + (-step if mirrored and c else step)) % n
            moves.append((2 * y + c, 2 * to + c))
    return lax.ppermute(value, ("y", "c"), moves)


def shape(rows, columns, dtype=BF):
    return jax.ShapeDtypeStruct((rows, columns), dtype)


def full(a):
    return pl.BlockSpec(a.shape, lambda i: (0,) * len(a.shape))


def lead(a, index):
    return pl.BlockSpec((1, *a.shape[1:]), lambda i: (index,) + (0,) * (len(a.shape) - 1))


def call(kernel, name, out_shape, operands, flops=0, scratch=(), vmem=8):
    pairs = [o if isinstance(o, tuple) else (o, None) for o in operands]
    size = sum(a.size * a.dtype.itemsize for a, _ in pairs)
    size += sum(s.size * s.dtype.itemsize for s in out_shape)
    return pl.pallas_call(
        kernel,
        out_shape=out_shape,
        grid=(1,),
        in_specs=[full(a) if k is None else lead(a, k) for a, k in pairs],
        out_specs=[full(s) for s in out_shape],
        scratch_shapes=scratch,
        compiler_params=pltpu.CompilerParams(vmem_limit_bytes=vmem * 1024 * 1024),
        cost_estimate=pl.CostEstimate(flops=flops, bytes_accessed=size, transcendentals=0),
        name=name,
    )(*[a for a, _ in pairs])


def call_loading(kernel, name, out_shape, arrays):
    n = len(arrays)

    def body(*refs):
        sources, outs = refs[:n], refs[n : n + len(out_shape)]
        copies, sems = refs[n + len(out_shape) : -1], refs[-1]
        moves = [
            pltpu.make_async_copy(a, b, sems.at[k])
            for k, (a, b) in enumerate(zip(sources, copies))
        ]
        for m in moves:
            m.start()
        for m in moves:
            m.wait()
        kernel(*copies, *outs)

    return pl.pallas_call(
        body,
        out_shape=out_shape,
        in_specs=[pl.BlockSpec(memory_space=pl.ANY)] * n,
        out_specs=[pl.BlockSpec(memory_space=pltpu.VMEM)] * len(out_shape),
        scratch_shapes=[pltpu.VMEM(a.shape, a.dtype) for a in arrays]
        + [pltpu.SemaphoreType.DMA((n,))],
        compiler_params=pltpu.CompilerParams(vmem_limit_bytes=56 * 1024 * 1024),
        name=name,
    )(*arrays)


def high_low(value):
    high = value.astype(BF).astype(F32)
    return [high, value - high]


def lines_of(lines, width, dtype):
    m = lines[0].shape[1]
    rest = EXTRA - sum(line.shape[0] for line in lines)
    block = jnp.concatenate(lines + [jnp.zeros((rest, m), F32)], axis=0)
    if m < width:
        block = jnp.concatenate([block, jnp.zeros((EXTRA, width - m), F32)], axis=1)
    return block.astype(dtype)


def share_kernel(w_in, b_in, w_out, out):
    units = w_out.shape[1]
    out[0:units] = w_in[0].astype(F32).T.astype(BF)
    out[units : units + EXTRA] = lines_of([b_in[...].astype(F32)], out.shape[1], BF)
    out[units + EXTRA :] = w_out[0]


def prepare_kernel(routes, slots, combine, tokens, grads, raw, places, *outs):
    n_expert = len(outs)
    cap = outs[0].shape[0]
    n_tok = tokens.shape[0]
    turned = routes[...] - lax.axis_index("x")
    turned = jnp.where(turned < 0, turned + n_expert, turned)
    place = jnp.where(slots[...] < cap, turned * cap + slots[...], -1)
    places[...] = place
    raw[0:n_tok] = grads[...]
    side = [place.astype(F32), combine[...].astype(F32)]
    raw[n_tok:] = lines_of(side, grads.shape[1], BF)
    spots = lax.broadcasted_iota(jnp.int32, (n_expert * cap, n_tok), 0)
    picks = jnp.where((place[0:1, :] == spots) | (place[1:2, :] == spots), 1.0, 0.0)
    rows = dot(picks.astype(BF), tokens[...], NN).astype(BF)
    for s, out in enumerate(outs):
        out[...] = rows[s * cap : (s + 1) * cap]


def douts_kernel(own, below, above, far, *outs):
    cap = outs[0].shape[1]
    n_tok = own.shape[0] - EXTRA
    for z, raw in enumerate((own[...], below[...], above[...], far[...])):
        side = raw[n_tok : n_tok + 4, 0:n_tok].astype(F32)
        spots = lax.broadcasted_iota(jnp.int32, (len(outs) * cap, n_tok), 0)
        place = side[0:2].astype(jnp.int32)
        picks = jnp.where(place[0:1] == spots, side[2:3], 0.0)
        picks = picks + jnp.where(place[1:2] == spots, side[3:4], 0.0)
        rows = dot(picks.astype(BF), raw[0:n_tok], NN).astype(BF)
        for s, out in enumerate(outs):
            out[z] = rows[s * cap : (s + 1) * cap]


def rows_kernel(n_x, n_z, n_d, with_bias, *refs):
    n_d = n_z * n_d
    xs, ds = refs[:n_x], refs[n_x : n_x + n_d]
    mine, other, direct, mirror, far_w, b_out, *outs = refs[n_x + n_d :]
    x, d, dpre, hidden, *dxs = outs
    shares = [
        (mine, other),
        (direct.at[0], direct.at[1]),
        (mirror.at[1], mirror.at[0]),
        (far_w.at[0], far_w.at[1]),
    ]
    width = x.shape[1]
    for parts, whole in ((xs, x), (ds, d)):
        at = 0
        for p in parts:
            count = p.shape[-2]
            whole[at : at + count] = p[...].reshape(count, width)
            at += count
    n_y = len(shares)
    unit = (mine.shape[0] - EXTRA) // 2
    xb = x[...]
    db = d[...]

    def w_in_of(k):
        return jnp.concatenate([r[0:unit] for r in shares[k]], axis=0)

    def dots(k):
        bias = jnp.concatenate([r[unit : unit + 1, 0:unit] for r in shares[k]], axis=1)
        w_out = jnp.concatenate([r[unit + EXTRA :] for r in shares[k]], axis=0)
        return dot(xb, w_in_of(k), NT) + bias.astype(F32), dot(db, w_out, NT)

    term = total = grad = None
    now = dots(0)
    for k in range(n_y):
        pre, back = now
        if k + 1 < n_y:
            now = dots(k + 1)
        cdf = 0.5 * (1.0 + lax.erf(pre * 0.7071067811865476))
        dens = jnp.exp(-0.5 * pre * pre) * 0.3989422804014327
        hidden32 = pre * cdf
        new = (back * (cdf + pre * dens)).astype(BF)
        hid = hidden32.astype(BF)
        for c in range(2):
            dpre[c, :, k * unit : (k + 1) * unit] = new[:, c * unit : (c + 1) * unit]
            hidden[c, :, k * unit : (k + 1) * unit] = hid[:, c * unit : (c + 1) * unit]
        by_row = hidden32 * back
        term = by_row if k == 0 else term + by_row
        if k > 0:
            part = dot(grad, w_in_of(k - 1), NN)
            total = part if k == 1 else total + part
        grad = new
    total = total + dot(grad, w_in_of(n_y - 1), NN)
    line = jnp.sum(term.T, axis=0, keepdims=True)
    m = x.shape[0] // n_z
    if n_z == 1:
        low, high = dxs
        cut = low.shape[0]
        low[...] = total[0:cut].astype(BF)
        high[0 : m - cut] = total[cut:].astype(BF)
        high[m - cut :] = lines_of(high_low(line), width, BF)
    else:
        for z, out in enumerate(dxs):
            out[0:m] = total[z * m : (z + 1) * m]
            own = line[:, z * m : (z + 1) * m]
            if z == 0:
                by_bias = (d[0:m].astype(F32) * b_out[...].astype(F32)).T
                own = own + jnp.sum(by_bias, axis=0, keepdims=True)
            out[m:] = lines_of([own], width, F32)


def rows_set(xs, ds, w, b_out):
    n_z = len(ds)
    width = b_out.shape[1]
    m = sum(a.shape[0] for a in xs)
    units = 4 * (w[0].shape[0] - EXTRA)
    part = jax.ShapeDtypeStruct((2, m, units // 2), BF)
    if n_z == 1:
        dxs = [shape(m // 2, width), shape(m // 2 + EXTRA, width)]
    else:
        dxs = [shape(m // n_z + EXTRA, width, F32)] * n_z
    return call(
        functools.partial(rows_kernel, len(xs), n_z, len(ds[0]), n_z > 1),
        "rows",
        [shape(m, width), shape(m, width), part, part, *dxs],
        [*xs, *[p for z in ds for p in z], *w, b_out],
        flops=6 * m * units * width,
        vmem=14 if n_z == 1 else 28,
    )


def weights_sums(n_sets, refs):
    xs, ds, dpres, hiddens = (refs[k * n_sets : (k + 1) * n_sets] for k in range(4))
    grad_in = sum(dot(p[0], x[...], TN) for p, x in zip(dpres, xs))
    grad_out = sum(dot(h[0], d[...], TN) for h, d in zip(hiddens, ds))
    sum_in = sum(jnp.sum(p[0].astype(F32), axis=0, keepdims=True) for p in dpres)
    sum_out = sum(jnp.sum(d[...].astype(F32), axis=0, keepdims=True) for d in ds)
    gap = jnp.zeros((1, sum_out.shape[1] - sum_in.shape[1]), F32)
    return grad_in, grad_out, jnp.concatenate([sum_in, gap], axis=1), sum_out


def away_kernel(n_sets, *refs):
    out = refs[4 * n_sets]
    grad_in, grad_out, sum_in, sum_out = weights_sums(n_sets, refs)
    units = grad_in.shape[0]
    out[0:units] = grad_in.astype(BF)
    out[units : 2 * units] = grad_out.astype(BF)
    out[2 * units :] = lines_of(high_low(sum_in) + high_low(sum_out), out.shape[1], BF)


def home_kernel(n_sets, *refs):
    got, *outs = refs[4 * n_sets :]
    grad_in, grad_out, sum_in, sum_out = weights_sums(n_sets, refs)
    units, width = grad_in.shape
    side = got[2 * units : 2 * units + 4].astype(F32)
    sum_out = sum_out + side[2:3] + side[3:4]
    side = side[0:1] + side[1:2]
    n_y = len(outs)
    unit = units // n_y
    for k, out in enumerate(outs):
        here = slice(k * unit, (k + 1) * unit)
        there = (0, 2, 1, 3)[k] * unit
        line = sum_in[:, here] + side[:, there : there + unit]
        line = jnp.concatenate([line, jnp.zeros((1, width - unit), F32)], axis=1)
        total = grad_in[here] + got[there : there + unit].astype(F32)
        out[0:unit] = total.astype(out.dtype)
        total = grad_out[here] + got[units + there : units + there + unit].astype(F32)
        out[unit : 2 * unit] = total.astype(out.dtype)
        if k == 0:
            lines = [line, jnp.zeros_like(line), sum_out]
        else:
            lines = high_low(line) + high_low(sum_out)
        out[2 * unit :] = lines_of(lines, width, out.dtype)


def weights_part(sets, core, got):
    x, d, dpre, hidden = zip(*sets)
    width = x[0].shape[1]
    units = dpre[0].shape[2]
    n_y = 4
    operands = [*x, *d, *[(p, core) for p in dpre], *[(h, core) for h in hidden]]
    flops = 4 * sum(a.shape[0] for a in x) * units * width
    if got is None:
        kernel = functools.partial(away_kernel, len(sets))
        out = [shape(2 * units + EXTRA, width)]
        return call(kernel, "away", out, operands, flops, vmem=20)[0]
    unit = units // n_y
    return call(
        functools.partial(home_kernel, len(sets)),
        "home",
        [shape(2 * unit + EXTRA, width, BF if r else F32) for r in range(n_y)],
        [*operands, got],
        flops,
        vmem=24,
    )


def last_kernel(own, a, b, c, grad_in, grad_bias_in, grad_out, grad_bias_out):
    units = grad_out.shape[1]
    total = own[...] + a[...].astype(F32) + b[...].astype(F32) + c[...].astype(F32)
    grad_in[0] = total[0:units].T.astype(BF)
    grad_out[0] = total[units : 2 * units].astype(BF)
    tail = total[2 * units :]
    grad_bias_in[...] = (tail[0:1] + tail[1:2])[:, 0:units]
    grad_bias_out[...] = tail[2:3] + tail[3:4]


def join_kernel(below, above, got_below, got_above, out_below, out_above):
    m = below.shape[0] - EXTRA
    width = below.shape[1]
    cut = got_above.shape[0]
    out_above[0:cut] = (above[0:cut] + got_above[...].astype(F32)).astype(BF)
    out_above[cut:m] = above[cut:m].astype(BF)
    out_above[m:] = lines_of(high_low(above[m : m + 1]), width, BF)
    out_below[0:cut] = below[0:cut].astype(BF)
    out_below[cut:m] = (below[cut:m] + got_below[0 : m - cut].astype(F32)).astype(BF)
    side = got_below[m - cut : m - cut + 2].astype(F32)
    out_below[m:] = lines_of(high_low(below[m : m + 1] + side[0:1] + side[1:2]), width, BF)


def sum_kernel(own, a, b, out):
    n_expert = out.shape[0]
    here = lax.axis_index("x")
    m = own.shape[0] - EXTRA
    total = own[...] + a[...].astype(F32) + b[...].astype(F32)
    lines = lines_of(high_low(total[m : m + 1] + total[m + 1 : m + 2]), own.shape[1], BF)
    cap = m // n_expert
    for s in range(n_expert):
        to = lax.rem(here + (n_expert - s), n_expert)
        out[to, 0:cap] = total[s * cap : (s + 1) * cap].astype(BF)
        out[to, cap:] = lines


def finish_kernel(places, weights, pieces, out, by_weight):
    n_expert = pieces.shape[0]
    cap = pieces.shape[1] - EXTRA
    n_tok = places.shape[1]
    here = lax.axis_index("x")
    total = None
    sums = [None, None]
    spots = lax.broadcasted_iota(jnp.int32, (n_expert * cap, n_tok), 0)
    picks = [jnp.where(places[k : k + 1, :] == spots, 1.0, 0.0) for k in range(2)]
    both = (picks[0] + picks[1]).astype(BF)
    for s in range(n_expert):
        piece = pieces.at[lax.rem(here + s, n_expert)]
        part = dot(both[s * cap : (s + 1) * cap], piece[0:cap], TN)
        total = part if total is None else total + part
        inside = (spots >= s * cap) & (spots < (s + 1) * cap)
        for k in range(2):
            pick = jnp.where(inside, picks[k], 0.0).astype(BF)
            found = dot(piece[cap:, 0 : n_expert * cap], pick, NN)
            line = found[0:1] + found[1:2]
            sums[k] = line if sums[k] is None else sums[k] + line
    out[...] = total.astype(BF)
    by_weight[...] = jnp.concatenate(sums, axis=0) / weights[...].astype(F32)


def on_device(tokens, grads_out, routes, slots, combine, w_in, b_in, w_out, b_out):
    n_expert = lax.axis_size("x")
    tok_rows, width = tokens.shape
    cap = 2 * tok_rows // n_expert
    units = w_in.shape[2]

    barrier = lax.optimization_barrier

    raw, places, *x_sent = call_loading(
        prepare_kernel,
        "prepare",
        [shape(tok_rows + EXTRA, width), shape(2, tok_rows, jnp.int32)]
        + [shape(cap, width)] * n_expert,
        [routes.T, slots.T, combine.T, tokens, grads_out],
    )
    raw_below = shift(raw, "z", 1)
    raw_above = shift(raw, "z", -1)
    x_got = [x_sent[0]] + [shift(x_sent[s], "x", s) for s in range(1, n_expert)]
    raw_below, raw_above, w_in, w_out, b_in, *x_got = barrier(
        (raw_below, raw_above, w_in, w_out, b_in, *x_got)
    )

    raw_far = shift(raw_below, "z", 1)
    mine = call_loading(
        share_kernel, "share", [shape(2 * units + EXTRA, width)], [w_in, b_in, w_out]
    )[0]
    other = shift(mine, "c", 1)
    x_own = jnp.concatenate(x_got, axis=0)
    both = jnp.stack([mine, other])
    x_own, raw_far, both = barrier((x_own, raw_far, both))

    d_sent = call(
        douts_kernel,
        "douts",
        [jax.ShapeDtypeStruct((4, cap, width), BF)] * n_expert,
        [raw, raw_below, raw_above, raw_far],
    )
    x_below = shift(x_own, "z", 1)
    x_above = shift(x_own, "z", -1)
    direct = shift_y(both, 1, True)
    d_1 = shift(d_sent[1], "x", 1)
    d_3 = shift(d_sent[3], "x", -1)
    x_below, x_above, direct, d_1, d_3, d_2 = barrier(
        (x_below, x_above, direct, d_1, d_3, d_sent[2])
    )

    d_2 = shift(d_2, "x", 2)
    far_w = shift_y(direct, 1, True)
    x_far = shift(x_below, "z", 1)
    mirror = shift(direct, "c", 1)
    d = [d_sent[0], d_1, d_2, d_3]
    w = [mine, other, direct, mirror, far_w]

    far = rows_set([x_far], [[(a, 3) for a in d]], w, b_out)
    x_own, low, high = lax.optimization_barrier((x_own, far[4], far[5]))
    got_above = shift(low, "z", 1)
    got_below = shift(high, "z", -1)
    near = rows_set([x_own, x_below, x_above], [[(a, z) for a in d] for z in range(3)], w, b_out)
    sets = [far[:4], near[:4]]

    away = weights_part(sets, 1, None)
    away, got_above, got_below = lax.optimization_barrier((away, got_above, got_below))
    home = weights_part(sets, 0, shift(away, "c", 1))

    own, below, above = near[4:]
    like = shape(*own.shape)
    out_below, out_above = call(
        join_kernel, "join", [like, like], [below, above, got_below, got_above]
    )
    parts = [shift(out_above, "z", 1), shift(out_below, "z", -1)]
    like = jax.ShapeDtypeStruct((n_expert, cap + EXTRA, width), BF)
    pieces = call(sum_kernel, "sum_z", [like], [own, *parts])[0]
    final = lax.all_to_all(pieces, "x", 0, 0, tiled=True)
    moved = [
        shift_y(home[3], 2, False),
        shift_y(home[1], -1, True),
        shift_y(home[2], 1, True),
    ]
    grad_tokens, by_weight = call(
        finish_kernel,
        "finish",
        [shape(tok_rows, width), shape(2, tok_rows, F32)],
        [places, combine.T, final],
    )
    grad_w_in, grad_b_in, grad_w_out, grad_b_out = call(
        last_kernel,
        "last",
        [
            jax.ShapeDtypeStruct(w_in.shape, BF),
            shape(1, units, F32),
            jax.ShapeDtypeStruct(w_out.shape, BF),
            shape(1, width, F32),
        ],
        [home[0], *moved],
    )
    return (grad_tokens, by_weight.T, grad_w_in, grad_b_in, grad_w_out, grad_b_out)


def solution(mesh):
    fine = Mesh(mesh.devices.reshape(4, 4, 4, 2), ("x", "z", "y", "c"))
    zero = ("z", "y", "c")
    rows = P(("x", "z", "y", "c"), None)
    in_specs = (rows,) * 5 + (
        P("x", None, zero),
        P("x", zero),
        P("x", zero, None),
        P("x", None),
    )
    out_specs = (rows, rows) + in_specs[5:]
    return jax.shard_map(
        on_device, mesh=fine, in_specs=in_specs, out_specs=out_specs, check_vma=False
    )
```

time: 353 us -> 118 us (0.33)
  waiting for transfers between devices: 185 us -> 52.3 us
  matrix products: 50.9 us -> 0 us
  other arithmetic: 28.3 us -> 0.14 us
  blocking collectives: 36.7 us -> 13.4 us
  Pallas kernels: 0 us -> 20 us
  between operations: 13.9 us -> 0.85 us
  local copies, waits for them, and re-layouts: 9.16 us -> 0.03 us
  starting transfers between devices: 26.7 us -> 31 us
    all_gather x4 -> x0, waiting for transfers between devices: 93.3 us -> none  [the longest x1 47.1 us: on_device(): lax.all_gather(w_out, 'zero', axis=1, tiled=True)]
    all_to_all x6 -> x0, waiting for transfers between devices: 90.3 us -> none  [the longest x1 45 us: on_device(): lax.all_to_all(dpre, 'zero', split_axis=1, concat_axis=0, tiled=True)]
    ppermute x0 -> x24, waiting for transfers between devices: none -> 52.3 us  [the longest x19 48.3 us: shift(): return lax.ppermute(value, axis, [(i, (i + step) % n) for i in range(n)])]
    dot_general x10 -> x0, matrix products: 50.9 us -> none  [the longest x2 22.8 us: group_partials(): jnp.einsum('nra,nrb->nab', left_g, right_g, preferred_element_type=jnp.fl...]
    ppermute x0 -> x24, starting transfers between devices: none -> 31 us  [the longest x19 25.1 us: shift(): return lax.ppermute(value, axis, [(i, (i + step) % n) for i in range(n)])]
    all_to_all x6 -> x0, starting transfers between devices: 26.5 us -> none  [the longest x1 5.82 us: on_device(): lax.all_to_all(dpre, 'zero', split_axis=1, concat_axis=0, tiled=True)]
    reduce_sum x5 -> x0, other arithmetic: 24.5 us -> none  [the longest x2 11.8 us: group_partials(): return jnp.sum(parts.astype(jnp.float32), axis=0).astype(jnp.bfloat16)]
    all_gather x1 -> x0, blocking collectives: 22.9 us -> none  [on_device(): lax.all_gather(b_in, 'zero', axis=1, tiled=True)]
  transfers between devices with their start and end apart: 10 -> 24, of which waited for: 8 -> 12; matrix products, arithmetic and copies ran while one was open for 15% -> 0% of each run, Pallas kernels for 0% -> 11%
where the time goes in v2:
time: 118 us
  waiting for transfers between devices  52.3 us (44%)
  starting transfers between devices  31 us (26%)
  Pallas kernels  20 us (17%)
  blocking collectives  13.4 us (11%)
    ppermute x19, waiting for transfers between devices, shift(): return lax.ppermute(value, axis, [(i, (i + step) % n) for i in range(n)])  48.3 us
    ppermute x19, starting transfers between devices, shift(): return lax.ppermute(value, axis, [(i, (i + step) % n) for i in range(n)])  25.1 us
    pallas_call x9, Pallas kernels, call(): pl.pallas_call(kernel, out_shape=out_shape, grid=(1,), in_specs=[full(a)...  15.7 us
    all_to_all x1, blocking collectives, on_device(): final = lax.all_to_all(pieces, 'x', 0, 0, tiled=True)  13.4 us
    ppermute x5, starting transfers between devices, shift_y(): return lax.ppermute(value, ('y', 'c'), moves)  5.84 us
    pallas_call x2, Pallas kernels, call_loading(): pl.pallas_call(body, out_shape=out_shape, in_specs=[pl.BlockSpec(memory_s...  4.25 us
    ppermute x5, waiting for transfers between devices, shift_y(): return lax.ppermute(value, ('y', 'c'), moves)  4.02 us
  transfers between devices with their start and end apart: 24, of which 12 were waited for; matrix products, arithmetic and copies ran while one was open for 0% of the time, Pallas kernels for 11%

profile of v2, /device:TPU:0, one launch (start us, length us, event | category | flops | bytes accessed | tf_op | source)
XLA Modules:
  0.0 117.7 jit_solution(1012473242107837883)
XLA Ops:
  0.6 2.2 %prepare.1 = (bf16[144,1024]{1,0:T(8,128)(2,1)}, s32[2,128]{1,0:T(2,128)}, bf16[64,1024]{1,0:T(8,128)(2,1)}, bf16[64,1024]{1,0:T(8,128)(2,1)}, bf16[64,1024]{1,0:T(8,128)(2,1)}, /*index=5*/bf16[64,1024]{1,0:T(8,128)(2,1)}) custom-call(s32[2,128]{1,0:T(2,128)} %bitcast.10, s32[2,128]{1,0:T(2,128)} %bitcast.11, bf16[2,128]{1,0:T(2,128)(2,1)} %bitcast.8, ...), custom_call_target="tpu_custom_call" | custom-call | tf_op jit(solution)/shard_map/prepare/pallas_call | solution.py:82
  2.9 0.0 copy-start.5
  2.9 4.2 %collective-permute-start.1 = (bf16[144,1024]{1,0:T(8,128)(2,1)}, bf16[144,1024]{1,0:T(8,128)(2,1)S(1)}, u32[]{:S(2)}, u32[]{:S(2)}) collective-permute-start(bf16[144,1024]{1,0:T(8,128)(2,1)} %get-tuple-element.66.own), channel_id=1, source_target_pairs={{0,24},{8,0},{16,8},{24,16},{1,25},{9,1},{17,9},{25,17},{2,26},{10... | collective-permute-start | bytes 884744 | tf_op jit(solution)/shard_map/ppermute | solution.py:24
  7.1 0.0 collective-permute-start
  7.1 1.5 %collective-permute-start.2 = (bf16[64,1024]{1,0:T(8,128)(2,1)}, bf16[64,1024]{1,0:T(8,128)(2,1)S(1)}, u32[]{:S(2)}, u32[]{:S(2)}) collective-permute-start(bf16[64,1024]{1,0:T(8,128)(2,1)} %get-tuple-element.68), channel_id=1, source_target_pairs={{0,32},{32,64},{64,96},{96,0},{1,33},{33,65},{65,97},{97,1},{2,34}... | collective-permute-start | bytes 393224 | tf_op jit(solution)/shard_map/ppermute | solution.py:24
  8.6 2.7 %collective-permute-start.3 = (bf16[64,1024]{1,0:T(8,128)(2,1)}, bf16[64,1024]{1,0:T(8,128)(2,1)S(1)}, u32[]{:S(2)}, u32[]{:S(2)}) collective-permute-start(bf16[64,1024]{1,0:T(8,128)(2,1)} %get-tuple-element.69), channel_id=1, source_target_pairs={{0,64},{32,96},{64,0},{96,32},{1,65},{33,97},{65,1},{97,33},{2,66}... | collective-permute-start | bytes 393224 | tf_op jit(solution)/shard_map/ppermute | solution.py:24
  11.3 1.4 %collective-permute-start.4 = (bf16[64,1024]{1,0:T(8,128)(2,1)}, bf16[64,1024]{1,0:T(8,128)(2,1)S(1)}, u32[]{:S(2)}, u32[]{:S(2)}) collective-permute-start(bf16[64,1024]{1,0:T(8,128)(2,1)} %get-tuple-element.70), channel_id=1, source_target_pairs={{0,96},{32,0},{64,32},{96,64},{1,97},{33,1},{65,33},{97,65},{2,98}... | collective-permute-start | bytes 393224 | tf_op jit(solution)/shard_map/ppermute | solution.py:24
  12.7 1.2 %collective-permute-done.2 = bf16[64,1024]{1,0:T(8,128)(2,1)S(1)} collective-permute-done((bf16[64,1024]{1,0:T(8,128)(2,1)}, bf16[64,1024]{1,0:T(8,128)(2,1)S(1)}, u32[]{:S(2)}, u32[]{:S(2)}) %collective-permute-start.2) | collective-permute-done | bytes 131104 | tf_op jit(solution)/shard_map/ppermute | solution.py:24
  14.0 3.3 %collective-permute-done.3 = bf16[64,1024]{1,0:T(8,128)(2,1)S(1)} collective-permute-done((bf16[64,1024]{1,0:T(8,128)(2,1)}, bf16[64,1024]{1,0:T(8,128)(2,1)S(1)}, u32[]{:S(2)}, u32[]{:S(2)}) %collective-permute-start.3) | collective-permute-done | bytes 131104 | tf_op jit(solution)/shard_map/ppermute | solution.py:24
  17.3 0.0 collective-permute-done.4
  17.3 0.0 collective-permute-done.1.above
  17.3 0.0 collective-permute-done.below
  17.3 2.0 %share.1.refs_5_.refs_15_ = bf16[272,1024]{1,0:T(8,128)(2,1)} custom-call(bf16[1,1024,128]{2,1,0:T(8,128)(2,1)} %refs_0_, bf16[1,128]{1,0:T(2,128)(2,1)} %refs_1_, bf16[1,128,1024]{2,1,0:T(8,128)(2,1)} %refs_2_), custom_call_target="tpu_custom_call" | custom-call | tf_op jit(solution)/shard_map/share/pallas_call | solution.py:82
  19.3 0.1 collective-permute-start.6
  19.4 0.1 collective-permute-start.5
  19.5 2.0 %collective-permute-done.6.refs_6_.refs_16_ = bf16[272,1024]{1,0:T(8,128)(2,1)S(1)} collective-permute-done((bf16[272,1024]{1,0:T(8,128)(2,1)}, bf16[272,1024]{1,0:T(8,128)(2,1)S(1)}, u32[]{:S(2)}, u32[]{:S(2)}) %collective-permute-start.6) | collective-permute-done | bytes 557088 | tf_op jit(solution)/shard_map/ppermute | solution.py:24
  21.6 0.1 pad_maximum_fusion
  21.7 0.0 copy-start.2
  21.7 8.4 %collective-permute-done.5.far = bf16[144,1024]{1,0:T(8,128)(2,1)S(1)} collective-permute-done((bf16[144,1024]{1,0:T(8,128)(2,1)S(1)}, bf16[144,1024]{1,0:T(8,128)(2,1)S(1)}, u32[]{:S(2)}, u32[]{:S(2)}) %collective-permute-start.5) | collective-permute-done | bytes 294944 | tf_op jit(solution)/shard_map/ppermute | solution.py:24
  30.1 1.6 %collective-permute-start.9 = (bf16[2,272,1024]{2,1,0:T(8,128)(2,1)S(1)}, bf16[2,272,1024]{2,1,0:T(8,128)(2,1)S(1)}, u32[]{:S(2)}, u32[]{:S(2)}) collective-permute-start(bf16[2,272,1024]{2,1,0:T(8,128)(2,1)S(1)} %pad_maximum_fusion), channel_id=1, source_target_pairs={{0,2},{1,7},{2,4},{3,1},{4,6},{5,3},{6,0},{7,5},{8,10},{9,15},{10,... | collective-permute-start | bytes 3342344 | tf_op jit(solution)/shard_map/ppermute | solution.py:34
  31.6 1.8 %collective-permute-start.8 = (bf16[256,1024]{1,0:T(8,128)(2,1)S(1)}, bf16[256,1024]{1,0:T(8,128)(2,1)S(1)}, u32[]{:S(2)}, u32[]{:S(2)}) collective-permute-start(bf16[256,1024]{1,0:T(8,128)(2,1)S(1)} %pad_maximum_fusion.1.refs_0_), channel_id=1, source_target_pairs={{0,24},{8,0},{16,8},{24,16},{1,25},{9,1},{17,9},{25,17},{2,26},{10... | collective-permute-start | bytes 1572872 | tf_op jit(solution)/shard_map/ppermute | solution.py:24
  33.4 0.3 collective-permute-start.7
  33.7 0.7 douts.1
  34.4 1.4 %collective-permute-start.10 = (bf16[4,64,1024]{2,1,0:T(8,128)(2,1)S(1)}, bf16[4,64,1024]{2,1,0:T(8,128)(2,1)S(1)}, u32[]{:S(2)}, u32[]{:S(2)}) collective-permute-start(bf16[4,64,1024]{2,1,0:T(8,128)(2,1)S(1)} %get-tuple-element.83), channel_id=1, source_target_pairs={{0,32},{32,64},{64,96},{96,0},{1,33},{33,65},{65,97},{97,1},{2,34}... | collective-permute-start | bytes 1572872 | tf_op jit(solution)/shard_map/ppermute | solution.py:24
  35.7 1.9 %collective-permute-start.11 = (bf16[4,64,1024]{2,1,0:T(8,128)(2,1)S(1)}, bf16[4,64,1024]{2,1,0:T(8,128)(2,1)S(1)}, u32[]{:S(2)}, u32[]{:S(2)}) collective-permute-start(bf16[4,64,1024]{2,1,0:T(8,128)(2,1)S(1)} %get-tuple-element.84), channel_id=1, source_target_pairs={{0,96},{32,0},{64,32},{96,64},{1,97},{33,1},{65,33},{97,65},{2,98}... | collective-permute-start | bytes 1572872 | tf_op jit(solution)/shard_map/ppermute | solution.py:24
  37.7 8.7 %collective-permute-done.8.refs_2_ = bf16[256,1024]{1,0:T(8,128)(2,1)S(1)} collective-permute-done((bf16[256,1024]{1,0:T(8,128)(2,1)S(1)}, bf16[256,1024]{1,0:T(8,128)(2,1)S(1)}, u32[]{:S(2)}, u32[]{:S(2)}) %collective-permute-start.8) | collective-permute-done | bytes 524320 | tf_op jit(solution)/shard_map/ppermute | solution.py:24
  46.3 2.6 %collective-permute-done.7.refs_1_ = bf16[256,1024]{1,0:T(8,128)(2,1)S(1)} collective-permute-done((bf16[256,1024]{1,0:T(8,128)(2,1)S(1)}, bf16[256,1024]{1,0:T(8,128)(2,1)S(1)}, u32[]{:S(2)}, u32[]{:S(2)}) %collective-permute-start.7) | collective-permute-done | bytes 524320 | tf_op jit(solution)/shard_map/ppermute | solution.py:24
  49.0 0.8 collective-permute-done.10.refs_2_.refs_4_.refs_8_.refs_12_
  49.8 0.0 collective-permute-done.11.refs_4_.refs_6_.refs_10_.refs_14_
  49.8 0.0 collective-permute-done.9.refs_7_.refs_17_
  49.8 0.0 collective-permute-start.15
  49.8 0.1 collective-permute-start.14
  49.9 2.7 %collective-permute-start.13 = (bf16[4,64,1024]{2,1,0:T(8,128)(2,1)S(1)}, bf16[4,64,1024]{2,1,0:T(8,128)(2,1)S(1)}, u32[]{:S(2)}, u32[]{:S(2)}) collective-permute-start(bf16[4,64,1024]{2,1,0:T(8,128)(2,1)S(1)} %get-tuple-element.89), channel_id=1, source_target_pairs={{0,64},{32,96},{64,0},{96,32},{1,65},{33,97},{65,1},{97,33},{2,66}... | collective-permute-start | bytes 1572872 | tf_op jit(solution)/shard_map/ppermute | solution.py:24
  52.6 0.3 collective-permute-start.12
  52.9 12.8 %collective-permute-done.13.refs_3_.refs_5_.refs_9_.refs_13_ = bf16[4,64,1024]{2,1,0:T(8,128)(2,1)S(1)} collective-permute-done((bf16[4,64,1024]{2,1,0:T(8,128)(2,1)S(1)}, bf16[4,64,1024]{2,1,0:T(8,128)(2,1)S(1)}, u32[]{:S(2)}, u32[]{:S(2)}) %collective-permute-start.13) | collective-permute-done | bytes 524320 | tf_op jit(solution)/shard_map/ppermute | solution.py:24
  65.7 2.1 %collective-permute-done.12.refs_0_ = bf16[256,1024]{1,0:T(8,128)(2,1)S(1)} collective-permute-done((bf16[256,1024]{1,0:T(8,128)(2,1)S(1)}, bf16[256,1024]{1,0:T(8,128)(2,1)S(1)}, u32[]{:S(2)}, u32[]{:S(2)}) %collective-permute-start.12) | collective-permute-done | bytes 524320 | tf_op jit(solution)/shard_map/ppermute | solution.py:24
  67.8 0.0 collective-permute-done.15.refs_9_.refs_19_
  67.8 0.0 collective-permute-done.14.refs_8_.refs_18_
  67.8 2.1 %rows.2 = (bf16[256,1024]{1,0:T(8,128)(2,1)S(1)}, bf16[256,1024]{1,0:T(8,128)(2,1)S(1)}, bf16[2,256,512]{2,1,0:T(8,128)(2,1)S(1)}, bf16[2,256,512]{2,1,0:T(8,128...) custom-call(bf16[256,1024]{1,0:T(8,128)(2,1)S(1)} %collective-permute-done.12.refs_0_, ...), custom_call_target="tpu_custom_call" | custom-call | flops 1610612736 | bytes 9734144 | tf_op jit(solution)/shard_map/rows/pallas_call | solution.py:53
  70.0 0.1 collective-permute-start.16
  70.0 3.2 %collective-permute-start.17 = (bf16[144,1024]{1,0:T(8,128)(2,1)S(1)}, bf16[144,1024]{1,0:T(8,128)(2,1)S(1)}, u32[]{:S(2)}, u32[]{:S(2)}) collective-permute-start(bf16[144,1024]{1,0:T(8,128)(2,1)S(1)} %get-tuple-element.108), channel_id=1, source_target_pairs={{0,24},{8,0},{16,8},{24,16},{1,25},{9,1},{17,9},{25,17},{2,26},{10... | collective-permute-start | bytes 884744 | tf_op jit(solution)/shard_map/ppermute | solution.py:24
  73.3 5.6 %rows.3 = (bf16[768,1024]{1,0:T(8,128)(2,1)S(1)}, bf16[768,1024]{1,0:T(8,128)(2,1)S(1)}, bf16[2,768,512]{2,1,0:T(8,128)(2,1)S(1)}, bf16[2,768,512]{2,1,0:T(8,128...) custom-call(bf16[256,1024]{1,0:T(8,128)(2,1)S(1)} %pad_maximum_fusion.1.refs_0_, ...), custom_call_target="tpu_custom_call" | custom-call | flops 4831838208 | bytes 21956608 | tf_op jit(solution)/shard_map/rows/pallas_call | solution.py:53
  78.8 2.4 %away.1 = bf16[1040,1024]{1,0:T(8,128)(2,1)S(1)} custom-call(bf16[256,1024]{1,0:T(8,128)(2,1)S(1)} %get-tuple-element.99.refs_0_, bf16[768,1024]{1,0:T(8,128)(2,1)S(1)} %get-tuple-element.100.refs_1_, bf16[256,1024]{1,0:T(8,128)(2,1)S(1)} %get-tuple-element.101.refs_2_, bf16[768,1024]{1,0:T(8,128)(2,1)S(1)} %get-tuple-element.102.refs_3_, ...), custom_call_target="tpu_custom_call" | custom-call | flops 2147483648 | bytes 10518528 | tf_op jit(solution)/shard_map/away/pallas_call | solution.py:53
  81.2 0.0 collective-permute-done.16.got_above
  81.2 0.0 collective-permute-done.17.got_below
  81.2 0.1 collective-permute-start.20
  81.3 0.2 join.1
  81.5 0.1 collective-permute-start.18
  81.6 3.2 %collective-permute-start.19 = (bf16[272,1024]{1,0:T(8,128)(2,1)S(1)}, bf16[272,1024]{1,0:T(8,128)(2,1)S(1)}, u32[]{:S(2)}, u32[]{:S(2)}) collective-permute-start(bf16[272,1024]{1,0:T(8,128)(2,1)S(1)} %get-tuple-element.112), channel_id=1, source_target_pairs={{0,24},{8,0},{16,8},{24,16},{1,25},{9,1},{17,9},{25,17},{2,26},{10... | collective-permute-start | bytes 1671176 | tf_op jit(solution)/shard_map/ppermute | solution.py:24
  84.8 0.7 collective-permute-done.20.refs_8_
  85.5 2.4 %home.1 = (f32[272,1024]{1,0:T(8,128)S(1)}, bf16[272,1024]{1,0:T(8,128)(2,1)S(1)}, bf16[272,1024]{1,0:T(8,128)(2,1)S(1)}, bf16[272,1024]{1,0:T(8,128)(2,1)S(1)}) custom-call(bf16[256,1024]{1,0:T(8,128)(2,1)S(1)} %get-tuple-element.99.refs_0_, bf16[768,1024]{1,0:T(8,128)(2,1)S(1)} %get-tuple-element.100.refs_1_, ...), custom_call_target="tpu_custom_call" | custom-call | flops 2147483648 | bytes 13303808 | tf_op jit(solution)/shard_map/home/pallas_call | solution.py:53
  87.9 2.2 %collective-permute-start.21 = (bf16[272,1024]{1,0:T(8,128)(2,1)S(1)}, bf16[272,1024]{1,0:T(8,128)(2,1)S(1)}, u32[]{:S(2)}, u32[]{:S(2)}) collective-permute-start(bf16[272,1024]{1,0:T(8,128)(2,1)S(1)} %get-tuple-element.117), channel_id=1, source_target_pairs={{0,4},{1,5},{2,6},{3,7},{4,0},{5,1},{6,2},{7,3},{8,12},{9,13},{10,... | collective-permute-start | bytes 1671176 | tf_op jit(solution)/shard_map/ppermute | solution.py:34
  90.1 1.1 collective-permute-start.22
  91.3 0.9 collective-permute-start.23
  92.2 5.6 %collective-permute-done.18.a = bf16[272,1024]{1,0:T(8,128)(2,1)S(1)} collective-permute-done((bf16[272,1024]{1,0:T(8,128)(2,1)S(1)}, bf16[272,1024]{1,0:T(8,128)(2,1)S(1)}, u32[]{:S(2)}, u32[]{:S(2)}) %collective-permute-start.18) | collective-permute-done | bytes 557088 | tf_op jit(solution)/shard_map/ppermute | solution.py:24
  97.8 0.0 collective-permute-done.19.b
  97.8 0.2 sum_z.1
  98.0 0.0 copy-start.3
  98.0 0.0 copy-start.4
  98.0 13.4 %all_to_all.5.pieces = bf16[4,80,1024]{2,1,0:T(8,128)(2,1)S(1)} all-to-all(bf16[4,80,1024]{2,1,0:T(8,128)(2,1)S(1)} %sum_z.1), channel_id=1, replica_groups=mesh['x'=4,'z'=4,'y'=4,'c'=2] {'x'}, dimensions={0} | all-to-all | bytes 1310720 | tf_op jit(solution)/shard_map/all_to_all | solution.py:435
  111.5 1.2 %finish.1 = (bf16[128,1024]{1,0:T(8,128)(2,1)}, f32[2,128]{1,0:T(2,128)}) custom-call(s32[2,128]{1,0:T(2,128)S(1)} %copy-done.4, bf16[2,128]{1,0:T(2,128)(2,1)S(1)} %bitcast.9, bf16[4,80,1024]{2,1,0:T(8,128)(2,1)S(1)} %all_to_all.5.pieces), custom_call_target="tpu_custom_call" | custom-call | bytes 920064 | tf_op jit(solution)/shard_map/finish/pallas_call | solution.py:53
  112.7 4.0 %collective-permute-done.22.b = bf16[272,1024]{1,0:T(8,128)(2,1)S(1)} collective-permute-done((bf16[272,1024]{1,0:T(8,128)(2,1)S(1)}, bf16[272,1024]{1,0:T(8,128)(2,1)S(1)}, u32[]{:S(2)}, u32[]{:S(2)}) %collective-permute-start.22) | collective-permute-done | bytes 557088 | tf_op jit(solution)/shard_map/ppermute | solution.py:34
  116.7 0.0 collective-permute-done.23.c
  116.7 1.1 last.1
  (10 shorter events, 0.1 us)
Async XLA Ops:
  2.9 16.6 %copy-start.5 = (bf16[64,1024]{1,0:T(8,128)(2,1)S(1)}, bf16[64,1024]{1,0:T(8,128)(2,1)}, u32[]{:S(2)}) copy-start(bf16[64,1024]{1,0:T(8,128)(2,1)} %get-tuple-element.71) | copy-start | bytes 393220
  2.9 14.4 %collective-permute-start.1 = (bf16[144,1024]{1,0:T(8,128)(2,1)}, bf16[144,1024]{1,0:T(8,128)(2,1)S(1)}, u32[]{:S(2)}, u32[]{:S(2)}) collective-permute-start(bf16[144,1024]{1,0:T(8,128)(2,1)} %get-tuple-element.66.own), channel_id=1, source_target_pairs={{0,24},{8,0},{16,8},{24,16},{1,25},{9,1},{17,9},{25,17},{2,26},{10... | collective-permute-start | bytes 884744 | tf_op jit(solution)/shard_map/ppermute | solution.py:24
  7.1 10.2 %collective-permute-start = (bf16[144,1024]{1,0:T(8,128)(2,1)}, bf16[144,1024]{1,0:T(8,128)(2,1)S(1)}, u32[]{:S(2)}, u32[]{:S(2)}) collective-permute-start(bf16[144,1024]{1,0:T(8,128)(2,1)} %get-tuple-element.66.own), channel_id=1, source_target_pairs={{0,8},{8,16},{16,24},{24,0},{1,9},{9,17},{17,25},{25,1},{2,10},{10... | collective-permute-start | bytes 884744 | tf_op jit(solution)/shard_map/ppermute | solution.py:24
  7.1 6.9 %collective-permute-start.2 = (bf16[64,1024]{1,0:T(8,128)(2,1)}, bf16[64,1024]{1,0:T(8,128)(2,1)S(1)}, u32[]{:S(2)}, u32[]{:S(2)}) collective-permute-start(bf16[64,1024]{1,0:T(8,128)(2,1)} %get-tuple-element.68), channel_id=1, source_target_pairs={{0,32},{32,64},{64,96},{96,0},{1,33},{33,65},{65,97},{97,1},{2,34}... | collective-permute-start | bytes 393224 | tf_op jit(solution)/shard_map/ppermute | solution.py:24
  8.6 8.7 %collective-permute-start.3 = (bf16[64,1024]{1,0:T(8,128)(2,1)}, bf16[64,1024]{1,0:T(8,128)(2,1)S(1)}, u32[]{:S(2)}, u32[]{:S(2)}) collective-permute-start(bf16[64,1024]{1,0:T(8,128)(2,1)} %get-tuple-element.69), channel_id=1, source_target_pairs={{0,64},{32,96},{64,0},{96,32},{1,65},{33,97},{65,1},{97,33},{2,66}... | collective-permute-start | bytes 393224 | tf_op jit(solution)/shard_map/ppermute | solution.py:24
  11.3 6.0 %collective-permute-start.4 = (bf16[64,1024]{1,0:T(8,128)(2,1)}, bf16[64,1024]{1,0:T(8,128)(2,1)S(1)}, u32[]{:S(2)}, u32[]{:S(2)}) collective-permute-start(bf16[64,1024]{1,0:T(8,128)(2,1)} %get-tuple-element.70), channel_id=1, source_target_pairs={{0,96},{32,0},{64,32},{96,64},{1,97},{33,1},{65,33},{97,65},{2,98}... | collective-permute-start | bytes 393224 | tf_op jit(solution)/shard_map/ppermute | solution.py:24
  19.3 2.3 %copy-start = (bf16[272,1024]{1,0:T(8,128)(2,1)S(1)}, bf16[272,1024]{1,0:T(8,128)(2,1)}, u32[]{:S(2)}) copy-start(bf16[272,1024]{1,0:T(8,128)(2,1)} %share.1.refs_5_.refs_15_) | copy-start | bytes 1671172
  19.3 2.2 %collective-permute-start.6 = (bf16[272,1024]{1,0:T(8,128)(2,1)}, bf16[272,1024]{1,0:T(8,128)(2,1)S(1)}, u32[]{:S(2)}, u32[]{:S(2)}) collective-permute-start(bf16[272,1024]{1,0:T(8,128)(2,1)} %share.1.refs_5_.refs_15_), channel_id=1, source_target_pairs={{0,1},{1,0},{2,3},{3,2},{4,5},{5,4},{6,7},{7,6},{8,9},{9,8},{10,11... | collective-permute-start | bytes 1671176 | tf_op jit(solution)/shard_map/ppermute | solution.py:24
  19.4 10.7 %collective-permute-start.5 = (bf16[144,1024]{1,0:T(8,128)(2,1)S(1)}, bf16[144,1024]{1,0:T(8,128)(2,1)S(1)}, u32[]{:S(2)}, u32[]{:S(2)}) collective-permute-start(bf16[144,1024]{1,0:T(8,128)(2,1)S(1)} %collective-permute-done.below), channel_id=1, source_target_pairs={{0,8},{8,16},{16,24},{24,0},{1,9},{9,17},{17,25},{25,1},{2,10},{10... | collective-permute-start | bytes 884744 | tf_op jit(solution)/shard_map/ppermute | solution.py:24
  21.5 12.1 %copy-start.1 = (bf16[144,1024]{1,0:T(8,128)(2,1)S(1)}, bf16[144,1024]{1,0:T(8,128)(2,1)}, u32[]{:S(2)}) copy-start(bf16[144,1024]{1,0:T(8,128)(2,1)} %get-tuple-element.66.own) | copy-start | bytes 884740
  21.7 46.2 %copy-start.2 = (bf16[1,1024]{1,0:T(2,128)(2,1)S(1)}, bf16[1,1024]{1,0:T(2,128)(2,1)}, u32[]{:S(2)}) copy-start(bf16[1,1024]{1,0:T(2,128)(2,1)} %refs_20_.1) | copy-start | bytes 6148
  30.1 19.7 %collective-permute-start.9 = (bf16[2,272,1024]{2,1,0:T(8,128)(2,1)S(1)}, bf16[2,272,1024]{2,1,0:T(8,128)(2,1)S(1)}, u32[]{:S(2)}, u32[]{:S(2)}) collective-permute-start(bf16[2,272,1024]{2,1,0:T(8,128)(2,1)S(1)} %pad_maximum_fusion), channel_id=1, source_target_pairs={{0,2},{1,7},{2,4},{3,1},{4,6},{5,3},{6,0},{7,5},{8,10},{9,15},{10,... | collective-permute-start | bytes 3342344 | tf_op jit(solution)/shard_map/ppermute | solution.py:34
  31.6 14.7 %collective-permute-start.8 = (bf16[256,1024]{1,0:T(8,128)(2,1)S(1)}, bf16[256,1024]{1,0:T(8,128)(2,1)S(1)}, u32[]{:S(2)}, u32[]{:S(2)}) collective-permute-start(bf16[256,1024]{1,0:T(8,128)(2,1)S(1)} %pad_maximum_fusion.1.refs_0_), channel_id=1, source_target_pairs={{0,24},{8,0},{16,8},{24,16},{1,25},{9,1},{17,9},{25,17},{2,26},{10... | collective-permute-start | bytes 1572872 | tf_op jit(solution)/shard_map/ppermute | solution.py:24
  33.4 15.6 %collective-permute-start.7 = (bf16[256,1024]{1,0:T(8,128)(2,1)S(1)}, bf16[256,1024]{1,0:T(8,128)(2,1)S(1)}, u32[]{:S(2)}, u32[]{:S(2)}) collective-permute-start(bf16[256,1024]{1,0:T(8,128)(2,1)S(1)} %pad_maximum_fusion.1.refs_0_), channel_id=1, source_target_pairs={{0,8},{8,16},{16,24},{24,0},{1,9},{9,17},{17,25},{25,1},{2,10},{10... | collective-permute-start | bytes 1572872 | tf_op jit(solution)/shard_map/ppermute | solution.py:24
  34.4 15.4 %collective-permute-start.10 = (bf16[4,64,1024]{2,1,0:T(8,128)(2,1)S(1)}, bf16[4,64,1024]{2,1,0:T(8,128)(2,1)S(1)}, u32[]{:S(2)}, u32[]{:S(2)}) collective-permute-start(bf16[4,64,1024]{2,1,0:T(8,128)(2,1)S(1)} %get-tuple-element.83), channel_id=1, source_target_pairs={{0,32},{32,64},{64,96},{96,0},{1,33},{33,65},{65,97},{97,1},{2,34}... | collective-permute-start | bytes 1572872 | tf_op jit(solution)/shard_map/ppermute | solution.py:24
  35.7 14.1 %collective-permute-start.11 = (bf16[4,64,1024]{2,1,0:T(8,128)(2,1)S(1)}, bf16[4,64,1024]{2,1,0:T(8,128)(2,1)S(1)}, u32[]{:S(2)}, u32[]{:S(2)}) collective-permute-start(bf16[4,64,1024]{2,1,0:T(8,128)(2,1)S(1)} %get-tuple-element.84), channel_id=1, source_target_pairs={{0,96},{32,0},{64,32},{96,64},{1,97},{33,1},{65,33},{97,65},{2,98}... | collective-permute-start | bytes 1572872 | tf_op jit(solution)/shard_map/ppermute | solution.py:24
  49.8 18.0 %collective-permute-start.15 = (bf16[2,272,1024]{2,1,0:T(8,128)(2,1)S(1)}, bf16[2,272,1024]{2,1,0:T(8,128)(2,1)S(1)}, u32[]{:S(2)}, u32[]{:S(2)}) collective-permute-start(bf16[2,272,1024]{2,1,0:T(8,128)(2,1)S(1)} %collective-permute-done.9.refs_7_.refs_17_), channel_id=1, source_target_pairs={{0,2},{1,7},{2,4},{3,1},{4,6},{5,3},{6,0},{7,5},{8,10},{9,15},{10,... | collective-permute-start | bytes 3342344 | tf_op jit(solution)/shard_map/ppermute | solution.py:34
  49.8 18.0 %collective-permute-start.14 = (bf16[2,272,1024]{2,1,0:T(8,128)(2,1)S(1)}, bf16[2,272,1024]{2,1,0:T(8,128)(2,1)S(1)}, u32[]{:S(2)}, u32[]{:S(2)}) collective-permute-start(bf16[2,272,1024]{2,1,0:T(8,128)(2,1)S(1)} %collective-permute-done.9.refs_7_.refs_17_), channel_id=1, source_target_pairs={{0,1},{1,0},{2,3},{3,2},{4,5},{5,4},{6,7},{7,6},{8,9},{9,8},{10,11... | collective-permute-start | bytes 3342344 | tf_op jit(solution)/shard_map/ppermute | solution.py:24
  49.9 15.8 %collective-permute-start.13 = (bf16[4,64,1024]{2,1,0:T(8,128)(2,1)S(1)}, bf16[4,64,1024]{2,1,0:T(8,128)(2,1)S(1)}, u32[]{:S(2)}, u32[]{:S(2)}) collective-permute-start(bf16[4,64,1024]{2,1,0:T(8,128)(2,1)S(1)} %get-tuple-element.89), channel_id=1, source_target_pairs={{0,64},{32,96},{64,0},{96,32},{1,65},{33,97},{65,1},{97,33},{2,66}... | collective-permute-start | bytes 1572872 | tf_op jit(solution)/shard_map/ppermute | solution.py:24
  52.6 15.2 %collective-permute-start.12 = (bf16[256,1024]{1,0:T(8,128)(2,1)S(1)}, bf16[256,1024]{1,0:T(8,128)(2,1)S(1)}, u32[]{:S(2)}, u32[]{:S(2)}) collective-permute-start(bf16[256,1024]{1,0:T(8,128)(2,1)S(1)} %collective-permute-done.7.refs_1_), channel_id=1, source_target_pairs={{0,8},{8,16},{16,24},{24,0},{1,9},{9,17},{17,25},{25,1},{2,10},{10... | collective-permute-start | bytes 1572872 | tf_op jit(solution)/shard_map/ppermute | solution.py:24
  70.0 11.2 %collective-permute-start.16 = (bf16[128,1024]{1,0:T(8,128)(2,1)S(1)}, bf16[128,1024]{1,0:T(8,128)(2,1)S(1)}, u32[]{:S(2)}, u32[]{:S(2)}) collective-permute-start(bf16[128,1024]{1,0:T(8,128)(2,1)S(1)} %get-tuple-element.107), channel_id=1, source_target_pairs={{0,8},{8,16},{16,24},{24,0},{1,9},{9,17},{17,25},{25,1},{2,10},{10... | collective-permute-start | bytes 786440 | tf_op jit(solution)/shard_map/ppermute | solution.py:24
  70.0 11.2 %collective-permute-start.17 = (bf16[144,1024]{1,0:T(8,128)(2,1)S(1)}, bf16[144,1024]{1,0:T(8,128)(2,1)S(1)}, u32[]{:S(2)}, u32[]{:S(2)}) collective-permute-start(bf16[144,1024]{1,0:T(8,128)(2,1)S(1)} %get-tuple-element.108), channel_id=1, source_target_pairs={{0,24},{8,0},{16,8},{24,16},{1,25},{9,1},{17,9},{25,17},{2,26},{10... | collective-permute-start | bytes 884744 | tf_op jit(solution)/shard_map/ppermute | solution.py:24
  81.2 4.3 %collective-permute-start.20 = (bf16[1040,1024]{1,0:T(8,128)(2,1)S(1)}, bf16[1040,1024]{1,0:T(8,128)(2,1)S(1)}, u32[]{:S(2)}, u32[]{:S(2)}) collective-permute-start(bf16[1040,1024]{1,0:T(8,128)(2,1)S(1)} %away.1), channel_id=1, source_target_pairs={{0,1},{1,0},{2,3},{3,2},{4,5},{5,4},{6,7},{7,6},{8,9},{9,8},{10,11... | collective-permute-start | bytes 6389768 | tf_op jit(solution)/shard_map/ppermute | solution.py:24
  81.5 16.3 %collective-permute-start.18 = (bf16[272,1024]{1,0:T(8,128)(2,1)S(1)}, bf16[272,1024]{1,0:T(8,128)(2,1)S(1)}, u32[]{:S(2)}, u32[]{:S(2)}) collective-permute-start(bf16[272,1024]{1,0:T(8,128)(2,1)S(1)} %get-tuple-element.111), channel_id=1, source_target_pairs={{0,8},{8,16},{16,24},{24,0},{1,9},{9,17},{17,25},{25,1},{2,10},{10... | collective-permute-start | bytes 1671176 | tf_op jit(solution)/shard_map/ppermute | solution.py:24
  81.6 16.2 %collective-permute-start.19 = (bf16[272,1024]{1,0:T(8,128)(2,1)S(1)}, bf16[272,1024]{1,0:T(8,128)(2,1)S(1)}, u32[]{:S(2)}, u32[]{:S(2)}) collective-permute-start(bf16[272,1024]{1,0:T(8,128)(2,1)S(1)} %get-tuple-element.112), channel_id=1, source_target_pairs={{0,24},{8,0},{16,8},{24,16},{1,25},{9,1},{17,9},{25,17},{2,26},{10... | collective-permute-start | bytes 1671176 | tf_op jit(solution)/shard_map/ppermute | solution.py:24
  87.9 24.8 %collective-permute-start.21 = (bf16[272,1024]{1,0:T(8,128)(2,1)S(1)}, bf16[272,1024]{1,0:T(8,128)(2,1)S(1)}, u32[]{:S(2)}, u32[]{:S(2)}) collective-permute-start(bf16[272,1024]{1,0:T(8,128)(2,1)S(1)} %get-tuple-element.117), channel_id=1, source_target_pairs={{0,4},{1,5},{2,6},{3,7},{4,0},{5,1},{6,2},{7,3},{8,12},{9,13},{10,... | collective-permute-start | bytes 1671176 | tf_op jit(solution)/shard_map/ppermute | solution.py:34
  90.1 26.5 %collective-permute-start.22 = (bf16[272,1024]{1,0:T(8,128)(2,1)S(1)}, bf16[272,1024]{1,0:T(8,128)(2,1)S(1)}, u32[]{:S(2)}, u32[]{:S(2)}) collective-permute-start(bf16[272,1024]{1,0:T(8,128)(2,1)S(1)} %get-tuple-element.118), channel_id=1, source_target_pairs={{0,6},{1,3},{2,0},{3,5},{4,2},{5,7},{6,4},{7,1},{8,14},{9,11},{10,... | collective-permute-start | bytes 1671176 | tf_op jit(solution)/shard_map/ppermute | solution.py:34
  91.3 25.4 %collective-permute-start.23 = (bf16[272,1024]{1,0:T(8,128)(2,1)S(1)}, bf16[272,1024]{1,0:T(8,128)(2,1)S(1)}, u32[]{:S(2)}, u32[]{:S(2)}) collective-permute-start(bf16[272,1024]{1,0:T(8,128)(2,1)S(1)} %get-tuple-element.119), channel_id=1, source_target_pairs={{0,2},{1,7},{2,4},{3,1},{4,6},{5,3},{6,0},{7,5},{8,10},{9,15},{10,... | collective-permute-start | bytes 1671176 | tf_op jit(solution)/shard_map/ppermute | solution.py:34
  98.0 13.5 %copy-start.3 = (bf16[128,2]{0,1:T(2,128)(2,1)S(1)}, bf16[128,2]{0,1:T(2,128)(2,1)}, u32[]{:S(2)}) copy-start(bf16[128,2]{0,1:T(2,128)(2,1)} %param.13) | copy-start | bytes 1540
  98.0 13.5 %copy-start.4 = (s32[2,128]{1,0:T(2,128)S(1)}, s32[2,128]{1,0:T(2,128)}, u32[]{:S(2)}) copy-start(s32[2,128]{1,0:T(2,128)} %get-tuple-element.65.places) | copy-start | bytes 3076

commit v3 on v2

v3 whole, which is shorter than its diff:
```python
import functools

import jax
import jax.numpy as jnp
from jax import lax
from jax.experimental import pallas as pl
from jax.experimental.pallas import tpu as pltpu
from jax.sharding import Mesh, PartitionSpec as P

BF = jnp.bfloat16
F32 = jnp.float32
EXTRA = 16
NT = (((1,), (1,)), ((), ()))
NN = (((1,), (0,)), ((), ()))
TN = (((0,), (0,)), ((), ()))


def dot(a, b, dims):
    return lax.dot_general(a, b, dims, preferred_element_type=F32)


def shift(value, axis, step):
    n = lax.axis_size(axis)
    return lax.ppermute(value, axis, [(i, (i + step) % n) for i in range(n)])


def shift_y(value, step, mirrored):
    n = lax.axis_size("y")
    moves = []
    for y in range(n):
        for c in range(2):
            to = (y + (-step if mirrored and c else step)) % n
            moves.append((2 * y + c, 2 * to + c))
    return lax.ppermute(value, ("y", "c"), moves)


def shape(rows, columns, dtype=BF):
    return jax.ShapeDtypeStruct((rows, columns), dtype)


def full(a):
    return pl.BlockSpec(a.shape, lambda i: (0,) * len(a.shape))


def span(a, first, rows):
    return pl.BlockSpec((rows, a.shape[1]), lambda i: (first // rows, 0))


def lead(a, index):
    return pl.BlockSpec((1, *a.shape[1:]), lambda i: (index,) + (0,) * (len(a.shape) - 1))


def call(kernel, name, out_shape, operands, flops=0, scratch=(), vmem=8):
    parts = [o if isinstance(o, tuple) else (o,) for o in operands]
    size = sum(p[0].size * p[0].dtype.itemsize for p in parts)
    size += sum(s.size * s.dtype.itemsize for s in out_shape)
    return pl.pallas_call(
        kernel,
        out_shape=out_shape,
        grid=(1,),
        in_specs=[(full, lead, span)[len(p) - 1](*p) for p in parts],
        out_specs=[full(s) for s in out_shape],
        scratch_shapes=scratch,
        compiler_params=pltpu.CompilerParams(vmem_limit_bytes=vmem * 1024 * 1024),
        cost_estimate=pl.CostEstimate(flops=flops, bytes_accessed=size, transcendentals=0),
        name=name,
    )(*[p[0] for p in parts])


def call_loading(kernel, name, out_shape, arrays):
    n = len(arrays)

    def body(*refs):
        sources, outs = refs[:n], refs[n : n + len(out_shape)]
        copies, sems = refs[n + len(out_shape) : -1], refs[-1]
        moves = [
            pltpu.make_async_copy(a, b, sems.at[k])
            for k, (a, b) in enumerate(zip(sources, copies))
        ]
        for m in moves:
            m.start()
        for m in moves:
            m.wait()
        kernel(*copies, *outs)

    return pl.pallas_call(
        body,
        out_shape=out_shape,
        in_specs=[pl.BlockSpec(memory_space=pl.ANY)] * n,
        out_specs=[pl.BlockSpec(memory_space=pltpu.VMEM)] * len(out_shape),
        scratch_shapes=[pltpu.VMEM(a.shape, a.dtype) for a in arrays]
        + [pltpu.SemaphoreType.DMA((n,))],
        compiler_params=pltpu.CompilerParams(vmem_limit_bytes=56 * 1024 * 1024),
        name=name,
    )(*arrays)


def high_low(value):
    high = value.astype(BF).astype(F32)
    return [high, value - high]


def lines_of(lines, width, dtype):
    m = lines[0].shape[1]
    rest = EXTRA - sum(line.shape[0] for line in lines)
    block = jnp.concatenate(lines + [jnp.zeros((rest, m), F32)], axis=0)
    if m < width:
        block = jnp.concatenate([block, jnp.zeros((EXTRA, width - m), F32)], axis=1)
    return block.astype(dtype)


def prepare_kernel(
    routes, slots, combine, tokens, grads, w_in, b_in, w_out, share, raw, places, *outs
):
    units = w_out.shape[1]
    share[0:units] = w_in[0].astype(F32).T.astype(BF)
    share[units : units + EXTRA] = lines_of([b_in[...].astype(F32)], share.shape[1], BF)
    share[units + EXTRA :] = w_out[0]
    n_expert = len(outs)
    cap = outs[0].shape[0]
    n_tok = tokens.shape[0]
    turned = routes[...] - lax.axis_index("x")
    turned = jnp.where(turned < 0, turned + n_expert, turned)
    place = jnp.where(slots[...] < cap, turned * cap + slots[...], -1)
    places[...] = place
    raw[0:n_tok] = grads[...]
    side = [place.astype(F32), combine[...].astype(F32)]
    raw[n_tok:] = lines_of(side, grads.shape[1], BF)
    spots = lax.broadcasted_iota(jnp.int32, (n_expert * cap, n_tok), 0)
    picks = jnp.where((place[0:1, :] == spots) | (place[1:2, :] == spots), 1.0, 0.0)
    rows = dot(picks.astype(BF), tokens[...], NN).astype(BF)
    for s, out in enumerate(outs):
        out[...] = rows[s * cap : (s + 1) * cap]


def douts_kernel(own, below, above, far, *outs):
    cap = outs[0].shape[1]
    n_tok = own.shape[0] - EXTRA
    for z, raw in enumerate((own[...], below[...], above[...], far[...])):
        side = raw[n_tok : n_tok + 4, 0:n_tok].astype(F32)
        spots = lax.broadcasted_iota(jnp.int32, (len(outs) * cap, n_tok), 0)
        place = side[0:2].astype(jnp.int32)
        picks = jnp.where(place[0:1] == spots, side[2:3], 0.0)
        picks = picks + jnp.where(place[1:2] == spots, side[3:4], 0.0)
        rows = dot(picks.astype(BF), raw[0:n_tok], NN).astype(BF)
        for s, out in enumerate(outs):
            out[z] = rows[s * cap : (s + 1) * cap]


def rows_kernel(n_x, n_d, blocks, *refs):
    xs, ds = refs[:n_x], refs[n_x : n_x + n_d]
    mine, other, direct, mirror, far_w, b_out, *outs = refs[n_x + n_d :]
    x, d, dpre, hidden, *dxs = outs
    shares = [
        (mine, other),
        (direct.at[0], direct.at[1]),
        (mirror.at[1], mirror.at[0]),
        (far_w.at[0], far_w.at[1]),
    ]
    width = x.shape[1]
    for parts, whole in ((xs, x), (ds, d)):
        at = 0
        for p in parts:
            count = p.shape[-2]
            whole[at : at + count] = p[...].reshape(count, width)
            at += count
    n_y = len(shares)
    unit = (mine.shape[0] - EXTRA) // 2
    xb = x[...]
    db = d[...]

    def w_in_of(k):
        return jnp.concatenate([r[0:unit] for r in shares[k]], axis=0)

    def dots(k):
        bias = jnp.concatenate([r[unit : unit + 1, 0:unit] for r in shares[k]], axis=1)
        w_out = jnp.concatenate([r[unit + EXTRA :] for r in shares[k]], axis=0)
        return dot(xb, w_in_of(k), NT) + bias.astype(F32), dot(db, w_out, NT)

    term = total = grad = None
    now = dots(0)
    for k in range(n_y):
        pre, back = now
        if k + 1 < n_y:
            now = dots(k + 1)
        cdf = 0.5 * (1.0 + lax.erf(pre * 0.7071067811865476))
        dens = jnp.exp(-0.5 * pre * pre) * 0.3989422804014327
        hidden32 = pre * cdf
        new = (back * (cdf + pre * dens)).astype(BF)
        hid = hidden32.astype(BF)
        for c in range(2):
            dpre[c, :, k * unit : (k + 1) * unit] = new[:, c * unit : (c + 1) * unit]
            hidden[c, :, k * unit : (k + 1) * unit] = hid[:, c * unit : (c + 1) * unit]
        by_row = hidden32 * back
        term = by_row if k == 0 else term + by_row
        if k > 0:
            part = dot(grad, w_in_of(k - 1), NN)
            total = part if k == 1 else total + part
        grad = new
    total = total + dot(grad, w_in_of(n_y - 1), NN)
    line = jnp.sum(term.T, axis=0, keepdims=True)
    at = 0
    for (count, is_own), out in zip(blocks, dxs):
        out[0:count] = total[at : at + count].astype(out.dtype)
        here = line[:, at : at + count]
        if is_own:
            by_bias = (d[at : at + count].astype(F32) * b_out[...].astype(F32)).T
            here = here + jnp.sum(by_bias, axis=0, keepdims=True)
            out[count:] = lines_of([here], width, F32)
        else:
            out[count:] = lines_of(high_low(here), width, BF)
        at += count


def rows_set(xs, ds, blocks, w, b_out):
    width = b_out.shape[1]
    m = sum(count for count, _ in blocks)
    units = 4 * (w[0].shape[0] - EXTRA)
    part = jax.ShapeDtypeStruct((2, m, units // 2), BF)
    dxs = [shape(count + EXTRA, width, F32 if own else BF) for count, own in blocks]
    return call(
        functools.partial(rows_kernel, len(xs), len(ds), blocks),
        "rows",
        [shape(m, width), shape(m, width), part, part, *dxs],
        [*xs, *ds, *w, b_out],
        flops=6 * m * units * width,
        vmem=26,
    )


def sums_kernel(x, d, dpre, hidden, out):
    for c in range(2):
        grads = weight_sums(x[...], d[...], dpre[c], hidden[c])
        at = 0
        for g in grads:
            out[c, at : at + g.shape[0]] = g
            at += g.shape[0]


def weight_sums(x, d, dpre, hidden):
    grad_in = dot(dpre, x, TN)
    grad_out = dot(hidden, d, TN)
    line_in = jnp.sum(dpre.astype(F32), axis=0, keepdims=True)
    line_out = jnp.sum(d.astype(F32), axis=0, keepdims=True)
    line_in = jnp.concatenate(
        [line_in, jnp.zeros((1, d.shape[1] - dpre.shape[1]), F32)], axis=1
    )
    return grad_in, grad_out, lines_of([line_in, line_out], d.shape[1], F32)


def away_kernel(near, x, d, dpre, hidden, out):
    grad_in, grad_out, lines = weight_sums(x[...], d[...], dpre[0], hidden[0])
    units = grad_in.shape[0]
    out[0:units] = (near[0, 0:units] + grad_in).astype(BF)
    out[units : 2 * units] = (near[0, units : 2 * units] + grad_out).astype(BF)
    lines = near[0, 2 * units :] + lines
    out[2 * units :] = lines_of(high_low(lines[0:1]) + high_low(lines[1:2]), out.shape[1], BF)


def home_kernel(near, x, d, dpre, hidden, out):
    at = 0
    for g in weight_sums(x[...], d[...], dpre[0], hidden[0]):
        rows = slice(at, at + g.shape[0])
        out[rows] = near[0, rows] + g
        at += g.shape[0]


def merge_kernel(own, got, *outs):
    units = (own.shape[0] - EXTRA) // 2
    width = own.shape[1]
    lines = own[2 * units : 2 * units + 2]
    side = got[2 * units : 2 * units + 4].astype(F32)
    sum_out = lines[1:2] + side[2:3] + side[3:4]
    side = side[0:1] + side[1:2]
    n_y = len(outs)
    unit = units // n_y
    for k, out in enumerate(outs):
        here = k * unit
        there = (0, 2, 1, 3)[k] * unit
        line = lines[0:1, here : here + unit] + side[:, there : there + unit]
        line = jnp.concatenate([line, jnp.zeros((1, width - unit), F32)], axis=1)
        for at in (0, unit):
            rows = slice(at, at + unit)
            here_at, there_at = n_y * at + here, n_y * at + there
            total = own[here_at : here_at + unit] + got[there_at : there_at + unit].astype(F32)
            out[rows] = total.astype(out.dtype)
        if k == 0:
            both = [line, jnp.zeros_like(line), sum_out]
        else:
            both = high_low(line) + high_low(sum_out)
        out[2 * unit :] = lines_of(both, width, out.dtype)


def last_kernel(own, a, b, c, grad_in, grad_bias_in, grad_out, grad_bias_out):
    units = grad_out.shape[1]
    total = own[...] + a[...].astype(F32) + b[...].astype(F32) + c[...].astype(F32)
    grad_in[0] = total[0:units].T.astype(BF)
    grad_out[0] = total[units : 2 * units].astype(BF)
    tail = total[2 * units :]
    grad_bias_in[...] = (tail[0:1] + tail[1:2])[:, 0:units]
    grad_bias_out[...] = tail[2:3] + tail[3:4]


ORDER = (0, 1, 3, 2)


def sum_kernel(n_early, *refs):
    early, late, (far, out) = refs[:3], refs[3:6], refs[6:]
    n_expert = out.shape[0]
    here = lax.axis_index("x")
    width = far.shape[1]
    m = far.shape[0] - EXTRA
    cap = m // n_expert
    e = sum(r[...].astype(F32) for r in early)
    t = sum(r[...].astype(F32) for r in late)
    cut = n_early * cap
    line = [v[n : n + 1, 0:n] + v[n + 1 : n + 2, 0:n] for v, n in ((e, cut), (t, m - cut))]
    side = far[m : m + 2].astype(F32)
    line = jnp.concatenate(line, axis=1) + side[0:1, 0:m] + side[1:2, 0:m]
    lines = lines_of(high_low(line), width, BF)
    for k, s in enumerate(ORDER):
        to = lax.rem(here + (n_expert - s), n_expert)
        rows = slice(k * cap, (k + 1) * cap)
        total = e[rows] if k < n_early else t[k * cap - cut : (k + 1) * cap - cut]
        out[to, 0:cap] = (total + far[rows].astype(F32)).astype(BF)
        out[to, cap:] = lines


def finish_kernel(places, weights, pieces, out, by_weight):
    n_expert = pieces.shape[0]
    cap = pieces.shape[1] - EXTRA
    n_tok = places.shape[1]
    here = lax.axis_index("x")
    total = None
    sums = [None, None]
    spots = lax.broadcasted_iota(jnp.int32, (n_expert * cap, n_tok), 0)
    picks = [jnp.where(places[k : k + 1, :] == spots, 1.0, 0.0) for k in range(2)]
    both = (picks[0] + picks[1]).astype(BF)
    for s in range(n_expert):
        piece = pieces.at[lax.rem(here + s, n_expert)]
        part = dot(both[s * cap : (s + 1) * cap], piece[0:cap], TN)
        total = part if total is None else total + part
        lane = spots - ORDER.index(s) * cap
        inside = (lane >= 0) & (lane < cap)
        for k in range(2):
            pick = inside & (places[k : k + 1, :] == lane + s * cap)
            pick = jnp.where(pick, 1.0, 0.0).astype(BF)
            found = dot(piece[cap:, 0 : n_expert * cap], pick, NN)
            line = found[0:1] + found[1:2]
            sums[k] = line if sums[k] is None else sums[k] + line
    out[...] = total.astype(BF)
    by_weight[...] = jnp.concatenate(sums, axis=0) / weights[...].astype(F32)


def on_device(tokens, grads_out, routes, slots, combine, w_in, b_in, w_out, b_out):
    n_expert = lax.axis_size("x")
    tok_rows, width = tokens.shape
    cap = 2 * tok_rows // n_expert
    units = w_in.shape[2]

    barrier = lax.optimization_barrier

    mine, raw, places, *x_sent = call_loading(
        prepare_kernel,
        "prepare",
        [
            shape(2 * units + EXTRA, width),
            shape(tok_rows + EXTRA, width),
            shape(2, tok_rows, jnp.int32),
        ]
        + [shape(cap, width)] * n_expert,
        [routes.T, slots.T, combine.T, tokens, grads_out, w_in, b_in, w_out],
    )
    raw_below = shift(raw, "z", 1)
    raw_above = shift(raw, "z", -1)
    x_1 = shift(x_sent[1], "x", 1)
    x_3 = shift(x_sent[3], "x", -1)
    other = shift(mine, "c", 1)
    raw_below, raw_above, x_1, x_2, x_3 = barrier((raw_below, raw_above, x_1, x_sent[2], x_3))
    direct = shift_y(jnp.stack([mine, other]), 1, True)

    raw_far = shift(raw_below, "z", 1)
    x_own = jnp.concatenate([x_sent[0], x_1, x_3, shift(x_2, "x", 2)], axis=0)
    x_own, raw_far, direct = barrier((x_own, raw_far, direct))

    d_sent = call(
        douts_kernel,
        "douts",
        [jax.ShapeDtypeStruct((4, cap, width), BF)] * n_expert,
        [raw, raw_below, raw_above, raw_far],
    )
    x_below = shift(x_own, "z", 1)
    x_above = shift(x_own, "z", -1)
    far_w = shift_y(direct, 1, True)
    d_1 = shift(d_sent[1], "x", 1)
    d_3 = shift(d_sent[3], "x", -1)
    x_below, x_above, direct, far_w, d_1, d_3, d_2 = barrier(
        (x_below, x_above, direct, far_w, d_1, d_3, d_sent[2])
    )
    mirror = shift(direct, "c", 1)
    w = [mine, other, direct, mirror, far_w]

    d_2 = shift(d_2, "x", 2)
    half = x_own.shape[0] // 2
    x_far_a = shift(x_below[:half], "z", 1)
    x_far_b = shift(x_above[half:], "z", -1)
    n_early = 3
    cut = n_early * cap
    sides = (x_own, x_below, x_above)
    early = rows_set(
        [(a, 0, cut) for a in sides],
        [(a, z) for z in range(3) for a in (d_sent[0], d_1, d_3)],
        [(cut, True), (cut, False), (cut, False)],
        w,
        b_out,
    )
    acc = call(
        sums_kernel,
        "sums",
        [jax.ShapeDtypeStruct((2, 8 * units + EXTRA, width), F32)],
        early[:4],
        flops=8 * 3 * cut * 4 * units * width,
        vmem=28,
    )[0]
    early_above = shift(early[6], "z", 1)
    early_below = shift(early[5], "z", -1)
    d_2, x_far_a, x_far_b, acc = barrier((d_2, x_far_a, x_far_b, acc))
    late = rows_set(
        [(a, cut, cap) for a in sides] + [x_far_a, x_far_b],
        [(d_2, z) for z in range(3)] + [(a, 3) for a in (d_sent[0], d_1, d_3, d_2)],
        [(cap, True), (cap, False), (cap, False), (n_expert * cap, False)],
        w,
        b_out,
    )

    ends = [late[0], late[1], late[2], late[3]]
    flops = 4 * 7 * cap * 4 * units * width
    out = shape(8 * units + EXTRA, width)
    operands = [(acc, 1), *ends[:2], (late[2], 1), (late[3], 1)]
    away = call(away_kernel, "away", [out], operands, flops, vmem=20)[0]
    away, early_above, early_below = barrier((away, early_above, early_below))
    got = shift(away, "c", 1)
    out = shape(8 * units + EXTRA, width, F32)
    operands = [(acc, 0), *ends[:2], (late[2], 0), (late[3], 0)]
    home = call(home_kernel, "home", [out], operands, flops, vmem=24)[0]
    home = call(
        merge_kernel,
        "merge",
        [shape(2 * units + EXTRA, width, BF if k else F32) for k in range(4)],
        [home, got],
        vmem=16,
    )

    far = shift(late[7], "z", 2)
    late_above = shift(late[6], "z", 1)
    late_below = shift(late[5], "z", -1)
    pieces = call(
        functools.partial(sum_kernel, n_early),
        "sum_z",
        [jax.ShapeDtypeStruct((n_expert, cap + EXTRA, width), BF)],
        [early[4], early_above, early_below, late[4], late_above, late_below, far],
    )[0]
    final = lax.all_to_all(pieces, "x", 0, 0, tiled=True)
    moved = [
        shift_y(home[3], 2, False),
        shift_y(home[1], -1, True),
        shift_y(home[2], 1, True),
    ]
    grad_tokens, by_weight = call(
        finish_kernel,
        "finish",
        [shape(tok_rows, width), shape(2, tok_rows, F32)],
        [places, combine.T, final],
    )
    grad_w_in, grad_b_in, grad_w_out, grad_b_out = call(
        last_kernel,
        "last",
        [
            jax.ShapeDtypeStruct(w_in.shape, BF),
            shape(1, units, F32),
            jax.ShapeDtypeStruct(w_out.shape, BF),
            shape(1, width, F32),
        ],
        [home[0], *moved],
    )
    return (grad_tokens, by_weight.T, grad_w_in, grad_b_in, grad_w_out, grad_b_out)


def solution(mesh):
    fine = Mesh(mesh.devices.reshape(4, 4, 4, 2), ("x", "z", "y", "c"))
    zero = ("z", "y", "c")
    rows = P(("x", "z", "y", "c"), None)
    in_specs = (rows,) * 5 + (
        P("x", None, zero),
        P("x", zero),
        P("x", zero, None),
        P("x", None),
    )
    out_specs = (rows, rows) + in_specs[5:]
    return jax.shard_map(
        on_device, mesh=fine, in_specs=in_specs, out_specs=out_specs, check_vma=False
    )
```

time: 118 us -> 111 us (0.941)
  waiting for transfers between devices: 52.3 us -> 37.4 us
  starting transfers between devices: 31 us -> 37.4 us
    ppermute x19 -> x21, waiting for transfers between devices: 48.3 us -> 37.4 us  [shift(): return lax.ppermute(value, axis, [(i, (i + step) % n) for i in range(n)])]
    ppermute x19 -> x21, starting transfers between devices: 25.1 us -> 29.8 us  [shift(): return lax.ppermute(value, axis, [(i, (i + step) % n) for i in range(n)])]
    ppermute x5, waiting for transfers between devices: 4.02 us -> 0.06 us  [shift_y(): return lax.ppermute(value, ('y', 'c'), moves)]
    ppermute x5, starting transfers between devices: 5.84 us -> 7.6 us  [shift_y(): return lax.ppermute(value, ('y', 'c'), moves)]
    pallas_call x2 -> x1, Pallas kernels: 4.25 us -> 2.63 us  [call_loading(): pl.pallas_call(body, out_shape=out_shape, in_specs=[pl.BlockSpec(memory_s...]
    pallas_call x9 -> x10, Pallas kernels: 15.7 us -> 17.3 us  [call(): pl.pallas_call(kernel, out_shape=out_shape, grid=(1,), in_specs=[(full, l...]
  transfers between devices with their start and end apart: 24 -> 26, of which waited for: 12 -> 13; matrix products, arithmetic and copies ran while one was open for 0% -> 0% of each run, Pallas kernels for 11% -> 15%
where the time goes in v3:
time: 111 us
  starting transfers between devices  37.4 us (34%)
  waiting for transfers between devices  37.4 us (34%)
  Pallas kernels  19.9 us (18%)
  blocking collectives  13.8 us (12%)
  other arithmetic  1.19 us (1%)
    ppermute x21, waiting for transfers between devices, shift(): return lax.ppermute(value, axis, [(i, (i + step) % n) for i in range(n)])  37.4 us
    ppermute x21, starting transfers between devices, shift(): return lax.ppermute(value, axis, [(i, (i + step) % n) for i in range(n)])  29.8 us
    pallas_call x10, Pallas kernels, call(): pl.pallas_call(kernel, out_shape=out_shape, grid=(1,), in_specs=[(full, l...  17.3 us
    all_to_all x1, blocking collectives, on_device(): final = lax.all_to_all(pieces, 'x', 0, 0, tiled=True)  13.8 us
    ppermute x5, starting transfers between devices, shift_y(): return lax.ppermute(value, ('y', 'c'), moves)  7.6 us
    pallas_call x1, Pallas kernels, call_loading(): pl.pallas_call(body, out_shape=out_shape, in_specs=[pl.BlockSpec(memory_s...  2.63 us
  transfers between devices with their start and end apart: 26, of which 13 were waited for; matrix products, arithmetic and copies ran while one was open for 0% of the time, Pallas kernels for 15%

profile of v3, /device:TPU:0, one launch (start us, length us, event | category | flops | bytes accessed | tf_op | source)
XLA Modules:
  0.0 110.6 jit_solution(13237996899464647224)
XLA Ops:
  0.6 2.6 %prepare.1 = (bf16[272,1024]{1,0:T(8,128)(2,1)}, bf16[144,1024]{1,0:T(8,128)(2,1)}, s32[2,128]{1,0:T(2,128)}, bf16[64,1024]{1,0:T(8,128)(2,1)}, bf16[64,1024]{1,...) custom-call(s32[2,128]{1,0:T(2,128)} %bitcast.10, s32[2,128]{1,0:T(2,128)} %bitcast.11, ...), custom_call_target="tpu_custom_call" | custom-call | tf_op jit(solution)/shard_map/prepare/pallas_call | solution.py:86
  3.3 0.0 copy-start.8
  3.3 0.0 copy-start.6
  3.3 0.0 copy-start.5
  3.3 0.1 collective-permute-start.6
  3.4 2.2 %collective-permute-done.6.refs_13_ = bf16[272,1024]{1,0:T(8,128)(2,1)S(1)} collective-permute-done((bf16[272,1024]{1,0:T(8,128)(2,1)}, bf16[272,1024]{1,0:T(8,128)(2,1)S(1)}, u32[]{:S(2)}, u32[]{:S(2)}) %collective-permute-start.6) | collective-permute-done | bytes 557088 | tf_op jit(solution)/shard_map/ppermute | solution.py:24
  5.6 1.2 %pad_maximum_fusion = bf16[2,272,1024]{2,1,0:T(8,128)(2,1)S(1)} fusion(bf16[1,272,1024]{2,1,0:T(8,128)(2,1)S(1)} %bitcast.7, bf16[1,272,1024]{2,1,0:T(8,128)(2,1)} %bitcast.6), kind=kLoop, calls=%fused_computation | loop fusion | flops 557056 | bytes 2228224 | tf_op jit(solution)/shard_map/stack | solution.py:380
  6.7 1.7 %collective-permute-start.7 = (bf16[2,272,1024]{2,1,0:T(8,128)(2,1)S(1)}, bf16[2,272,1024]{2,1,0:T(8,128)(2,1)S(1)}, u32[]{:S(2)}, u32[]{:S(2)}) collective-permute-start(bf16[2,272,1024]{2,1,0:T(8,128)(2,1)S(1)} %pad_maximum_fusion), channel_id=1, source_target_pairs={{0,2},{1,7},{2,4},{3,1},{4,6},{5,3},{6,0},{7,5},{8,10},{9,15},{10,... | collective-permute-start | bytes 3342344 | tf_op jit(solution)/shard_map/ppermute | solution.py:34
  8.5 4.0 %collective-permute-start.1 = (bf16[144,1024]{1,0:T(8,128)(2,1)S(1)}, bf16[144,1024]{1,0:T(8,128)(2,1)S(1)}, u32[]{:S(2)}, u32[]{:S(2)}) collective-permute-start(bf16[144,1024]{1,0:T(8,128)(2,1)S(1)} %copy-done.1), channel_id=1, source_target_pairs={{0,24},{8,0},{16,8},{24,16},{1,25},{9,1},{17,9},{25,17},{2,26},{10... | collective-permute-start | bytes 884744 | tf_op jit(solution)/shard_map/ppermute | solution.py:24
  12.5 0.0 collective-permute-start
  12.5 1.5 %collective-permute-start.2 = (bf16[64,1024]{1,0:T(8,128)(2,1)S(1)}, bf16[64,1024]{1,0:T(8,128)(2,1)S(1)}, u32[]{:S(2)}, u32[]{:S(2)}) collective-permute-start(bf16[64,1024]{1,0:T(8,128)(2,1)S(1)} %copy-done.8), channel_id=1, source_target_pairs={{0,32},{32,64},{64,96},{96,0},{1,33},{33,65},{65,97},{97,1},{2,34}... | collective-permute-start | bytes 393224 | tf_op jit(solution)/shard_map/ppermute | solution.py:24
  14.0 1.7 %collective-permute-start.3 = (bf16[64,1024]{1,0:T(8,128)(2,1)S(1)}, bf16[64,1024]{1,0:T(8,128)(2,1)S(1)}, u32[]{:S(2)}, u32[]{:S(2)}) collective-permute-start(bf16[64,1024]{1,0:T(8,128)(2,1)S(1)} %copy-done.7), channel_id=1, source_target_pairs={{0,96},{32,0},{64,32},{96,64},{1,97},{33,1},{65,33},{97,65},{2,98}... | collective-permute-start | bytes 393224 | tf_op jit(solution)/shard_map/ppermute | solution.py:24
  15.8 4.3 %collective-permute-done.2 = bf16[64,1024]{1,0:T(8,128)(2,1)S(1)} collective-permute-done((bf16[64,1024]{1,0:T(8,128)(2,1)S(1)}, bf16[64,1024]{1,0:T(8,128)(2,1)S(1)}, u32[]{:S(2)}, u32[]{:S(2)}) %collective-permute-start.2) | collective-permute-done | bytes 131104 | tf_op jit(solution)/shard_map/ppermute | solution.py:24
  20.1 0.1 collective-permute-done.3
  20.1 0.0 collective-permute-done.1.above
  20.2 3.4 %collective-permute-done.below = bf16[144,1024]{1,0:T(8,128)(2,1)S(1)} collective-permute-done((bf16[144,1024]{1,0:T(8,128)(2,1)S(1)}, bf16[144,1024]{1,0:T(8,128)(2,1)S(1)}, u32[]{:S(2)}, u32[]{:S(2)}) %collective-permute-start) | collective-permute-done | bytes 294944 | tf_op jit(solution)/shard_map/ppermute | solution.py:24
  23.6 0.0 collective-permute-start.5
  23.6 3.0 %collective-permute-start.4 = (bf16[64,1024]{1,0:T(8,128)(2,1)S(1)}, bf16[64,1024]{1,0:T(8,128)(2,1)S(1)}, u32[]{:S(2)}, u32[]{:S(2)}) collective-permute-start(bf16[64,1024]{1,0:T(8,128)(2,1)S(1)} %copy-done.6), channel_id=1, source_target_pairs={{0,64},{32,96},{64,0},{96,32},{1,65},{33,97},{65,1},{97,33},{2,66}... | collective-permute-start | bytes 393224 | tf_op jit(solution)/shard_map/ppermute | solution.py:24
  26.6 4.0 %collective-permute-done.4 = bf16[64,1024]{1,0:T(8,128)(2,1)S(1)} collective-permute-done((bf16[64,1024]{1,0:T(8,128)(2,1)S(1)}, bf16[64,1024]{1,0:T(8,128)(2,1)S(1)}, u32[]{:S(2)}, u32[]{:S(2)}) %collective-permute-start.4) | collective-permute-done | bytes 131104 | tf_op jit(solution)/shard_map/ppermute | solution.py:24
  30.6 0.0 copy-start.4
  30.6 3.1 %collective-permute-done.5.far = bf16[144,1024]{1,0:T(8,128)(2,1)S(1)} collective-permute-done((bf16[144,1024]{1,0:T(8,128)(2,1)S(1)}, bf16[144,1024]{1,0:T(8,128)(2,1)S(1)}, u32[]{:S(2)}, u32[]{:S(2)}) %collective-permute-start.5) | collective-permute-done | bytes 294944 | tf_op jit(solution)/shard_map/ppermute | solution.py:24
  33.8 2.0 %collective-permute-start.8 = (bf16[256,1024]{1,0:T(8,128)(2,1)S(1)}, bf16[256,1024]{1,0:T(8,128)(2,1)S(1)}, u32[]{:S(2)}, u32[]{:S(2)}) collective-permute-start(bf16[256,1024]{1,0:T(8,128)(2,1)S(1)} %pad_maximum_fusion.1.refs_0_), channel_id=1, source_target_pairs={{0,8},{8,16},{16,24},{24,0},{1,9},{9,17},{17,25},{25,1},{2,10},{10... | collective-permute-start | bytes 1572872 | tf_op jit(solution)/shard_map/ppermute | solution.py:24
  35.8 0.7 douts.1
  36.5 1.6 %collective-permute-start.11 = (bf16[4,64,1024]{2,1,0:T(8,128)(2,1)S(1)}, bf16[4,64,1024]{2,1,0:T(8,128)(2,1)S(1)}, u32[]{:S(2)}, u32[]{:S(2)}) collective-permute-start(bf16[4,64,1024]{2,1,0:T(8,128)(2,1)S(1)} %get-tuple-element.79), channel_id=1, source_target_pairs={{0,32},{32,64},{64,96},{96,0},{1,33},{33,65},{65,97},{97,1},{2,34}... | collective-permute-start | bytes 1572872 | tf_op jit(solution)/shard_map/ppermute | solution.py:24
  38.1 1.7 %collective-permute-start.12 = (bf16[4,64,1024]{2,1,0:T(8,128)(2,1)S(1)}, bf16[4,64,1024]{2,1,0:T(8,128)(2,1)S(1)}, u32[]{:S(2)}, u32[]{:S(2)}) collective-permute-start(bf16[4,64,1024]{2,1,0:T(8,128)(2,1)S(1)} %get-tuple-element.80), channel_id=1, source_target_pairs={{0,96},{32,0},{64,32},{96,64},{1,97},{33,1},{65,33},{97,65},{2,98}... | collective-permute-start | bytes 1572872 | tf_op jit(solution)/shard_map/ppermute | solution.py:24
  39.8 7.1 %collective-permute-done.9.refs_2_ = bf16[256,1024]{1,0:T(8,128)(2,1)S(1)} collective-permute-done((bf16[256,1024]{1,0:T(8,128)(2,1)S(1)}, bf16[256,1024]{1,0:T(8,128)(2,1)S(1)}, u32[]{:S(2)}, u32[]{:S(2)}) %collective-permute-start.9) | collective-permute-done | bytes 524320 | tf_op jit(solution)/shard_map/ppermute | solution.py:24
  46.9 1.3 %collective-permute-done.8.refs_1_ = bf16[256,1024]{1,0:T(8,128)(2,1)S(1)} collective-permute-done((bf16[256,1024]{1,0:T(8,128)(2,1)S(1)}, bf16[256,1024]{1,0:T(8,128)(2,1)S(1)}, u32[]{:S(2)}, u32[]{:S(2)}) %collective-permute-start.8) | collective-permute-done | bytes 524320 | tf_op jit(solution)/shard_map/ppermute | solution.py:24
  48.2 2.1 %collective-permute-done.11.refs_4_.refs_7_.refs_10_.refs_9_ = bf16[4,64,1024]{2,1,0:T(8,128)(2,1)S(1)} collective-permute-done((bf16[4,64,1024]{2,1,0:T(8,128)(2,1)S(1)}, bf16[4,64,1024]{2,1,0:T(8,128)(2,1)S(1)}, u32[]{:S(2)}, u32[]{:S(2)}) %collective-permute-start.11) | collective-permute-done | bytes 524320 | tf_op jit(solution)/shard_map/ppermute | solution.py:24
  50.4 0.1 collective-permute-done.12.refs_5_.refs_8_.refs_11_.refs_10_
  50.5 0.1 collective-permute-done.10.refs_16_
  50.6 1.6 %collective-permute-start.16 = (bf16[128,1024]{1,0:T(8,128)(2,1)S(1)}, bf16[128,1024]{1,0:T(8,128)(2,1)S(1)}, u32[]{:S(2)}, u32[]{:S(2)}) collective-permute-start(bf16[128,1024]{1,0:T(8,128)(2,1)S(1)} %slice.7), channel_id=1, source_target_pairs={{0,24},{8,0},{16,8},{24,16},{1,25},{9,1},{17,9},{25,17},{2,26},{10... | collective-permute-start | bytes 786440 | tf_op jit(solution)/shard_map/ppermute | solution.py:24
  52.2 0.5 collective-permute-start.15
  52.7 3.1 %collective-permute-start.14 = (bf16[4,64,1024]{2,1,0:T(8,128)(2,1)S(1)}, bf16[4,64,1024]{2,1,0:T(8,128)(2,1)S(1)}, u32[]{:S(2)}, u32[]{:S(2)}) collective-permute-start(bf16[4,64,1024]{2,1,0:T(8,128)(2,1)S(1)} %get-tuple-element.90), channel_id=1, source_target_pairs={{0,64},{32,96},{64,0},{96,32},{1,65},{33,97},{65,1},{97,33},{2,66}... | collective-permute-start | bytes 1572872 | tf_op jit(solution)/shard_map/ppermute | solution.py:24
  55.7 4.2 %rows.2 = (bf16[576,1024]{1,0:T(8,128)(2,1)S(1)}, bf16[576,1024]{1,0:T(8,128)(2,1)S(1)}, bf16[2,576,512]{2,1,0:T(8,128)(2,1)S(1)}, bf16[2,576,512]{2,1,0:T(8,128...) custom-call(bf16[256,1024]{1,0:T(8,128)(2,1)S(1)} %pad_maximum_fusion.1.refs_0_, ...), custom_call_target="tpu_custom_call" | custom-call | flops 3623878656 | bytes 17172480 | tf_op jit(solution)/shard_map/rows/pallas_call | solution.py:57
  59.9 0.1 collective-permute-start.17
  60.0 3.2 %collective-permute-start.18 = (bf16[208,1024]{1,0:T(8,128)(2,1)S(1)}, bf16[208,1024]{1,0:T(8,128)(2,1)S(1)}, u32[]{:S(2)}, u32[]{:S(2)}) collective-permute-start(bf16[208,1024]{1,0:T(8,128)(2,1)S(1)} %get-tuple-element.104), channel_id=1, source_target_pairs={{0,24},{8,0},{16,8},{24,16},{1,25},{9,1},{17,9},{25,17},{2,26},{10... | collective-permute-start | bytes 1277960 | tf_op jit(solution)/shard_map/ppermute | solution.py:24
  63.3 3.5 %sums.1.near = f32[2,1040,1024]{2,1,0:T(8,128)S(1)} custom-call(bf16[576,1024]{1,0:T(8,128)(2,1)S(1)} %get-tuple-element.91.x, bf16[576,1024]{1,0:T(8,128)(2,1)S(1)} %get-tuple-element.92.d, bf16[2,576,512]{2,1,0:T(8,128)(2,1)S(1)} %get-tuple-element.93.dpre, bf16[2,576,512]{2,1,0:T(8,128)(2,1)S(1)} %get-tuple-element.94.hidden), custom_call_target="tpu_custom_call" | custom-call | flops 2415919104 | bytes 13238272 | tf_op jit(solution)/shard_map/sums/pallas_call | solution.py:57
  66.7 0.0 collective-permute-done.16.refs_4_
  66.7 1.2 %collective-permute-done.14.refs_5_.refs_6_.refs_7_.refs_11_ = bf16[4,64,1024]{2,1,0:T(8,128)(2,1)S(1)} collective-permute-done((bf16[4,64,1024]{2,1,0:T(8,128)(2,1)S(1)}, bf16[4,64,1024]{2,1,0:T(8,128)(2,1)S(1)}, u32[]{:S(2)}, u32[]{:S(2)}) %collective-permute-start.14) | collective-permute-done | bytes 524320 | tf_op jit(solution)/shard_map/ppermute | solution.py:24
  67.9 3.3 %rows.3 = (bf16[448,1024]{1,0:T(8,128)(2,1)S(1)}, bf16[448,1024]{1,0:T(8,128)(2,1)S(1)}, bf16[2,448,512]{2,1,0:T(8,128)(2,1)S(1)}, bf16[2,448,512]{2,1,0:T(8,128...) custom-call(bf16[256,1024]{1,0:T(8,128)(2,1)S(1)} %pad_maximum_fusio, ...), custom_call_target="tpu_custom_call" | custom-call | flops 2818572288 | bytes 15108096 | tf_op jit(solution)/shard_map/rows/pallas_call | solution.py:57
  71.3 1.3 %away.1 = bf16[1040,1024]{1,0:T(8,128)(2,1)S(1)} custom-call(f32[2,1040,1024]{2,1,0:T(8,128)S(1)} %sums.1.near, bf16[448,1024]{1,0:T(8,128)(2,1)S(1)} %get-tuple-element.99.x, bf16[448,1024]{1,0:T(8,128)(2,1)S(1)} %get-tuple-element.100.d, bf16[2,448,512]{2,1,0:T(8,128)(2,1)S(1)} %get-tuple-element.101.dpre, bf16[2,448,512]{2,1,0:T(8,128)(2,1)S(1)} %get-tuple-element.102.hidden), custom_call_target="tpu_custom_call" | custom-call | flops 939524096 | bytes 14319616 | tf_op jit(solution)/shard_map/away/pallas_call | solution.py:57
  72.6 0.0 collective-permute-done.17.refs_1_
  72.6 0.0 collective-permute-done.18.refs_2_
  72.6 0.1 collective-permute-start.22
  72.7 2.3 %collective-permute-start.21 = (bf16[272,1024]{1,0:T(8,128)(2,1)S(1)}, bf16[272,1024]{1,0:T(8,128)(2,1)S(1)}, u32[]{:S(2)}, u32[]{:S(2)}) collective-permute-start(bf16[272,1024]{1,0:T(8,128)(2,1)S(1)} %get-tuple-element.110), channel_id=1, source_target_pairs={{0,16},{8,24},{16,0},{24,8},{1,17},{9,25},{17,1},{25,9},{2,18},{10... | collective-permute-start | bytes 1671176 | tf_op jit(solution)/shard_map/ppermute | solution.py:24
  75.0 1.5 %collective-permute-start.19 = (bf16[80,1024]{1,0:T(8,128)(2,1)S(1)}, bf16[80,1024]{1,0:T(8,128)(2,1)S(1)}, u32[]{:S(2)}, u32[]{:S(2)}) collective-permute-start(bf16[80,1024]{1,0:T(8,128)(2,1)S(1)} %get-tuple-element.108), channel_id=1, source_target_pairs={{0,8},{8,16},{16,24},{24,0},{1,9},{9,17},{17,25},{25,1},{2,10},{10... | collective-permute-start | bytes 491528 | tf_op jit(solution)/shard_map/ppermute | solution.py:24
  76.4 1.8 %collective-permute-start.20 = (bf16[80,1024]{1,0:T(8,128)(2,1)S(1)}, bf16[80,1024]{1,0:T(8,128)(2,1)S(1)}, u32[]{:S(2)}, u32[]{:S(2)}) collective-permute-start(bf16[80,1024]{1,0:T(8,128)(2,1)S(1)} %get-tuple-element.109), channel_id=1, source_target_pairs={{0,24},{8,0},{16,8},{24,16},{1,25},{9,1},{17,9},{25,17},{2,26},{10... | collective-permute-start | bytes 491528 | tf_op jit(solution)/shard_map/ppermute | solution.py:24
  78.2 1.3 %home.1.own = f32[1040,1024]{1,0:T(8,128)S(1)} custom-call(f32[2,1040,1024]{2,1,0:T(8,128)S(1)} %sums.1.near, bf16[448,1024]{1,0:T(8,128)(2,1)S(1)} %get-tuple-element.99.x, bf16[448,1024]{1,0:T(8,128)(2,1)S(1)} %get-tuple-element.100.d, bf16[2,448,512]{2,1,0:T(8,128)(2,1)S(1)} %get-tuple-element.101.dpre, bf16[2,448,512]{2,1,0:T(8,128)(2,1)S(1)} %get-tuple-element.102.hidden), custom_call_target="tpu_custom_call" | custom-call | flops 939524096 | bytes 16449536 | tf_op jit(solution)/shard_map/home/pallas_call | solution.py:57
  79.5 0.0 collective-permute-done.22.got
  79.5 0.4 merge.1
  79.9 0.1 collective-permute-start.23
  80.0 4.3 %collective-permute-start.24 = (bf16[272,1024]{1,0:T(8,128)(2,1)S(1)}, bf16[272,1024]{1,0:T(8,128)(2,1)S(1)}, u32[]{:S(2)}, u32[]{:S(2)}) collective-permute-start(bf16[272,1024]{1,0:T(8,128)(2,1)S(1)} %get-tuple-element.116), channel_id=1, source_target_pairs={{0,6},{1,3},{2,0},{3,5},{4,2},{5,7},{6,4},{7,1},{8,14},{9,11},{10,... | collective-permute-start | bytes 1671176 | tf_op jit(solution)/shard_map/ppermute | solution.py:34
  84.3 8.4 %collective-permute-done.19.refs_4_ = bf16[80,1024]{1,0:T(8,128)(2,1)S(1)} collective-permute-done((bf16[80,1024]{1,0:T(8,128)(2,1)S(1)}, bf16[80,1024]{1,0:T(8,128)(2,1)S(1)}, u32[]{:S(2)}, u32[]{:S(2)}) %collective-permute-start.19) | collective-permute-done | bytes 163872 | tf_op jit(solution)/shard_map/ppermute | solution.py:24
  92.8 1.4 %collective-permute-start.25 = (bf16[272,1024]{1,0:T(8,128)(2,1)S(1)}, bf16[272,1024]{1,0:T(8,128)(2,1)S(1)}, u32[]{:S(2)}, u32[]{:S(2)}) collective-permute-start(bf16[272,1024]{1,0:T(8,128)(2,1)S(1)} %get-tuple-element.117), channel_id=1, source_target_pairs={{0,2},{1,7},{2,4},{3,1},{4,6},{5,3},{6,0},{7,5},{8,10},{9,15},{10,... | collective-permute-start | bytes 1671176 | tf_op jit(solution)/shard_map/ppermute | solution.py:34
  94.2 0.0 collective-permute-done.20.refs_5_
  94.2 0.4 sum_z.1
  94.6 0.0 copy-start.2
  94.6 0.0 copy-start.3
  94.6 13.8 %all_to_all.5.pieces = bf16[4,80,1024]{2,1,0:T(8,128)(2,1)S(1)} all-to-all(bf16[4,80,1024]{2,1,0:T(8,128)(2,1)S(1)} %sum_z.1), channel_id=1, replica_groups=mesh['x'=4,'z'=4,'y'=4,'c'=2] {'x'}, dimensions={0} | all-to-all | bytes 1310720 | tf_op jit(solution)/shard_map/all_to_all | solution.py:463
  108.4 1.2 %finish.1 = (bf16[128,1024]{1,0:T(8,128)(2,1)}, f32[2,128]{1,0:T(2,128)}) custom-call(s32[2,128]{1,0:T(2,128)S(1)} %copy-done.3, bf16[2,128]{1,0:T(2,128)(2,1)S(1)} %bitcast.9, bf16[4,80,1024]{2,1,0:T(8,128)(2,1)S(1)} %all_to_all.5.pieces), custom_call_target="tpu_custom_call" | custom-call | bytes 920064 | tf_op jit(solution)/shard_map/finish/pallas_call | solution.py:57
  109.6 0.0 collective-permute-done.23.a
  109.6 0.0 collective-permute-done.24.b
  109.6 0.0 collective-permute-done.25.c
  109.6 1.0 last.1
  (22 shorter events, 0.1 us)
Async XLA Ops:
  3.3 5.2 %copy-start.1 = (bf16[144,1024]{1,0:T(8,128)(2,1)S(1)}, bf16[144,1024]{1,0:T(8,128)(2,1)}, u32[]{:S(2)}) copy-start(bf16[144,1024]{1,0:T(8,128)(2,1)} %get-tuple-element.66.own) | copy-start | bytes 884740
  3.3 9.2 %copy-start.8 = (bf16[64,1024]{1,0:T(8,128)(2,1)S(1)}, bf16[64,1024]{1,0:T(8,128)(2,1)}, u32[]{:S(2)}) copy-start(bf16[64,1024]{1,0:T(8,128)(2,1)} %get-tuple-element.67) | copy-start | bytes 393220
  3.3 10.7 %copy-start.7 = (bf16[64,1024]{1,0:T(8,128)(2,1)S(1)}, bf16[64,1024]{1,0:T(8,128)(2,1)}, u32[]{:S(2)}) copy-start(bf16[64,1024]{1,0:T(8,128)(2,1)} %get-tuple-element.69) | copy-start | bytes 393220
  3.3 20.3 %copy-start.6 = (bf16[64,1024]{1,0:T(8,128)(2,1)S(1)}, bf16[64,1024]{1,0:T(8,128)(2,1)}, u32[]{:S(2)}) copy-start(bf16[64,1024]{1,0:T(8,128)(2,1)} %get-tuple-element.72) | copy-start | bytes 393220
  3.3 27.3 %copy-start.5 = (bf16[64,1024]{1,0:T(8,128)(2,1)S(1)}, bf16[64,1024]{1,0:T(8,128)(2,1)}, u32[]{:S(2)}) copy-start(bf16[64,1024]{1,0:T(8,128)(2,1)} %get-tuple-element.65) | copy-start | bytes 393220
  3.3 2.2 %collective-permute-start.6 = (bf16[272,1024]{1,0:T(8,128)(2,1)}, bf16[272,1024]{1,0:T(8,128)(2,1)S(1)}, u32[]{:S(2)}, u32[]{:S(2)}) collective-permute-start(bf16[272,1024]{1,0:T(8,128)(2,1)} %get-tuple-element.74.refs_12_), channel_id=1, source_target_pairs={{0,1},{1,0},{2,3},{3,2},{4,5},{5,4},{6,7},{7,6},{8,9},{9,8},{10,11... | collective-permute-start | bytes 1671176 | tf_op jit(solution)/shard_map/ppermute | solution.py:24
  6.7 27.1 %collective-permute-start.7 = (bf16[2,272,1024]{2,1,0:T(8,128)(2,1)S(1)}, bf16[2,272,1024]{2,1,0:T(8,128)(2,1)S(1)}, u32[]{:S(2)}, u32[]{:S(2)}) collective-permute-start(bf16[2,272,1024]{2,1,0:T(8,128)(2,1)S(1)} %pad_maximum_fusion), channel_id=1, source_target_pairs={{0,2},{1,7},{2,4},{3,1},{4,6},{5,3},{6,0},{7,5},{8,10},{9,15},{10,... | collective-permute-start | bytes 3342344 | tf_op jit(solution)/shard_map/ppermute | solution.py:34
  8.5 11.7 %collective-permute-start.1 = (bf16[144,1024]{1,0:T(8,128)(2,1)S(1)}, bf16[144,1024]{1,0:T(8,128)(2,1)S(1)}, u32[]{:S(2)}, u32[]{:S(2)}) collective-permute-start(bf16[144,1024]{1,0:T(8,128)(2,1)S(1)} %copy-done.1), channel_id=1, source_target_pairs={{0,24},{8,0},{16,8},{24,16},{1,25},{9,1},{17,9},{25,17},{2,26},{10... | collective-permute-start | bytes 884744 | tf_op jit(solution)/shard_map/ppermute | solution.py:24
  12.5 11.1 %collective-permute-start = (bf16[144,1024]{1,0:T(8,128)(2,1)S(1)}, bf16[144,1024]{1,0:T(8,128)(2,1)S(1)}, u32[]{:S(2)}, u32[]{:S(2)}) collective-permute-start(bf16[144,1024]{1,0:T(8,128)(2,1)S(1)} %copy-done.1), channel_id=1, source_target_pairs={{0,8},{8,16},{16,24},{24,0},{1,9},{9,17},{17,25},{25,1},{2,10},{10... | collective-permute-start | bytes 884744 | tf_op jit(solution)/shard_map/ppermute | solution.py:24
  12.5 7.5 %collective-permute-start.2 = (bf16[64,1024]{1,0:T(8,128)(2,1)S(1)}, bf16[64,1024]{1,0:T(8,128)(2,1)S(1)}, u32[]{:S(2)}, u32[]{:S(2)}) collective-permute-start(bf16[64,1024]{1,0:T(8,128)(2,1)S(1)} %copy-done.8), channel_id=1, source_target_pairs={{0,32},{32,64},{64,96},{96,0},{1,33},{33,65},{65,97},{97,1},{2,34}... | collective-permute-start | bytes 393224 | tf_op jit(solution)/shard_map/ppermute | solution.py:24
  14.0 6.1 %collective-permute-start.3 = (bf16[64,1024]{1,0:T(8,128)(2,1)S(1)}, bf16[64,1024]{1,0:T(8,128)(2,1)S(1)}, u32[]{:S(2)}, u32[]{:S(2)}) collective-permute-start(bf16[64,1024]{1,0:T(8,128)(2,1)S(1)} %copy-done.7), channel_id=1, source_target_pairs={{0,96},{32,0},{64,32},{96,64},{1,97},{33,1},{65,33},{97,65},{2,98}... | collective-permute-start | bytes 393224 | tf_op jit(solution)/shard_map/ppermute | solution.py:24
  23.6 10.2 %collective-permute-start.5 = (bf16[144,1024]{1,0:T(8,128)(2,1)S(1)}, bf16[144,1024]{1,0:T(8,128)(2,1)S(1)}, u32[]{:S(2)}, u32[]{:S(2)}) collective-permute-start(bf16[144,1024]{1,0:T(8,128)(2,1)S(1)} %collective-permute-done.below), channel_id=1, source_target_pairs={{0,8},{8,16},{16,24},{24,0},{1,9},{9,17},{17,25},{25,1},{2,10},{10... | collective-permute-start | bytes 884744 | tf_op jit(solution)/shard_map/ppermute | solution.py:24
  23.6 7.0 %collective-permute-start.4 = (bf16[64,1024]{1,0:T(8,128)(2,1)S(1)}, bf16[64,1024]{1,0:T(8,128)(2,1)S(1)}, u32[]{:S(2)}, u32[]{:S(2)}) collective-permute-start(bf16[64,1024]{1,0:T(8,128)(2,1)S(1)} %copy-done.6), channel_id=1, source_target_pairs={{0,64},{32,96},{64,0},{96,32},{1,65},{33,97},{65,1},{97,33},{2,66}... | collective-permute-start | bytes 393224 | tf_op jit(solution)/shard_map/ppermute | solution.py:24
  30.6 25.1 %copy-start = (bf16[272,1024]{1,0:T(8,128)(2,1)S(1)}, bf16[272,1024]{1,0:T(8,128)(2,1)}, u32[]{:S(2)}) copy-start(bf16[272,1024]{1,0:T(8,128)(2,1)} %get-tuple-element.74.refs_12_) | copy-start | bytes 1671172
  30.6 25.1 %copy-start.4 = (bf16[1,1024]{1,0:T(2,128)(2,1)S(1)}, bf16[1,1024]{1,0:T(2,128)(2,1)}, u32[]{:S(2)}) copy-start(bf16[1,1024]{1,0:T(2,128)(2,1)} %refs_17_.3) | copy-start | bytes 6148
  33.8 16.7 %collective-permute-start.10 = (bf16[2,272,1024]{2,1,0:T(8,128)(2,1)S(1)}, bf16[2,272,1024]{2,1,0:T(8,128)(2,1)S(1)}, u32[]{:S(2)}, u32[]{:S(2)}) collective-permute-start(bf16[2,272,1024]{2,1,0:T(8,128)(2,1)S(1)} %collective-permute-done.7.refs_14_), channel_id=1, source_target_pairs={{0,2},{1,7},{2,4},{3,1},{4,6},{5,3},{6,0},{7,5},{8,10},{9,15},{10,... | collective-permute-start | bytes 3342344 | tf_op jit(solution)/shard_map/ppermute | solution.py:34
  33.8 13.1 %collective-permute-start.9 = (bf16[256,1024]{1,0:T(8,128)(2,1)S(1)}, bf16[256,1024]{1,0:T(8,128)(2,1)S(1)}, u32[]{:S(2)}, u32[]{:S(2)}) collective-permute-start(bf16[256,1024]{1,0:T(8,128)(2,1)S(1)} %pad_maximum_fusion.1.refs_0_), channel_id=1, source_target_pairs={{0,24},{8,0},{16,8},{24,16},{1,25},{9,1},{17,9},{25,17},{2,26},{10... | collective-permute-start | bytes 1572872 | tf_op jit(solution)/shard_map/ppermute | solution.py:24
  33.8 14.4 %collective-permute-start.8 = (bf16[256,1024]{1,0:T(8,128)(2,1)S(1)}, bf16[256,1024]{1,0:T(8,128)(2,1)S(1)}, u32[]{:S(2)}, u32[]{:S(2)}) collective-permute-start(bf16[256,1024]{1,0:T(8,128)(2,1)S(1)} %pad_maximum_fusion.1.refs_0_), channel_id=1, source_target_pairs={{0,8},{8,16},{16,24},{24,0},{1,9},{9,17},{17,25},{25,1},{2,10},{10... | collective-permute-start | bytes 1572872 | tf_op jit(solution)/shard_map/ppermute | solution.py:24
  36.5 13.8 %collective-permute-start.11 = (bf16[4,64,1024]{2,1,0:T(8,128)(2,1)S(1)}, bf16[4,64,1024]{2,1,0:T(8,128)(2,1)S(1)}, u32[]{:S(2)}, u32[]{:S(2)}) collective-permute-start(bf16[4,64,1024]{2,1,0:T(8,128)(2,1)S(1)} %get-tuple-element.79), channel_id=1, source_target_pairs={{0,32},{32,64},{64,96},{96,0},{1,33},{33,65},{65,97},{97,1},{2,34}... | collective-permute-start | bytes 1572872 | tf_op jit(solution)/shard_map/ppermute | solution.py:24
  38.1 12.3 %collective-permute-start.12 = (bf16[4,64,1024]{2,1,0:T(8,128)(2,1)S(1)}, bf16[4,64,1024]{2,1,0:T(8,128)(2,1)S(1)}, u32[]{:S(2)}, u32[]{:S(2)}) collective-permute-start(bf16[4,64,1024]{2,1,0:T(8,128)(2,1)S(1)} %get-tuple-element.80), channel_id=1, source_target_pairs={{0,96},{32,0},{64,32},{96,64},{1,97},{33,1},{65,33},{97,65},{2,98}... | collective-permute-start | bytes 1572872 | tf_op jit(solution)/shard_map/ppermute | solution.py:24
  50.5 5.2 %collective-permute-start.13 = (bf16[2,272,1024]{2,1,0:T(8,128)(2,1)S(1)}, bf16[2,272,1024]{2,1,0:T(8,128)(2,1)S(1)}, u32[]{:S(2)}, u32[]{:S(2)}) collective-permute-start(bf16[2,272,1024]{2,1,0:T(8,128)(2,1)S(1)} %collective-permute-done.7.refs_14_), channel_id=1, source_target_pairs={{0,1},{1,0},{2,3},{3,2},{4,5},{5,4},{6,7},{7,6},{8,9},{9,8},{10,11... | collective-permute-start | bytes 3342344 | tf_op jit(solution)/shard_map/ppermute | solution.py:24
  50.6 16.2 %collective-permute-start.16 = (bf16[128,1024]{1,0:T(8,128)(2,1)S(1)}, bf16[128,1024]{1,0:T(8,128)(2,1)S(1)}, u32[]{:S(2)}, u32[]{:S(2)}) collective-permute-start(bf16[128,1024]{1,0:T(8,128)(2,1)S(1)} %slice.7), channel_id=1, source_target_pairs={{0,24},{8,0},{16,8},{24,16},{1,25},{9,1},{17,9},{25,17},{2,26},{10... | collective-permute-start | bytes 786440 | tf_op jit(solution)/shard_map/ppermute | solution.py:24
  52.2 14.6 %collective-permute-start.15 = (bf16[128,1024]{1,0:T(8,128)(2,1)S(1)}, bf16[128,1024]{1,0:T(8,128)(2,1)S(1)}, u32[]{:S(2)}, u32[]{:S(2)}) collective-permute-start(bf16[128,1024]{1,0:T(8,128)(2,1)S(1)} %slice.6), channel_id=1, source_target_pairs={{0,8},{8,16},{16,24},{24,0},{1,9},{9,17},{17,25},{25,1},{2,10},{10... | collective-permute-start | bytes 786440 | tf_op jit(solution)/shard_map/ppermute | solution.py:24
  52.7 15.3 %collective-permute-start.14 = (bf16[4,64,1024]{2,1,0:T(8,128)(2,1)S(1)}, bf16[4,64,1024]{2,1,0:T(8,128)(2,1)S(1)}, u32[]{:S(2)}, u32[]{:S(2)}) collective-permute-start(bf16[4,64,1024]{2,1,0:T(8,128)(2,1)S(1)} %get-tuple-element.90), channel_id=1, source_target_pairs={{0,64},{32,96},{64,0},{96,32},{1,65},{33,97},{65,1},{97,33},{2,66}... | collective-permute-start | bytes 1572872 | tf_op jit(solution)/shard_map/ppermute | solution.py:24
  59.9 12.7 %collective-permute-start.17 = (bf16[208,1024]{1,0:T(8,128)(2,1)S(1)}, bf16[208,1024]{1,0:T(8,128)(2,1)S(1)}, u32[]{:S(2)}, u32[]{:S(2)}) collective-permute-start(bf16[208,1024]{1,0:T(8,128)(2,1)S(1)} %get-tuple-element.103), channel_id=1, source_target_pairs={{0,8},{8,16},{16,24},{24,0},{1,9},{9,17},{17,25},{25,1},{2,10},{10... | collective-permute-start | bytes 1277960 | tf_op jit(solution)/shard_map/ppermute | solution.py:24
  60.0 12.6 %collective-permute-start.18 = (bf16[208,1024]{1,0:T(8,128)(2,1)S(1)}, bf16[208,1024]{1,0:T(8,128)(2,1)S(1)}, u32[]{:S(2)}, u32[]{:S(2)}) collective-permute-start(bf16[208,1024]{1,0:T(8,128)(2,1)S(1)} %get-tuple-element.104), channel_id=1, source_target_pairs={{0,24},{8,0},{16,8},{24,16},{1,25},{9,1},{17,9},{25,17},{2,26},{10... | collective-permute-start | bytes 1277960 | tf_op jit(solution)/shard_map/ppermute | solution.py:24
  72.6 6.9 %collective-permute-start.22 = (bf16[1040,1024]{1,0:T(8,128)(2,1)S(1)}, bf16[1040,1024]{1,0:T(8,128)(2,1)S(1)}, u32[]{:S(2)}, u32[]{:S(2)}) collective-permute-start(bf16[1040,1024]{1,0:T(8,128)(2,1)S(1)} %away.1), channel_id=1, source_target_pairs={{0,1},{1,0},{2,3},{3,2},{4,5},{5,4},{6,7},{7,6},{8,9},{9,8},{10,11... | collective-permute-start | bytes 6389768 | tf_op jit(solution)/shard_map/ppermute | solution.py:24
  72.7 21.5 %collective-permute-start.21 = (bf16[272,1024]{1,0:T(8,128)(2,1)S(1)}, bf16[272,1024]{1,0:T(8,128)(2,1)S(1)}, u32[]{:S(2)}, u32[]{:S(2)}) collective-permute-start(bf16[272,1024]{1,0:T(8,128)(2,1)S(1)} %get-tuple-element.110), channel_id=1, source_target_pairs={{0,16},{8,24},{16,0},{24,8},{1,17},{9,25},{17,1},{25,9},{2,18},{10... | collective-permute-start | bytes 1671176 | tf_op jit(solution)/shard_map/ppermute | solution.py:24
  75.0 17.8 %collective-permute-start.19 = (bf16[80,1024]{1,0:T(8,128)(2,1)S(1)}, bf16[80,1024]{1,0:T(8,128)(2,1)S(1)}, u32[]{:S(2)}, u32[]{:S(2)}) collective-permute-start(bf16[80,1024]{1,0:T(8,128)(2,1)S(1)} %get-tuple-element.108), channel_id=1, source_target_pairs={{0,8},{8,16},{16,24},{24,0},{1,9},{9,17},{17,25},{25,1},{2,10},{10... | collective-permute-start | bytes 491528 | tf_op jit(solution)/shard_map/ppermute | solution.py:24
  76.4 17.8 %collective-permute-start.20 = (bf16[80,1024]{1,0:T(8,128)(2,1)S(1)}, bf16[80,1024]{1,0:T(8,128)(2,1)S(1)}, u32[]{:S(2)}, u32[]{:S(2)}) collective-permute-start(bf16[80,1024]{1,0:T(8,128)(2,1)S(1)} %get-tuple-element.109), channel_id=1, source_target_pairs={{0,24},{8,0},{16,8},{24,16},{1,25},{9,1},{17,9},{25,17},{2,26},{10... | collective-permute-start | bytes 491528 | tf_op jit(solution)/shard_map/ppermute | solution.py:24
  79.9 29.7 %collective-permute-start.23 = (bf16[272,1024]{1,0:T(8,128)(2,1)S(1)}, bf16[272,1024]{1,0:T(8,128)(2,1)S(1)}, u32[]{:S(2)}, u32[]{:S(2)}) collective-permute-start(bf16[272,1024]{1,0:T(8,128)(2,1)S(1)} %get-tuple-element.115), channel_id=1, source_target_pairs={{0,4},{1,5},{2,6},{3,7},{4,0},{5,1},{6,2},{7,3},{8,12},{9,13},{10,... | collective-permute-start | bytes 1671176 | tf_op jit(solution)/shard_map/ppermute | solution.py:34
  80.0 29.6 %collective-permute-start.24 = (bf16[272,1024]{1,0:T(8,128)(2,1)S(1)}, bf16[272,1024]{1,0:T(8,128)(2,1)S(1)}, u32[]{:S(2)}, u32[]{:S(2)}) collective-permute-start(bf16[272,1024]{1,0:T(8,128)(2,1)S(1)} %get-tuple-element.116), channel_id=1, source_target_pairs={{0,6},{1,3},{2,0},{3,5},{4,2},{5,7},{6,4},{7,1},{8,14},{9,11},{10,... | collective-permute-start | bytes 1671176 | tf_op jit(solution)/shard_map/ppermute | solution.py:34
  92.8 16.8 %collective-permute-start.25 = (bf16[272,1024]{1,0:T(8,128)(2,1)S(1)}, bf16[272,1024]{1,0:T(8,128)(2,1)S(1)}, u32[]{:S(2)}, u32[]{:S(2)}) collective-permute-start(bf16[272,1024]{1,0:T(8,128)(2,1)S(1)} %get-tuple-element.117), channel_id=1, source_target_pairs={{0,2},{1,7},{2,4},{3,1},{4,6},{5,3},{6,0},{7,5},{8,10},{9,15},{10,... | collective-permute-start | bytes 1671176 | tf_op jit(solution)/shard_map/ppermute | solution.py:34
  94.6 13.8 %copy-start.2 = (bf16[128,2]{0,1:T(2,128)(2,1)S(1)}, bf16[128,2]{0,1:T(2,128)(2,1)}, u32[]{:S(2)}) copy-start(bf16[128,2]{0,1:T(2,128)(2,1)} %param.13) | copy-start | bytes 1540
  94.6 13.8 %copy-start.3 = (s32[2,128]{1,0:T(2,128)S(1)}, s32[2,128]{1,0:T(2,128)}, u32[]{:S(2)}) copy-start(s32[2,128]{1,0:T(2,128)} %get-tuple-element.64.places) | copy-start | bytes 3076

commit v4 on v3

--- a/solution.py
+++ b/solution.py
@@ -22,16 +22,6 @@
 def shift(value, axis, step):
     n = lax.axis_size(axis)
     return lax.ppermute(value, axis, [(i, (i + step) % n) for i in range(n)])
-
-
-def shift_y(value, step, mirrored):
-    n = lax.axis_size("y")
-    moves = []
-    for y in range(n):
-        for c in range(2):
-            to = (y + (-step if mirrored and c else step)) % n
-            moves.append((2 * y + c, 2 * to + c))
-    return lax.ppermute(value, ("y", "c"), moves)
 
 
 def shape(rows, columns, dtype=BF):
@@ -149,14 +139,9 @@
 
 def rows_kernel(n_x, n_d, blocks, *refs):
     xs, ds = refs[:n_x], refs[n_x : n_x + n_d]
-    mine, other, direct, mirror, far_w, b_out, *outs = refs[n_x + n_d :]
+    mine, below, above, far, other, b_out, *outs = refs[n_x + n_d :]
     x, d, dpre, hidden, *dxs = outs
-    shares = [
-        (mine, other),
-        (direct.at[0], direct.at[1]),
-        (mirror.at[1], mirror.at[0]),
-        (far_w.at[0], far_w.at[1]),
-    ]
+    shares = [(ours, other.at[k]) for k, ours in enumerate((mine, below, above, far))]
     width = x.shape[1]
     for parts, whole in ((xs, x), (ds, d)):
         at = 0
@@ -228,6 +213,18 @@
     )
 
 
+def join_kernel(*refs):
+    at = 0
+    for ref in refs[:-1]:
+        refs[-1][at : at + ref.shape[0]] = ref[...]
+        at += ref.shape[0]
+
+
+def stack_kernel(*refs):
+    for k, ref in enumerate(refs[:-1]):
+        refs[-1][k] = ref[...]
+
+
 def sums_kernel(x, d, dpre, hidden, out):
     for c in range(2):
         grads = weight_sums(x[...], d[...], dpre[c], hidden[c])
@@ -276,13 +273,12 @@
     unit = units // n_y
     for k, out in enumerate(outs):
         here = k * unit
-        there = (0, 2, 1, 3)[k] * unit
-        line = lines[0:1, here : here + unit] + side[:, there : there + unit]
+        line = lines[0:1, here : here + unit] + side[:, here : here + unit]
         line = jnp.concatenate([line, jnp.zeros((1, width - unit), F32)], axis=1)
         for at in (0, unit):
             rows = slice(at, at + unit)
-            here_at, there_at = n_y * at + here, n_y * at + there
-            total = own[here_at : here_at + unit] + got[there_at : there_at + unit].astype(F32)
+            from_ = slice(n_y * at + here, n_y * at + here + unit)
+            total = own[from_] + got[from_].astype(F32)
             out[rows] = total.astype(out.dtype)
         if k == 0:
             both = [line, jnp.zeros_like(line), sum_out]
@@ -375,13 +371,13 @@
     raw_above = shift(raw, "z", -1)
     x_1 = shift(x_sent[1], "x", 1)
     x_3 = shift(x_sent[3], "x", -1)
-    other = shift(mine, "c", 1)
+    w_below = shift(mine, "y", 1)
+    w_above = shift(mine, "y", -1)
     raw_below, raw_above, x_1, x_2, x_3 = barrier((raw_below, raw_above, x_1, x_sent[2], x_3))
-    direct = shift_y(jnp.stack([mine, other]), 1, True)
-
     raw_far = shift(raw_below, "z", 1)
-    x_own = jnp.concatenate([x_sent[0], x_1, x_3, shift(x_2, "x", 2)], axis=0)
-    x_own, raw_far, direct = barrier((x_own, raw_far, direct))
+    x_own = [x_sent[0], x_1, x_3, shift(x_2, "x", 2)]
+    x_own = call(join_kernel, "join", [shape(n_expert * cap, width)], x_own)[0]
+    x_own, raw_far, w_below, w_above = barrier((x_own, raw_far, w_below, w_above))
 
     d_sent = call(
         douts_kernel,
@@ -391,14 +387,15 @@
     )
     x_below = shift(x_own, "z", 1)
     x_above = shift(x_own, "z", -1)
-    far_w = shift_y(direct, 1, True)
+    w_far = shift(w_below, "y", 1)
     d_1 = shift(d_sent[1], "x", 1)
     d_3 = shift(d_sent[3], "x", -1)
-    x_below, x_above, direct, far_w, d_1, d_3, d_2 = barrier(
-        (x_below, x_above, direct, far_w, d_1, d_3, d_sent[2])
-    )
-    mirror = shift(direct, "c", 1)
-    w = [mine, other, direct, mirror, far_w]
+    x_below, x_above, w_far, d_1, d_3, d_2 = barrier(
+        (x_below, x_above, w_far, d_1, d_3, d_sent[2])
+    )
+    ours = [mine, w_below, w_above, w_far]
+    every = call(stack_kernel, "stack", [jax.ShapeDtypeStruct((4, *mine.shape), BF)], ours, vmem=12)
+    w = [*ours, shift(every[0], "c", 1)]
 
     d_2 = shift(d_2, "x", 2)
     half = x_own.shape[0] // 2
@@ -461,11 +458,7 @@
         [early[4], early_above, early_below, late[4], late_above, late_below, far],
     )[0]
     final = lax.all_to_all(pieces, "x", 0, 0, tiled=True)
-    moved = [
-        shift_y(home[3], 2, False),
-        shift_y(home[1], -1, True),
-        shift_y(home[2], 1, True),
-    ]
+    moved = [shift(home[k], "y", step) for k, step in ((3, 2), (1, -1), (2, 1))]
     grad_tokens, by_weight = call(
         finish_kernel,
         "finish",

time: 111 us -> 107 us (0.964)
  waiting for transfers between devices: 37.4 us -> 28.1 us
  starting transfers between devices: 37.4 us -> 41.3 us
  local copies, waits for them, and re-layouts: 0.09 us -> 1.92 us
  other arithmetic: 1.19 us -> 0 us
    ppermute x21 -> x26, starting transfers between devices: 29.8 us -> 41.3 us  [shift(): return lax.ppermute(value, axis, [(i, (i + step) % n) for i in range(n)])]
    ppermute x21 -> x26, waiting for transfers between devices: 37.4 us -> 28.1 us  [shift(): return lax.ppermute(value, axis, [(i, (i + step) % n) for i in range(n)])]
    ppermute x5 -> x0, starting transfers between devices: 7.6 us -> none  [shift_y(): return lax.ppermute(value, ('y', 'c'), moves)]
    unnamed x18 -> x12, local copies, waits for them, and re-layouts: 0.05 us -> 1.89 us
    another operation x1 -> x0, other arithmetic: 1.16 us -> none  [on_device(): direct = shift_y(jnp.stack([mine, other]), 1, True)]
    pallas_call x10 -> x12, Pallas kernels: 17.3 us -> 17.4 us  [call(): pl.pallas_call(kernel, out_shape=out_shape, grid=(1,), in_specs=[(full, l...]
  transfers between devices with their start and end apart: 26 -> 26, of which waited for: 13 -> 10; matrix products, arithmetic and copies ran while one was open for 0% -> 0% of each run, Pallas kernels for 15% -> 15%
where the time goes in v4:
time: 107 us
  starting transfers between devices  41.3 us (39%)
  waiting for transfers between devices  28.1 us (26%)
  Pallas kernels  20 us (19%)
  blocking collectives  14.9 us (14%)
  local copies, waits for them, and re-layouts  1.92 us (2%)
    ppermute x26, starting transfers between devices, shift(): return lax.ppermute(value, axis, [(i, (i + step) % n) for i in range(n)])  41.3 us
    ppermute x26, waiting for transfers between devices, shift(): return lax.ppermute(value, axis, [(i, (i + step) % n) for i in range(n)])  28.1 us
    pallas_call x12, Pallas kernels, call(): pl.pallas_call(kernel, out_shape=out_shape, grid=(1,), in_specs=[(full, l...  17.4 us
    all_to_all x1, blocking collectives, on_device(): final = lax.all_to_all(pieces, 'x', 0, 0, tiled=True)  14.9 us
    pallas_call x1, Pallas kernels, call_loading(): pl.pallas_call(body, out_shape=out_shape, in_specs=[pl.BlockSpec(memory_s...  2.63 us
  transfers between devices with their start and end apart: 26, of which 10 were waited for; matrix products, arithmetic and copies ran while one was open for 0% of the time, Pallas kernels for 15%

profile of v4, /device:TPU:0, one launch (start us, length us, event | category | flops | bytes accessed | tf_op | source)
XLA Modules:
  0.0 107.1 jit_solution(10847339064054989589)
XLA Ops:
  0.6 2.6 %prepare.1 = (bf16[272,1024]{1,0:T(8,128)(2,1)}, bf16[144,1024]{1,0:T(8,128)(2,1)}, s32[2,128]{1,0:T(2,128)}, bf16[64,1024]{1,0:T(8,128)(2,1)}, bf16[64,1024]{1,...) custom-call(s32[2,128]{1,0:T(2,128)} %bitcast.6, s32[2,128]{1,0:T(2,128)} %bitcast.7, ...), custom_call_target="tpu_custom_call" | custom-call | tf_op jit(solution)/shard_map/prepare/pallas_call | solution.py:76
  3.3 4.2 %collective-permute-start.1 = (bf16[144,1024]{1,0:T(8,128)(2,1)}, bf16[144,1024]{1,0:T(8,128)(2,1)S(1)}, u32[]{:S(2)}, u32[]{:S(2)}) collective-permute-start(bf16[144,1024]{1,0:T(8,128)(2,1)} %get-tuple-element.66.own), channel_id=1, source_target_pairs={{0,24},{8,0},{16,8},{24,16},{1,25},{9,1},{17,9},{25,17},{2,26},{10... | collective-permute-start | bytes 884744 | tf_op jit(solution)/shard_map/ppermute | solution.py:24
  7.5 0.0 collective-permute-start
  7.5 1.5 %collective-permute-start.2 = (bf16[64,1024]{1,0:T(8,128)(2,1)}, bf16[64,1024]{1,0:T(8,128)(2,1)S(1)}, u32[]{:S(2)}, u32[]{:S(2)}) collective-permute-start(bf16[64,1024]{1,0:T(8,128)(2,1)} %get-tuple-element.67), channel_id=1, source_target_pairs={{0,32},{32,64},{64,96},{96,0},{1,33},{33,65},{65,97},{97,1},{2,34}... | collective-permute-start | bytes 393224 | tf_op jit(solution)/shard_map/ppermute | solution.py:24
  9.0 3.0 %collective-permute-start.7 = (bf16[272,1024]{1,0:T(8,128)(2,1)}, bf16[272,1024]{1,0:T(8,128)(2,1)S(1)}, u32[]{:S(2)}, u32[]{:S(2)}) collective-permute-start(bf16[272,1024]{1,0:T(8,128)(2,1)} %get-tuple-element.74.refs_0_.refs_12_), channel_id=1, source_target_pairs={{0,6},{2,0},{4,2},{6,4},{1,7},{3,1},{5,3},{7,5},{8,14},{10,8},{12,... | collective-permute-start | bytes 1671176 | tf_op jit(solution)/shard_map/ppermute | solution.py:24
  12.0 0.0 collective-permute-start.6
  12.0 1.9 %collective-permute-done.2.refs_1_ = bf16[64,1024]{1,0:T(8,128)(2,1)S(1)} collective-permute-done((bf16[64,1024]{1,0:T(8,128)(2,1)}, bf16[64,1024]{1,0:T(8,128)(2,1)S(1)}, u32[]{:S(2)}, u32[]{:S(2)}) %collective-permute-start.2) | collective-permute-done | bytes 131104 | tf_op jit(solution)/shard_map/ppermute | solution.py:24
  13.9 1.5 %collective-permute-start.3 = (bf16[64,1024]{1,0:T(8,128)(2,1)}, bf16[64,1024]{1,0:T(8,128)(2,1)S(1)}, u32[]{:S(2)}, u32[]{:S(2)}) collective-permute-start(bf16[64,1024]{1,0:T(8,128)(2,1)} %get-tuple-element.69), channel_id=1, source_target_pairs={{0,96},{32,0},{64,32},{96,64},{1,97},{33,1},{65,33},{97,65},{2,98}... | collective-permute-start | bytes 393224 | tf_op jit(solution)/shard_map/ppermute | solution.py:24
  15.4 3.6 %collective-permute-done.3.refs_2_ = bf16[64,1024]{1,0:T(8,128)(2,1)S(1)} collective-permute-done((bf16[64,1024]{1,0:T(8,128)(2,1)}, bf16[64,1024]{1,0:T(8,128)(2,1)S(1)}, u32[]{:S(2)}, u32[]{:S(2)}) %collective-permute-start.3) | collective-permute-done | bytes 131104 | tf_op jit(solution)/shard_map/ppermute | solution.py:24
  19.1 0.0 collective-permute-done.1.above
  19.1 0.0 collective-permute-done.below
  19.1 0.0 collective-permute-start.5
  19.1 1.9 %collective-permute-start.4 = (bf16[64,1024]{1,0:T(8,128)(2,1)}, bf16[64,1024]{1,0:T(8,128)(2,1)S(1)}, u32[]{:S(2)}, u32[]{:S(2)}) collective-permute-start(bf16[64,1024]{1,0:T(8,128)(2,1)} %get-tuple-element.72), channel_id=1, source_target_pairs={{0,64},{32,96},{64,0},{96,32},{1,65},{33,97},{65,1},{97,33},{2,66}... | collective-permute-start | bytes 393224 | tf_op jit(solution)/shard_map/ppermute | solution.py:24
  21.0 4.9 %collective-permute-done.4.refs_3_ = bf16[64,1024]{1,0:T(8,128)(2,1)S(1)} collective-permute-done((bf16[64,1024]{1,0:T(8,128)(2,1)}, bf16[64,1024]{1,0:T(8,128)(2,1)S(1)}, u32[]{:S(2)}, u32[]{:S(2)}) %collective-permute-start.4) | collective-permute-done | bytes 131104 | tf_op jit(solution)/shard_map/ppermute | solution.py:24
  25.8 0.9 copy-done.2
  26.8 0.0 collective-permute-done.7.refs_2_.refs_14_
  26.8 0.1 collective-permute-done.6.refs_1_.refs_13_
  26.9 0.1 collective-permute-done.5.far
  27.0 1.6 %collective-permute-start.10 = (bf16[272,1024]{1,0:T(8,128)(2,1)S(1)}, bf16[272,1024]{1,0:T(8,128)(2,1)S(1)}, u32[]{:S(2)}, u32[]{:S(2)}) collective-permute-start(bf16[272,1024]{1,0:T(8,128)(2,1)S(1)} %collective-permute-done.6.refs_1_.refs_13_), channel_id=1, source_target_pairs={{0,2},{2,4},{4,6},{6,0},{1,3},{3,5},{5,7},{7,1},{8,10},{10,12},{12... | collective-permute-start | bytes 1671176 | tf_op jit(solution)/shard_map/ppermute | solution.py:24
  28.6 3.1 %collective-permute-start.9 = (bf16[256,1024]{1,0:T(8,128)(2,1)S(1)}, bf16[256,1024]{1,0:T(8,128)(2,1)S(1)}, u32[]{:S(2)}, u32[]{:S(2)}) collective-permute-start(bf16[256,1024]{1,0:T(8,128)(2,1)S(1)} %join.1.refs_0_), channel_id=1, source_target_pairs={{0,24},{8,0},{16,8},{24,16},{1,25},{9,1},{17,9},{25,17},{2,26},{10... | collective-permute-start | bytes 1572872 | tf_op jit(solution)/shard_map/ppermute | solution.py:24
  31.7 0.0 collective-permute-start.8
  31.7 1.0 copy-done.1
  32.6 0.7 douts.1
  33.3 0.4 collective-permute-start.11
  33.7 2.9 %collective-permute-start.12 = (bf16[4,64,1024]{2,1,0:T(8,128)(2,1)S(1)}, bf16[4,64,1024]{2,1,0:T(8,128)(2,1)S(1)}, u32[]{:S(2)}, u32[]{:S(2)}) collective-permute-start(bf16[4,64,1024]{2,1,0:T(8,128)(2,1)S(1)} %get-tuple-element.80), channel_id=1, source_target_pairs={{0,96},{32,0},{64,32},{96,64},{1,97},{33,1},{65,33},{97,65},{2,98}... | collective-permute-start | bytes 1572872 | tf_op jit(solution)/shard_map/ppermute | solution.py:24
  36.6 2.5 %collective-permute-done.9.refs_2_ = bf16[256,1024]{1,0:T(8,128)(2,1)S(1)} collective-permute-done((bf16[256,1024]{1,0:T(8,128)(2,1)S(1)}, bf16[256,1024]{1,0:T(8,128)(2,1)S(1)}, u32[]{:S(2)}, u32[]{:S(2)}) %collective-permute-start.9) | collective-permute-done | bytes 524320 | tf_op jit(solution)/shard_map/ppermute | solution.py:24
  39.2 3.4 %collective-permute-done.8.refs_1_ = bf16[256,1024]{1,0:T(8,128)(2,1)S(1)} collective-permute-done((bf16[256,1024]{1,0:T(8,128)(2,1)S(1)}, bf16[256,1024]{1,0:T(8,128)(2,1)S(1)}, u32[]{:S(2)}, u32[]{:S(2)}) %collective-permute-start.8) | collective-permute-done | bytes 524320 | tf_op jit(solution)/shard_map/ppermute | solution.py:24
  42.6 1.7 %collective-permute-done.11.refs_4_.refs_7_.refs_10_.refs_9_ = bf16[4,64,1024]{2,1,0:T(8,128)(2,1)S(1)} collective-permute-done((bf16[4,64,1024]{2,1,0:T(8,128)(2,1)S(1)}, bf16[4,64,1024]{2,1,0:T(8,128)(2,1)S(1)}, u32[]{:S(2)}, u32[]{:S(2)}) %collective-permute-start.11) | collective-permute-done | bytes 524320 | tf_op jit(solution)/shard_map/ppermute | solution.py:24
  44.3 0.0 collective-permute-done.12.refs_5_.refs_8_.refs_11_.refs_10_
  44.3 0.0 copy-start.5
  44.3 0.1 stack.1
  44.5 0.1 collective-permute-start.13
  44.6 3.0 %collective-permute-start.16 = (bf16[128,1024]{1,0:T(8,128)(2,1)S(1)}, bf16[128,1024]{1,0:T(8,128)(2,1)S(1)}, u32[]{:S(2)}, u32[]{:S(2)}) collective-permute-start(bf16[128,1024]{1,0:T(8,128)(2,1)S(1)} %slice.7), channel_id=1, source_target_pairs={{0,24},{8,0},{16,8},{24,16},{1,25},{9,1},{17,9},{25,17},{2,26},{10... | collective-permute-start | bytes 786440 | tf_op jit(solution)/shard_map/ppermute | solution.py:24
  47.6 2.8 %collective-permute-start.14 = (bf16[4,64,1024]{2,1,0:T(8,128)(2,1)S(1)}, bf16[4,64,1024]{2,1,0:T(8,128)(2,1)S(1)}, u32[]{:S(2)}, u32[]{:S(2)}) collective-permute-start(bf16[4,64,1024]{2,1,0:T(8,128)(2,1)S(1)} %get-tuple-element.90), channel_id=1, source_target_pairs={{0,64},{32,96},{64,0},{96,32},{1,65},{33,97},{65,1},{97,33},{2,66}... | collective-permute-start | bytes 1572872 | tf_op jit(solution)/shard_map/ppermute | solution.py:24
  50.4 0.0 collective-permute-done.13.refs_16_
  50.4 4.2 %rows.2 = (bf16[576,1024]{1,0:T(8,128)(2,1)S(1)}, bf16[576,1024]{1,0:T(8,128)(2,1)S(1)}, bf16[2,576,512]{2,1,0:T(8,128)(2,1)S(1)}, bf16[2,576,512]{2,1,0:T(8,128...) custom-call(bf16[256,1024]{1,0:T(8,128)(2,1)S(1)} %join.1.refs_0_, ...), custom_call_target="tpu_custom_call" | custom-call | flops 3623878656 | bytes 17172480 | tf_op jit(solution)/shard_map/rows/pallas_call | solution.py:47
  54.6 0.3 collective-permute-start.17
  54.9 3.3 %collective-permute-start.18 = (bf16[208,1024]{1,0:T(8,128)(2,1)S(1)}, bf16[208,1024]{1,0:T(8,128)(2,1)S(1)}, u32[]{:S(2)}, u32[]{:S(2)}) collective-permute-start(bf16[208,1024]{1,0:T(8,128)(2,1)S(1)} %get-tuple-element.104), channel_id=1, source_target_pairs={{0,24},{8,0},{16,8},{24,16},{1,25},{9,1},{17,9},{25,17},{2,26},{10... | collective-permute-start | bytes 1277960 | tf_op jit(solution)/shard_map/ppermute | solution.py:24
  58.2 3.5 %sums.1.near = f32[2,1040,1024]{2,1,0:T(8,128)S(1)} custom-call(bf16[576,1024]{1,0:T(8,128)(2,1)S(1)} %get-tuple-element.91.x, bf16[576,1024]{1,0:T(8,128)(2,1)S(1)} %get-tuple-element.92.d, bf16[2,576,512]{2,1,0:T(8,128)(2,1)S(1)} %get-tuple-element.93.dpre, bf16[2,576,512]{2,1,0:T(8,128)(2,1)S(1)} %get-tuple-element.94.hidden), custom_call_target="tpu_custom_call" | custom-call | flops 2415919104 | bytes 13238272 | tf_op jit(solution)/shard_map/sums/pallas_call | solution.py:47
  61.7 1.5 %collective-permute-done.14.refs_5_.refs_6_.refs_7_.refs_11_ = bf16[4,64,1024]{2,1,0:T(8,128)(2,1)S(1)} collective-permute-done((bf16[4,64,1024]{2,1,0:T(8,128)(2,1)S(1)}, bf16[4,64,1024]{2,1,0:T(8,128)(2,1)S(1)}, u32[]{:S(2)}, u32[]{:S(2)}) %collective-permute-start.14) | collective-permute-done | bytes 524320 | tf_op jit(solution)/shard_map/ppermute | solution.py:24
  63.2 3.3 %rows.3 = (bf16[448,1024]{1,0:T(8,128)(2,1)S(1)}, bf16[448,1024]{1,0:T(8,128)(2,1)S(1)}, bf16[2,448,512]{2,1,0:T(8,128)(2,1)S(1)}, bf16[2,448,512]{2,1,0:T(8,128...) custom-call(bf16[256,1024]{1,0:T(8,128)(2,1)S(1)} %join.1.refs_0_, ...), custom_call_target="tpu_custom_call" | custom-call | flops 2818572288 | bytes 15108096 | tf_op jit(solution)/shard_map/rows/pallas_call | solution.py:47
  66.5 1.3 %away.1 = bf16[1040,1024]{1,0:T(8,128)(2,1)S(1)} custom-call(f32[2,1040,1024]{2,1,0:T(8,128)S(1)} %sums.1.near, bf16[448,1024]{1,0:T(8,128)(2,1)S(1)} %get-tuple-element.99.x, bf16[448,1024]{1,0:T(8,128)(2,1)S(1)} %get-tuple-element.100.d, bf16[2,448,512]{2,1,0:T(8,128)(2,1)S(1)} %get-tuple-element.101.dpre, bf16[2,448,512]{2,1,0:T(8,128)(2,1)S(1)} %get-tuple-element.102.hidden), custom_call_target="tpu_custom_call" | custom-call | flops 939524096 | bytes 14319616 | tf_op jit(solution)/shard_map/away/pallas_call | solution.py:47
  67.8 0.0 collective-permute-done.17.refs_1_
  67.9 0.0 collective-permute-done.18.refs_2_
  67.9 0.1 collective-permute-start.22
  68.0 2.5 %collective-permute-start.21 = (bf16[272,1024]{1,0:T(8,128)(2,1)S(1)}, bf16[272,1024]{1,0:T(8,128)(2,1)S(1)}, u32[]{:S(2)}, u32[]{:S(2)}) collective-permute-start(bf16[272,1024]{1,0:T(8,128)(2,1)S(1)} %get-tuple-element.110), channel_id=1, source_target_pairs={{0,16},{8,24},{16,0},{24,8},{1,17},{9,25},{17,1},{25,9},{2,18},{10... | collective-permute-start | bytes 1671176 | tf_op jit(solution)/shard_map/ppermute | solution.py:24
  70.5 1.4 %collective-permute-start.19 = (bf16[80,1024]{1,0:T(8,128)(2,1)S(1)}, bf16[80,1024]{1,0:T(8,128)(2,1)S(1)}, u32[]{:S(2)}, u32[]{:S(2)}) collective-permute-start(bf16[80,1024]{1,0:T(8,128)(2,1)S(1)} %get-tuple-element.108), channel_id=1, source_target_pairs={{0,8},{8,16},{16,24},{24,0},{1,9},{9,17},{17,25},{25,1},{2,10},{10... | collective-permute-start | bytes 491528 | tf_op jit(solution)/shard_map/ppermute | solution.py:24
  71.9 1.9 %collective-permute-start.20 = (bf16[80,1024]{1,0:T(8,128)(2,1)S(1)}, bf16[80,1024]{1,0:T(8,128)(2,1)S(1)}, u32[]{:S(2)}, u32[]{:S(2)}) collective-permute-start(bf16[80,1024]{1,0:T(8,128)(2,1)S(1)} %get-tuple-element.109), channel_id=1, source_target_pairs={{0,24},{8,0},{16,8},{24,16},{1,25},{9,1},{17,9},{25,17},{2,26},{10... | collective-permute-start | bytes 491528 | tf_op jit(solution)/shard_map/ppermute | solution.py:24
  73.7 1.3 %home.1.own = f32[1040,1024]{1,0:T(8,128)S(1)} custom-call(f32[2,1040,1024]{2,1,0:T(8,128)S(1)} %sums.1.near, bf16[448,1024]{1,0:T(8,128)(2,1)S(1)} %get-tuple-element.99.x, bf16[448,1024]{1,0:T(8,128)(2,1)S(1)} %get-tuple-element.100.d, bf16[2,448,512]{2,1,0:T(8,128)(2,1)S(1)} %get-tuple-element.101.dpre, bf16[2,448,512]{2,1,0:T(8,128)(2,1)S(1)} %get-tuple-element.102.hidden), custom_call_target="tpu_custom_call" | custom-call | flops 939524096 | bytes 16449536 | tf_op jit(solution)/shard_map/home/pallas_call | solution.py:47
  75.1 0.4 merge.1
  75.4 3.0 %collective-permute-start.23 = (bf16[272,1024]{1,0:T(8,128)(2,1)S(1)}, bf16[272,1024]{1,0:T(8,128)(2,1)S(1)}, u32[]{:S(2)}, u32[]{:S(2)}) collective-permute-start(bf16[272,1024]{1,0:T(8,128)(2,1)S(1)} %get-tuple-element.115), channel_id=1, source_target_pairs={{0,4},{2,6},{4,0},{6,2},{1,5},{3,7},{5,1},{7,3},{8,12},{10,14},{12... | collective-permute-start | bytes 1671176 | tf_op jit(solution)/shard_map/ppermute | solution.py:24
  78.4 1.3 %collective-permute-start.24 = (bf16[272,1024]{1,0:T(8,128)(2,1)S(1)}, bf16[272,1024]{1,0:T(8,128)(2,1)S(1)}, u32[]{:S(2)}, u32[]{:S(2)}) collective-permute-start(bf16[272,1024]{1,0:T(8,128)(2,1)S(1)} %get-tuple-element.116), channel_id=1, source_target_pairs={{0,6},{2,0},{4,2},{6,4},{1,7},{3,1},{5,3},{7,5},{8,14},{10,8},{12,... | collective-permute-start | bytes 1671176 | tf_op jit(solution)/shard_map/ppermute | solution.py:24
  79.8 8.2 %collective-permute-done.19.refs_4_ = bf16[80,1024]{1,0:T(8,128)(2,1)S(1)} collective-permute-done((bf16[80,1024]{1,0:T(8,128)(2,1)S(1)}, bf16[80,1024]{1,0:T(8,128)(2,1)S(1)}, u32[]{:S(2)}, u32[]{:S(2)}) %collective-permute-start.19) | collective-permute-done | bytes 163872 | tf_op jit(solution)/shard_map/ppermute | solution.py:24
  88.0 1.6 %collective-permute-start.25 = (bf16[272,1024]{1,0:T(8,128)(2,1)S(1)}, bf16[272,1024]{1,0:T(8,128)(2,1)S(1)}, u32[]{:S(2)}, u32[]{:S(2)}) collective-permute-start(bf16[272,1024]{1,0:T(8,128)(2,1)S(1)} %get-tuple-element.117), channel_id=1, source_target_pairs={{0,2},{2,4},{4,6},{6,0},{1,3},{3,5},{5,7},{7,1},{8,10},{10,12},{12... | collective-permute-start | bytes 1671176 | tf_op jit(solution)/shard_map/ppermute | solution.py:24
  89.6 0.0 collective-permute-done.20.refs_5_
  89.6 0.0 collective-permute-done.21.refs_6_
  89.6 0.0 copy-start.4
  89.6 0.4 sum_z.1
  90.0 14.9 %all_to_all.5.pieces = bf16[4,80,1024]{2,1,0:T(8,128)(2,1)S(1)} all-to-all(bf16[4,80,1024]{2,1,0:T(8,128)(2,1)S(1)} %sum_z.1), channel_id=1, replica_groups=mesh['x'=4,'z'=4,'y'=4,'c'=2] {'x'}, dimensions={0} | all-to-all | bytes 1310720 | tf_op jit(solution)/shard_map/all_to_all | solution.py:460
  104.9 1.2 %finish.1 = (bf16[128,1024]{1,0:T(8,128)(2,1)}, f32[2,128]{1,0:T(2,128)}) custom-call(s32[2,128]{1,0:T(2,128)S(1)} %copy-done.4, bf16[2,128]{1,0:T(2,128)(2,1)S(1)} %bitcast.5, bf16[4,80,1024]{2,1,0:T(8,128)(2,1)S(1)} %all_to_all.5.pieces), custom_call_target="tpu_custom_call" | custom-call | bytes 920064 | tf_op jit(solution)/shard_map/finish/pallas_call | solution.py:47
  106.1 0.0 collective-permute-done.23.a
  106.1 0.0 collective-permute-done.24.b
  106.1 0.0 collective-permute-done.25.c
  106.1 1.0 last.1
  (16 shorter events, 0.1 us)
Async XLA Ops:
  3.3 41.0 %copy-start = (bf16[272,1024]{1,0:T(8,128)(2,1)S(1)}, bf16[272,1024]{1,0:T(8,128)(2,1)}, u32[]{:S(2)}) copy-start(bf16[272,1024]{1,0:T(8,128)(2,1)} %get-tuple-element.74.refs_0_.refs_12_) | copy-start | bytes 1671172
  3.3 15.8 %collective-permute-start.1 = (bf16[144,1024]{1,0:T(8,128)(2,1)}, bf16[144,1024]{1,0:T(8,128)(2,1)S(1)}, u32[]{:S(2)}, u32[]{:S(2)}) collective-permute-start(bf16[144,1024]{1,0:T(8,128)(2,1)} %get-tuple-element.66.own), channel_id=1, source_target_pairs={{0,24},{8,0},{16,8},{24,16},{1,25},{9,1},{17,9},{25,17},{2,26},{10... | collective-permute-start | bytes 884744 | tf_op jit(solution)/shard_map/ppermute | solution.py:24
  7.5 11.6 %collective-permute-start = (bf16[144,1024]{1,0:T(8,128)(2,1)}, bf16[144,1024]{1,0:T(8,128)(2,1)S(1)}, u32[]{:S(2)}, u32[]{:S(2)}) collective-permute-start(bf16[144,1024]{1,0:T(8,128)(2,1)} %get-tuple-element.66.own), channel_id=1, source_target_pairs={{0,8},{8,16},{16,24},{24,0},{1,9},{9,17},{17,25},{25,1},{2,10},{10... | collective-permute-start | bytes 884744 | tf_op jit(solution)/shard_map/ppermute | solution.py:24
  7.5 6.4 %collective-permute-start.2 = (bf16[64,1024]{1,0:T(8,128)(2,1)}, bf16[64,1024]{1,0:T(8,128)(2,1)S(1)}, u32[]{:S(2)}, u32[]{:S(2)}) collective-permute-start(bf16[64,1024]{1,0:T(8,128)(2,1)} %get-tuple-element.67), channel_id=1, source_target_pairs={{0,32},{32,64},{64,96},{96,0},{1,33},{33,65},{65,97},{97,1},{2,34}... | collective-permute-start | bytes 393224 | tf_op jit(solution)/shard_map/ppermute | solution.py:24
  9.0 17.8 %collective-permute-start.7 = (bf16[272,1024]{1,0:T(8,128)(2,1)}, bf16[272,1024]{1,0:T(8,128)(2,1)S(1)}, u32[]{:S(2)}, u32[]{:S(2)}) collective-permute-start(bf16[272,1024]{1,0:T(8,128)(2,1)} %get-tuple-element.74.refs_0_.refs_12_), channel_id=1, source_target_pairs={{0,6},{2,0},{4,2},{6,4},{1,7},{3,1},{5,3},{7,5},{8,14},{10,8},{12,... | collective-permute-start | bytes 1671176 | tf_op jit(solution)/shard_map/ppermute | solution.py:24
  12.0 14.9 %collective-permute-start.6 = (bf16[272,1024]{1,0:T(8,128)(2,1)}, bf16[272,1024]{1,0:T(8,128)(2,1)S(1)}, u32[]{:S(2)}, u32[]{:S(2)}) collective-permute-start(bf16[272,1024]{1,0:T(8,128)(2,1)} %get-tuple-element.74.refs_0_.refs_12_), channel_id=1, source_target_pairs={{0,2},{2,4},{4,6},{6,0},{1,3},{3,5},{5,7},{7,1},{8,10},{10,12},{12... | collective-permute-start | bytes 1671176 | tf_op jit(solution)/shard_map/ppermute | solution.py:24
  13.9 5.2 %collective-permute-start.3 = (bf16[64,1024]{1,0:T(8,128)(2,1)}, bf16[64,1024]{1,0:T(8,128)(2,1)S(1)}, u32[]{:S(2)}, u32[]{:S(2)}) collective-permute-start(bf16[64,1024]{1,0:T(8,128)(2,1)} %get-tuple-element.69), channel_id=1, source_target_pairs={{0,96},{32,0},{64,32},{96,64},{1,97},{33,1},{65,33},{97,65},{2,98}... | collective-permute-start | bytes 393224 | tf_op jit(solution)/shard_map/ppermute | solution.py:24
  19.1 8.0 %collective-permute-start.5 = (bf16[144,1024]{1,0:T(8,128)(2,1)S(1)}, bf16[144,1024]{1,0:T(8,128)(2,1)S(1)}, u32[]{:S(2)}, u32[]{:S(2)}) collective-permute-start(bf16[144,1024]{1,0:T(8,128)(2,1)S(1)} %collective-permute-done.below), channel_id=1, source_target_pairs={{0,8},{8,16},{16,24},{24,0},{1,9},{9,17},{17,25},{25,1},{2,10},{10... | collective-permute-start | bytes 884744 | tf_op jit(solution)/shard_map/ppermute | solution.py:24
  19.1 6.8 %collective-permute-start.4 = (bf16[64,1024]{1,0:T(8,128)(2,1)}, bf16[64,1024]{1,0:T(8,128)(2,1)S(1)}, u32[]{:S(2)}, u32[]{:S(2)}) collective-permute-start(bf16[64,1024]{1,0:T(8,128)(2,1)} %get-tuple-element.72), channel_id=1, source_target_pairs={{0,64},{32,96},{64,0},{96,32},{1,65},{33,97},{65,1},{97,33},{2,66}... | collective-permute-start | bytes 393224 | tf_op jit(solution)/shard_map/ppermute | solution.py:24
  25.8 0.9 copy-start.2
  27.0 17.3 %collective-permute-start.10 = (bf16[272,1024]{1,0:T(8,128)(2,1)S(1)}, bf16[272,1024]{1,0:T(8,128)(2,1)S(1)}, u32[]{:S(2)}, u32[]{:S(2)}) collective-permute-start(bf16[272,1024]{1,0:T(8,128)(2,1)S(1)} %collective-permute-done.6.refs_1_.refs_13_), channel_id=1, source_target_pairs={{0,2},{2,4},{4,6},{6,0},{1,3},{3,5},{5,7},{7,1},{8,10},{10,12},{12... | collective-permute-start | bytes 1671176 | tf_op jit(solution)/shard_map/ppermute | solution.py:24
  28.6 10.6 %collective-permute-start.9 = (bf16[256,1024]{1,0:T(8,128)(2,1)S(1)}, bf16[256,1024]{1,0:T(8,128)(2,1)S(1)}, u32[]{:S(2)}, u32[]{:S(2)}) collective-permute-start(bf16[256,1024]{1,0:T(8,128)(2,1)S(1)} %join.1.refs_0_), channel_id=1, source_target_pairs={{0,24},{8,0},{16,8},{24,16},{1,25},{9,1},{17,9},{25,17},{2,26},{10... | collective-permute-start | bytes 1572872 | tf_op jit(solution)/shard_map/ppermute | solution.py:24
  31.7 10.9 %collective-permute-start.8 = (bf16[256,1024]{1,0:T(8,128)(2,1)S(1)}, bf16[256,1024]{1,0:T(8,128)(2,1)S(1)}, u32[]{:S(2)}, u32[]{:S(2)}) collective-permute-start(bf16[256,1024]{1,0:T(8,128)(2,1)S(1)} %join.1.refs_0_), channel_id=1, source_target_pairs={{0,8},{8,16},{16,24},{24,0},{1,9},{9,17},{17,25},{25,1},{2,10},{10... | collective-permute-start | bytes 1572872 | tf_op jit(solution)/shard_map/ppermute | solution.py:24
  31.7 1.0 copy-start.1
  33.3 11.0 %collective-permute-start.11 = (bf16[4,64,1024]{2,1,0:T(8,128)(2,1)S(1)}, bf16[4,64,1024]{2,1,0:T(8,128)(2,1)S(1)}, u32[]{:S(2)}, u32[]{:S(2)}) collective-permute-start(bf16[4,64,1024]{2,1,0:T(8,128)(2,1)S(1)} %get-tuple-element.79), channel_id=1, source_target_pairs={{0,32},{32,64},{64,96},{96,0},{1,33},{33,65},{65,97},{97,1},{2,34}... | collective-permute-start | bytes 1572872 | tf_op jit(solution)/shard_map/ppermute | solution.py:24
  33.7 10.6 %collective-permute-start.12 = (bf16[4,64,1024]{2,1,0:T(8,128)(2,1)S(1)}, bf16[4,64,1024]{2,1,0:T(8,128)(2,1)S(1)}, u32[]{:S(2)}, u32[]{:S(2)}) collective-permute-start(bf16[4,64,1024]{2,1,0:T(8,128)(2,1)S(1)} %get-tuple-element.80), channel_id=1, source_target_pairs={{0,96},{32,0},{64,32},{96,64},{1,97},{33,1},{65,33},{97,65},{2,98}... | collective-permute-start | bytes 1572872 | tf_op jit(solution)/shard_map/ppermute | solution.py:24
  44.3 6.1 %copy-start.5 = (bf16[1,1024]{1,0:T(2,128)(2,1)S(1)}, bf16[1,1024]{1,0:T(2,128)(2,1)}, u32[]{:S(2)}) copy-start(bf16[1,1024]{1,0:T(2,128)(2,1)} %refs_17_.3) | copy-start | bytes 6148
  44.5 6.0 %collective-permute-start.13 = (bf16[4,272,1024]{2,1,0:T(8,128)(2,1)S(1)}, bf16[4,272,1024]{2,1,0:T(8,128)(2,1)S(1)}, u32[]{:S(2)}, u32[]{:S(2)}) collective-permute-start(bf16[4,272,1024]{2,1,0:T(8,128)(2,1)S(1)} %stack.1), channel_id=1, source_target_pairs={{0,1},{1,0},{2,3},{3,2},{4,5},{5,4},{6,7},{7,6},{8,9},{9,8},{10,11... | collective-permute-start | bytes 6684680 | tf_op jit(solution)/shard_map/ppermute | solution.py:24
  44.6 17.0 %collective-permute-start.16 = (bf16[128,1024]{1,0:T(8,128)(2,1)S(1)}, bf16[128,1024]{1,0:T(8,128)(2,1)S(1)}, u32[]{:S(2)}, u32[]{:S(2)}) collective-permute-start(bf16[128,1024]{1,0:T(8,128)(2,1)S(1)} %slice.7), channel_id=1, source_target_pairs={{0,24},{8,0},{16,8},{24,16},{1,25},{9,1},{17,9},{25,17},{2,26},{10... | collective-permute-start | bytes 786440 | tf_op jit(solution)/shard_map/ppermute | solution.py:24
  47.6 14.0 %collective-permute-start.15 = (bf16[128,1024]{1,0:T(8,128)(2,1)S(1)}, bf16[128,1024]{1,0:T(8,128)(2,1)S(1)}, u32[]{:S(2)}, u32[]{:S(2)}) collective-permute-start(bf16[128,1024]{1,0:T(8,128)(2,1)S(1)} %slice.6), channel_id=1, source_target_pairs={{0,8},{8,16},{16,24},{24,0},{1,9},{9,17},{17,25},{25,1},{2,10},{10... | collective-permute-start | bytes 786440 | tf_op jit(solution)/shard_map/ppermute | solution.py:24
  47.6 15.5 %collective-permute-start.14 = (bf16[4,64,1024]{2,1,0:T(8,128)(2,1)S(1)}, bf16[4,64,1024]{2,1,0:T(8,128)(2,1)S(1)}, u32[]{:S(2)}, u32[]{:S(2)}) collective-permute-start(bf16[4,64,1024]{2,1,0:T(8,128)(2,1)S(1)} %get-tuple-element.90), channel_id=1, source_target_pairs={{0,64},{32,96},{64,0},{96,32},{1,65},{33,97},{65,1},{97,33},{2,66}... | collective-permute-start | bytes 1572872 | tf_op jit(solution)/shard_map/ppermute | solution.py:24
  54.6 13.2 %collective-permute-start.17 = (bf16[208,1024]{1,0:T(8,128)(2,1)S(1)}, bf16[208,1024]{1,0:T(8,128)(2,1)S(1)}, u32[]{:S(2)}, u32[]{:S(2)}) collective-permute-start(bf16[208,1024]{1,0:T(8,128)(2,1)S(1)} %get-tuple-element.103), channel_id=1, source_target_pairs={{0,8},{8,16},{16,24},{24,0},{1,9},{9,17},{17,25},{25,1},{2,10},{10... | collective-permute-start | bytes 1277960 | tf_op jit(solution)/shard_map/ppermute | solution.py:24
  54.9 12.9 %collective-permute-start.18 = (bf16[208,1024]{1,0:T(8,128)(2,1)S(1)}, bf16[208,1024]{1,0:T(8,128)(2,1)S(1)}, u32[]{:S(2)}, u32[]{:S(2)}) collective-permute-start(bf16[208,1024]{1,0:T(8,128)(2,1)S(1)} %get-tuple-element.104), channel_id=1, source_target_pairs={{0,24},{8,0},{16,8},{24,16},{1,25},{9,1},{17,9},{25,17},{2,26},{10... | collective-permute-start | bytes 1277960 | tf_op jit(solution)/shard_map/ppermute | solution.py:24
  67.9 7.2 %collective-permute-start.22 = (bf16[1040,1024]{1,0:T(8,128)(2,1)S(1)}, bf16[1040,1024]{1,0:T(8,128)(2,1)S(1)}, u32[]{:S(2)}, u32[]{:S(2)}) collective-permute-start(bf16[1040,1024]{1,0:T(8,128)(2,1)S(1)} %away.1), channel_id=1, source_target_pairs={{0,1},{1,0},{2,3},{3,2},{4,5},{5,4},{6,7},{7,6},{8,9},{9,8},{10,11... | collective-permute-start | bytes 6389768 | tf_op jit(solution)/shard_map/ppermute | solution.py:24
  68.0 21.6 %collective-permute-start.21 = (bf16[272,1024]{1,0:T(8,128)(2,1)S(1)}, bf16[272,1024]{1,0:T(8,128)(2,1)S(1)}, u32[]{:S(2)}, u32[]{:S(2)}) collective-permute-start(bf16[272,1024]{1,0:T(8,128)(2,1)S(1)} %get-tuple-element.110), channel_id=1, source_target_pairs={{0,16},{8,24},{16,0},{24,8},{1,17},{9,25},{17,1},{25,9},{2,18},{10... | collective-permute-start | bytes 1671176 | tf_op jit(solution)/shard_map/ppermute | solution.py:24
  70.5 17.5 %collective-permute-start.19 = (bf16[80,1024]{1,0:T(8,128)(2,1)S(1)}, bf16[80,1024]{1,0:T(8,128)(2,1)S(1)}, u32[]{:S(2)}, u32[]{:S(2)}) collective-permute-start(bf16[80,1024]{1,0:T(8,128)(2,1)S(1)} %get-tuple-element.108), channel_id=1, source_target_pairs={{0,8},{8,16},{16,24},{24,0},{1,9},{9,17},{17,25},{25,1},{2,10},{10... | collective-permute-start | bytes 491528 | tf_op jit(solution)/shard_map/ppermute | solution.py:24
  71.9 17.7 %collective-permute-start.20 = (bf16[80,1024]{1,0:T(8,128)(2,1)S(1)}, bf16[80,1024]{1,0:T(8,128)(2,1)S(1)}, u32[]{:S(2)}, u32[]{:S(2)}) collective-permute-start(bf16[80,1024]{1,0:T(8,128)(2,1)S(1)} %get-tuple-element.109), channel_id=1, source_target_pairs={{0,24},{8,0},{16,8},{24,16},{1,25},{9,1},{17,9},{25,17},{2,26},{10... | collective-permute-start | bytes 491528 | tf_op jit(solution)/shard_map/ppermute | solution.py:24
  75.4 30.6 %collective-permute-start.23 = (bf16[272,1024]{1,0:T(8,128)(2,1)S(1)}, bf16[272,1024]{1,0:T(8,128)(2,1)S(1)}, u32[]{:S(2)}, u32[]{:S(2)}) collective-permute-start(bf16[272,1024]{1,0:T(8,128)(2,1)S(1)} %get-tuple-element.115), channel_id=1, source_target_pairs={{0,4},{2,6},{4,0},{6,2},{1,5},{3,7},{5,1},{7,3},{8,12},{10,14},{12... | collective-permute-start | bytes 1671176 | tf_op jit(solution)/shard_map/ppermute | solution.py:24
  78.4 27.6 %collective-permute-start.24 = (bf16[272,1024]{1,0:T(8,128)(2,1)S(1)}, bf16[272,1024]{1,0:T(8,128)(2,1)S(1)}, u32[]{:S(2)}, u32[]{:S(2)}) collective-permute-start(bf16[272,1024]{1,0:T(8,128)(2,1)S(1)} %get-tuple-element.116), channel_id=1, source_target_pairs={{0,6},{2,0},{4,2},{6,4},{1,7},{3,1},{5,3},{7,5},{8,14},{10,8},{12,... | collective-permute-start | bytes 1671176 | tf_op jit(solution)/shard_map/ppermute | solution.py:24
  88.0 18.0 %collective-permute-start.25 = (bf16[272,1024]{1,0:T(8,128)(2,1)S(1)}, bf16[272,1024]{1,0:T(8,128)(2,1)S(1)}, u32[]{:S(2)}, u32[]{:S(2)}) collective-permute-start(bf16[272,1024]{1,0:T(8,128)(2,1)S(1)} %get-tuple-element.117), channel_id=1, source_target_pairs={{0,2},{2,4},{4,6},{6,0},{1,3},{3,5},{5,7},{7,1},{8,10},{10,12},{12... | collective-permute-start | bytes 1671176 | tf_op jit(solution)/shard_map/ppermute | solution.py:24
  89.6 15.3 %copy-start.3 = (bf16[128,2]{0,1:T(2,128)(2,1)S(1)}, bf16[128,2]{0,1:T(2,128)(2,1)}, u32[]{:S(2)}) copy-start(bf16[128,2]{0,1:T(2,128)(2,1)} %param.13) | copy-start | bytes 1540
  89.6 15.3 %copy-start.4 = (s32[2,128]{1,0:T(2,128)S(1)}, s32[2,128]{1,0:T(2,128)}, u32[]{:S(2)}) copy-start(s32[2,128]{1,0:T(2,128)} %get-tuple-element.64.places) | copy-start | bytes 3076

commit v5 on v4

--- a/solution.py
+++ b/solution.py
@@ -107,7 +107,7 @@
     share[units : units + EXTRA] = lines_of([b_in[...].astype(F32)], share.shape[1], BF)
     share[units + EXTRA :] = w_out[0]
     n_expert = len(outs)
-    cap = outs[0].shape[0]
+    cap = outs[0].shape[1]
     n_tok = tokens.shape[0]
     turned = routes[...] - lax.axis_index("x")
     turned = jnp.where(turned < 0, turned + n_expert, turned)
@@ -117,16 +117,21 @@
     side = [place.astype(F32), combine[...].astype(F32)]
     raw[n_tok:] = lines_of(side, grads.shape[1], BF)
     spots = lax.broadcasted_iota(jnp.int32, (n_expert * cap, n_tok), 0)
-    picks = jnp.where((place[0:1, :] == spots) | (place[1:2, :] == spots), 1.0, 0.0)
-    rows = dot(picks.astype(BF), tokens[...], NN).astype(BF)
+    first, second = place[0:1] == spots, place[1:2] == spots
+    picks = jnp.where(first | second, 1.0, 0.0)
+    weights = combine[...].astype(F32)
+    scaled = jnp.where(first, weights[0:1], 0.0) + jnp.where(second, weights[1:2], 0.0)
+    rows_x = dot(picks.astype(BF), tokens[...], NN).astype(BF)
+    rows_d = dot(scaled.astype(BF), grads[...], NN).astype(BF)
     for s, out in enumerate(outs):
-        out[...] = rows[s * cap : (s + 1) * cap]
-
-
-def douts_kernel(own, below, above, far, *outs):
+        out[0] = rows_x[s * cap : (s + 1) * cap]
+        out[1] = rows_d[s * cap : (s + 1) * cap]
+
+
+def douts_kernel(below, above, far, *outs):
     cap = outs[0].shape[1]
-    n_tok = own.shape[0] - EXTRA
-    for z, raw in enumerate((own[...], below[...], above[...], far[...])):
+    n_tok = below.shape[0] - EXTRA
+    for z, raw in enumerate((below[...], above[...], far[...])):
         side = raw[n_tok : n_tok + 4, 0:n_tok].astype(F32)
         spots = lax.broadcasted_iota(jnp.int32, (len(outs) * cap, n_tok), 0)
         place = side[0:2].astype(jnp.int32)
@@ -214,10 +219,9 @@
 
 
 def join_kernel(*refs):
-    at = 0
-    for ref in refs[:-1]:
-        refs[-1][at : at + ref.shape[0]] = ref[...]
-        at += ref.shape[0]
+    cap = refs[0].shape[1]
+    for k, ref in enumerate(refs[:-1]):
+        refs[-1][k * cap : (k + 1) * cap] = ref[0]
 
 
 def stack_kernel(*refs):
@@ -364,7 +368,7 @@
             shape(tok_rows + EXTRA, width),
             shape(2, tok_rows, jnp.int32),
         ]
-        + [shape(cap, width)] * n_expert,
+        + [jax.ShapeDtypeStruct((2, cap, width), BF)] * n_expert,
         [routes.T, slots.T, combine.T, tokens, grads_out, w_in, b_in, w_out],
     )
     raw_below = shift(raw, "z", 1)
@@ -375,15 +379,16 @@
     w_above = shift(mine, "y", -1)
     raw_below, raw_above, x_1, x_2, x_3 = barrier((raw_below, raw_above, x_1, x_sent[2], x_3))
     raw_far = shift(raw_below, "z", 1)
-    x_own = [x_sent[0], x_1, x_3, shift(x_2, "x", 2)]
-    x_own = call(join_kernel, "join", [shape(n_expert * cap, width)], x_own)[0]
+    x_2 = shift(x_2, "x", 2)
+    x_got = [x_sent[0], x_1, x_3, x_2]
+    x_own = call(join_kernel, "join", [shape(n_expert * cap, width)], x_got)[0]
     x_own, raw_far, w_below, w_above = barrier((x_own, raw_far, w_below, w_above))
 
     d_sent = call(
         douts_kernel,
         "douts",
-        [jax.ShapeDtypeStruct((4, cap, width), BF)] * n_expert,
-        [raw, raw_below, raw_above, raw_far],
+        [jax.ShapeDtypeStruct((3, cap, width), BF)] * n_expert,
+        [raw_below, raw_above, raw_far],
     )
     x_below = shift(x_own, "z", 1)
     x_above = shift(x_own, "z", -1)
@@ -406,7 +411,7 @@
     sides = (x_own, x_below, x_above)
     early = rows_set(
         [(a, 0, cut) for a in sides],
-        [(a, z) for z in range(3) for a in (d_sent[0], d_1, d_3)],
+        [(a, 1) for a in x_got[:3]] + [(a, z) for z in range(2) for a in (d_sent[0], d_1, d_3)],
         [(cut, True), (cut, False), (cut, False)],
         w,
         b_out,
@@ -424,7 +429,7 @@
     d_2, x_far_a, x_far_b, acc = barrier((d_2, x_far_a, x_far_b, acc))
     late = rows_set(
         [(a, cut, cap) for a in sides] + [x_far_a, x_far_b],
-        [(d_2, z) for z in range(3)] + [(a, 3) for a in (d_sent[0], d_1, d_3, d_2)],
+        [(x_2, 1), (d_2, 0), (d_2, 1)] + [(a, 2) for a in (d_sent[0], d_1, d_3, d_2)],
         [(cap, True), (cap, False), (cap, False), (n_expert * cap, False)],
         w,
         b_out,

time: 107 us -> 105 us (0.981)
  starting transfers between devices: 41.3 us -> 39.4 us
  waiting for transfers between devices: 28.1 us -> 29.8 us
  blocking collectives: 14.9 us -> 13.8 us
    ppermute x26, starting transfers between devices: 41.3 us -> 39.4 us  [shift(): return lax.ppermute(value, axis, [(i, (i + step) % n) for i in range(n)])]
    ppermute x26, waiting for transfers between devices: 28.1 us -> 29.8 us  [shift(): return lax.ppermute(value, axis, [(i, (i + step) % n) for i in range(n)])]
  transfers between devices with their start and end apart: 26 -> 26, of which waited for: 10 -> 9; matrix products, arithmetic and copies ran while one was open for 0% -> 0% of each run, Pallas kernels for 15% -> 15%
where the time goes in v5:
time: 105 us
  starting transfers between devices  39.4 us (38%)
  waiting for transfers between devices  29.8 us (28%)
  Pallas kernels  20.3 us (19%)
  blocking collectives  13.8 us (13%)
    ppermute x26, starting transfers between devices, shift(): return lax.ppermute(value, axis, [(i, (i + step) % n) for i in range(n)])  39.4 us
    ppermute x26, waiting for transfers between devices, shift(): return lax.ppermute(value, axis, [(i, (i + step) % n) for i in range(n)])  29.8 us
    pallas_call x12, Pallas kernels, call(): pl.pallas_call(kernel, out_shape=out_shape, grid=(1,), in_specs=[(full, l...  17.3 us
    all_to_all x1, blocking collectives, on_device(): final = lax.all_to_all(pieces, 'x', 0, 0, tiled=True)  13.8 us
    pallas_call x1, Pallas kernels, call_loading(): pl.pallas_call(body, out_shape=out_shape, in_specs=[pl.BlockSpec(memory_s...  2.97 us
  transfers between devices with their start and end apart: 26, of which 9 were waited for; matrix products, arithmetic and copies ran while one was open for 0% of the time, Pallas kernels for 15%

profile of v5, /device:TPU:0, one launch (start us, length us, event | category | flops | bytes accessed | tf_op | source)
XLA Modules:
  0.0 105.1 jit_solution(14938760428005762161)
XLA Ops:
  0.6 3.0 %prepare.1 = (bf16[272,1024]{1,0:T(8,128)(2,1)}, bf16[144,1024]{1,0:T(8,128)(2,1)}, s32[2,128]{1,0:T(2,128)}, bf16[2,64,1024]{2,1,0:T(8,128)(2,1)}, bf16[2,64,10...) custom-call(s32[2,128]{1,0:T(2,128)} %bitcast.6, s32[2,128]{1,0:T(2,128)} %bitcast.7, ...), custom_call_target="tpu_custom_call" | custom-call | tf_op jit(solution)/shard_map/prepare/pallas_call | solution.py:76
  3.6 1.6 %collective-permute-start.2 = (bf16[2,64,1024]{2,1,0:T(8,128)(2,1)}, bf16[2,64,1024]{2,1,0:T(8,128)(2,1)S(1)}, u32[]{:S(2)}, u32[]{:S(2)}) collective-permute-start(bf16[2,64,1024]{2,1,0:T(8,128)(2,1)} %get-tuple-element.67), channel_id=1, source_target_pairs={{0,32},{32,64},{64,96},{96,0},{1,33},{33,65},{65,97},{97,1},{2,34}... | collective-permute-start | bytes 786440 | tf_op jit(solution)/shard_map/ppermute | solution.py:24
  5.3 4.0 %collective-permute-start.1 = (bf16[144,1024]{1,0:T(8,128)(2,1)}, bf16[144,1024]{1,0:T(8,128)(2,1)S(1)}, u32[]{:S(2)}, u32[]{:S(2)}) collective-permute-start(bf16[144,1024]{1,0:T(8,128)(2,1)} %get-tuple-element.66), channel_id=1, source_target_pairs={{0,24},{8,0},{16,8},{24,16},{1,25},{9,1},{17,9},{25,17},{2,26},{10... | collective-permute-start | bytes 884744 | tf_op jit(solution)/shard_map/ppermute | solution.py:24
  9.3 0.0 collective-permute-start
  9.3 1.7 %collective-permute-start.3 = (bf16[2,64,1024]{2,1,0:T(8,128)(2,1)}, bf16[2,64,1024]{2,1,0:T(8,128)(2,1)S(1)}, u32[]{:S(2)}, u32[]{:S(2)}) collective-permute-start(bf16[2,64,1024]{2,1,0:T(8,128)(2,1)} %get-tuple-element.69), channel_id=1, source_target_pairs={{0,96},{32,0},{64,32},{96,64},{1,97},{33,1},{65,33},{97,65},{2,98}... | collective-permute-start | bytes 786440 | tf_op jit(solution)/shard_map/ppermute | solution.py:24
  11.1 3.0 %collective-permute-start.7 = (bf16[272,1024]{1,0:T(8,128)(2,1)}, bf16[272,1024]{1,0:T(8,128)(2,1)S(1)}, u32[]{:S(2)}, u32[]{:S(2)}) collective-permute-start(bf16[272,1024]{1,0:T(8,128)(2,1)} %get-tuple-element.74.refs_0_.refs_12_), channel_id=1, source_target_pairs={{0,6},{2,0},{4,2},{6,4},{1,7},{3,1},{5,3},{7,5},{8,14},{10,8},{12,... | collective-permute-start | bytes 1671176 | tf_op jit(solution)/shard_map/ppermute | solution.py:24
  14.1 0.0 collective-permute-done.2.refs_1_.refs_4_
  14.1 0.7 collective-permute-start.6
  14.8 2.2 %collective-permute-done.3.refs_2_.refs_5_ = bf16[2,64,1024]{2,1,0:T(8,128)(2,1)S(1)} collective-permute-done((bf16[2,64,1024]{2,1,0:T(8,128)(2,1)}, bf16[2,64,1024]{2,1,0:T(8,128)(2,1)S(1)}, u32[]{:S(2)}, u32[]{:S(2)}) %collective-permute-start.3) | collective-permute-done | bytes 262176 | tf_op jit(solution)/shard_map/ppermute | solution.py:24
  17.0 0.0 collective-permute-done.1.above
  17.0 1.9 %collective-permute-done.below = bf16[144,1024]{1,0:T(8,128)(2,1)S(1)} collective-permute-done((bf16[144,1024]{1,0:T(8,128)(2,1)}, bf16[144,1024]{1,0:T(8,128)(2,1)S(1)}, u32[]{:S(2)}, u32[]{:S(2)}) %collective-permute-start) | collective-permute-done | bytes 294944 | tf_op jit(solution)/shard_map/ppermute | solution.py:24
  18.9 0.0 collective-permute-start.5
  18.9 2.7 %collective-permute-start.4 = (bf16[2,64,1024]{2,1,0:T(8,128)(2,1)}, bf16[2,64,1024]{2,1,0:T(8,128)(2,1)S(1)}, u32[]{:S(2)}, u32[]{:S(2)}) collective-permute-start(bf16[2,64,1024]{2,1,0:T(8,128)(2,1)} %get-tuple-element.72), channel_id=1, source_target_pairs={{0,64},{32,96},{64,0},{96,32},{1,65},{33,97},{65,1},{97,33},{2,66}... | collective-permute-start | bytes 786440 | tf_op jit(solution)/shard_map/ppermute | solution.py:24
  21.7 5.5 %collective-permute-done.4.refs_3_.refs_5_ = bf16[2,64,1024]{2,1,0:T(8,128)(2,1)S(1)} collective-permute-done((bf16[2,64,1024]{2,1,0:T(8,128)(2,1)}, bf16[2,64,1024]{2,1,0:T(8,128)(2,1)S(1)}, u32[]{:S(2)}, u32[]{:S(2)}) %collective-permute-start.4) | collective-permute-done | bytes 262176 | tf_op jit(solution)/shard_map/ppermute | solution.py:24
  27.2 0.9 copy-done.1
  28.2 0.0 collective-permute-done.7.refs_2_.refs_14_
  28.2 0.5 collective-permute-done.6.refs_1_.refs_13_
  28.7 0.0 collective-permute-done.5.far
  28.7 1.1 %collective-permute-start.10 = (bf16[272,1024]{1,0:T(8,128)(2,1)S(1)}, bf16[272,1024]{1,0:T(8,128)(2,1)S(1)}, u32[]{:S(2)}, u32[]{:S(2)}) collective-permute-start(bf16[272,1024]{1,0:T(8,128)(2,1)S(1)} %collective-permute-done.6.refs_1_.refs_13_), channel_id=1, source_target_pairs={{0,2},{2,4},{4,6},{6,0},{1,3},{3,5},{5,7},{7,1},{8,10},{10,12},{12... | collective-permute-start | bytes 1671176 | tf_op jit(solution)/shard_map/ppermute | solution.py:24
  29.9 3.0 %collective-permute-start.9 = (bf16[256,1024]{1,0:T(8,128)(2,1)S(1)}, bf16[256,1024]{1,0:T(8,128)(2,1)S(1)}, u32[]{:S(2)}, u32[]{:S(2)}) collective-permute-start(bf16[256,1024]{1,0:T(8,128)(2,1)S(1)} %join.1.refs_0_), channel_id=1, source_target_pairs={{0,24},{8,0},{16,8},{24,16},{1,25},{9,1},{17,9},{25,17},{2,26},{10... | collective-permute-start | bytes 1572872 | tf_op jit(solution)/shard_map/ppermute | solution.py:24
  32.9 0.0 collective-permute-start.8
  32.9 0.5 douts.1
  33.5 1.6 %collective-permute-start.11 = (bf16[3,64,1024]{2,1,0:T(8,128)(2,1)S(1)}, bf16[3,64,1024]{2,1,0:T(8,128)(2,1)S(1)}, u32[]{:S(2)}, u32[]{:S(2)}) collective-permute-start(bf16[3,64,1024]{2,1,0:T(8,128)(2,1)S(1)} %get-tuple-element.79), channel_id=1, source_target_pairs={{0,32},{32,64},{64,96},{96,0},{1,33},{33,65},{65,97},{97,1},{2,34}... | collective-permute-start | bytes 1179656 | tf_op jit(solution)/shard_map/ppermute | solution.py:24
  35.0 1.7 %collective-permute-start.12 = (bf16[3,64,1024]{2,1,0:T(8,128)(2,1)S(1)}, bf16[3,64,1024]{2,1,0:T(8,128)(2,1)S(1)}, u32[]{:S(2)}, u32[]{:S(2)}) collective-permute-start(bf16[3,64,1024]{2,1,0:T(8,128)(2,1)S(1)} %get-tuple-element.80), channel_id=1, source_target_pairs={{0,96},{32,0},{64,32},{96,64},{1,97},{33,1},{65,33},{97,65},{2,98}... | collective-permute-start | bytes 1179656 | tf_op jit(solution)/shard_map/ppermute | solution.py:24
  36.8 6.2 %collective-permute-done.11.refs_7_.refs_10_.refs_9_ = bf16[3,64,1024]{2,1,0:T(8,128)(2,1)S(1)} collective-permute-done((bf16[3,64,1024]{2,1,0:T(8,128)(2,1)S(1)}, bf16[3,64,1024]{2,1,0:T(8,128)(2,1)S(1)}, u32[]{:S(2)}, u32[]{:S(2)}) %collective-permute-start.11) | collective-permute-done | bytes 393248 | tf_op jit(solution)/shard_map/ppermute | solution.py:24
  42.9 0.0 collective-permute-done.12.refs_8_.refs_11_.refs_10_
  42.9 0.0 collective-permute-done.9.refs_2_
  42.9 2.2 %collective-permute-done.8.refs_1_ = bf16[256,1024]{1,0:T(8,128)(2,1)S(1)} collective-permute-done((bf16[256,1024]{1,0:T(8,128)(2,1)S(1)}, bf16[256,1024]{1,0:T(8,128)(2,1)S(1)}, u32[]{:S(2)}, u32[]{:S(2)}) %collective-permute-start.8) | collective-permute-done | bytes 524320 | tf_op jit(solution)/shard_map/ppermute | solution.py:24
  45.1 0.0 collective-permute-done.10.refs_3_.refs_15_
  45.1 0.0 copy-start.5
  45.1 0.1 stack.1
  45.3 0.1 collective-permute-start.13
  45.4 1.0 collective-permute-start.16
  46.5 1.1 %collective-permute-start.15 = (bf16[128,1024]{1,0:T(8,128)(2,1)S(1)}, bf16[128,1024]{1,0:T(8,128)(2,1)S(1)}, u32[]{:S(2)}, u32[]{:S(2)}) collective-permute-start(bf16[128,1024]{1,0:T(8,128)(2,1)S(1)} %slice.6), channel_id=1, source_target_pairs={{0,8},{8,16},{16,24},{24,0},{1,9},{9,17},{17,25},{25,1},{2,10},{10... | collective-permute-start | bytes 786440 | tf_op jit(solution)/shard_map/ppermute | solution.py:24
  47.5 1.9 %collective-permute-start.14 = (bf16[3,64,1024]{2,1,0:T(8,128)(2,1)S(1)}, bf16[3,64,1024]{2,1,0:T(8,128)(2,1)S(1)}, u32[]{:S(2)}, u32[]{:S(2)}) collective-permute-start(bf16[3,64,1024]{2,1,0:T(8,128)(2,1)S(1)} %get-tuple-element.90), channel_id=1, source_target_pairs={{0,64},{32,96},{64,0},{96,32},{1,65},{33,97},{65,1},{97,33},{2,66}... | collective-permute-start | bytes 1179656 | tf_op jit(solution)/shard_map/ppermute | solution.py:24
  49.5 0.2 collective-permute-done.13.refs_16_
  49.7 4.2 %rows.2 = (bf16[576,1024]{1,0:T(8,128)(2,1)S(1)}, bf16[576,1024]{1,0:T(8,128)(2,1)S(1)}, bf16[2,576,512]{2,1,0:T(8,128)(2,1)S(1)}, bf16[2,576,512]{2,1,0:T(8,128...) custom-call(bf16[256,1024]{1,0:T(8,128)(2,1)S(1)} %join.1.refs_0_, ...), custom_call_target="tpu_custom_call" | custom-call | flops 3623878656 | bytes 15599616 | tf_op jit(solution)/shard_map/rows/pallas_call | solution.py:47
  53.9 0.1 collective-permute-start.17
  54.0 3.2 %collective-permute-start.18 = (bf16[208,1024]{1,0:T(8,128)(2,1)S(1)}, bf16[208,1024]{1,0:T(8,128)(2,1)S(1)}, u32[]{:S(2)}, u32[]{:S(2)}) collective-permute-start(bf16[208,1024]{1,0:T(8,128)(2,1)S(1)} %get-tuple-element.104), channel_id=1, source_target_pairs={{0,24},{8,0},{16,8},{24,16},{1,25},{9,1},{17,9},{25,17},{2,26},{10... | collective-permute-start | bytes 1277960 | tf_op jit(solution)/shard_map/ppermute | solution.py:24
  57.2 3.5 %sums.1.near = f32[2,1040,1024]{2,1,0:T(8,128)S(1)} custom-call(bf16[576,1024]{1,0:T(8,128)(2,1)S(1)} %get-tuple-element.91.x, bf16[576,1024]{1,0:T(8,128)(2,1)S(1)} %get-tuple-element.92.d, bf16[2,576,512]{2,1,0:T(8,128)(2,1)S(1)} %get-tuple-element.93.dpre, bf16[2,576,512]{2,1,0:T(8,128)(2,1)S(1)} %get-tuple-element.94.hidden), custom_call_target="tpu_custom_call" | custom-call | flops 2415919104 | bytes 13238272 | tf_op jit(solution)/shard_map/sums/pallas_call | solution.py:47
  60.7 0.0 collective-permute-done.16.refs_4_
  60.7 0.0 collective-permute-done.15.refs_3_
  60.7 3.3 %rows.3 = (bf16[448,1024]{1,0:T(8,128)(2,1)S(1)}, bf16[448,1024]{1,0:T(8,128)(2,1)S(1)}, bf16[2,448,512]{2,1,0:T(8,128)(2,1)S(1)}, bf16[2,448,512]{2,1,0:T(8,128...) custom-call(bf16[256,1024]{1,0:T(8,128)(2,1)S(1)} %join.1.refs_0_, ...), custom_call_target="tpu_custom_call" | custom-call | flops 2818572288 | bytes 14059520 | tf_op jit(solution)/shard_map/rows/pallas_call | solution.py:47
  64.1 1.3 %away.1 = bf16[1040,1024]{1,0:T(8,128)(2,1)S(1)} custom-call(f32[2,1040,1024]{2,1,0:T(8,128)S(1)} %sums.1.near, bf16[448,1024]{1,0:T(8,128)(2,1)S(1)} %get-tuple-element.99.x, bf16[448,1024]{1,0:T(8,128)(2,1)S(1)} %get-tuple-element.100.d, bf16[2,448,512]{2,1,0:T(8,128)(2,1)S(1)} %get-tuple-element.101.dpre, bf16[2,448,512]{2,1,0:T(8,128)(2,1)S(1)} %get-tuple-element.102.hidden), custom_call_target="tpu_custom_call" | custom-call | flops 939524096 | bytes 14319616 | tf_op jit(solution)/shard_map/away/pallas_call | solution.py:47
  65.4 1.7 %collective-permute-done.17.refs_1_ = bf16[208,1024]{1,0:T(8,128)(2,1)S(1)} collective-permute-done((bf16[208,1024]{1,0:T(8,128)(2,1)S(1)}, bf16[208,1024]{1,0:T(8,128)(2,1)S(1)}, u32[]{:S(2)}, u32[]{:S(2)}) %collective-permute-start.17) | collective-permute-done | bytes 426016 | tf_op jit(solution)/shard_map/ppermute | solution.py:24
  67.1 1.5 %collective-permute-start.21 = (bf16[272,1024]{1,0:T(8,128)(2,1)S(1)}, bf16[272,1024]{1,0:T(8,128)(2,1)S(1)}, u32[]{:S(2)}, u32[]{:S(2)}) collective-permute-start(bf16[272,1024]{1,0:T(8,128)(2,1)S(1)} %get-tuple-element.110), channel_id=1, source_target_pairs={{0,16},{8,24},{16,0},{24,8},{1,17},{9,25},{17,1},{25,9},{2,18},{10... | collective-permute-start | bytes 1671176 | tf_op jit(solution)/shard_map/ppermute | solution.py:24
  68.5 2.3 %collective-permute-start.19 = (bf16[80,1024]{1,0:T(8,128)(2,1)S(1)}, bf16[80,1024]{1,0:T(8,128)(2,1)S(1)}, u32[]{:S(2)}, u32[]{:S(2)}) collective-permute-start(bf16[80,1024]{1,0:T(8,128)(2,1)S(1)} %get-tuple-element.108), channel_id=1, source_target_pairs={{0,8},{8,16},{16,24},{24,0},{1,9},{9,17},{17,25},{25,1},{2,10},{10... | collective-permute-start | bytes 491528 | tf_op jit(solution)/shard_map/ppermute | solution.py:24
  70.9 0.9 collective-permute-start.20
  71.8 1.3 %home.1.own = f32[1040,1024]{1,0:T(8,128)S(1)} custom-call(f32[2,1040,1024]{2,1,0:T(8,128)S(1)} %sums.1.near, bf16[448,1024]{1,0:T(8,128)(2,1)S(1)} %get-tuple-element.99.x, bf16[448,1024]{1,0:T(8,128)(2,1)S(1)} %get-tuple-element.100.d, bf16[2,448,512]{2,1,0:T(8,128)(2,1)S(1)} %get-tuple-element.101.dpre, bf16[2,448,512]{2,1,0:T(8,128)(2,1)S(1)} %get-tuple-element.102.hidden), custom_call_target="tpu_custom_call" | custom-call | flops 939524096 | bytes 16449536 | tf_op jit(solution)/shard_map/home/pallas_call | solution.py:47
  73.1 0.0 collective-permute-done.22.got
  73.1 0.4 merge.1
  73.5 3.0 %collective-permute-start.23 = (bf16[272,1024]{1,0:T(8,128)(2,1)S(1)}, bf16[272,1024]{1,0:T(8,128)(2,1)S(1)}, u32[]{:S(2)}, u32[]{:S(2)}) collective-permute-start(bf16[272,1024]{1,0:T(8,128)(2,1)S(1)} %get-tuple-element.115), channel_id=1, source_target_pairs={{0,4},{2,6},{4,0},{6,2},{1,5},{3,7},{5,1},{7,3},{8,12},{10,14},{12... | collective-permute-start | bytes 1671176 | tf_op jit(solution)/shard_map/ppermute | solution.py:24
  76.4 1.3 %collective-permute-start.24 = (bf16[272,1024]{1,0:T(8,128)(2,1)S(1)}, bf16[272,1024]{1,0:T(8,128)(2,1)S(1)}, u32[]{:S(2)}, u32[]{:S(2)}) collective-permute-start(bf16[272,1024]{1,0:T(8,128)(2,1)S(1)} %get-tuple-element.116), channel_id=1, source_target_pairs={{0,6},{2,0},{4,2},{6,4},{1,7},{3,1},{5,3},{7,5},{8,14},{10,8},{12,... | collective-permute-start | bytes 1671176 | tf_op jit(solution)/shard_map/ppermute | solution.py:24
  77.8 9.3 %collective-permute-done.19.refs_4_ = bf16[80,1024]{1,0:T(8,128)(2,1)S(1)} collective-permute-done((bf16[80,1024]{1,0:T(8,128)(2,1)S(1)}, bf16[80,1024]{1,0:T(8,128)(2,1)S(1)}, u32[]{:S(2)}, u32[]{:S(2)}) %collective-permute-start.19) | collective-permute-done | bytes 163872 | tf_op jit(solution)/shard_map/ppermute | solution.py:24
  87.1 1.6 %collective-permute-start.25 = (bf16[272,1024]{1,0:T(8,128)(2,1)S(1)}, bf16[272,1024]{1,0:T(8,128)(2,1)S(1)}, u32[]{:S(2)}, u32[]{:S(2)}) collective-permute-start(bf16[272,1024]{1,0:T(8,128)(2,1)S(1)} %get-tuple-element.117), channel_id=1, source_target_pairs={{0,2},{2,4},{4,6},{6,0},{1,3},{3,5},{5,7},{7,1},{8,10},{10,12},{12... | collective-permute-start | bytes 1671176 | tf_op jit(solution)/shard_map/ppermute | solution.py:24
  88.7 0.0 collective-permute-done.20.refs_5_
  88.7 0.0 copy-start.4
  88.7 0.3 sum_z.1
  89.1 13.8 %all_to_all.5.pieces = bf16[4,80,1024]{2,1,0:T(8,128)(2,1)S(1)} all-to-all(bf16[4,80,1024]{2,1,0:T(8,128)(2,1)S(1)} %sum_z.1), channel_id=1, replica_groups=mesh['x'=4,'z'=4,'y'=4,'c'=2] {'x'}, dimensions={0} | all-to-all | bytes 1310720 | tf_op jit(solution)/shard_map/all_to_all | solution.py:465
  102.9 1.2 %finish.1 = (bf16[128,1024]{1,0:T(8,128)(2,1)}, f32[2,128]{1,0:T(2,128)}) custom-call(s32[2,128]{1,0:T(2,128)S(1)} %copy-done.4, bf16[2,128]{1,0:T(2,128)(2,1)S(1)} %bitcast.5, bf16[4,80,1024]{2,1,0:T(8,128)(2,1)S(1)} %all_to_all.5.pieces), custom_call_target="tpu_custom_call" | custom-call | bytes 920064 | tf_op jit(solution)/shard_map/finish/pallas_call | solution.py:47
  104.1 0.0 collective-permute-done.23.a
  104.1 0.0 collective-permute-done.24.b
  104.1 0.0 collective-permute-done.25.c
  104.1 1.0 last.1
  (16 shorter events, 0.1 us)
Async XLA Ops:
  3.6 41.5 %copy-start = (bf16[272,1024]{1,0:T(8,128)(2,1)S(1)}, bf16[272,1024]{1,0:T(8,128)(2,1)}, u32[]{:S(2)}) copy-start(bf16[272,1024]{1,0:T(8,128)(2,1)} %get-tuple-element.74.refs_0_.refs_12_) | copy-start | bytes 1671172
  3.6 10.4 %collective-permute-start.2 = (bf16[2,64,1024]{2,1,0:T(8,128)(2,1)}, bf16[2,64,1024]{2,1,0:T(8,128)(2,1)S(1)}, u32[]{:S(2)}, u32[]{:S(2)}) collective-permute-start(bf16[2,64,1024]{2,1,0:T(8,128)(2,1)} %get-tuple-element.67), channel_id=1, source_target_pairs={{0,32},{32,64},{64,96},{96,0},{1,33},{33,65},{65,97},{97,1},{2,34}... | collective-permute-start | bytes 786440 | tf_op jit(solution)/shard_map/ppermute | solution.py:24
  5.3 11.7 %collective-permute-start.1 = (bf16[144,1024]{1,0:T(8,128)(2,1)}, bf16[144,1024]{1,0:T(8,128)(2,1)S(1)}, u32[]{:S(2)}, u32[]{:S(2)}) collective-permute-start(bf16[144,1024]{1,0:T(8,128)(2,1)} %get-tuple-element.66), channel_id=1, source_target_pairs={{0,24},{8,0},{16,8},{24,16},{1,25},{9,1},{17,9},{25,17},{2,26},{10... | collective-permute-start | bytes 884744 | tf_op jit(solution)/shard_map/ppermute | solution.py:24
  9.3 9.6 %collective-permute-start = (bf16[144,1024]{1,0:T(8,128)(2,1)}, bf16[144,1024]{1,0:T(8,128)(2,1)S(1)}, u32[]{:S(2)}, u32[]{:S(2)}) collective-permute-start(bf16[144,1024]{1,0:T(8,128)(2,1)} %get-tuple-element.66), channel_id=1, source_target_pairs={{0,8},{8,16},{16,24},{24,0},{1,9},{9,17},{17,25},{25,1},{2,10},{10... | collective-permute-start | bytes 884744 | tf_op jit(solution)/shard_map/ppermute | solution.py:24
  9.3 7.7 %collective-permute-start.3 = (bf16[2,64,1024]{2,1,0:T(8,128)(2,1)}, bf16[2,64,1024]{2,1,0:T(8,128)(2,1)S(1)}, u32[]{:S(2)}, u32[]{:S(2)}) collective-permute-start(bf16[2,64,1024]{2,1,0:T(8,128)(2,1)} %get-tuple-element.69), channel_id=1, source_target_pairs={{0,96},{32,0},{64,32},{96,64},{1,97},{33,1},{65,33},{97,65},{2,98}... | collective-permute-start | bytes 786440 | tf_op jit(solution)/shard_map/ppermute | solution.py:24
  11.1 17.1 %collective-permute-start.7 = (bf16[272,1024]{1,0:T(8,128)(2,1)}, bf16[272,1024]{1,0:T(8,128)(2,1)S(1)}, u32[]{:S(2)}, u32[]{:S(2)}) collective-permute-start(bf16[272,1024]{1,0:T(8,128)(2,1)} %get-tuple-element.74.refs_0_.refs_12_), channel_id=1, source_target_pairs={{0,6},{2,0},{4,2},{6,4},{1,7},{3,1},{5,3},{7,5},{8,14},{10,8},{12,... | collective-permute-start | bytes 1671176 | tf_op jit(solution)/shard_map/ppermute | solution.py:24
  14.1 14.7 %collective-permute-start.6 = (bf16[272,1024]{1,0:T(8,128)(2,1)}, bf16[272,1024]{1,0:T(8,128)(2,1)S(1)}, u32[]{:S(2)}, u32[]{:S(2)}) collective-permute-start(bf16[272,1024]{1,0:T(8,128)(2,1)} %get-tuple-element.74.refs_0_.refs_12_), channel_id=1, source_target_pairs={{0,2},{2,4},{4,6},{6,0},{1,3},{3,5},{5,7},{7,1},{8,10},{10,12},{12... | collective-permute-start | bytes 1671176 | tf_op jit(solution)/shard_map/ppermute | solution.py:24
  18.9 9.8 %collective-permute-start.5 = (bf16[144,1024]{1,0:T(8,128)(2,1)S(1)}, bf16[144,1024]{1,0:T(8,128)(2,1)S(1)}, u32[]{:S(2)}, u32[]{:S(2)}) collective-permute-start(bf16[144,1024]{1,0:T(8,128)(2,1)S(1)} %collective-permute-done.below), channel_id=1, source_target_pairs={{0,8},{8,16},{16,24},{24,0},{1,9},{9,17},{17,25},{25,1},{2,10},{10... | collective-permute-start | bytes 884744 | tf_op jit(solution)/shard_map/ppermute | solution.py:24
  18.9 8.3 %collective-permute-start.4 = (bf16[2,64,1024]{2,1,0:T(8,128)(2,1)}, bf16[2,64,1024]{2,1,0:T(8,128)(2,1)S(1)}, u32[]{:S(2)}, u32[]{:S(2)}) collective-permute-start(bf16[2,64,1024]{2,1,0:T(8,128)(2,1)} %get-tuple-element.72), channel_id=1, source_target_pairs={{0,64},{32,96},{64,0},{96,32},{1,65},{33,97},{65,1},{97,33},{2,66}... | collective-permute-start | bytes 786440 | tf_op jit(solution)/shard_map/ppermute | solution.py:24
  27.2 1.0 copy-start.1
  28.7 16.4 %collective-permute-start.10 = (bf16[272,1024]{1,0:T(8,128)(2,1)S(1)}, bf16[272,1024]{1,0:T(8,128)(2,1)S(1)}, u32[]{:S(2)}, u32[]{:S(2)}) collective-permute-start(bf16[272,1024]{1,0:T(8,128)(2,1)S(1)} %collective-permute-done.6.refs_1_.refs_13_), channel_id=1, source_target_pairs={{0,2},{2,4},{4,6},{6,0},{1,3},{3,5},{5,7},{7,1},{8,10},{10,12},{12... | collective-permute-start | bytes 1671176 | tf_op jit(solution)/shard_map/ppermute | solution.py:24
  29.9 13.1 %collective-permute-start.9 = (bf16[256,1024]{1,0:T(8,128)(2,1)S(1)}, bf16[256,1024]{1,0:T(8,128)(2,1)S(1)}, u32[]{:S(2)}, u32[]{:S(2)}) collective-permute-start(bf16[256,1024]{1,0:T(8,128)(2,1)S(1)} %join.1.refs_0_), channel_id=1, source_target_pairs={{0,24},{8,0},{16,8},{24,16},{1,25},{9,1},{17,9},{25,17},{2,26},{10... | collective-permute-start | bytes 1572872 | tf_op jit(solution)/shard_map/ppermute | solution.py:24
  32.9 12.2 %collective-permute-start.8 = (bf16[256,1024]{1,0:T(8,128)(2,1)S(1)}, bf16[256,1024]{1,0:T(8,128)(2,1)S(1)}, u32[]{:S(2)}, u32[]{:S(2)}) collective-permute-start(bf16[256,1024]{1,0:T(8,128)(2,1)S(1)} %join.1.refs_0_), channel_id=1, source_target_pairs={{0,8},{8,16},{16,24},{24,0},{1,9},{9,17},{17,25},{25,1},{2,10},{10... | collective-permute-start | bytes 1572872 | tf_op jit(solution)/shard_map/ppermute | solution.py:24
  33.5 9.5 %collective-permute-start.11 = (bf16[3,64,1024]{2,1,0:T(8,128)(2,1)S(1)}, bf16[3,64,1024]{2,1,0:T(8,128)(2,1)S(1)}, u32[]{:S(2)}, u32[]{:S(2)}) collective-permute-start(bf16[3,64,1024]{2,1,0:T(8,128)(2,1)S(1)} %get-tuple-element.79), channel_id=1, source_target_pairs={{0,32},{32,64},{64,96},{96,0},{1,33},{33,65},{65,97},{97,1},{2,34}... | collective-permute-start | bytes 1179656 | tf_op jit(solution)/shard_map/ppermute | solution.py:24
  35.0 7.9 %collective-permute-start.12 = (bf16[3,64,1024]{2,1,0:T(8,128)(2,1)S(1)}, bf16[3,64,1024]{2,1,0:T(8,128)(2,1)S(1)}, u32[]{:S(2)}, u32[]{:S(2)}) collective-permute-start(bf16[3,64,1024]{2,1,0:T(8,128)(2,1)S(1)} %get-tuple-element.80), channel_id=1, source_target_pairs={{0,96},{32,0},{64,32},{96,64},{1,97},{33,1},{65,33},{97,65},{2,98}... | collective-permute-start | bytes 1179656 | tf_op jit(solution)/shard_map/ppermute | solution.py:24
  45.1 4.6 %copy-start.2 = (bf16[2,64,1024]{2,1,0:T(8,128)(2,1)S(1)}, bf16[2,64,1024]{2,1,0:T(8,128)(2,1)}, u32[]{:S(2)}) copy-start(bf16[2,64,1024]{2,1,0:T(8,128)(2,1)} %get-tuple-element.65.refs_0_.refs_3_) | copy-start | bytes 786436
  45.1 4.6 %copy-start.5 = (bf16[1,1024]{1,0:T(2,128)(2,1)S(1)}, bf16[1,1024]{1,0:T(2,128)(2,1)}, u32[]{:S(2)}) copy-start(bf16[1,1024]{1,0:T(2,128)(2,1)} %refs_17_.3) | copy-start | bytes 6148
  45.3 4.4 %collective-permute-start.13 = (bf16[4,272,1024]{2,1,0:T(8,128)(2,1)S(1)}, bf16[4,272,1024]{2,1,0:T(8,128)(2,1)S(1)}, u32[]{:S(2)}, u32[]{:S(2)}) collective-permute-start(bf16[4,272,1024]{2,1,0:T(8,128)(2,1)S(1)} %stack.1), channel_id=1, source_target_pairs={{0,1},{1,0},{2,3},{3,2},{4,5},{5,4},{6,7},{7,6},{8,9},{9,8},{10,11... | collective-permute-start | bytes 6684680 | tf_op jit(solution)/shard_map/ppermute | solution.py:24
  45.4 15.3 %collective-permute-start.16 = (bf16[128,1024]{1,0:T(8,128)(2,1)S(1)}, bf16[128,1024]{1,0:T(8,128)(2,1)S(1)}, u32[]{:S(2)}, u32[]{:S(2)}) collective-permute-start(bf16[128,1024]{1,0:T(8,128)(2,1)S(1)} %slice.7), channel_id=1, source_target_pairs={{0,24},{8,0},{16,8},{24,16},{1,25},{9,1},{17,9},{25,17},{2,26},{10... | collective-permute-start | bytes 786440 | tf_op jit(solution)/shard_map/ppermute | solution.py:24
  46.5 14.3 %collective-permute-start.15 = (bf16[128,1024]{1,0:T(8,128)(2,1)S(1)}, bf16[128,1024]{1,0:T(8,128)(2,1)S(1)}, u32[]{:S(2)}, u32[]{:S(2)}) collective-permute-start(bf16[128,1024]{1,0:T(8,128)(2,1)S(1)} %slice.6), channel_id=1, source_target_pairs={{0,8},{8,16},{16,24},{24,0},{1,9},{9,17},{17,25},{25,1},{2,10},{10... | collective-permute-start | bytes 786440 | tf_op jit(solution)/shard_map/ppermute | solution.py:24
  47.5 13.2 %collective-permute-start.14 = (bf16[3,64,1024]{2,1,0:T(8,128)(2,1)S(1)}, bf16[3,64,1024]{2,1,0:T(8,128)(2,1)S(1)}, u32[]{:S(2)}, u32[]{:S(2)}) collective-permute-start(bf16[3,64,1024]{2,1,0:T(8,128)(2,1)S(1)} %get-tuple-element.90), channel_id=1, source_target_pairs={{0,64},{32,96},{64,0},{96,32},{1,65},{33,97},{65,1},{97,33},{2,66}... | collective-permute-start | bytes 1179656 | tf_op jit(solution)/shard_map/ppermute | solution.py:24
  53.9 13.1 %collective-permute-start.17 = (bf16[208,1024]{1,0:T(8,128)(2,1)S(1)}, bf16[208,1024]{1,0:T(8,128)(2,1)S(1)}, u32[]{:S(2)}, u32[]{:S(2)}) collective-permute-start(bf16[208,1024]{1,0:T(8,128)(2,1)S(1)} %get-tuple-element.103), channel_id=1, source_target_pairs={{0,8},{8,16},{16,24},{24,0},{1,9},{9,17},{17,25},{25,1},{2,10},{10... | collective-permute-start | bytes 1277960 | tf_op jit(solution)/shard_map/ppermute | solution.py:24
  54.0 13.1 %collective-permute-start.18 = (bf16[208,1024]{1,0:T(8,128)(2,1)S(1)}, bf16[208,1024]{1,0:T(8,128)(2,1)S(1)}, u32[]{:S(2)}, u32[]{:S(2)}) collective-permute-start(bf16[208,1024]{1,0:T(8,128)(2,1)S(1)} %get-tuple-element.104), channel_id=1, source_target_pairs={{0,24},{8,0},{16,8},{24,16},{1,25},{9,1},{17,9},{25,17},{2,26},{10... | collective-permute-start | bytes 1277960 | tf_op jit(solution)/shard_map/ppermute | solution.py:24
  67.1 6.0 %collective-permute-start.22 = (bf16[1040,1024]{1,0:T(8,128)(2,1)S(1)}, bf16[1040,1024]{1,0:T(8,128)(2,1)S(1)}, u32[]{:S(2)}, u32[]{:S(2)}) collective-permute-start(bf16[1040,1024]{1,0:T(8,128)(2,1)S(1)} %away.1), channel_id=1, source_target_pairs={{0,1},{1,0},{2,3},{3,2},{4,5},{5,4},{6,7},{7,6},{8,9},{9,8},{10,11... | collective-permute-start | bytes 6389768 | tf_op jit(solution)/shard_map/ppermute | solution.py:24
  67.1 21.6 %collective-permute-start.21 = (bf16[272,1024]{1,0:T(8,128)(2,1)S(1)}, bf16[272,1024]{1,0:T(8,128)(2,1)S(1)}, u32[]{:S(2)}, u32[]{:S(2)}) collective-permute-start(bf16[272,1024]{1,0:T(8,128)(2,1)S(1)} %get-tuple-element.110), channel_id=1, source_target_pairs={{0,16},{8,24},{16,0},{24,8},{1,17},{9,25},{17,1},{25,9},{2,18},{10... | collective-permute-start | bytes 1671176 | tf_op jit(solution)/shard_map/ppermute | solution.py:24
  68.5 18.6 %collective-permute-start.19 = (bf16[80,1024]{1,0:T(8,128)(2,1)S(1)}, bf16[80,1024]{1,0:T(8,128)(2,1)S(1)}, u32[]{:S(2)}, u32[]{:S(2)}) collective-permute-start(bf16[80,1024]{1,0:T(8,128)(2,1)S(1)} %get-tuple-element.108), channel_id=1, source_target_pairs={{0,8},{8,16},{16,24},{24,0},{1,9},{9,17},{17,25},{25,1},{2,10},{10... | collective-permute-start | bytes 491528 | tf_op jit(solution)/shard_map/ppermute | solution.py:24
  70.9 17.8 %collective-permute-start.20 = (bf16[80,1024]{1,0:T(8,128)(2,1)S(1)}, bf16[80,1024]{1,0:T(8,128)(2,1)S(1)}, u32[]{:S(2)}, u32[]{:S(2)}) collective-permute-start(bf16[80,1024]{1,0:T(8,128)(2,1)S(1)} %get-tuple-element.109), channel_id=1, source_target_pairs={{0,24},{8,0},{16,8},{24,16},{1,25},{9,1},{17,9},{25,17},{2,26},{10... | collective-permute-start | bytes 491528 | tf_op jit(solution)/shard_map/ppermute | solution.py:24
  73.5 30.6 %collective-permute-start.23 = (bf16[272,1024]{1,0:T(8,128)(2,1)S(1)}, bf16[272,1024]{1,0:T(8,128)(2,1)S(1)}, u32[]{:S(2)}, u32[]{:S(2)}) collective-permute-start(bf16[272,1024]{1,0:T(8,128)(2,1)S(1)} %get-tuple-element.115), channel_id=1, source_target_pairs={{0,4},{2,6},{4,0},{6,2},{1,5},{3,7},{5,1},{7,3},{8,12},{10,14},{12... | collective-permute-start | bytes 1671176 | tf_op jit(solution)/shard_map/ppermute | solution.py:24
  76.4 27.6 %collective-permute-start.24 = (bf16[272,1024]{1,0:T(8,128)(2,1)S(1)}, bf16[272,1024]{1,0:T(8,128)(2,1)S(1)}, u32[]{:S(2)}, u32[]{:S(2)}) collective-permute-start(bf16[272,1024]{1,0:T(8,128)(2,1)S(1)} %get-tuple-element.116), channel_id=1, source_target_pairs={{0,6},{2,0},{4,2},{6,4},{1,7},{3,1},{5,3},{7,5},{8,14},{10,8},{12,... | collective-permute-start | bytes 1671176 | tf_op jit(solution)/shard_map/ppermute | solution.py:24
  87.1 17.0 %collective-permute-start.25 = (bf16[272,1024]{1,0:T(8,128)(2,1)S(1)}, bf16[272,1024]{1,0:T(8,128)(2,1)S(1)}, u32[]{:S(2)}, u32[]{:S(2)}) collective-permute-start(bf16[272,1024]{1,0:T(8,128)(2,1)S(1)} %get-tuple-element.117), channel_id=1, source_target_pairs={{0,2},{2,4},{4,6},{6,0},{1,3},{3,5},{5,7},{7,1},{8,10},{10,12},{12... | collective-permute-start | bytes 1671176 | tf_op jit(solution)/shard_map/ppermute | solution.py:24
  88.7 14.2 %copy-start.3 = (bf16[128,2]{0,1:T(2,128)(2,1)S(1)}, bf16[128,2]{0,1:T(2,128)(2,1)}, u32[]{:S(2)}) copy-start(bf16[128,2]{0,1:T(2,128)(2,1)} %param.13) | copy-start | bytes 1540
  88.7 14.2 %copy-start.4 = (s32[2,128]{1,0:T(2,128)S(1)}, s32[2,128]{1,0:T(2,128)}, u32[]{:S(2)}) copy-start(s32[2,128]{1,0:T(2,128)} %get-tuple-element.64.places) | copy-start | bytes 3076

commit v6 on v5

--- a/solution.py
+++ b/solution.py
@@ -103,7 +103,7 @@
     routes, slots, combine, tokens, grads, w_in, b_in, w_out, share, raw, places, *outs
 ):
     units = w_out.shape[1]
-    share[0:units] = w_in[0].astype(F32).T.astype(BF)
+    share[0:units] = w_in[0].T
     share[units : units + EXTRA] = lines_of([b_in[...].astype(F32)], share.shape[1], BF)
     share[units + EXTRA :] = w_out[0]
     n_expert = len(outs)
@@ -218,6 +218,10 @@
     )
 
 
+def keep_kernel(ref, out):
+    out[...] = ref[...]
+
+
 def join_kernel(*refs):
     cap = refs[0].shape[1]
     for k, ref in enumerate(refs[:-1]):
@@ -377,10 +381,13 @@
     x_3 = shift(x_sent[3], "x", -1)
     w_below = shift(mine, "y", 1)
     w_above = shift(mine, "y", -1)
-    raw_below, raw_above, x_1, x_2, x_3 = barrier((raw_below, raw_above, x_1, x_sent[2], x_3))
+    x_0 = call(keep_kernel, "keep", [jax.ShapeDtypeStruct((2, cap, width), BF)], [x_sent[0]])[0]
+    raw_below, raw_above, x_0, x_1, x_2, x_3 = barrier(
+        (raw_below, raw_above, x_0, x_1, x_sent[2], x_3)
+    )
     raw_far = shift(raw_below, "z", 1)
     x_2 = shift(x_2, "x", 2)
-    x_got = [x_sent[0], x_1, x_3, x_2]
+    x_got = [x_0, x_1, x_3, x_2]
     x_own = call(join_kernel, "join", [shape(n_expert * cap, width)], x_got)[0]
     x_own, raw_far, w_below, w_above = barrier((x_own, raw_far, w_below, w_above))
 

time: 105 us -> 105 us (level)
    pallas_call x12 -> x13, Pallas kernels: 17.3 us -> 17.3 us  [call(): pl.pallas_call(kernel, out_shape=out_shape, grid=(1,), in_specs=[(full, l...]
where the time goes in v6:
time: 105 us
  starting transfers between devices  38.9 us (37%)
  waiting for transfers between devices  30.2 us (29%)
  Pallas kernels  20.3 us (19%)
  blocking collectives  13.7 us (13%)
    ppermute x26, starting transfers between devices, shift(): return lax.ppermute(value, axis, [(i, (i + step) % n) for i in range(n)])  38.9 us
    ppermute x26, waiting for transfers between devices, shift(): return lax.ppermute(value, axis, [(i, (i + step) % n) for i in range(n)])  30.2 us
    pallas_call x13, Pallas kernels, call(): pl.pallas_call(kernel, out_shape=out_shape, grid=(1,), in_specs=[(full, l...  17.3 us
    all_to_all x1, blocking collectives, on_device(): final = lax.all_to_all(pieces, 'x', 0, 0, tiled=True)  13.7 us
    pallas_call x1, Pallas kernels, call_loading(): pl.pallas_call(body, out_shape=out_shape, in_specs=[pl.BlockSpec(memory_s...  2.96 us
  transfers between devices with their start and end apart: 26, of which 9 were waited for; matrix products, arithmetic and copies ran while one was open for 0% of the time, Pallas kernels for 15%

profile of v6, /device:TPU:0, one launch (start us, length us, event | category | flops | bytes accessed | tf_op | source)
XLA Modules:
  0.0 105.0 jit_solution(3659607750025090874)
XLA Ops:
  0.6 3.0 %prepare.1 = (bf16[272,1024]{1,0:T(8,128)(2,1)}, bf16[144,1024]{1,0:T(8,128)(2,1)}, s32[2,128]{1,0:T(2,128)}, bf16[2,64,1024]{2,1,0:T(8,128)(2,1)}, bf16[2,64,10...) custom-call(s32[2,128]{1,0:T(2,128)} %bitcast.6, s32[2,128]{1,0:T(2,128)} %bitcast.7, ...), custom_call_target="tpu_custom_call" | custom-call | tf_op jit(solution)/shard_map/prepare/pallas_call | solution.py:76
  3.6 1.6 %collective-permute-start.2 = (bf16[2,64,1024]{2,1,0:T(8,128)(2,1)}, bf16[2,64,1024]{2,1,0:T(8,128)(2,1)S(1)}, u32[]{:S(2)}, u32[]{:S(2)}) collective-permute-start(bf16[2,64,1024]{2,1,0:T(8,128)(2,1)} %get-tuple-element.68), channel_id=1, source_target_pairs={{0,32},{32,64},{64,96},{96,0},{1,33},{33,65},{65,97},{97,1},{2,34}... | collective-permute-start | bytes 786440 | tf_op jit(solution)/shard_map/ppermute | solution.py:24
  5.3 4.0 %collective-permute-start.1 = (bf16[144,1024]{1,0:T(8,128)(2,1)}, bf16[144,1024]{1,0:T(8,128)(2,1)S(1)}, u32[]{:S(2)}, u32[]{:S(2)}) collective-permute-start(bf16[144,1024]{1,0:T(8,128)(2,1)} %get-tuple-element.66), channel_id=1, source_target_pairs={{0,24},{8,0},{16,8},{24,16},{1,25},{9,1},{17,9},{25,17},{2,26},{10... | collective-permute-start | bytes 884744 | tf_op jit(solution)/shard_map/ppermute | solution.py:24
  9.3 0.0 collective-permute-start
  9.3 1.8 %collective-permute-start.3 = (bf16[2,64,1024]{2,1,0:T(8,128)(2,1)}, bf16[2,64,1024]{2,1,0:T(8,128)(2,1)S(1)}, u32[]{:S(2)}, u32[]{:S(2)}) collective-permute-start(bf16[2,64,1024]{2,1,0:T(8,128)(2,1)} %get-tuple-element.70), channel_id=1, source_target_pairs={{0,96},{32,0},{64,32},{96,64},{1,97},{33,1},{65,33},{97,65},{2,98}... | collective-permute-start | bytes 786440 | tf_op jit(solution)/shard_map/ppermute | solution.py:24
  11.0 3.0 %collective-permute-start.7 = (bf16[272,1024]{1,0:T(8,128)(2,1)}, bf16[272,1024]{1,0:T(8,128)(2,1)S(1)}, u32[]{:S(2)}, u32[]{:S(2)}) collective-permute-start(bf16[272,1024]{1,0:T(8,128)(2,1)} %get-tuple-element.76.refs_0_.refs_12_), channel_id=1, source_target_pairs={{0,6},{2,0},{4,2},{6,4},{1,7},{3,1},{5,3},{7,5},{8,14},{10,8},{12,... | collective-permute-start | bytes 1671176 | tf_op jit(solution)/shard_map/ppermute | solution.py:24
  14.1 0.0 collective-permute-done.2.refs_1_.refs_4_
  14.1 0.7 collective-permute-start.6
  14.8 0.9 copy-done.1
  15.8 1.2 %collective-permute-done.3.refs_2_.refs_5_ = bf16[2,64,1024]{2,1,0:T(8,128)(2,1)S(1)} collective-permute-done((bf16[2,64,1024]{2,1,0:T(8,128)(2,1)}, bf16[2,64,1024]{2,1,0:T(8,128)(2,1)S(1)}, u32[]{:S(2)}, u32[]{:S(2)}) %collective-permute-start.3) | collective-permute-done | bytes 262176 | tf_op jit(solution)/shard_map/ppermute | solution.py:24
  17.0 0.0 collective-permute-done.1.above
  17.0 1.9 %collective-permute-done.below = bf16[144,1024]{1,0:T(8,128)(2,1)S(1)} collective-permute-done((bf16[144,1024]{1,0:T(8,128)(2,1)}, bf16[144,1024]{1,0:T(8,128)(2,1)S(1)}, u32[]{:S(2)}, u32[]{:S(2)}) %collective-permute-start) | collective-permute-done | bytes 294944 | tf_op jit(solution)/shard_map/ppermute | solution.py:24
  18.9 0.0 collective-permute-start.5
  18.9 2.7 %collective-permute-start.4 = (bf16[2,64,1024]{2,1,0:T(8,128)(2,1)}, bf16[2,64,1024]{2,1,0:T(8,128)(2,1)S(1)}, u32[]{:S(2)}, u32[]{:S(2)}) collective-permute-start(bf16[2,64,1024]{2,1,0:T(8,128)(2,1)} %get-tuple-element.74), channel_id=1, source_target_pairs={{0,64},{32,96},{64,0},{96,32},{1,65},{33,97},{65,1},{97,33},{2,66}... | collective-permute-start | bytes 786440 | tf_op jit(solution)/shard_map/ppermute | solution.py:24
  21.6 5.6 %collective-permute-done.4.refs_3_.refs_5_ = bf16[2,64,1024]{2,1,0:T(8,128)(2,1)S(1)} collective-permute-done((bf16[2,64,1024]{2,1,0:T(8,128)(2,1)}, bf16[2,64,1024]{2,1,0:T(8,128)(2,1)S(1)}, u32[]{:S(2)}, u32[]{:S(2)}) %collective-permute-start.4) | collective-permute-done | bytes 262176 | tf_op jit(solution)/shard_map/ppermute | solution.py:24
  27.2 0.0 collective-permute-done.7.refs_2_.refs_14_
  27.2 1.5 %collective-permute-done.6.refs_1_.refs_13_ = bf16[272,1024]{1,0:T(8,128)(2,1)S(1)} collective-permute-done((bf16[272,1024]{1,0:T(8,128)(2,1)}, bf16[272,1024]{1,0:T(8,128)(2,1)S(1)}, u32[]{:S(2)}, u32[]{:S(2)}) %collective-permute-start.6) | collective-permute-done | bytes 557088 | tf_op jit(solution)/shard_map/ppermute | solution.py:24
  28.7 0.0 collective-permute-done.5.far
  28.7 0.2 collective-permute-start.10
  29.0 3.6 %collective-permute-start.9 = (bf16[256,1024]{1,0:T(8,128)(2,1)S(1)}, bf16[256,1024]{1,0:T(8,128)(2,1)S(1)}, u32[]{:S(2)}, u32[]{:S(2)}) collective-permute-start(bf16[256,1024]{1,0:T(8,128)(2,1)S(1)} %join.1.refs_0_), channel_id=1, source_target_pairs={{0,24},{8,0},{16,8},{24,16},{1,25},{9,1},{17,9},{25,17},{2,26},{10... | collective-permute-start | bytes 1572872 | tf_op jit(solution)/shard_map/ppermute | solution.py:24
  32.6 0.0 collective-permute-start.8
  32.6 0.5 douts.1
  33.1 0.9 collective-permute-start.11
  34.1 2.4 %collective-permute-start.12 = (bf16[3,64,1024]{2,1,0:T(8,128)(2,1)S(1)}, bf16[3,64,1024]{2,1,0:T(8,128)(2,1)S(1)}, u32[]{:S(2)}, u32[]{:S(2)}) collective-permute-start(bf16[3,64,1024]{2,1,0:T(8,128)(2,1)S(1)} %get-tuple-element.82), channel_id=1, source_target_pairs={{0,96},{32,0},{64,32},{96,64},{1,97},{33,1},{65,33},{97,65},{2,98}... | collective-permute-start | bytes 1179656 | tf_op jit(solution)/shard_map/ppermute | solution.py:24
  36.4 6.5 %collective-permute-done.11.refs_7_.refs_10_.refs_9_ = bf16[3,64,1024]{2,1,0:T(8,128)(2,1)S(1)} collective-permute-done((bf16[3,64,1024]{2,1,0:T(8,128)(2,1)S(1)}, bf16[3,64,1024]{2,1,0:T(8,128)(2,1)S(1)}, u32[]{:S(2)}, u32[]{:S(2)}) %collective-permute-start.11) | collective-permute-done | bytes 393248 | tf_op jit(solution)/shard_map/ppermute | solution.py:24
  42.9 0.0 collective-permute-done.12.refs_8_.refs_11_.refs_10_
  42.9 0.0 collective-permute-done.9.refs_2_
  42.9 2.2 %collective-permute-done.8.refs_1_ = bf16[256,1024]{1,0:T(8,128)(2,1)S(1)} collective-permute-done((bf16[256,1024]{1,0:T(8,128)(2,1)S(1)}, bf16[256,1024]{1,0:T(8,128)(2,1)S(1)}, u32[]{:S(2)}, u32[]{:S(2)}) %collective-permute-start.8) | collective-permute-done | bytes 524320 | tf_op jit(solution)/shard_map/ppermute | solution.py:24
  45.1 0.0 collective-permute-done.10.refs_3_.refs_15_
  45.1 0.1 stack.1
  45.3 0.1 collective-permute-start.13
  45.4 1.0 collective-permute-start.16
  46.4 1.1 %collective-permute-start.15 = (bf16[128,1024]{1,0:T(8,128)(2,1)S(1)}, bf16[128,1024]{1,0:T(8,128)(2,1)S(1)}, u32[]{:S(2)}, u32[]{:S(2)}) collective-permute-start(bf16[128,1024]{1,0:T(8,128)(2,1)S(1)} %slice.6), channel_id=1, source_target_pairs={{0,8},{8,16},{16,24},{24,0},{1,9},{9,17},{17,25},{25,1},{2,10},{10... | collective-permute-start | bytes 786440 | tf_op jit(solution)/shard_map/ppermute | solution.py:24
  47.5 1.8 %collective-permute-start.14 = (bf16[3,64,1024]{2,1,0:T(8,128)(2,1)S(1)}, bf16[3,64,1024]{2,1,0:T(8,128)(2,1)S(1)}, u32[]{:S(2)}, u32[]{:S(2)}) collective-permute-start(bf16[3,64,1024]{2,1,0:T(8,128)(2,1)S(1)} %get-tuple-element.92), channel_id=1, source_target_pairs={{0,64},{32,96},{64,0},{96,32},{1,65},{33,97},{65,1},{97,33},{2,66}... | collective-permute-start | bytes 1179656 | tf_op jit(solution)/shard_map/ppermute | solution.py:24
  49.3 0.4 collective-permute-done.13.refs_16_
  49.7 4.2 %rows.2 = (bf16[576,1024]{1,0:T(8,128)(2,1)S(1)}, bf16[576,1024]{1,0:T(8,128)(2,1)S(1)}, bf16[2,576,512]{2,1,0:T(8,128)(2,1)S(1)}, bf16[2,576,512]{2,1,0:T(8,128...) custom-call(bf16[256,1024]{1,0:T(8,128)(2,1)S(1)} %join.1.refs_0_, ...), custom_call_target="tpu_custom_call" | custom-call | flops 3623878656 | bytes 15599616 | tf_op jit(solution)/shard_map/rows/pallas_call | solution.py:47
  53.9 0.1 collective-permute-start.17
  54.0 3.2 %collective-permute-start.18 = (bf16[208,1024]{1,0:T(8,128)(2,1)S(1)}, bf16[208,1024]{1,0:T(8,128)(2,1)S(1)}, u32[]{:S(2)}, u32[]{:S(2)}) collective-permute-start(bf16[208,1024]{1,0:T(8,128)(2,1)S(1)} %get-tuple-element.106), channel_id=1, source_target_pairs={{0,24},{8,0},{16,8},{24,16},{1,25},{9,1},{17,9},{25,17},{2,26},{10... | collective-permute-start | bytes 1277960 | tf_op jit(solution)/shard_map/ppermute | solution.py:24
  57.2 3.5 %sums.1.near = f32[2,1040,1024]{2,1,0:T(8,128)S(1)} custom-call(bf16[576,1024]{1,0:T(8,128)(2,1)S(1)} %get-tuple-element.93.x, bf16[576,1024]{1,0:T(8,128)(2,1)S(1)} %get-tuple-element.94.d, bf16[2,576,512]{2,1,0:T(8,128)(2,1)S(1)} %get-tuple-element.95.dpre, bf16[2,576,512]{2,1,0:T(8,128)(2,1)S(1)} %get-tuple-element.96.hidden), custom_call_target="tpu_custom_call" | custom-call | flops 2415919104 | bytes 13238272 | tf_op jit(solution)/shard_map/sums/pallas_call | solution.py:47
  60.7 0.0 collective-permute-done.16.refs_4_
  60.7 0.0 collective-permute-done.15.refs_3_
  60.7 0.0 collective-permute-done.14.refs_6_.refs_7_.refs_11_
  60.7 3.3 %rows.3 = (bf16[448,1024]{1,0:T(8,128)(2,1)S(1)}, bf16[448,1024]{1,0:T(8,128)(2,1)S(1)}, bf16[2,448,512]{2,1,0:T(8,128)(2,1)S(1)}, bf16[2,448,512]{2,1,0:T(8,128...) custom-call(bf16[256,1024]{1,0:T(8,128)(2,1)S(1)} %join.1.refs_0_, ...), custom_call_target="tpu_custom_call" | custom-call | flops 2818572288 | bytes 14059520 | tf_op jit(solution)/shard_map/rows/pallas_call | solution.py:47
  64.0 1.3 %away.1 = bf16[1040,1024]{1,0:T(8,128)(2,1)S(1)} custom-call(f32[2,1040,1024]{2,1,0:T(8,128)S(1)} %sums.1.near, bf16[448,1024]{1,0:T(8,128)(2,1)S(1)} %get-tuple-element.101.x, bf16[448,1024]{1,0:T(8,128)(2,1)S(1)} %get-tuple-element.102.d, bf16[2,448,512]{2,1,0:T(8,128)(2,1)S(1)} %get-tuple-element.103.dpre, bf16[2,448,512]{2,1,0:T(8,128)(2,1)S(1)} %get-tuple-element.104.hidden), custom_call_target="tpu_custom_call" | custom-call | flops 939524096 | bytes 14319616 | tf_op jit(solution)/shard_map/away/pallas_call | solution.py:47
  65.4 1.7 %collective-permute-done.17.refs_1_ = bf16[208,1024]{1,0:T(8,128)(2,1)S(1)} collective-permute-done((bf16[208,1024]{1,0:T(8,128)(2,1)S(1)}, bf16[208,1024]{1,0:T(8,128)(2,1)S(1)}, u32[]{:S(2)}, u32[]{:S(2)}) %collective-permute-start.17) | collective-permute-done | bytes 426016 | tf_op jit(solution)/shard_map/ppermute | solution.py:24
  67.0 0.0 collective-permute-done.18.refs_2_
  67.0 0.0 collective-permute-start.22
  67.0 1.5 %collective-permute-start.21 = (bf16[272,1024]{1,0:T(8,128)(2,1)S(1)}, bf16[272,1024]{1,0:T(8,128)(2,1)S(1)}, u32[]{:S(2)}, u32[]{:S(2)}) collective-permute-start(bf16[272,1024]{1,0:T(8,128)(2,1)S(1)} %get-tuple-element.112), channel_id=1, source_target_pairs={{0,16},{8,24},{16,0},{24,8},{1,17},{9,25},{17,1},{25,9},{2,18},{10... | collective-permute-start | bytes 1671176 | tf_op jit(solution)/shard_map/ppermute | solution.py:24
  68.5 2.3 %collective-permute-start.19 = (bf16[80,1024]{1,0:T(8,128)(2,1)S(1)}, bf16[80,1024]{1,0:T(8,128)(2,1)S(1)}, u32[]{:S(2)}, u32[]{:S(2)}) collective-permute-start(bf16[80,1024]{1,0:T(8,128)(2,1)S(1)} %get-tuple-element.110), channel_id=1, source_target_pairs={{0,8},{8,16},{16,24},{24,0},{1,9},{9,17},{17,25},{25,1},{2,10},{10... | collective-permute-start | bytes 491528 | tf_op jit(solution)/shard_map/ppermute | solution.py:24
  70.9 0.9 collective-permute-start.20
  71.7 1.3 %home.1.own = f32[1040,1024]{1,0:T(8,128)S(1)} custom-call(f32[2,1040,1024]{2,1,0:T(8,128)S(1)} %sums.1.near, bf16[448,1024]{1,0:T(8,128)(2,1)S(1)} %get-tuple-element.101.x, bf16[448,1024]{1,0:T(8,128)(2,1)S(1)} %get-tuple-element.102.d, bf16[2,448,512]{2,1,0:T(8,128)(2,1)S(1)} %get-tuple-element.103.dpre, bf16[2,448,512]{2,1,0:T(8,128)(2,1)S(1)} %get-tuple-element.104.hidden), custom_call_target="tpu_custom_call" | custom-call | flops 939524096 | bytes 16449536 | tf_op jit(solution)/shard_map/home/pallas_call | solution.py:47
  73.1 0.4 merge.1
  73.5 3.0 %collective-permute-start.23 = (bf16[272,1024]{1,0:T(8,128)(2,1)S(1)}, bf16[272,1024]{1,0:T(8,128)(2,1)S(1)}, u32[]{:S(2)}, u32[]{:S(2)}) collective-permute-start(bf16[272,1024]{1,0:T(8,128)(2,1)S(1)} %get-tuple-element.117), channel_id=1, source_target_pairs={{0,4},{2,6},{4,0},{6,2},{1,5},{3,7},{5,1},{7,3},{8,12},{10,14},{12... | collective-permute-start | bytes 1671176 | tf_op jit(solution)/shard_map/ppermute | solution.py:24
  76.4 1.3 %collective-permute-start.24 = (bf16[272,1024]{1,0:T(8,128)(2,1)S(1)}, bf16[272,1024]{1,0:T(8,128)(2,1)S(1)}, u32[]{:S(2)}, u32[]{:S(2)}) collective-permute-start(bf16[272,1024]{1,0:T(8,128)(2,1)S(1)} %get-tuple-element.118), channel_id=1, source_target_pairs={{0,6},{2,0},{4,2},{6,4},{1,7},{3,1},{5,3},{7,5},{8,14},{10,8},{12,... | collective-permute-start | bytes 1671176 | tf_op jit(solution)/shard_map/ppermute | solution.py:24
  77.8 9.3 %collective-permute-done.19.refs_4_ = bf16[80,1024]{1,0:T(8,128)(2,1)S(1)} collective-permute-done((bf16[80,1024]{1,0:T(8,128)(2,1)S(1)}, bf16[80,1024]{1,0:T(8,128)(2,1)S(1)}, u32[]{:S(2)}, u32[]{:S(2)}) %collective-permute-start.19) | collective-permute-done | bytes 163872 | tf_op jit(solution)/shard_map/ppermute | solution.py:24
  87.1 1.6 %collective-permute-start.25 = (bf16[272,1024]{1,0:T(8,128)(2,1)S(1)}, bf16[272,1024]{1,0:T(8,128)(2,1)S(1)}, u32[]{:S(2)}, u32[]{:S(2)}) collective-permute-start(bf16[272,1024]{1,0:T(8,128)(2,1)S(1)} %get-tuple-element.119), channel_id=1, source_target_pairs={{0,2},{2,4},{4,6},{6,0},{1,3},{3,5},{5,7},{7,1},{8,10},{10,12},{12... | collective-permute-start | bytes 1671176 | tf_op jit(solution)/shard_map/ppermute | solution.py:24
  88.7 0.0 collective-permute-done.20.refs_5_
  88.7 0.0 collective-permute-done.21.refs_6_
  88.7 0.0 copy-start.3
  88.7 0.3 sum_z.1
  89.0 13.7 %all_to_all.5.pieces = bf16[4,80,1024]{2,1,0:T(8,128)(2,1)S(1)} all-to-all(bf16[4,80,1024]{2,1,0:T(8,128)(2,1)S(1)} %sum_z.1), channel_id=1, replica_groups=mesh['x'=4,'z'=4,'y'=4,'c'=2] {'x'}, dimensions={0} | all-to-all | bytes 1310720 | tf_op jit(solution)/shard_map/all_to_all | solution.py:472
  102.8 1.2 %finish.1 = (bf16[128,1024]{1,0:T(8,128)(2,1)}, f32[2,128]{1,0:T(2,128)}) custom-call(s32[2,128]{1,0:T(2,128)S(1)} %copy-done.3, bf16[2,128]{1,0:T(2,128)(2,1)S(1)} %bitcast.5, bf16[4,80,1024]{2,1,0:T(8,128)(2,1)S(1)} %all_to_all.5.pieces), custom_call_target="tpu_custom_call" | custom-call | bytes 920064 | tf_op jit(solution)/shard_map/finish/pallas_call | solution.py:47
  103.9 0.0 collective-permute-done.25.c
  103.9 1.0 last.1
  (15 shorter events, 0.1 us)
Async XLA Ops:
  3.6 41.5 %copy-start = (bf16[272,1024]{1,0:T(8,128)(2,1)S(1)}, bf16[272,1024]{1,0:T(8,128)(2,1)}, u32[]{:S(2)}) copy-start(bf16[272,1024]{1,0:T(8,128)(2,1)} %get-tuple-element.76.refs_0_.refs_12_) | copy-start | bytes 1671172
  3.6 10.4 %collective-permute-start.2 = (bf16[2,64,1024]{2,1,0:T(8,128)(2,1)}, bf16[2,64,1024]{2,1,0:T(8,128)(2,1)S(1)}, u32[]{:S(2)}, u32[]{:S(2)}) collective-permute-start(bf16[2,64,1024]{2,1,0:T(8,128)(2,1)} %get-tuple-element.68), channel_id=1, source_target_pairs={{0,32},{32,64},{64,96},{96,0},{1,33},{33,65},{65,97},{97,1},{2,34}... | collective-permute-start | bytes 786440 | tf_op jit(solution)/shard_map/ppermute | solution.py:24
  5.3 11.7 %collective-permute-start.1 = (bf16[144,1024]{1,0:T(8,128)(2,1)}, bf16[144,1024]{1,0:T(8,128)(2,1)S(1)}, u32[]{:S(2)}, u32[]{:S(2)}) collective-permute-start(bf16[144,1024]{1,0:T(8,128)(2,1)} %get-tuple-element.66), channel_id=1, source_target_pairs={{0,24},{8,0},{16,8},{24,16},{1,25},{9,1},{17,9},{25,17},{2,26},{10... | collective-permute-start | bytes 884744 | tf_op jit(solution)/shard_map/ppermute | solution.py:24
  9.3 9.6 %collective-permute-start = (bf16[144,1024]{1,0:T(8,128)(2,1)}, bf16[144,1024]{1,0:T(8,128)(2,1)S(1)}, u32[]{:S(2)}, u32[]{:S(2)}) collective-permute-start(bf16[144,1024]{1,0:T(8,128)(2,1)} %get-tuple-element.66), channel_id=1, source_target_pairs={{0,8},{8,16},{16,24},{24,0},{1,9},{9,17},{17,25},{25,1},{2,10},{10... | collective-permute-start | bytes 884744 | tf_op jit(solution)/shard_map/ppermute | solution.py:24
  9.3 7.7 %collective-permute-start.3 = (bf16[2,64,1024]{2,1,0:T(8,128)(2,1)}, bf16[2,64,1024]{2,1,0:T(8,128)(2,1)S(1)}, u32[]{:S(2)}, u32[]{:S(2)}) collective-permute-start(bf16[2,64,1024]{2,1,0:T(8,128)(2,1)} %get-tuple-element.70), channel_id=1, source_target_pairs={{0,96},{32,0},{64,32},{96,64},{1,97},{33,1},{65,33},{97,65},{2,98}... | collective-permute-start | bytes 786440 | tf_op jit(solution)/shard_map/ppermute | solution.py:24
  11.0 16.2 %collective-permute-start.7 = (bf16[272,1024]{1,0:T(8,128)(2,1)}, bf16[272,1024]{1,0:T(8,128)(2,1)S(1)}, u32[]{:S(2)}, u32[]{:S(2)}) collective-permute-start(bf16[272,1024]{1,0:T(8,128)(2,1)} %get-tuple-element.76.refs_0_.refs_12_), channel_id=1, source_target_pairs={{0,6},{2,0},{4,2},{6,4},{1,7},{3,1},{5,3},{7,5},{8,14},{10,8},{12,... | collective-permute-start | bytes 1671176 | tf_op jit(solution)/shard_map/ppermute | solution.py:24
  14.1 14.7 %collective-permute-start.6 = (bf16[272,1024]{1,0:T(8,128)(2,1)}, bf16[272,1024]{1,0:T(8,128)(2,1)S(1)}, u32[]{:S(2)}, u32[]{:S(2)}) collective-permute-start(bf16[272,1024]{1,0:T(8,128)(2,1)} %get-tuple-element.76.refs_0_.refs_12_), channel_id=1, source_target_pairs={{0,2},{2,4},{4,6},{6,0},{1,3},{3,5},{5,7},{7,1},{8,10},{10,12},{12... | collective-permute-start | bytes 1671176 | tf_op jit(solution)/shard_map/ppermute | solution.py:24
  14.8 0.9 copy-start.1
  18.9 9.8 %collective-permute-start.5 = (bf16[144,1024]{1,0:T(8,128)(2,1)S(1)}, bf16[144,1024]{1,0:T(8,128)(2,1)S(1)}, u32[]{:S(2)}, u32[]{:S(2)}) collective-permute-start(bf16[144,1024]{1,0:T(8,128)(2,1)S(1)} %collective-permute-done.below), channel_id=1, source_target_pairs={{0,8},{8,16},{16,24},{24,0},{1,9},{9,17},{17,25},{25,1},{2,10},{10... | collective-permute-start | bytes 884744 | tf_op jit(solution)/shard_map/ppermute | solution.py:24
  18.9 8.3 %collective-permute-start.4 = (bf16[2,64,1024]{2,1,0:T(8,128)(2,1)}, bf16[2,64,1024]{2,1,0:T(8,128)(2,1)S(1)}, u32[]{:S(2)}, u32[]{:S(2)}) collective-permute-start(bf16[2,64,1024]{2,1,0:T(8,128)(2,1)} %get-tuple-element.74), channel_id=1, source_target_pairs={{0,64},{32,96},{64,0},{96,32},{1,65},{33,97},{65,1},{97,33},{2,66}... | collective-permute-start | bytes 786440 | tf_op jit(solution)/shard_map/ppermute | solution.py:24
  28.7 16.4 %collective-permute-start.10 = (bf16[272,1024]{1,0:T(8,128)(2,1)S(1)}, bf16[272,1024]{1,0:T(8,128)(2,1)S(1)}, u32[]{:S(2)}, u32[]{:S(2)}) collective-permute-start(bf16[272,1024]{1,0:T(8,128)(2,1)S(1)} %collective-permute-done.6.refs_1_.refs_13_), channel_id=1, source_target_pairs={{0,2},{2,4},{4,6},{6,0},{1,3},{3,5},{5,7},{7,1},{8,10},{10,12},{12... | collective-permute-start | bytes 1671176 | tf_op jit(solution)/shard_map/ppermute | solution.py:24
  29.0 14.0 %collective-permute-start.9 = (bf16[256,1024]{1,0:T(8,128)(2,1)S(1)}, bf16[256,1024]{1,0:T(8,128)(2,1)S(1)}, u32[]{:S(2)}, u32[]{:S(2)}) collective-permute-start(bf16[256,1024]{1,0:T(8,128)(2,1)S(1)} %join.1.refs_0_), channel_id=1, source_target_pairs={{0,24},{8,0},{16,8},{24,16},{1,25},{9,1},{17,9},{25,17},{2,26},{10... | collective-permute-start | bytes 1572872 | tf_op jit(solution)/shard_map/ppermute | solution.py:24
  32.6 12.5 %collective-permute-start.8 = (bf16[256,1024]{1,0:T(8,128)(2,1)S(1)}, bf16[256,1024]{1,0:T(8,128)(2,1)S(1)}, u32[]{:S(2)}, u32[]{:S(2)}) collective-permute-start(bf16[256,1024]{1,0:T(8,128)(2,1)S(1)} %join.1.refs_0_), channel_id=1, source_target_pairs={{0,8},{8,16},{16,24},{24,0},{1,9},{9,17},{17,25},{25,1},{2,10},{10... | collective-permute-start | bytes 1572872 | tf_op jit(solution)/shard_map/ppermute | solution.py:24
  33.1 9.8 %collective-permute-start.11 = (bf16[3,64,1024]{2,1,0:T(8,128)(2,1)S(1)}, bf16[3,64,1024]{2,1,0:T(8,128)(2,1)S(1)}, u32[]{:S(2)}, u32[]{:S(2)}) collective-permute-start(bf16[3,64,1024]{2,1,0:T(8,128)(2,1)S(1)} %get-tuple-element.81), channel_id=1, source_target_pairs={{0,32},{32,64},{64,96},{96,0},{1,33},{33,65},{65,97},{97,1},{2,34}... | collective-permute-start | bytes 1179656 | tf_op jit(solution)/shard_map/ppermute | solution.py:24
  34.1 8.9 %collective-permute-start.12 = (bf16[3,64,1024]{2,1,0:T(8,128)(2,1)S(1)}, bf16[3,64,1024]{2,1,0:T(8,128)(2,1)S(1)}, u32[]{:S(2)}, u32[]{:S(2)}) collective-permute-start(bf16[3,64,1024]{2,1,0:T(8,128)(2,1)S(1)} %get-tuple-element.82), channel_id=1, source_target_pairs={{0,96},{32,0},{64,32},{96,64},{1,97},{33,1},{65,33},{97,65},{2,98}... | collective-permute-start | bytes 1179656 | tf_op jit(solution)/shard_map/ppermute | solution.py:24
  45.1 4.6 %copy-start.4 = (bf16[1,1024]{1,0:T(2,128)(2,1)S(1)}, bf16[1,1024]{1,0:T(2,128)(2,1)}, u32[]{:S(2)}) copy-start(bf16[1,1024]{1,0:T(2,128)(2,1)} %refs_17_.3) | copy-start | bytes 6148
  45.3 4.4 %collective-permute-start.13 = (bf16[4,272,1024]{2,1,0:T(8,128)(2,1)S(1)}, bf16[4,272,1024]{2,1,0:T(8,128)(2,1)S(1)}, u32[]{:S(2)}, u32[]{:S(2)}) collective-permute-start(bf16[4,272,1024]{2,1,0:T(8,128)(2,1)S(1)} %stack.1), channel_id=1, source_target_pairs={{0,1},{1,0},{2,3},{3,2},{4,5},{5,4},{6,7},{7,6},{8,9},{9,8},{10,11... | collective-permute-start | bytes 6684680 | tf_op jit(solution)/shard_map/ppermute | solution.py:24
  45.4 15.3 %collective-permute-start.16 = (bf16[128,1024]{1,0:T(8,128)(2,1)S(1)}, bf16[128,1024]{1,0:T(8,128)(2,1)S(1)}, u32[]{:S(2)}, u32[]{:S(2)}) collective-permute-start(bf16[128,1024]{1,0:T(8,128)(2,1)S(1)} %slice.7), channel_id=1, source_target_pairs={{0,24},{8,0},{16,8},{24,16},{1,25},{9,1},{17,9},{25,17},{2,26},{10... | collective-permute-start | bytes 786440 | tf_op jit(solution)/shard_map/ppermute | solution.py:24
  46.4 14.3 %collective-permute-start.15 = (bf16[128,1024]{1,0:T(8,128)(2,1)S(1)}, bf16[128,1024]{1,0:T(8,128)(2,1)S(1)}, u32[]{:S(2)}, u32[]{:S(2)}) collective-permute-start(bf16[128,1024]{1,0:T(8,128)(2,1)S(1)} %slice.6), channel_id=1, source_target_pairs={{0,8},{8,16},{16,24},{24,0},{1,9},{9,17},{17,25},{25,1},{2,10},{10... | collective-permute-start | bytes 786440 | tf_op jit(solution)/shard_map/ppermute | solution.py:24
  47.5 13.2 %collective-permute-start.14 = (bf16[3,64,1024]{2,1,0:T(8,128)(2,1)S(1)}, bf16[3,64,1024]{2,1,0:T(8,128)(2,1)S(1)}, u32[]{:S(2)}, u32[]{:S(2)}) collective-permute-start(bf16[3,64,1024]{2,1,0:T(8,128)(2,1)S(1)} %get-tuple-element.92), channel_id=1, source_target_pairs={{0,64},{32,96},{64,0},{96,32},{1,65},{33,97},{65,1},{97,33},{2,66}... | collective-permute-start | bytes 1179656 | tf_op jit(solution)/shard_map/ppermute | solution.py:24
  53.9 13.1 %collective-permute-start.17 = (bf16[208,1024]{1,0:T(8,128)(2,1)S(1)}, bf16[208,1024]{1,0:T(8,128)(2,1)S(1)}, u32[]{:S(2)}, u32[]{:S(2)}) collective-permute-start(bf16[208,1024]{1,0:T(8,128)(2,1)S(1)} %get-tuple-element.105), channel_id=1, source_target_pairs={{0,8},{8,16},{16,24},{24,0},{1,9},{9,17},{17,25},{25,1},{2,10},{10... | collective-permute-start | bytes 1277960 | tf_op jit(solution)/shard_map/ppermute | solution.py:24
  54.0 13.1 %collective-permute-start.18 = (bf16[208,1024]{1,0:T(8,128)(2,1)S(1)}, bf16[208,1024]{1,0:T(8,128)(2,1)S(1)}, u32[]{:S(2)}, u32[]{:S(2)}) collective-permute-start(bf16[208,1024]{1,0:T(8,128)(2,1)S(1)} %get-tuple-element.106), channel_id=1, source_target_pairs={{0,24},{8,0},{16,8},{24,16},{1,25},{9,1},{17,9},{25,17},{2,26},{10... | collective-permute-start | bytes 1277960 | tf_op jit(solution)/shard_map/ppermute | solution.py:24
  67.0 6.0 %collective-permute-start.22 = (bf16[1040,1024]{1,0:T(8,128)(2,1)S(1)}, bf16[1040,1024]{1,0:T(8,128)(2,1)S(1)}, u32[]{:S(2)}, u32[]{:S(2)}) collective-permute-start(bf16[1040,1024]{1,0:T(8,128)(2,1)S(1)} %away.1), channel_id=1, source_target_pairs={{0,1},{1,0},{2,3},{3,2},{4,5},{5,4},{6,7},{7,6},{8,9},{9,8},{10,11... | collective-permute-start | bytes 6389768 | tf_op jit(solution)/shard_map/ppermute | solution.py:24
  67.0 21.6 %collective-permute-start.21 = (bf16[272,1024]{1,0:T(8,128)(2,1)S(1)}, bf16[272,1024]{1,0:T(8,128)(2,1)S(1)}, u32[]{:S(2)}, u32[]{:S(2)}) collective-permute-start(bf16[272,1024]{1,0:T(8,128)(2,1)S(1)} %get-tuple-element.112), channel_id=1, source_target_pairs={{0,16},{8,24},{16,0},{24,8},{1,17},{9,25},{17,1},{25,9},{2,18},{10... | collective-permute-start | bytes 1671176 | tf_op jit(solution)/shard_map/ppermute | solution.py:24
  68.5 18.6 %collective-permute-start.19 = (bf16[80,1024]{1,0:T(8,128)(2,1)S(1)}, bf16[80,1024]{1,0:T(8,128)(2,1)S(1)}, u32[]{:S(2)}, u32[]{:S(2)}) collective-permute-start(bf16[80,1024]{1,0:T(8,128)(2,1)S(1)} %get-tuple-element.110), channel_id=1, source_target_pairs={{0,8},{8,16},{16,24},{24,0},{1,9},{9,17},{17,25},{25,1},{2,10},{10... | collective-permute-start | bytes 491528 | tf_op jit(solution)/shard_map/ppermute | solution.py:24
  70.9 17.8 %collective-permute-start.20 = (bf16[80,1024]{1,0:T(8,128)(2,1)S(1)}, bf16[80,1024]{1,0:T(8,128)(2,1)S(1)}, u32[]{:S(2)}, u32[]{:S(2)}) collective-permute-start(bf16[80,1024]{1,0:T(8,128)(2,1)S(1)} %get-tuple-element.111), channel_id=1, source_target_pairs={{0,24},{8,0},{16,8},{24,16},{1,25},{9,1},{17,9},{25,17},{2,26},{10... | collective-permute-start | bytes 491528 | tf_op jit(solution)/shard_map/ppermute | solution.py:24
  73.5 30.5 %collective-permute-start.23 = (bf16[272,1024]{1,0:T(8,128)(2,1)S(1)}, bf16[272,1024]{1,0:T(8,128)(2,1)S(1)}, u32[]{:S(2)}, u32[]{:S(2)}) collective-permute-start(bf16[272,1024]{1,0:T(8,128)(2,1)S(1)} %get-tuple-element.117), channel_id=1, source_target_pairs={{0,4},{2,6},{4,0},{6,2},{1,5},{3,7},{5,1},{7,3},{8,12},{10,14},{12... | collective-permute-start | bytes 1671176 | tf_op jit(solution)/shard_map/ppermute | solution.py:24
  76.4 27.5 %collective-permute-start.24 = (bf16[272,1024]{1,0:T(8,128)(2,1)S(1)}, bf16[272,1024]{1,0:T(8,128)(2,1)S(1)}, u32[]{:S(2)}, u32[]{:S(2)}) collective-permute-start(bf16[272,1024]{1,0:T(8,128)(2,1)S(1)} %get-tuple-element.118), channel_id=1, source_target_pairs={{0,6},{2,0},{4,2},{6,4},{1,7},{3,1},{5,3},{7,5},{8,14},{10,8},{12,... | collective-permute-start | bytes 1671176 | tf_op jit(solution)/shard_map/ppermute | solution.py:24
  87.1 16.8 %collective-permute-start.25 = (bf16[272,1024]{1,0:T(8,128)(2,1)S(1)}, bf16[272,1024]{1,0:T(8,128)(2,1)S(1)}, u32[]{:S(2)}, u32[]{:S(2)}) collective-permute-start(bf16[272,1024]{1,0:T(8,128)(2,1)S(1)} %get-tuple-element.119), channel_id=1, source_target_pairs={{0,2},{2,4},{4,6},{6,0},{1,3},{3,5},{5,7},{7,1},{8,10},{10,12},{12... | collective-permute-start | bytes 1671176 | tf_op jit(solution)/shard_map/ppermute | solution.py:24
  88.7 14.1 %copy-start.2 = (bf16[128,2]{0,1:T(2,128)(2,1)S(1)}, bf16[128,2]{0,1:T(2,128)(2,1)}, u32[]{:S(2)}) copy-start(bf16[128,2]{0,1:T(2,128)(2,1)} %param.13) | copy-start | bytes 1540
  88.7 14.1 %copy-start.3 = (s32[2,128]{1,0:T(2,128)S(1)}, s32[2,128]{1,0:T(2,128)}, u32[]{:S(2)}) copy-start(s32[2,128]{1,0:T(2,128)} %get-tuple-element.65.places) | copy-start | bytes 3076

commit v7 on v5

--- a/solution.py
+++ b/solution.py
@@ -144,9 +144,10 @@
 
 def rows_kernel(n_x, n_d, blocks, *refs):
     xs, ds = refs[:n_x], refs[n_x : n_x + n_d]
-    mine, below, above, far, other, b_out, *outs = refs[n_x + n_d :]
+    mine, below, above, far, other, others, b_out, *outs = refs[n_x + n_d :]
     x, d, dpre, hidden, *dxs = outs
-    shares = [(ours, other.at[k]) for k, ours in enumerate((mine, below, above, far))]
+    shares = [(mine, other)]
+    shares += [(ours, others.at[k]) for k, ours in enumerate((below, above, far))]
     width = x.shape[1]
     for parts, whole in ((xs, x), (ds, d)):
         at = 0
@@ -382,7 +383,8 @@
     x_2 = shift(x_2, "x", 2)
     x_got = [x_sent[0], x_1, x_3, x_2]
     x_own = call(join_kernel, "join", [shape(n_expert * cap, width)], x_got)[0]
-    x_own, raw_far, w_below, w_above = barrier((x_own, raw_far, w_below, w_above))
+    other = shift(mine, "c", 1)
+    x_own, raw_far, w_below, w_above, other = barrier((x_own, raw_far, w_below, w_above, other))
 
     d_sent = call(
         douts_kernel,
@@ -399,8 +401,9 @@
         (x_below, x_above, w_far, d_1, d_3, d_sent[2])
     )
     ours = [mine, w_below, w_above, w_far]
-    every = call(stack_kernel, "stack", [jax.ShapeDtypeStruct((4, *mine.shape), BF)], ours, vmem=12)
-    w = [*ours, shift(every[0], "c", 1)]
+    rest = [jax.ShapeDtypeStruct((3, *mine.shape), BF)]
+    rest = call(stack_kernel, "stack", rest, ours[1:], vmem=12)[0]
+    w = [*ours, other, shift(rest, "c", 1)]
 
     d_2 = shift(d_2, "x", 2)
     half = x_own.shape[0] // 2

time: 105 us -> 106 us (level)
  waiting for transfers between devices: 29.8 us -> 33.9 us
  starting transfers between devices: 39.4 us -> 35.6 us
    ppermute x26 -> x27, waiting for transfers between devices: 29.8 us -> 33.9 us  [shift(): return lax.ppermute(value, axis, [(i, (i + step) % n) for i in range(n)])]
    ppermute x26 -> x27, starting transfers between devices: 39.4 us -> 35.6 us  [shift(): return lax.ppermute(value, axis, [(i, (i + step) % n) for i in range(n)])]
  transfers between devices with their start and end apart: 26 -> 27, of which waited for: 9 -> 10; matrix products, arithmetic and copies ran while one was open for 0% -> 0% of each run, Pallas kernels for 15% -> 15%
where the time goes in v7:
time: 106 us
  starting transfers between devices  35.6 us (34%)
  waiting for transfers between devices  33.9 us (32%)
  Pallas kernels  20.2 us (19%)
  blocking collectives  14.2 us (13%)
    ppermute x27, starting transfers between devices, shift(): return lax.ppermute(value, axis, [(i, (i + step) % n) for i in range(n)])  35.6 us
    ppermute x27, waiting for transfers between devices, shift(): return lax.ppermute(value, axis, [(i, (i + step) % n) for i in range(n)])  33.9 us
    pallas_call x12, Pallas kernels, call(): pl.pallas_call(kernel, out_shape=out_shape, grid=(1,), in_specs=[(full, l...  17.3 us
    all_to_all x1, blocking collectives, on_device(): final = lax.all_to_all(pieces, 'x', 0, 0, tiled=True)  14.2 us
    pallas_call x1, Pallas kernels, call_loading(): pl.pallas_call(body, out_shape=out_shape, in_specs=[pl.BlockSpec(memory_s...  2.96 us
  transfers between devices with their start and end apart: 27, of which 10 were waited for; matrix products, arithmetic and copies ran while one was open for 0% of the time, Pallas kernels for 15%

profile of v7, /device:TPU:0, one launch (start us, length us, event | category | flops | bytes accessed | tf_op | source)
XLA Modules:
  0.0 105.7 jit_solution(13751075805087353482)
XLA Ops:
  0.6 3.0 %prepare.1 = (bf16[272,1024]{1,0:T(8,128)(2,1)}, bf16[144,1024]{1,0:T(8,128)(2,1)}, s32[2,128]{1,0:T(2,128)}, bf16[2,64,1024]{2,1,0:T(8,128)(2,1)}, bf16[2,64,10...) custom-call(s32[2,128]{1,0:T(2,128)} %bitcast.6, s32[2,128]{1,0:T(2,128)} %bitcast.7, ...), custom_call_target="tpu_custom_call" | custom-call | tf_op jit(solution)/shard_map/prepare/pallas_call | solution.py:76
  3.6 1.6 %collective-permute-start.2 = (bf16[2,64,1024]{2,1,0:T(8,128)(2,1)}, bf16[2,64,1024]{2,1,0:T(8,128)(2,1)S(1)}, u32[]{:S(2)}, u32[]{:S(2)}) collective-permute-start(bf16[2,64,1024]{2,1,0:T(8,128)(2,1)} %get-tuple-element.68), channel_id=1, source_target_pairs={{0,32},{32,64},{64,96},{96,0},{1,33},{33,65},{65,97},{97,1},{2,34}... | collective-permute-start | bytes 786440 | tf_op jit(solution)/shard_map/ppermute | solution.py:24
  5.2 1.7 %collective-permute-start.3 = (bf16[2,64,1024]{2,1,0:T(8,128)(2,1)}, bf16[2,64,1024]{2,1,0:T(8,128)(2,1)S(1)}, u32[]{:S(2)}, u32[]{:S(2)}) collective-permute-start(bf16[2,64,1024]{2,1,0:T(8,128)(2,1)} %get-tuple-element.70), channel_id=1, source_target_pairs={{0,96},{32,0},{64,32},{96,64},{1,97},{33,1},{65,33},{97,65},{2,98}... | collective-permute-start | bytes 786440 | tf_op jit(solution)/shard_map/ppermute | solution.py:24
  6.9 4.1 %collective-permute-start.1 = (bf16[144,1024]{1,0:T(8,128)(2,1)}, bf16[144,1024]{1,0:T(8,128)(2,1)S(1)}, u32[]{:S(2)}, u32[]{:S(2)}) collective-permute-start(bf16[144,1024]{1,0:T(8,128)(2,1)} %get-tuple-element.67), channel_id=1, source_target_pairs={{0,24},{8,0},{16,8},{24,16},{1,25},{9,1},{17,9},{25,17},{2,26},{10... | collective-permute-start | bytes 884744 | tf_op jit(solution)/shard_map/ppermute | solution.py:24
  11.0 0.0 collective-permute-start
  11.0 0.0 collective-permute-start.8
  11.0 2.0 %collective-permute-done.2.refs_1_.refs_4_ = bf16[2,64,1024]{2,1,0:T(8,128)(2,1)S(1)} collective-permute-done((bf16[2,64,1024]{2,1,0:T(8,128)(2,1)}, bf16[2,64,1024]{2,1,0:T(8,128)(2,1)S(1)}, u32[]{:S(2)}, u32[]{:S(2)}) %collective-permute-start.2) | collective-permute-done | bytes 262176 | tf_op jit(solution)/shard_map/ppermute | solution.py:24
  13.0 3.2 %collective-permute-start.7 = (bf16[272,1024]{1,0:T(8,128)(2,1)}, bf16[272,1024]{1,0:T(8,128)(2,1)S(1)}, u32[]{:S(2)}, u32[]{:S(2)}) collective-permute-start(bf16[272,1024]{1,0:T(8,128)(2,1)} %get-tuple-element.75.refs_12_), channel_id=1, source_target_pairs={{0,6},{2,0},{4,2},{6,4},{1,7},{3,1},{5,3},{7,5},{8,14},{10,8},{12,... | collective-permute-start | bytes 1671176 | tf_op jit(solution)/shard_map/ppermute | solution.py:24
  16.2 0.0 collective-permute-done.3.refs_2_.refs_5_
  16.2 0.0 collective-permute-start.6
  16.2 0.8 collective-permute-done.1.above
  17.0 3.3 %collective-permute-done.below = bf16[144,1024]{1,0:T(8,128)(2,1)S(1)} collective-permute-done((bf16[144,1024]{1,0:T(8,128)(2,1)}, bf16[144,1024]{1,0:T(8,128)(2,1)S(1)}, u32[]{:S(2)}, u32[]{:S(2)}) %collective-permute-start) | collective-permute-done | bytes 294944 | tf_op jit(solution)/shard_map/ppermute | solution.py:24
  20.4 0.0 collective-permute-start.5
  20.4 1.8 %collective-permute-start.4 = (bf16[2,64,1024]{2,1,0:T(8,128)(2,1)}, bf16[2,64,1024]{2,1,0:T(8,128)(2,1)S(1)}, u32[]{:S(2)}, u32[]{:S(2)}) collective-permute-start(bf16[2,64,1024]{2,1,0:T(8,128)(2,1)} %get-tuple-element.73), channel_id=1, source_target_pairs={{0,64},{32,96},{64,0},{96,32},{1,65},{33,97},{65,1},{97,33},{2,66}... | collective-permute-start | bytes 786440 | tf_op jit(solution)/shard_map/ppermute | solution.py:24
  22.2 6.3 %collective-permute-done.4.refs_3_.refs_5_ = bf16[2,64,1024]{2,1,0:T(8,128)(2,1)S(1)} collective-permute-done((bf16[2,64,1024]{2,1,0:T(8,128)(2,1)}, bf16[2,64,1024]{2,1,0:T(8,128)(2,1)S(1)}, u32[]{:S(2)}, u32[]{:S(2)}) %collective-permute-start.4) | collective-permute-done | bytes 262176 | tf_op jit(solution)/shard_map/ppermute | solution.py:24
  28.4 0.9 copy-done
  29.4 0.0 collective-permute-done.8.refs_16_
  29.4 0.0 collective-permute-done.7.refs_1_.refs_14_
  29.5 1.4 %collective-permute-done.6.refs_0_.refs_13_ = bf16[272,1024]{1,0:T(8,128)(2,1)S(1)} collective-permute-done((bf16[272,1024]{1,0:T(8,128)(2,1)}, bf16[272,1024]{1,0:T(8,128)(2,1)S(1)}, u32[]{:S(2)}, u32[]{:S(2)}) %collective-permute-start.6) | collective-permute-done | bytes 557088 | tf_op jit(solution)/shard_map/ppermute | solution.py:24
  30.9 0.0 collective-permute-done.5.far
  30.9 0.3 collective-permute-start.11
  31.1 3.8 %collective-permute-start.10 = (bf16[256,1024]{1,0:T(8,128)(2,1)S(1)}, bf16[256,1024]{1,0:T(8,128)(2,1)S(1)}, u32[]{:S(2)}, u32[]{:S(2)}) collective-permute-start(bf16[256,1024]{1,0:T(8,128)(2,1)S(1)} %join.1.refs_0_), channel_id=1, source_target_pairs={{0,24},{8,0},{16,8},{24,16},{1,25},{9,1},{17,9},{25,17},{2,26},{10... | collective-permute-start | bytes 1572872 | tf_op jit(solution)/shard_map/ppermute | solution.py:24
  34.9 0.0 collective-permute-start.9
  34.9 0.6 douts.1
  35.5 0.3 collective-permute-start.12
  35.8 3.0 %collective-permute-start.13 = (bf16[3,64,1024]{2,1,0:T(8,128)(2,1)S(1)}, bf16[3,64,1024]{2,1,0:T(8,128)(2,1)S(1)}, u32[]{:S(2)}, u32[]{:S(2)}) collective-permute-start(bf16[3,64,1024]{2,1,0:T(8,128)(2,1)S(1)} %get-tuple-element.81), channel_id=1, source_target_pairs={{0,96},{32,0},{64,32},{96,64},{1,97},{33,1},{65,33},{97,65},{2,98}... | collective-permute-start | bytes 1179656 | tf_op jit(solution)/shard_map/ppermute | solution.py:24
  38.8 6.5 %collective-permute-done.12.refs_7_.refs_10_.refs_9_ = bf16[3,64,1024]{2,1,0:T(8,128)(2,1)S(1)} collective-permute-done((bf16[3,64,1024]{2,1,0:T(8,128)(2,1)S(1)}, bf16[3,64,1024]{2,1,0:T(8,128)(2,1)S(1)}, u32[]{:S(2)}, u32[]{:S(2)}) %collective-permute-start.12) | collective-permute-done | bytes 393248 | tf_op jit(solution)/shard_map/ppermute | solution.py:24
  45.3 0.0 collective-permute-done.13.refs_8_.refs_11_.refs_10_
  45.3 0.0 collective-permute-done.10.refs_2_
  45.3 2.2 %collective-permute-done.9.refs_1_ = bf16[256,1024]{1,0:T(8,128)(2,1)S(1)} collective-permute-done((bf16[256,1024]{1,0:T(8,128)(2,1)S(1)}, bf16[256,1024]{1,0:T(8,128)(2,1)S(1)}, u32[]{:S(2)}, u32[]{:S(2)}) %collective-permute-start.9) | collective-permute-done | bytes 524320 | tf_op jit(solution)/shard_map/ppermute | solution.py:24
  47.4 0.0 collective-permute-done.11.refs_2_.refs_15_
  47.5 0.1 stack.1
  47.6 0.1 collective-permute-start.14
  47.7 1.0 collective-permute-start.17
  48.8 1.1 %collective-permute-start.16 = (bf16[128,1024]{1,0:T(8,128)(2,1)S(1)}, bf16[128,1024]{1,0:T(8,128)(2,1)S(1)}, u32[]{:S(2)}, u32[]{:S(2)}) collective-permute-start(bf16[128,1024]{1,0:T(8,128)(2,1)S(1)} %slice.6), channel_id=1, source_target_pairs={{0,8},{8,16},{16,24},{24,0},{1,9},{9,17},{17,25},{25,1},{2,10},{10... | collective-permute-start | bytes 786440 | tf_op jit(solution)/shard_map/ppermute | solution.py:24
  49.8 1.8 %collective-permute-start.15 = (bf16[3,64,1024]{2,1,0:T(8,128)(2,1)S(1)}, bf16[3,64,1024]{2,1,0:T(8,128)(2,1)S(1)}, u32[]{:S(2)}, u32[]{:S(2)}) collective-permute-start(bf16[3,64,1024]{2,1,0:T(8,128)(2,1)S(1)} %get-tuple-element.92), channel_id=1, source_target_pairs={{0,64},{32,96},{64,0},{96,32},{1,65},{33,97},{65,1},{97,33},{2,66}... | collective-permute-start | bytes 1179656 | tf_op jit(solution)/shard_map/ppermute | solution.py:24
  51.6 0.0 collective-permute-done.14.refs_17_
  51.6 4.2 %rows.2 = (bf16[576,1024]{1,0:T(8,128)(2,1)S(1)}, bf16[576,1024]{1,0:T(8,128)(2,1)S(1)}, bf16[2,576,512]{2,1,0:T(8,128)(2,1)S(1)}, bf16[2,576,512]{2,1,0:T(8,128...) custom-call(bf16[256,1024]{1,0:T(8,128)(2,1)S(1)} %join.1.refs_0_, ...), custom_call_target="tpu_custom_call" | custom-call | flops 3623878656 | bytes 15599616 | tf_op jit(solution)/shard_map/rows/pallas_call | solution.py:47
  55.9 0.1 collective-permute-start.18
  56.0 3.2 %collective-permute-start.19 = (bf16[208,1024]{1,0:T(8,128)(2,1)S(1)}, bf16[208,1024]{1,0:T(8,128)(2,1)S(1)}, u32[]{:S(2)}, u32[]{:S(2)}) collective-permute-start(bf16[208,1024]{1,0:T(8,128)(2,1)S(1)} %get-tuple-element.106), channel_id=1, source_target_pairs={{0,24},{8,0},{16,8},{24,16},{1,25},{9,1},{17,9},{25,17},{2,26},{10... | collective-permute-start | bytes 1277960 | tf_op jit(solution)/shard_map/ppermute | solution.py:24
  59.2 3.5 %sums.1.near = f32[2,1040,1024]{2,1,0:T(8,128)S(1)} custom-call(bf16[576,1024]{1,0:T(8,128)(2,1)S(1)} %get-tuple-element.93.x, bf16[576,1024]{1,0:T(8,128)(2,1)S(1)} %get-tuple-element.94.d, bf16[2,576,512]{2,1,0:T(8,128)(2,1)S(1)} %get-tuple-element.95.dpre, bf16[2,576,512]{2,1,0:T(8,128)(2,1)S(1)} %get-tuple-element.96.hidden), custom_call_target="tpu_custom_call" | custom-call | flops 2415919104 | bytes 13238272 | tf_op jit(solution)/shard_map/sums/pallas_call | solution.py:47
  62.6 0.0 collective-permute-done.17.refs_4_
  62.7 0.0 collective-permute-done.16.refs_3_
  62.7 0.0 collective-permute-done.15.refs_6_.refs_7_.refs_11_
  62.7 3.3 %rows.3 = (bf16[448,1024]{1,0:T(8,128)(2,1)S(1)}, bf16[448,1024]{1,0:T(8,128)(2,1)S(1)}, bf16[2,448,512]{2,1,0:T(8,128)(2,1)S(1)}, bf16[2,448,512]{2,1,0:T(8,128...) custom-call(bf16[256,1024]{1,0:T(8,128)(2,1)S(1)} %join.1.refs_0_, ...), custom_call_target="tpu_custom_call" | custom-call | flops 2818572288 | bytes 14059520 | tf_op jit(solution)/shard_map/rows/pallas_call | solution.py:47
  66.0 1.3 %away.1 = bf16[1040,1024]{1,0:T(8,128)(2,1)S(1)} custom-call(f32[2,1040,1024]{2,1,0:T(8,128)S(1)} %sums.1.near, bf16[448,1024]{1,0:T(8,128)(2,1)S(1)} %get-tuple-element.101.x, bf16[448,1024]{1,0:T(8,128)(2,1)S(1)} %get-tuple-element.102.d, bf16[2,448,512]{2,1,0:T(8,128)(2,1)S(1)} %get-tuple-element.103.dpre, bf16[2,448,512]{2,1,0:T(8,128)(2,1)S(1)} %get-tuple-element.104.hidden), custom_call_target="tpu_custom_call" | custom-call | flops 939524096 | bytes 14319616 | tf_op jit(solution)/shard_map/away/pallas_call | solution.py:47
  67.3 1.2 %collective-permute-done.18.refs_1_ = bf16[208,1024]{1,0:T(8,128)(2,1)S(1)} collective-permute-done((bf16[208,1024]{1,0:T(8,128)(2,1)S(1)}, bf16[208,1024]{1,0:T(8,128)(2,1)S(1)}, u32[]{:S(2)}, u32[]{:S(2)}) %collective-permute-start.18) | collective-permute-done | bytes 426016 | tf_op jit(solution)/shard_map/ppermute | solution.py:24
  68.6 0.0 collective-permute-done.19.refs_2_
  68.6 0.0 collective-permute-start.23
  68.6 2.1 %collective-permute-start.22 = (bf16[272,1024]{1,0:T(8,128)(2,1)S(1)}, bf16[272,1024]{1,0:T(8,128)(2,1)S(1)}, u32[]{:S(2)}, u32[]{:S(2)}) collective-permute-start(bf16[272,1024]{1,0:T(8,128)(2,1)S(1)} %get-tuple-element.112), channel_id=1, source_target_pairs={{0,16},{8,24},{16,0},{24,8},{1,17},{9,25},{17,1},{25,9},{2,18},{10... | collective-permute-start | bytes 1671176 | tf_op jit(solution)/shard_map/ppermute | solution.py:24
  70.7 1.7 %collective-permute-start.20 = (bf16[80,1024]{1,0:T(8,128)(2,1)S(1)}, bf16[80,1024]{1,0:T(8,128)(2,1)S(1)}, u32[]{:S(2)}, u32[]{:S(2)}) collective-permute-start(bf16[80,1024]{1,0:T(8,128)(2,1)S(1)} %get-tuple-element.110), channel_id=1, source_target_pairs={{0,8},{8,16},{16,24},{24,0},{1,9},{9,17},{17,25},{25,1},{2,10},{10... | collective-permute-start | bytes 491528 | tf_op jit(solution)/shard_map/ppermute | solution.py:24
  72.4 1.5 %collective-permute-start.21 = (bf16[80,1024]{1,0:T(8,128)(2,1)S(1)}, bf16[80,1024]{1,0:T(8,128)(2,1)S(1)}, u32[]{:S(2)}, u32[]{:S(2)}) collective-permute-start(bf16[80,1024]{1,0:T(8,128)(2,1)S(1)} %get-tuple-element.111), channel_id=1, source_target_pairs={{0,24},{8,0},{16,8},{24,16},{1,25},{9,1},{17,9},{25,17},{2,26},{10... | collective-permute-start | bytes 491528 | tf_op jit(solution)/shard_map/ppermute | solution.py:24
  73.9 1.3 %home.1.own = f32[1040,1024]{1,0:T(8,128)S(1)} custom-call(f32[2,1040,1024]{2,1,0:T(8,128)S(1)} %sums.1.near, bf16[448,1024]{1,0:T(8,128)(2,1)S(1)} %get-tuple-element.101.x, bf16[448,1024]{1,0:T(8,128)(2,1)S(1)} %get-tuple-element.102.d, bf16[2,448,512]{2,1,0:T(8,128)(2,1)S(1)} %get-tuple-element.103.dpre, bf16[2,448,512]{2,1,0:T(8,128)(2,1)S(1)} %get-tuple-element.104.hidden), custom_call_target="tpu_custom_call" | custom-call | flops 939524096 | bytes 16449536 | tf_op jit(solution)/shard_map/home/pallas_call | solution.py:47
  75.2 0.0 collective-permute-done.23.got
  75.2 0.4 merge.1
  75.6 1.8 %collective-permute-start.24 = (bf16[272,1024]{1,0:T(8,128)(2,1)S(1)}, bf16[272,1024]{1,0:T(8,128)(2,1)S(1)}, u32[]{:S(2)}, u32[]{:S(2)}) collective-permute-start(bf16[272,1024]{1,0:T(8,128)(2,1)S(1)} %get-tuple-element.117), channel_id=1, source_target_pairs={{0,4},{2,6},{4,0},{6,2},{1,5},{3,7},{5,1},{7,3},{8,12},{10,14},{12... | collective-permute-start | bytes 1671176 | tf_op jit(solution)/shard_map/ppermute | solution.py:24
  77.4 1.3 %collective-permute-start.25 = (bf16[272,1024]{1,0:T(8,128)(2,1)S(1)}, bf16[272,1024]{1,0:T(8,128)(2,1)S(1)}, u32[]{:S(2)}, u32[]{:S(2)}) collective-permute-start(bf16[272,1024]{1,0:T(8,128)(2,1)S(1)} %get-tuple-element.118), channel_id=1, source_target_pairs={{0,6},{2,0},{4,2},{6,4},{1,7},{3,1},{5,3},{7,5},{8,14},{10,8},{12,... | collective-permute-start | bytes 1671176 | tf_op jit(solution)/shard_map/ppermute | solution.py:24
  78.8 9.9 %collective-permute-done.20.refs_4_ = bf16[80,1024]{1,0:T(8,128)(2,1)S(1)} collective-permute-done((bf16[80,1024]{1,0:T(8,128)(2,1)S(1)}, bf16[80,1024]{1,0:T(8,128)(2,1)S(1)}, u32[]{:S(2)}, u32[]{:S(2)}) %collective-permute-start.20) | collective-permute-done | bytes 163872 | tf_op jit(solution)/shard_map/ppermute | solution.py:24
  88.6 0.0 collective-permute-start.26
  88.6 0.3 collective-permute-done.21.refs_5_
  89.0 0.3 sum_z.1
  89.3 14.2 %all_to_all.5.pieces = bf16[4,80,1024]{2,1,0:T(8,128)(2,1)S(1)} all-to-all(bf16[4,80,1024]{2,1,0:T(8,128)(2,1)S(1)} %sum_z.1), channel_id=1, replica_groups=mesh['x'=4,'z'=4,'y'=4,'c'=2] {'x'}, dimensions={0} | all-to-all | bytes 1310720 | tf_op jit(solution)/shard_map/all_to_all | solution.py:468
  103.5 1.2 %finish.1 = (bf16[128,1024]{1,0:T(8,128)(2,1)}, f32[2,128]{1,0:T(2,128)}) custom-call(s32[2,128]{1,0:T(2,128)S(1)} %copy-done.3, bf16[2,128]{1,0:T(2,128)(2,1)S(1)} %bitcast.5, bf16[4,80,1024]{2,1,0:T(8,128)(2,1)S(1)} %all_to_all.5.pieces), custom_call_target="tpu_custom_call" | custom-call | bytes 920064 | tf_op jit(solution)/shard_map/finish/pallas_call | solution.py:47
  104.7 1.0 last.1
  (18 shorter events, 0.1 us)
Async XLA Ops:
  3.6 9.4 %collective-permute-start.2 = (bf16[2,64,1024]{2,1,0:T(8,128)(2,1)}, bf16[2,64,1024]{2,1,0:T(8,128)(2,1)S(1)}, u32[]{:S(2)}, u32[]{:S(2)}) collective-permute-start(bf16[2,64,1024]{2,1,0:T(8,128)(2,1)} %get-tuple-element.68), channel_id=1, source_target_pairs={{0,32},{32,64},{64,96},{96,0},{1,33},{33,65},{65,97},{97,1},{2,34}... | collective-permute-start | bytes 786440 | tf_op jit(solution)/shard_map/ppermute | solution.py:24
  5.2 11.0 %collective-permute-start.3 = (bf16[2,64,1024]{2,1,0:T(8,128)(2,1)}, bf16[2,64,1024]{2,1,0:T(8,128)(2,1)S(1)}, u32[]{:S(2)}, u32[]{:S(2)}) collective-permute-start(bf16[2,64,1024]{2,1,0:T(8,128)(2,1)} %get-tuple-element.70), channel_id=1, source_target_pairs={{0,96},{32,0},{64,32},{96,64},{1,97},{33,1},{65,33},{97,65},{2,98}... | collective-permute-start | bytes 786440 | tf_op jit(solution)/shard_map/ppermute | solution.py:24
  6.9 10.1 %collective-permute-start.1 = (bf16[144,1024]{1,0:T(8,128)(2,1)}, bf16[144,1024]{1,0:T(8,128)(2,1)S(1)}, u32[]{:S(2)}, u32[]{:S(2)}) collective-permute-start(bf16[144,1024]{1,0:T(8,128)(2,1)} %get-tuple-element.67), channel_id=1, source_target_pairs={{0,24},{8,0},{16,8},{24,16},{1,25},{9,1},{17,9},{25,17},{2,26},{10... | collective-permute-start | bytes 884744 | tf_op jit(solution)/shard_map/ppermute | solution.py:24
  11.0 9.3 %collective-permute-start = (bf16[144,1024]{1,0:T(8,128)(2,1)}, bf16[144,1024]{1,0:T(8,128)(2,1)S(1)}, u32[]{:S(2)}, u32[]{:S(2)}) collective-permute-start(bf16[144,1024]{1,0:T(8,128)(2,1)} %get-tuple-element.67), channel_id=1, source_target_pairs={{0,8},{8,16},{16,24},{24,0},{1,9},{9,17},{17,25},{25,1},{2,10},{10... | collective-permute-start | bytes 884744 | tf_op jit(solution)/shard_map/ppermute | solution.py:24
  11.0 18.4 %collective-permute-start.8 = (bf16[272,1024]{1,0:T(8,128)(2,1)}, bf16[272,1024]{1,0:T(8,128)(2,1)S(1)}, u32[]{:S(2)}, u32[]{:S(2)}) collective-permute-start(bf16[272,1024]{1,0:T(8,128)(2,1)} %get-tuple-element.75.refs_12_), channel_id=1, source_target_pairs={{0,1},{1,0},{2,3},{3,2},{4,5},{5,4},{6,7},{7,6},{8,9},{9,8},{10,11... | collective-permute-start | bytes 1671176 | tf_op jit(solution)/shard_map/ppermute | solution.py:24
  13.0 16.4 %collective-permute-start.7 = (bf16[272,1024]{1,0:T(8,128)(2,1)}, bf16[272,1024]{1,0:T(8,128)(2,1)S(1)}, u32[]{:S(2)}, u32[]{:S(2)}) collective-permute-start(bf16[272,1024]{1,0:T(8,128)(2,1)} %get-tuple-element.75.refs_12_), channel_id=1, source_target_pairs={{0,6},{2,0},{4,2},{6,4},{1,7},{3,1},{5,3},{7,5},{8,14},{10,8},{12,... | collective-permute-start | bytes 1671176 | tf_op jit(solution)/shard_map/ppermute | solution.py:24
  16.2 14.6 %collective-permute-start.6 = (bf16[272,1024]{1,0:T(8,128)(2,1)}, bf16[272,1024]{1,0:T(8,128)(2,1)S(1)}, u32[]{:S(2)}, u32[]{:S(2)}) collective-permute-start(bf16[272,1024]{1,0:T(8,128)(2,1)} %get-tuple-element.75.refs_12_), channel_id=1, source_target_pairs={{0,2},{2,4},{4,6},{6,0},{1,3},{3,5},{5,7},{7,1},{8,10},{10,12},{12... | collective-permute-start | bytes 1671176 | tf_op jit(solution)/shard_map/ppermute | solution.py:24
  20.4 10.5 %collective-permute-start.5 = (bf16[144,1024]{1,0:T(8,128)(2,1)S(1)}, bf16[144,1024]{1,0:T(8,128)(2,1)S(1)}, u32[]{:S(2)}, u32[]{:S(2)}) collective-permute-start(bf16[144,1024]{1,0:T(8,128)(2,1)S(1)} %collective-permute-done.below), channel_id=1, source_target_pairs={{0,8},{8,16},{16,24},{24,0},{1,9},{9,17},{17,25},{25,1},{2,10},{10... | collective-permute-start | bytes 884744 | tf_op jit(solution)/shard_map/ppermute | solution.py:24
  20.4 8.1 %collective-permute-start.4 = (bf16[2,64,1024]{2,1,0:T(8,128)(2,1)}, bf16[2,64,1024]{2,1,0:T(8,128)(2,1)S(1)}, u32[]{:S(2)}, u32[]{:S(2)}) collective-permute-start(bf16[2,64,1024]{2,1,0:T(8,128)(2,1)} %get-tuple-element.73), channel_id=1, source_target_pairs={{0,64},{32,96},{64,0},{96,32},{1,65},{33,97},{65,1},{97,33},{2,66}... | collective-permute-start | bytes 786440 | tf_op jit(solution)/shard_map/ppermute | solution.py:24
  28.4 1.0 copy-start
  30.9 16.6 %collective-permute-start.11 = (bf16[272,1024]{1,0:T(8,128)(2,1)S(1)}, bf16[272,1024]{1,0:T(8,128)(2,1)S(1)}, u32[]{:S(2)}, u32[]{:S(2)}) collective-permute-start(bf16[272,1024]{1,0:T(8,128)(2,1)S(1)} %collective-permute-done.6.refs_0_.refs_13_), channel_id=1, source_target_pairs={{0,2},{2,4},{4,6},{6,0},{1,3},{3,5},{5,7},{7,1},{8,10},{10,12},{12... | collective-permute-start | bytes 1671176 | tf_op jit(solution)/shard_map/ppermute | solution.py:24
  31.1 14.1 %collective-permute-start.10 = (bf16[256,1024]{1,0:T(8,128)(2,1)S(1)}, bf16[256,1024]{1,0:T(8,128)(2,1)S(1)}, u32[]{:S(2)}, u32[]{:S(2)}) collective-permute-start(bf16[256,1024]{1,0:T(8,128)(2,1)S(1)} %join.1.refs_0_), channel_id=1, source_target_pairs={{0,24},{8,0},{16,8},{24,16},{1,25},{9,1},{17,9},{25,17},{2,26},{10... | collective-permute-start | bytes 1572872 | tf_op jit(solution)/shard_map/ppermute | solution.py:24
  34.9 12.5 %collective-permute-start.9 = (bf16[256,1024]{1,0:T(8,128)(2,1)S(1)}, bf16[256,1024]{1,0:T(8,128)(2,1)S(1)}, u32[]{:S(2)}, u32[]{:S(2)}) collective-permute-start(bf16[256,1024]{1,0:T(8,128)(2,1)S(1)} %join.1.refs_0_), channel_id=1, source_target_pairs={{0,8},{8,16},{16,24},{24,0},{1,9},{9,17},{17,25},{25,1},{2,10},{10... | collective-permute-start | bytes 1572872 | tf_op jit(solution)/shard_map/ppermute | solution.py:24
  35.5 9.8 %collective-permute-start.12 = (bf16[3,64,1024]{2,1,0:T(8,128)(2,1)S(1)}, bf16[3,64,1024]{2,1,0:T(8,128)(2,1)S(1)}, u32[]{:S(2)}, u32[]{:S(2)}) collective-permute-start(bf16[3,64,1024]{2,1,0:T(8,128)(2,1)S(1)} %get-tuple-element.80), channel_id=1, source_target_pairs={{0,32},{32,64},{64,96},{96,0},{1,33},{33,65},{65,97},{97,1},{2,34}... | collective-permute-start | bytes 1179656 | tf_op jit(solution)/shard_map/ppermute | solution.py:24
  35.8 9.4 %collective-permute-start.13 = (bf16[3,64,1024]{2,1,0:T(8,128)(2,1)S(1)}, bf16[3,64,1024]{2,1,0:T(8,128)(2,1)S(1)}, u32[]{:S(2)}, u32[]{:S(2)}) collective-permute-start(bf16[3,64,1024]{2,1,0:T(8,128)(2,1)S(1)} %get-tuple-element.81), channel_id=1, source_target_pairs={{0,96},{32,0},{64,32},{96,64},{1,97},{33,1},{65,33},{97,65},{2,98}... | collective-permute-start | bytes 1179656 | tf_op jit(solution)/shard_map/ppermute | solution.py:24
  47.4 4.2 %copy-start.1 = (bf16[2,64,1024]{2,1,0:T(8,128)(2,1)S(1)}, bf16[2,64,1024]{2,1,0:T(8,128)(2,1)}, u32[]{:S(2)}) copy-start(bf16[2,64,1024]{2,1,0:T(8,128)(2,1)} %get-tuple-element.66.refs_0_.refs_3_) | copy-start | bytes 786436
  47.4 4.2 %copy-start.4 = (bf16[272,1024]{1,0:T(8,128)(2,1)S(1)}, bf16[272,1024]{1,0:T(8,128)(2,1)}, u32[]{:S(2)}) copy-start(bf16[272,1024]{1,0:T(8,128)(2,1)} %get-tuple-element.75.refs_12_) | copy-start | bytes 1671172
  47.4 4.2 %copy-start.5 = (bf16[1,1024]{1,0:T(2,128)(2,1)S(1)}, bf16[1,1024]{1,0:T(2,128)(2,1)}, u32[]{:S(2)}) copy-start(bf16[1,1024]{1,0:T(2,128)(2,1)} %refs_18_.3) | copy-start | bytes 6148
  47.6 4.1 %collective-permute-start.14 = (bf16[3,272,1024]{2,1,0:T(8,128)(2,1)S(1)}, bf16[3,272,1024]{2,1,0:T(8,128)(2,1)S(1)}, u32[]{:S(2)}, u32[]{:S(2)}) collective-permute-start(bf16[3,272,1024]{2,1,0:T(8,128)(2,1)S(1)} %stack.1), channel_id=1, source_target_pairs={{0,1},{1,0},{2,3},{3,2},{4,5},{5,4},{6,7},{7,6},{8,9},{9,8},{10,11... | collective-permute-start | bytes 5013512 | tf_op jit(solution)/shard_map/ppermute | solution.py:24
  47.7 14.9 %collective-permute-start.17 = (bf16[128,1024]{1,0:T(8,128)(2,1)S(1)}, bf16[128,1024]{1,0:T(8,128)(2,1)S(1)}, u32[]{:S(2)}, u32[]{:S(2)}) collective-permute-start(bf16[128,1024]{1,0:T(8,128)(2,1)S(1)} %slice.7), channel_id=1, source_target_pairs={{0,24},{8,0},{16,8},{24,16},{1,25},{9,1},{17,9},{25,17},{2,26},{10... | collective-permute-start | bytes 786440 | tf_op jit(solution)/shard_map/ppermute | solution.py:24
  48.8 13.9 %collective-permute-start.16 = (bf16[128,1024]{1,0:T(8,128)(2,1)S(1)}, bf16[128,1024]{1,0:T(8,128)(2,1)S(1)}, u32[]{:S(2)}, u32[]{:S(2)}) collective-permute-start(bf16[128,1024]{1,0:T(8,128)(2,1)S(1)} %slice.6), channel_id=1, source_target_pairs={{0,8},{8,16},{16,24},{24,0},{1,9},{9,17},{17,25},{25,1},{2,10},{10... | collective-permute-start | bytes 786440 | tf_op jit(solution)/shard_map/ppermute | solution.py:24
  49.8 12.9 %collective-permute-start.15 = (bf16[3,64,1024]{2,1,0:T(8,128)(2,1)S(1)}, bf16[3,64,1024]{2,1,0:T(8,128)(2,1)S(1)}, u32[]{:S(2)}, u32[]{:S(2)}) collective-permute-start(bf16[3,64,1024]{2,1,0:T(8,128)(2,1)S(1)} %get-tuple-element.92), channel_id=1, source_target_pairs={{0,64},{32,96},{64,0},{96,32},{1,65},{33,97},{65,1},{97,33},{2,66}... | collective-permute-start | bytes 1179656 | tf_op jit(solution)/shard_map/ppermute | solution.py:24
  55.9 12.7 %collective-permute-start.18 = (bf16[208,1024]{1,0:T(8,128)(2,1)S(1)}, bf16[208,1024]{1,0:T(8,128)(2,1)S(1)}, u32[]{:S(2)}, u32[]{:S(2)}) collective-permute-start(bf16[208,1024]{1,0:T(8,128)(2,1)S(1)} %get-tuple-element.105), channel_id=1, source_target_pairs={{0,8},{8,16},{16,24},{24,0},{1,9},{9,17},{17,25},{25,1},{2,10},{10... | collective-permute-start | bytes 1277960 | tf_op jit(solution)/shard_map/ppermute | solution.py:24
  56.0 12.6 %collective-permute-start.19 = (bf16[208,1024]{1,0:T(8,128)(2,1)S(1)}, bf16[208,1024]{1,0:T(8,128)(2,1)S(1)}, u32[]{:S(2)}, u32[]{:S(2)}) collective-permute-start(bf16[208,1024]{1,0:T(8,128)(2,1)S(1)} %get-tuple-element.106), channel_id=1, source_target_pairs={{0,24},{8,0},{16,8},{24,16},{1,25},{9,1},{17,9},{25,17},{2,26},{10... | collective-permute-start | bytes 1277960 | tf_op jit(solution)/shard_map/ppermute | solution.py:24
  68.6 6.7 %collective-permute-start.23 = (bf16[1040,1024]{1,0:T(8,128)(2,1)S(1)}, bf16[1040,1024]{1,0:T(8,128)(2,1)S(1)}, u32[]{:S(2)}, u32[]{:S(2)}) collective-permute-start(bf16[1040,1024]{1,0:T(8,128)(2,1)S(1)} %away.1), channel_id=1, source_target_pairs={{0,1},{1,0},{2,3},{3,2},{4,5},{5,4},{6,7},{7,6},{8,9},{9,8},{10,11... | collective-permute-start | bytes 6389768 | tf_op jit(solution)/shard_map/ppermute | solution.py:24
  68.6 20.4 %collective-permute-start.22 = (bf16[272,1024]{1,0:T(8,128)(2,1)S(1)}, bf16[272,1024]{1,0:T(8,128)(2,1)S(1)}, u32[]{:S(2)}, u32[]{:S(2)}) collective-permute-start(bf16[272,1024]{1,0:T(8,128)(2,1)S(1)} %get-tuple-element.112), channel_id=1, source_target_pairs={{0,16},{8,24},{16,0},{24,8},{1,17},{9,25},{17,1},{25,9},{2,18},{10... | collective-permute-start | bytes 1671176 | tf_op jit(solution)/shard_map/ppermute | solution.py:24
  70.7 18.0 %collective-permute-start.20 = (bf16[80,1024]{1,0:T(8,128)(2,1)S(1)}, bf16[80,1024]{1,0:T(8,128)(2,1)S(1)}, u32[]{:S(2)}, u32[]{:S(2)}) collective-permute-start(bf16[80,1024]{1,0:T(8,128)(2,1)S(1)} %get-tuple-element.110), channel_id=1, source_target_pairs={{0,8},{8,16},{16,24},{24,0},{1,9},{9,17},{17,25},{25,1},{2,10},{10... | collective-permute-start | bytes 491528 | tf_op jit(solution)/shard_map/ppermute | solution.py:24
  72.4 16.6 %collective-permute-start.21 = (bf16[80,1024]{1,0:T(8,128)(2,1)S(1)}, bf16[80,1024]{1,0:T(8,128)(2,1)S(1)}, u32[]{:S(2)}, u32[]{:S(2)}) collective-permute-start(bf16[80,1024]{1,0:T(8,128)(2,1)S(1)} %get-tuple-element.111), channel_id=1, source_target_pairs={{0,24},{8,0},{16,8},{24,16},{1,25},{9,1},{17,9},{25,17},{2,26},{10... | collective-permute-start | bytes 491528 | tf_op jit(solution)/shard_map/ppermute | solution.py:24
  75.6 29.1 %collective-permute-start.24 = (bf16[272,1024]{1,0:T(8,128)(2,1)S(1)}, bf16[272,1024]{1,0:T(8,128)(2,1)S(1)}, u32[]{:S(2)}, u32[]{:S(2)}) collective-permute-start(bf16[272,1024]{1,0:T(8,128)(2,1)S(1)} %get-tuple-element.117), channel_id=1, source_target_pairs={{0,4},{2,6},{4,0},{6,2},{1,5},{3,7},{5,1},{7,3},{8,12},{10,14},{12... | collective-permute-start | bytes 1671176 | tf_op jit(solution)/shard_map/ppermute | solution.py:24
  77.4 27.2 %collective-permute-start.25 = (bf16[272,1024]{1,0:T(8,128)(2,1)S(1)}, bf16[272,1024]{1,0:T(8,128)(2,1)S(1)}, u32[]{:S(2)}, u32[]{:S(2)}) collective-permute-start(bf16[272,1024]{1,0:T(8,128)(2,1)S(1)} %get-tuple-element.118), channel_id=1, source_target_pairs={{0,6},{2,0},{4,2},{6,4},{1,7},{3,1},{5,3},{7,5},{8,14},{10,8},{12,... | collective-permute-start | bytes 1671176 | tf_op jit(solution)/shard_map/ppermute | solution.py:24
  88.6 16.1 %collective-permute-start.26 = (bf16[272,1024]{1,0:T(8,128)(2,1)S(1)}, bf16[272,1024]{1,0:T(8,128)(2,1)S(1)}, u32[]{:S(2)}, u32[]{:S(2)}) collective-permute-start(bf16[272,1024]{1,0:T(8,128)(2,1)S(1)} %get-tuple-element.119), channel_id=1, source_target_pairs={{0,2},{2,4},{4,6},{6,0},{1,3},{3,5},{5,7},{7,1},{8,10},{10,12},{12... | collective-permute-start | bytes 1671176 | tf_op jit(solution)/shard_map/ppermute | solution.py:24
  89.0 14.5 %copy-start.2 = (bf16[128,2]{0,1:T(2,128)(2,1)S(1)}, bf16[128,2]{0,1:T(2,128)(2,1)}, u32[]{:S(2)}) copy-start(bf16[128,2]{0,1:T(2,128)(2,1)} %param.13) | copy-start | bytes 1540
  89.0 14.5 %copy-start.3 = (s32[2,128]{1,0:T(2,128)S(1)}, s32[2,128]{1,0:T(2,128)}, u32[]{:S(2)}) copy-start(s32[2,128]{1,0:T(2,128)} %get-tuple-element.65.places) | copy-start | bytes 3076
